TPU v7x, 256 devices: a whole 4x4x8 slice. The times are simulated.
256 devices in a mesh: seq: 32 (over x, z_lo, core), mp: 8 (over z_hi, y).
Axes of the slice: x: 4, y: 4, z: 8 (z_hi: 2, z_lo: 4; z = z_hi * 4 + z_lo), core: 2. Of those that a mesh axis runs over, the one named last changes fastest.
Arguments:
- tokens: bfloat16 [16384, 4096], P('seq'), may hold values from -6 to 6
- in_weight: bfloat16 [3, 4096, 4096], P(None, 'seq', 'mp'), may hold values from -0.09375 to 0.09375
- short_filter: float32 [3, 7, 4096], P(None, None, 'mp'), may hold values from -2.4 to 2.4
- residues: float32 [4096, 16], P('mp'), may hold values from -2.1 to 2.1
- rates: float32 [4096, 16], P('mp'), may hold values from 3.0517578e-05 to 0.05
- skip: float32 [4096], P('mp'), may hold values from -4 to 4
Outputs:
- mixed: bfloat16 [16384, 4096], P('seq', 'mp')
All inputs are finite; a program needn't handle non-finite values.
Results may differ from a plain program's by a relative error of at most 0.0065.
Values may be sent and summed in bfloat16 or wider, within the bound.
No kernel may reach another device: no remote copies, remote signals or barrier semaphores. Data moves between devices by JAX's collectives and lax.ppermute only.
A program may use at most 128 MiB of HBM per device.

v0:
```python
import math

import jax
import jax.numpy as jnp
from jax import lax
from jax.sharding import PartitionSpec as P

SHORT = 7
RADIX = 16


exact = lax.Precision.HIGHEST


def from_behind(value, axis, steps):
    count = lax.axis_size(axis)
    leading, last = (max(0, -steps), min(count, count - steps))
    return lax.ppermute(value, axis, [(source, source + steps) for source in range(leading, last)])


def twiddles(row_index, col_index, modulus, sign):
    product = row_index[:, None] * col_index[None, :] % modulus
    angle = sign * 2.0 * math.pi / modulus * product.astype(jnp.float32)
    return (jnp.cos(angle), jnp.sin(angle))


def apply_dft(cosine, sine, real_part, imag_part, form):
    new_real = jnp.einsum(form, cosine, real_part, precision=exact) - jnp.einsum(
        form, sine, imag_part, precision=exact
    )
    new_imag = jnp.einsum(form, cosine, imag_part, precision=exact) + jnp.einsum(
        form, sine, real_part, precision=exact
    )
    return (new_real, new_imag)


def rotate(real_part, imag_part, cosine, sine):
    return (real_part * cosine - imag_part * sine, real_part * sine + imag_part * cosine)


def outer_forward(block, seq_count, my_index):
    length, channels = block.shape
    group_rows = length // seq_count
    outer_points = 2 * seq_count
    cube = block.reshape(seq_count, group_rows, channels)
    cosine, sine = twiddles(jnp.arange(outer_points), jnp.arange(seq_count), outer_points, -1.0)
    real_part = jnp.einsum("ka,agc->kgc", cosine, cube, precision=exact)
    imag_part = jnp.einsum("ka,agc->kgc", sine, cube, precision=exact)
    positions = my_index * group_rows + jnp.arange(group_rows)
    cosine, sine = twiddles(jnp.arange(outer_points), positions, 2 * length * seq_count, -1.0)
    real_part, imag_part = rotate(real_part, imag_part, cosine[:, :, None], sine[:, :, None])
    return jnp.stack([real_part, imag_part])


def inner_forward(spectra):
    length, channels = (spectra.shape[2], spectra.shape[3])
    radix_two = length // RADIX
    real_part = spectra[0].reshape(2, RADIX, radix_two, channels)
    imag_part = spectra[1].reshape(2, RADIX, radix_two, channels)
    cosine, sine = twiddles(jnp.arange(RADIX), jnp.arange(RADIX), RADIX, -1.0)
    real_part, imag_part = apply_dft(cosine, sine, real_part, imag_part, "kj,bjmc->bkmc")
    cosine, sine = twiddles(jnp.arange(RADIX), jnp.arange(radix_two), length, -1.0)
    real_part, imag_part = rotate(
        real_part, imag_part, cosine[None, :, :, None], sine[None, :, :, None]
    )
    cosine, sine = twiddles(jnp.arange(radix_two), jnp.arange(radix_two), radix_two, -1.0)
    return apply_dft(cosine, sine, real_part, imag_part, "km,bjmc->bjkc")


def inner_inverse(real_part, imag_part):
    radix_two, channels = (real_part.shape[2], real_part.shape[3])
    length = RADIX * radix_two
    cosine, sine = twiddles(jnp.arange(radix_two), jnp.arange(radix_two), radix_two, 1.0)
    real_part, imag_part = apply_dft(cosine, sine, real_part, imag_part, "jm,bkmc->bkjc")
    cosine, sine = twiddles(jnp.arange(RADIX), jnp.arange(radix_two), length, 1.0)
    real_part, imag_part = rotate(
        real_part, imag_part, cosine[None, :, :, None], sine[None, :, :, None]
    )
    cosine, sine = twiddles(jnp.arange(RADIX), jnp.arange(RADIX), RADIX, 1.0)
    real_part, imag_part = apply_dft(cosine, sine, real_part, imag_part, "jk,bkmc->bjmc")
    return jnp.stack(
        [real_part.reshape(2, length, channels), imag_part.reshape(2, length, channels)]
    )


def outer_inverse(spectra, seq_count, my_index):
    outer_points, group_rows = (spectra.shape[1], spectra.shape[2])
    length = group_rows * seq_count
    positions = my_index * group_rows + jnp.arange(group_rows)
    cosine, sine = twiddles(jnp.arange(outer_points), positions, 2 * length * seq_count, 1.0)
    real_part, imag_part = rotate(spectra[0], spectra[1], cosine[:, :, None], sine[:, :, None])
    cosine, sine = twiddles(jnp.arange(seq_count), jnp.arange(outer_points), outer_points, 1.0)
    result = jnp.einsum("ak,kgc->agc", cosine, real_part, precision=exact) - jnp.einsum(
        "ak,kgc->agc", sine, imag_part, precision=exact
    )
    return result / (2.0 * length * seq_count)


def local_filter(residues, rates, positions):

    def add_mode(which, total):
        decay_rate = rates[:, which]
        scale = residues[:, which] * jnp.sqrt(-jnp.expm1(-2.0 * decay_rate))
        return total + scale[None, :] * jnp.exp(-positions[:, None] * decay_rate[None, :])

    empty = jnp.zeros((positions.shape[0], residues.shape[0]), jnp.float32)
    return lax.fori_loop(0, residues.shape[1], add_mode, empty)


def local(tokens, in_weight, short_filter, residues, rates, skip):
    seq_count = lax.axis_size("seq")
    my_index = lax.axis_index("seq")
    length = tokens.shape[0]
    channels = skip.shape[0]
    projected = jnp.einsum(
        "td,sdc->stc",
        tokens,
        lax.all_gather(in_weight, "seq", axis=1, tiled=True),
        preferred_element_type=jnp.float32,
    ).astype(jnp.bfloat16)
    tail_rows = projected[:, length - (SHORT - 1) :, :]
    before = from_behind(tail_rows, "seq", 1)
    extended = jnp.concatenate([before, projected], axis=1).astype(jnp.float32)
    features = jnp.zeros((3, length, channels), jnp.float32)
    for offset in range(SHORT):
        start = SHORT - 1 - offset
        features = (
            features + short_filter[:, offset, None, :] * extended[:, start : start + length, :]
        )
    signal = features[1] * features[2]
    positions = (my_index * length + jnp.arange(length)).astype(jnp.float32)
    filt = local_filter(residues, rates, positions)
    signal_cols, filter_cols = (
        lax.all_to_all(signal, "seq", split_axis=0, concat_axis=0, tiled=True),
        lax.all_to_all(filt, "seq", split_axis=0, concat_axis=0, tiled=True),
    )
    signal_part = outer_forward(signal_cols, seq_count, my_index)
    filter_part = outer_forward(filter_cols, seq_count, my_index)
    signal_spec, filter_spec = (
        lax.all_to_all(signal_part, "seq", split_axis=1, concat_axis=2, tiled=True),
        lax.all_to_all(filter_part, "seq", split_axis=1, concat_axis=2, tiled=True),
    )
    signal_real, signal_imag = inner_forward(signal_spec)
    filter_real, filter_imag = inner_forward(filter_spec)
    product_real = signal_real * filter_real - signal_imag * filter_imag
    product_imag = signal_real * filter_imag + signal_imag * filter_real
    partial_value = inner_inverse(product_real, product_imag)
    partial_value = lax.all_to_all(partial_value, "seq", split_axis=2, concat_axis=1, tiled=True)
    results = outer_inverse(partial_value, seq_count, my_index)
    conv = lax.all_to_all(results, "seq", split_axis=0, concat_axis=1, tiled=True).reshape(
        length, channels
    )
    return (features[0] * (conv + skip[None, :] * signal)).astype(jnp.bfloat16)


def solution(mesh):
    placed = (
        P("seq", None),
        P(None, "seq", "mp"),
        P(None, None, "mp"),
        P("mp", None),
        P("mp", None),
        P("mp"),
    )
    return jax.shard_map(
        local, mesh=mesh, in_specs=placed, out_specs=P("seq", "mp"), check_vma=False
    )
```

profile of v0, /device:TPU:1, one launch (start us, length us, event | category | flops | bytes accessed | tf_op | source)
XLA Modules:
  0.0 619.5 jit_solution(9507568941011222675)
XLA Ops:
  7.3 62.1 %while.16 = (s32[]{:T(128)}, f32[512,512]{1,0:T(8,128)}, f32[512,16]{0,1:T(8,128)}, f32[512,16]{0,1:T(8,128)}, s32[]{:T(128)}, /*index=5*/s32[]{:T(128)}, s32[]{:T(128)}) while((s32[]{:T(128)}, f32[512,512]{1,0:T(8,128)}, f32[512,16]{0,1:T(8,128)}, f32[512,16]{0,1:T(8,128)}, s32[]{:T(128)}, /*index=5*/s32[]{:T(128)}, ...), condition=%wide.region_1.0_spmd.clone, body=%wide.region_0.0_spmd.clone.sunk | while | flops 1051651 | bytes 2119779 | solution.py:107
  11.5 2.5 select_add_fusion.2
  15.4 2.5 select_add_fusion.2
  19.4 2.5 select_add_fusion.2
  23.3 2.5 select_add_fusion.2
  27.2 2.5 select_add_fusion.2
  31.2 2.5 select_add_fusion.2
  35.2 2.5 select_add_fusion.2
  39.2 2.5 select_add_fusion.2
  43.1 2.5 select_add_fusion.2
  47.1 2.5 select_add_fusion.2
  51.1 2.5 select_add_fusion.2
  55.0 2.5 select_add_fusion.2
  59.0 2.5 select_add_fusion.2
  63.0 2.5 select_add_fusion.2
  66.9 2.5 select_add_fusion.2
  69.4 10.2 %all-to-all-start.2 = ((f32[32,16,512]{2,1,0:T(8,128)}), f32[32,16,512]{2,1,0:T(8,128)}, u32[]{:S(2)}, u32[]{:S(2)}) async-start(f32[32,16,512]{2,1,0:T(8,128)} %bitcast.26), calls=%async_computation.2 | async-start | bytes 2097152 | tf_op jit(solution)/shard_map/all_to_all | solution.py:135
  79.7 23.5 %all-gather.2.cloned.1.call-done = bf16[3,4096,512]{2,1,0:T(8,128)(2,1)} async-done(((bf16[3,128,512]{2,1,0:T(8,128)(2,1)}), bf16[3,4096,512]{2,1,0:T(8,128)(2,1)}) %all-gather.2.cloned.1.call-update) | async-done | bytes 12582928 | tf_op jit(solution)/shard_map/all_gather | solution.py:118
  103.2 10.9 %fusion.105 = bf16[3,512,512]{2,1,0:T(8,128)(2,1)S(1)} fusion(bf16[3,4096,512]{2,1,0:T(8,128)(2,1)} %all-gather.2.cloned.1.call-done, bf16[512,4096]{1,0:T(8,128)(2,1)} %param.8), kind=kOutput, calls=%fused_computation.116 | convolution fusion | flops 6443237376 | bytes 18350080 | tf_op jit(solution)/shard_map/td,sdc->stc/dot_general | solution.py:115
  114.1 12.4 %collective-permute-start = (bf16[3,6,512]{2,1,0:T(8,128)(2,1)S(1)}, bf16[3,6,512]{2,1,0:T(8,128)(2,1)S(1)}, u32[]{:S(2)}, u32[]{:S(2)}) collective-permute-start(bf16[3,6,512]{2,1,0:T(8,128)(2,1)S(1)} %slice.102), channel_id=1, source_target_pairs={{0,8},{8,16},{16,24},{24,32},{32,40},{40,48},{48,56},{56,64},{64,7... | collective-permute-start | bytes 55304 | tf_op jit(solution)/shard_map/ppermute | solution.py:18
  128.0 2.6 fusion.4
  131.8 5.2 all-to-all-start
  137.2 5.0 fusion.117
  142.1 4.9 fusion.119
  147.1 17.4 %all-to-all-done = f32[32,16,512]{2,1,0:T(8,128)} async-done(((f32[32,16,512]{2,1,0:T(8,128)}), f32[32,16,512]{2,1,0:T(8,128)}, u32[]{:S(2)}, u32[]{:S(2)}) %all-to-all-start) | async-done | bytes 1048608 | tf_op jit(solution)/shard_map/all_to_all | solution.py:134
  164.5 3.7 fusion.121
  168.2 7.1 %subtract_bitcast_fusion.2 = (f32[1,64,16,512]{3,1,2,0:T(8,128)}, f32[1,64,16,512]{3,1,2,0:T(8,128)}, f32[1,64,16,512]{3,1,2,0:T(8,128)S(1)}, f32[1,64,16,512]{3,1,2,0:T(8,128)S(1)}) fusion(f32[64,16,512]{2,0,1:T(8,128)S(1)} %copy-done.2, f32[64,16,512]{2,0,1:T(8,128)} %fusion.119, f32[64,16]{0,1:T(8,128)S(1)} %get-tuple-element.200, ...), kind=kOutput, calls=%fused_computation.61 | convolution fusion | flops 207646720 | bytes 15736832 | tf_op jit(solution)/shard_map/ka,agc->kgc/dot_general | solution.py:47
  175.9 4.6 copy.173
  180.5 4.8 all-to-all-start.1
  185.2 2.8 pad_maximum_fusion.1
  188.0 4.4 copy.187
  192.4 87.4 %all-to-all-done.1 = f32[2,64,16,512]{3,2,0,1:T(8,128)} async-done(((f32[2,64,16,512]{3,2,0,1:T(8,128)}), f32[2,64,16,512]{3,2,0,1:T(8,128)}, u32[]{:S(2)}, u32[]{:S(2)}) %all-to-all-start.1) | async-done | bytes 4194336 | tf_op jit(solution)/shard_map/all_to_all | solution.py:140
  279.9 5.6 all-to-all-start.3
  285.8 2.6 copy.174
  290.7 4.5 fusion.62
  295.2 4.6 fusion.60
  299.8 80.3 %all-to-all-done.3 = f32[2,64,16,512]{3,2,0,1:T(8,128)} async-done(((f32[2,64,16,512]{3,2,0,1:T(8,128)}), f32[2,64,16,512]{3,2,0,1:T(8,128)}, u32[]{:S(2)}, u32[]{:S(2)}) %all-to-all-start.3) | async-done | bytes 4194336 | tf_op jit(solution)/shard_map/all_to_all | solution.py:141
  380.1 2.6 copy.188
  383.8 3.2 fusion.46
  387.0 3.6 fusion.44
  392.2 3.4 fusion.71
  395.7 3.4 fusion.74
  399.3 3.6 fusion.83
  402.9 4.4 fusion.20
  407.3 3.3 fusion.38
  410.6 3.5 fusion.36
  414.2 3.3 fusion.54
  417.5 3.3 fusion.52
  420.8 3.5 fusion.89
  424.4 4.0 fusion.92
  428.3 3.5 fusion.77
  431.8 4.6 multiply_subtract_fusion
  443.2 2.7 subtract_bitcast_fusion.1
  445.9 3.2 fusion.30
  449.1 3.7 fusion.28
  452.8 3.4 subtract_bitcast_fusion
  457.4 3.4 add_bitcast_fusion
  462.5 5.4 copy.207
  467.9 5.6 all-to-all-start.4
  473.7 94.4 %all-to-all-done.4 = f32[2,2,512,512]{3,1,0,2:T(2,128)} async-done(((f32[2,2,512,512]{3,1,0,2:T(2,128)}), f32[2,2,512,512]{3,1,0,2:T(2,128)}, u32[]{:S(2)}, u32[]{:S(2)}) %all-to-all-start.4) | async-done | bytes 4194336 | tf_op jit(solution)/shard_map/all_to_all | solution.py:148
  568.1 3.5 copy.208
  573.4 2.4 fusion.24
  575.8 2.4 fusion.111
  578.8 32.4 %all_to_all.69 = f32[32,16,512]{2,1,0:T(8,128)S(1)} all-to-all(f32[32,16,512]{2,1,0:T(8,128)S(1)} %copy.215), channel_id=1, replica_groups=mesh['seq'=32,'mp'=8] {'seq'}, dimensions={0} | all-to-all | bytes 2097152 | tf_op jit(solution)/shard_map/all_to_all | solution.py:150
  (102 shorter events, 47.5 us)
Async XLA Ops:
  6.5 96.7 %all-gather.2.cloned.1.call-start = ((), (), s32[]{:S(2)}) async-start(), calls=%async_computation.6 | async-start | bytes 12976128 | tf_op jit(solution)/shard_map/all_gather | solution.py:118
  69.4 10.2 %copy-start.4 = (f32[3,7,512]{2,1,0:T(8,128)S(1)}, f32[3,7,512]{2,1,0:T(8,128)}, u32[]{:S(2)}) copy-start(f32[3,7,512]{2,1,0:T(8,128)} %param.10) | copy-start | bytes 129028
  69.4 62.4 %all-to-all-start.2 = ((f32[32,16,512]{2,1,0:T(8,128)}), f32[32,16,512]{2,1,0:T(8,128)}, u32[]{:S(2)}, u32[]{:S(2)}) async-start(f32[32,16,512]{2,1,0:T(8,128)} %bitcast.26), calls=%async_computation.2 | async-start | bytes 2097152 | tf_op jit(solution)/shard_map/all_to_all | solution.py:135
  114.1 13.4 %collective-permute-start = (bf16[3,6,512]{2,1,0:T(8,128)(2,1)S(1)}, bf16[3,6,512]{2,1,0:T(8,128)(2,1)S(1)}, u32[]{:S(2)}, u32[]{:S(2)}) collective-permute-start(bf16[3,6,512]{2,1,0:T(8,128)(2,1)S(1)} %slice.102), channel_id=1, source_target_pairs={{0,8},{8,16},{16,24},{24,32},{32,40},{40,48},{48,56},{56,64},{64,7... | collective-permute-start | bytes 55304 | tf_op jit(solution)/shard_map/ppermute | solution.py:18
  131.8 32.7 %all-to-all-start = ((f32[32,16,512]{2,1,0:T(8,128)}), f32[32,16,512]{2,1,0:T(8,128)}, u32[]{:S(2)}, u32[]{:S(2)}) async-start(f32[32,16,512]{2,1,0:T(8,128)} %bitcast.248), calls=%async_computation | async-start | bytes 2097152 | tf_op jit(solution)/shard_map/all_to_all | solution.py:134
  164.5 3.8 copy-start.2
  180.5 99.4 %all-to-all-start.1 = ((f32[2,64,16,512]{3,2,0,1:T(8,128)}), f32[2,64,16,512]{3,2,0,1:T(8,128)}, u32[]{:S(2)}, u32[]{:S(2)}) async-start(f32[2,64,16,512]{3,2,0,1:T(8,128)} %copy.173), calls=%async_computation.1 | async-start | bytes 8388608 | tf_op jit(solution)/shard_map/all_to_all | solution.py:140
  279.9 100.3 %all-to-all-start.3 = ((f32[2,64,16,512]{3,2,0,1:T(8,128)}), f32[2,64,16,512]{3,2,0,1:T(8,128)}, u32[]{:S(2)}, u32[]{:S(2)}) async-start(f32[2,64,16,512]{3,2,0,1:T(8,128)} %copy.187), calls=%async_computation.3 | async-start | bytes 8388608 | tf_op jit(solution)/shard_map/all_to_all | solution.py:141
  387.0 3.7 copy-start.3
  390.6 1.6 copy-start.1
  392.2 3.4 copy-start
  467.9 100.2 %all-to-all-start.4 = ((f32[2,2,512,512]{3,1,0,2:T(2,128)}), f32[2,2,512,512]{3,1,0,2:T(2,128)}, u32[]{:S(2)}, u32[]{:S(2)}) async-start(f32[2,2,512,512]{3,1,0,2:T(2,128)} %copy.207), calls=%async_computation.4 | async-start | bytes 8388608 | tf_op jit(solution)/shard_map/all_to_all | solution.py:148
  578.1 33.0 %copy-start.5 = (f32[512]{0:T(512)S(1)}, f32[512]{0:T(512)}, u32[]{:S(2)}) copy-start(f32[512]{0:T(512)} %param.13) | copy-start | bytes 6148
Sparse Core Ops, SparseCore 0:
  9.2 93.9 all-gather.1
where the time goes:
time: 627 us; the launch traced here: 620 us
  waiting for transfers between devices  305 us (49%)
  matrix products  119 us (19%)
  other arithmetic  60.8 us (10%)
  local copies, waits for them, and re-layouts  44.4 us (7%)
  starting transfers between devices  43.8 us (7%)
  blocking collectives  32.4 us (5%)
  between operations  14.1 us (2%)
    all_to_all x1, waiting for transfers between devices, local(): lax.all_to_all(partial_value, 'seq', split_axis=2, concat_axis=1, tiled=T...  94.4 us
    all_to_all x1, waiting for transfers between devices, local(): lax.all_to_all(signal_part, 'seq', split_axis=1, concat_axis=2, tiled=True)  87.4 us
    all_to_all x1, waiting for transfers between devices, local(): lax.all_to_all(filter_part, 'seq', split_axis=1, concat_axis=2, tiled=True)  80.3 us
    add x16, other arithmetic, add_mode(): total + scale[None, :] * jnp.exp(-positions[:, None] * decay_rate[None, :])  38.7 us
    all_to_all x1, blocking collectives, local(): lax.all_to_all(results, 'seq', split_axis=0, concat_axis=1, tiled=True)  32.4 us
    all_gather x1, waiting for transfers between devices, local(): lax.all_gather(in_weight, 'seq', axis=1, tiled=True)  23.5 us
    dot_general x6, matrix products, apply_dft(): jnp.einsum(form, sine, real_part, precision=exact)  22.5 us
    dot_general x6, matrix products, apply_dft(): jnp.einsum(form, cosine, imag_part, precision=exact)  21.1 us
  transfers between devices with their start and end apart: 7, of which 6 were waited for; matrix products, arithmetic and copies ran while one was open for 18% of the time, Pallas kernels for 0%

commit v1 on v0

v1 whole, which is shorter than its diff:
```python
import functools
import math

import jax
import jax.numpy as jnp
from jax import lax
from jax.experimental import pallas as pl
from jax.experimental.pallas import tpu as pltpu
from jax.sharding import PartitionSpec as P

SHORT = 7
X, Z, CORES = 4, 4, 2
CHIPS = X * Z
HALO = 16
LANES = 128
SEGMENTS = 8

ANY = pl.BlockSpec(memory_space=pl.ANY)
VMEM = pl.BlockSpec(memory_space=pltpu.VMEM)
SMEM = pl.BlockSpec(memory_space=pltpu.SMEM)


def place(x, z, core):
    return (x * Z + z) * CORES + core


def permute(value, target):
    pairs = []
    for x in range(X):
        for z in range(Z):
            for core in range(CORES):
                to = target(x, z, core)
                if to is not None:
                    pairs.append((place(x, z, core), place(*to)))
    return lax.ppermute(value, "seq", pairs)


def along_x(value, steps):
    return permute(value, lambda x, z, core: ((x + steps) % X, z, core))


def along_z(value, steps):
    return permute(value, lambda x, z, core: (x, (z + steps) % Z, core))


def swap_cores(value):
    return permute(value, lambda x, z, core: (x, z, 1 - core))


def next_chip(value):
    def target(x, z, core):
        chip = x * Z + z + 1
        return (chip // Z, chip % Z, core) if chip < CHIPS else None

    return permute(value, target)


def together(*values):
    return lax.optimization_barrier(values)


def gather_chips(block):
    half = block.shape[1] // 2
    up, down = along_z(block, 1), along_z(block, 3)
    right, left = along_x(block, 1), along_x(block, 3)
    up, right, left = together(up, right, left)
    (held, _) = together(block, up)
    across = along_z(held, 2)
    pieces = [(0, 0, 0, block), (1, 0, 0, right), (3, 0, 0, left)]
    previous = (0, right, left)
    for steps, source in ((1, up), (3, down), (2, across)):
        before, right, left = previous
        far_right = along_x(right[:, :half], 1)
        far_left = along_x(left[:, half:], 3)
        right, left = along_x(source, 1), along_x(source, 3)
        if steps == 1:
            right, left, far_right, far_left, down = together(right, left, far_right, far_left, down)
        elif steps == 3:
            right, left, far_right, far_left, across = together(
                right, left, far_right, far_left, across
            )
        else:
            right, left, far_right, far_left = together(right, left, far_right, far_left)
        pieces += [(2, before, 0, far_right), (2, before, half, far_left)]
        source = {1: up, 3: down, 2: across}[steps]
        pieces += [(0, steps, 0, source), (1, steps, 0, right), (3, steps, 0, left)]
        previous = (steps, right, left)
    before, right, left = previous
    pieces += [
        (2, before, 0, along_x(right[:, :half], 1)),
        (2, before, half, along_x(left[:, half:], 3)),
    ]
    return pieces


def rounded(value):
    return value.astype(jnp.bfloat16).astype(jnp.float32)


def signal_kernel(
    plan, where, *refs
):
    count = len(plan)
    pieces = refs[:count]
    mine, other, halo, taps, decay, amplitude, power = refs[count : count + 7]
    signal, start_conv, before, ends = refs[count + 7 : count + 11]
    rows, weights, key, value, sems = refs[count + 11 :]
    x, z, core = where[0], where[1], where[2]
    length, depth = mine.shape
    channels = weights.shape[2]
    steps = 2 * length // SEGMENTS
    order = ((HALO, mine, core), (HALO, other, 1 - core))
    copies = []
    offset = 0
    for at, (x_steps, z_steps, row, height) in enumerate(plan):
        chip = (x - x_steps + X) % X * Z + (z - z_steps + Z) % Z
        column = pl.multiple_of(chip * (depth // CHIPS) + row, LANES)
        group = [
            pltpu.make_async_copy(
                pieces[at], weights.at[:, pl.ds(offset, height), :], sems.at[at, 0]
            ),
            pltpu.make_async_copy(
                halo.at[:, pl.ds(column, height)],
                rows.at[pl.ds(0, HALO), pl.ds(offset, height)],
                sems.at[at, 1],
            ),
        ]
        for which, (first, array, block) in enumerate(order):
            group.append(
                pltpu.make_async_copy(
                    array.at[:, pl.ds(column, height)],
                    rows.at[
                        pl.ds(pl.multiple_of(first + block * length, HALO), length),
                        pl.ds(offset, height),
                    ],
                    sems.at[at, 2 + which],
                )
            )
        for copy in group:
            copy.start()
        copies.append((offset, height, group))
        offset += height
    parts = 4
    for part in range(parts):
        low, high = part * depth // parts, (part + 1) * depth // parts
        for offset, height, group in copies:
            if low <= offset < high:
                for copy in group:
                    copy.wait()
        last = part == parts - 1
        for stream, total in ((0, key), (1, value)):
            product = jnp.dot(
                rows[:, low:high], weights[stream, low:high, :], preferred_element_type=jnp.float32
            )
            for group in range(channels // LANES):
                share = product[:, group * LANES : (group + 1) * LANES]
                if part > 0:
                    share = total[group] + share
                total[group] = rounded(share) if last else share
    for low in range(0, channels, LANES):
        lanes = pl.ds(low, LANES)
        group = low // LANES

        def spread(ref, *index):
            return jnp.broadcast_to(ref[(*index, lanes)].reshape(1, LANES), (SEGMENTS, LANES))

        def load(ref, step):
            return ref[group, pl.ds(HALO + step, SEGMENTS, stride=steps), :]

        key_taps = [spread(taps, 1, offset) for offset in range(SHORT)]
        value_taps = [spread(taps, 2, offset) for offset in range(SHORT)]

        def featurize(step, carry):
            keys, values = carry
            keys = (load(key, step),) + keys
            values = (load(value, step),) + values
            total_key = key_taps[0] * keys[0]
            total_value = value_taps[0] * values[0]
            for offset in range(1, SHORT):
                total_key += key_taps[offset] * keys[offset]
                total_value += value_taps[offset] * values[offset]
            signal[step, :, lanes] = total_key * total_value
            return keys[:-1], values[:-1]

        lax.fori_loop(
            0,
            steps,
            featurize,
            (
                tuple(load(key, -offset) for offset in range(1, SHORT)),
                tuple(load(value, -offset) for offset in range(1, SHORT)),
            ),
            unroll=4,
        )
        modes = decay.shape[0]
        decays = [spread(decay, mode) for mode in range(modes)]
        amplitudes = [spread(amplitude, mode) for mode in range(modes)]

        def scan(step, states):
            here = signal[step, :, lanes]
            states = tuple(decays[mode] * states[mode] + here for mode in range(modes))
            terms = [amplitudes[mode] * states[mode] for mode in range(modes)]
            while len(terms) > 1:
                terms = [terms[at] + terms[at + 1] for at in range(0, len(terms), 2)]
            start_conv[step, :, lanes] = terms[0]
            return states

        empty = jnp.zeros((SEGMENTS, LANES), jnp.float32)
        states = lax.fori_loop(0, steps, scan, (empty,) * modes, unroll=2)
        segment = lax.broadcasted_iota(jnp.int32, (SEGMENTS, LANES), 0)
        for mode in range(modes):
            state = states[mode]
            for level, distance in enumerate((1, 2, 4)):
                moved = pltpu.roll(state, distance, 0)
                state = state + jnp.where(
                    segment >= distance, spread(power, level, mode) * moved, 0.0
                )
            before[mode, :, lanes] = jnp.where(segment >= 1, pltpu.roll(state, 1, 0), 0.0)
            ends[pl.ds(mode, 1), lanes] = state[SEGMENTS - 1 :, :]


def signals(where, pieces, mine, other, halo, taps, decay, amplitude, power):
    plan = tuple((x_steps, z_steps, row, array.shape[1]) for x_steps, z_steps, row, array in pieces)
    arrays = [array for _, _, _, array in pieces]
    length, depth = mine.shape
    modes, channels = decay.shape
    steps = 2 * length // SEGMENTS
    shape = jax.ShapeDtypeStruct
    return pl.pallas_call(
        functools.partial(signal_kernel, plan),
        out_shape=(
            shape((steps, SEGMENTS, channels), jnp.float32),
            shape((steps, SEGMENTS, channels), jnp.float32),
            shape((modes, SEGMENTS, channels), jnp.float32),
            shape((modes, channels), jnp.float32),
        ),
        in_specs=[SMEM] + [ANY] * (len(arrays) + 3) + [VMEM] * 4,
        out_specs=(VMEM,) * 4,
        scratch_shapes=[
            pltpu.VMEM((HALO + 2 * length, depth), jnp.bfloat16),
            pltpu.VMEM((2, depth, channels), jnp.bfloat16),
            pltpu.VMEM((channels // LANES, HALO + 2 * length, LANES), jnp.float32),
            pltpu.VMEM((channels // LANES, HALO + 2 * length, LANES), jnp.float32),
            pltpu.SemaphoreType.DMA((len(arrays), 4)),
        ],
        compiler_params=pltpu.CompilerParams(vmem_limit_bytes=48 * 1024 * 1024),
        name="signals",
    )(where, *arrays, mine, other, halo, taps, decay, amplitude, power)


def carry_kernel(
    where, signal, start_conv, before, carried, decay, amplitude, power, skip, keep, send, whole
):
    core = where[2]
    steps, _, channels = signal.shape
    length = keep.shape[0]
    modes = decay.shape[0]
    for low in range(0, channels, LANES):
        lanes = pl.ds(low, LANES)

        def spread(ref, *index):
            return jnp.broadcast_to(ref[(*index, lanes)].reshape(1, LANES), (SEGMENTS, LANES))

        direct = spread(skip, 0)
        decays = [spread(decay, mode) for mode in range(modes)]
        states = tuple(
            spread(amplitude, mode)
            * decays[mode]
            * (before[mode, :, lanes] + power[mode, :, lanes] * spread(carried, mode))
            for mode in range(modes)
        )

        def add(step, states):
            terms = list(states)
            while len(terms) > 1:
                terms = [terms[at] + terms[at + 1] for at in range(0, len(terms), 2)]
            total = start_conv[step, :, lanes] + terms[0] + direct * signal[step, :, lanes]
            whole[low // LANES, pl.ds(step, SEGMENTS, stride=steps), :] = total
            return tuple(decays[mode] * states[mode] for mode in range(modes))

        lax.fori_loop(0, steps, add, states, unroll=4)
    for group in range(channels // LANES):
        lanes = pl.ds(group * LANES, LANES)
        for out, block in ((keep, core), (send, 1 - core)):
            first = pl.multiple_of(block * length, SEGMENTS)
            out[:, lanes] = whole[group, pl.ds(first, length), :]


def carries(where, signal, start_conv, before, carried, decay, amplitude, power, skip):
    steps, _, channels = signal.shape
    length = steps * SEGMENTS // 2
    shape = jax.ShapeDtypeStruct
    return pl.pallas_call(
        carry_kernel,
        out_shape=(shape((length, channels), jnp.float32),) * 2,
        in_specs=[SMEM] + [VMEM] * 8,
        out_specs=(VMEM,) * 2,
        scratch_shapes=[pltpu.VMEM((channels // LANES, 2 * length, LANES), jnp.float32)],
        compiler_params=pltpu.CompilerParams(vmem_limit_bytes=32 * 1024 * 1024),
        name="carries",
    )(where, signal, start_conv, before, carried, decay, amplitude, power, skip)


def gate_kernel(where, tokens, halo, weight, taps, keep, taken, mixed, rows, weights, query, sems):
    core = where[2]
    length, depth = tokens.shape
    channels = weight.shape[1]
    parts = 4
    size = depth // parts
    copies = []
    for part in range(parts):
        span = pl.ds(part * size, size)
        group = (
            pltpu.make_async_copy(halo.at[:, span], rows.at[pl.ds(0, HALO), span], sems.at[part, 0]),
            pltpu.make_async_copy(
                tokens.at[:, span], rows.at[pl.ds(HALO, length), span], sems.at[part, 1]
            ),
            pltpu.make_async_copy(weight.at[span, :], weights.at[span, :], sems.at[part, 2]),
        )
        for copy in group:
            copy.start()
        copies.append(group)
    for part in range(parts):
        for copy in copies[part]:
            copy.wait()
        low, high = part * size, (part + 1) * size
        product = jnp.dot(
            rows[:, low:high], weights[low:high, :], preferred_element_type=jnp.float32
        )
        if part > 0:
            product = query[...] + product
        query[...] = rounded(product) if part == parts - 1 else product
    half = channels // 2
    block = 64
    for low in range(0, channels, LANES):
        lanes = pl.ds(low, LANES)
        inner = pl.ds(low % half, LANES)
        mine = core == low // half
        for row in range(0, length, block):
            total = taps[0, 0, lanes].reshape(1, LANES) * query[pl.ds(HALO + row, block), lanes]
            for offset in range(1, SHORT):
                total += (
                    taps[0, offset, lanes].reshape(1, LANES)
                    * query[pl.ds(HALO + row - offset, block), lanes]
                )
            span = pl.ds(row, block)
            conv = jnp.where(mine, keep[span, inner], taken[span, inner])
            mixed[span, lanes] = (total * conv).astype(jnp.bfloat16)


def gated(where, tokens, halo, weight, taps, keep, taken):
    length, depth = tokens.shape
    channels = weight.shape[1]
    return pl.pallas_call(
        gate_kernel,
        out_shape=jax.ShapeDtypeStruct((length, channels), jnp.bfloat16),
        in_specs=[SMEM, ANY, ANY, ANY, VMEM, VMEM, VMEM],
        out_specs=VMEM,
        scratch_shapes=[
            pltpu.VMEM((HALO + length, depth), jnp.bfloat16),
            pltpu.VMEM((depth, channels), jnp.bfloat16),
            pltpu.VMEM((HALO + length, channels), jnp.float32),
            pltpu.SemaphoreType.DMA((4, 3)),
        ],
        compiler_params=pltpu.CompilerParams(vmem_limit_bytes=32 * 1024 * 1024),
        name="gated",
    )(where, tokens, halo, weight, taps, keep, taken)


def carried_states(ends, rate, x, z, span):
    others = [along_z(ends, steps) for steps in range(1, Z)]
    carry = jnp.zeros_like(ends)
    line = ends * jnp.exp(-rate * (span * (Z - 1 - z)))
    for steps, state in zip(range(1, Z), others):
        source = (z - steps) % Z
        line = line + state * jnp.exp(-rate * (span * (Z - 1 - source)))
        carry = carry + jnp.where(z >= steps, state, 0.0) * jnp.exp(-rate * (span * (steps - 1)))
    others = [along_x(line, steps) for steps in range(1, X)]
    far = jnp.zeros_like(ends)
    for steps, state in zip(range(1, X), others):
        far = far + jnp.where(x >= steps, state, 0.0) * jnp.exp(-rate * (Z * span * (steps - 1)))
    return carry + far * jnp.exp(-rate * (span * z))


def local(tokens, in_weight, short_filter, residues, rates, skip):
    index = lax.axis_index("seq")
    core = index % CORES
    z = index // CORES % Z
    x = index // (CORES * Z)
    where = jnp.stack([x, z, core]).astype(jnp.int32)
    length = tokens.shape[0]
    channels = skip.shape[0]
    half = channels // 2
    span = CORES * length
    first = core == 0

    query_weight = lax.all_gather(in_weight[0], "seq", axis=0, tiled=True)

    low, high = in_weight[1:, :, :half], in_weight[1:, :, half:]
    own = jnp.where(first, low, high)
    received = swap_cores(jnp.where(first, high, low))
    block = jnp.concatenate(
        [jnp.where(first, own, received), jnp.where(first, received, own)], axis=1
    )
    pieces = gather_chips(block)

    other = swap_cores(tokens)
    tail, other_tail = tokens[length - HALO :], other[length - HALO :]
    halo = next_chip(jnp.where(first, other_tail, tail))
    query_halo = jnp.where(first, halo, other_tail)

    def half_of(array, axis):
        return lax.dynamic_slice_in_dim(array, core * half, half, axis)

    rate = half_of(rates, 0).T
    residue = half_of(residues, 0).T
    decay = jnp.exp(-rate)
    amplitude = residue * jnp.sqrt(-jnp.expm1(-2.0 * rate))
    step = span // SEGMENTS
    power = jnp.stack([jnp.exp(-rate * (step * distance)) for distance in (1, 2, 4)])
    starts = jnp.arange(SEGMENTS, dtype=jnp.float32)[None, :, None] * step
    start_power = jnp.exp(-rate[:, None, :] * starts)

    signal, start_conv, before, ends = signals(
        where, pieces, tokens, other, halo, half_of(short_filter, 2), decay, amplitude, power
    )
    carried = carried_states(ends, rate, x, z, span)
    keep, send = carries(
        where,
        signal,
        start_conv,
        before,
        carried,
        decay,
        amplitude,
        start_power,
        half_of(skip, 0)[None, :],
    )
    taken = swap_cores(send)
    return gated(where, tokens, query_halo, query_weight, short_filter, keep, taken)


def solution(mesh):
    placed = (
        P("seq", None),
        P(None, "seq", "mp"),
        P(None, None, "mp"),
        P("mp", None),
        P("mp", None),
        P("mp"),
    )
    return jax.shard_map(
        local, mesh=mesh, in_specs=placed, out_specs=P("seq", "mp"), check_vma=False
    )
```

time: 627 us -> 160 us (0.26); the launches traced: 620 us -> 159 us
  waiting for transfers between devices: 305 us -> 44.7 us
  matrix products: 119 us -> 0 us
  other arithmetic: 60.8 us -> 9.77 us
  blocking collectives: 32.4 us -> 0 us
  Pallas kernels: 0 us -> 22.8 us
  local copies, waits for them, and re-layouts: 44.4 us -> 23.2 us
    all_to_all x5 -> x0, waiting for transfers between devices: 280 us -> none  [the longest x1 94.4 us: local(): lax.all_to_all(partial_value, 'seq', split_axis=2, concat_axis=1, tiled=T...]
    dot_general x31 -> x0, matrix products: 119 us -> none  [the longest x6 22.5 us: apply_dft(): jnp.einsum(form, sine, real_part, precision=exact)]
    ppermute x1 -> x29, waiting for transfers between devices: 0.9 us -> 44.7 us  [permute(): return lax.ppermute(value, 'seq', pairs)]
    add x18 -> x2, other arithmetic: 41.2 us -> 1.5 us  [the longest x1 0.76 us: carried_states(): line = line + state * jnp.exp(-rate * (span * (Z - 1 - source)))]
    ppermute x1 -> x29, starting transfers between devices: 12.4 us -> 44.9 us  [permute(): return lax.ppermute(value, 'seq', pairs)]
    all_to_all x1 -> x0, blocking collectives: 32.4 us -> none  [local(): lax.all_to_all(results, 'seq', split_axis=0, concat_axis=1, tiled=True)]
    all_to_all x5 -> x0, starting transfers between devices: 31.4 us -> none  [the longest x1 10.2 us: local(): lax.all_to_all(filt, 'seq', split_axis=0, concat_axis=0, tiled=True)]
    all_gather x1, waiting for transfers between devices: 23.5 us -> 0.01 us  [local(): query_weight = lax.all_gather(in_weight[0], 'seq', axis=0, tiled=True)]
  transfers between devices with their start and end apart: 7 -> 30, of which waited for: 6 -> 13; matrix products, arithmetic and copies ran while one was open for 18% -> 8% of each run, Pallas kernels for 0% -> 10%
where the time goes in v1:
time: 160 us; the launch traced here: 159 us
  starting transfers between devices  44.9 us (28%)
  waiting for transfers between devices  44.7 us (28%)
  local copies, waits for them, and re-layouts  23.2 us (14%)
  Pallas kernels  22.8 us (14%)
  between operations  13.7 us (9%)
  other arithmetic  9.77 us (6%)
    ppermute x29, starting transfers between devices, permute(): return lax.ppermute(value, 'seq', pairs)  44.9 us
    ppermute x29, waiting for transfers between devices, permute(): return lax.ppermute(value, 'seq', pairs)  44.7 us
    unnamed x56, local copies, waits for them, and re-layouts  18.7 us
    pallas_call x1, Pallas kernels, signals(): pl.pallas_call(functools.partial(signal_kernel, plan), out_shape=(shape((...  14.1 us
    pallas_call x1, Pallas kernels, gated(): pl.pallas_call(gate_kernel, out_shape=jax.ShapeDtypeStruct((length, chann...  6.46 us
  transfers between devices with their start and end apart: 30, of which 13 were waited for; matrix products, arithmetic and copies ran while one was open for 8% of the time, Pallas kernels for 10%

profile of v1, /device:TPU:1, one launch (start us, length us, event | category | flops | bytes accessed | tf_op | source)
XLA Modules:
  0.0 159.1 jit_solution(15657771765794460415)
XLA Ops:
  6.5 1.6 slice.41
  8.1 3.3 %collective-permute-start = (bf16[512,4096]{1,0:T(8,128)(2,1)}, bf16[512,4096]{1,0:T(8,128)(2,1)}, u32[]{:S(2)}, u32[]{:S(2)}) collective-permute-start(bf16[512,4096]{1,0:T(8,128)(2,1)} %tokens.1), channel_id=1, source_target_pairs={{0,8},{8,0},{16,24},{24,16},{32,40},{40,32},{48,56},{56,48},{64,72... | collective-permute-start | bytes 12582920 | tf_op jit(solution)/shard_map/ppermute | solution.py:35
  11.5 1.0 broadcast_select_fusion.2
  12.6 5.9 %collective-permute-done.2 = bf16[2,128,256]{2,1,0:T(8,128)(2,1)S(1)} collective-permute-done((bf16[2,128,256]{2,1,0:T(8,128)(2,1)S(1)}, bf16[2,128,256]{2,1,0:T(8,128)(2,1)S(1)}, u32[]{:S(2)}, u32[]{:S(2)}) %collective-permute-start.2) | collective-permute-done | bytes 131104 | tf_op jit(solution)/shard_map/ppermute | solution.py:35
  18.4 1.0 broadcast_select_fusion.1
  19.6 1.1 collective-permute-start.4
  20.7 1.7 %collective-permute-start.5 = (bf16[2,256,256]{2,1,0:T(8,128)(2,1)S(1)}, bf16[2,256,256]{2,1,0:T(8,128)(2,1)S(1)}, u32[]{:S(2)}, u32[]{:S(2)}) collective-permute-start(bf16[2,256,256]{2,1,0:T(8,128)(2,1)S(1)} %pad_maximum_fusion.refs_0_), channel_id=1, source_target_pairs={{0,192},{8,200},{16,208},{24,216},{32,224},{40,232},{48,240},{56,2... | collective-permute-start | bytes 786440 | tf_op jit(solution)/shard_map/ppermute | solution.py:35
  22.3 3.2 %collective-permute-start.10 = (bf16[2,256,256]{2,1,0:T(8,128)(2,1)S(1)}, bf16[2,256,256]{2,1,0:T(8,128)(2,1)S(1)}, u32[]{:S(2)}, u32[]{:S(2)}) collective-permute-start(bf16[2,256,256]{2,1,0:T(8,128)(2,1)S(1)} %pad_maximum_fusion.refs_0_), channel_id=1, source_target_pairs={{0,48},{8,56},{16,0},{24,8},{32,16},{40,24},{48,32},{56,40},{64,11... | collective-permute-start | bytes 786440 | tf_op jit(solution)/shard_map/ppermute | solution.py:35
  25.5 3.4 %collective-permute-done.3.refs_5_ = bf16[2,256,256]{2,1,0:T(8,128)(2,1)S(1)} collective-permute-done((bf16[2,256,256]{2,1,0:T(8,128)(2,1)S(1)}, bf16[2,256,256]{2,1,0:T(8,128)(2,1)S(1)}, u32[]{:S(2)}, u32[]{:S(2)}) %collective-permute-start.3) | collective-permute-done | bytes 262176 | tf_op jit(solution)/shard_map/ppermute | solution.py:35
  28.9 1.0 collective-permute-start.6
  29.9 1.3 collective-permute-start.8
  31.2 1.5 collective-permute-start.9
  32.7 7.1 %collective-permute-done.10.refs_10_ = bf16[2,256,256]{2,1,0:T(8,128)(2,1)S(1)} collective-permute-done((bf16[2,256,256]{2,1,0:T(8,128)(2,1)S(1)}, bf16[2,256,256]{2,1,0:T(8,128)(2,1)S(1)}, u32[]{:S(2)}, u32[]{:S(2)}) %collective-permute-start.10) | collective-permute-done | bytes 262176 | tf_op jit(solution)/shard_map/ppermute | solution.py:35
  39.8 2.4 %collective-permute-start.7 = (bf16[2,256,256]{2,1,0:T(8,128)(2,1)S(1)}, bf16[2,256,256]{2,1,0:T(8,128)(2,1)S(1)}, u32[]{:S(2)}, u32[]{:S(2)}) collective-permute-start(bf16[2,256,256]{2,1,0:T(8,128)(2,1)S(1)} %collective-permute-done.3.refs_5_), channel_id=1, source_target_pairs={{0,192},{8,200},{16,208},{24,216},{32,224},{40,232},{48,240},{56,2... | collective-permute-start | bytes 786440 | tf_op jit(solution)/shard_map/ppermute | solution.py:35
  42.8 1.5 collective-permute-start.11
  44.4 1.2 collective-permute-start.12
  45.6 1.3 exponential_bitcast_fusion.2
  46.9 4.9 %collective-permute-done.7.refs_7_ = bf16[2,256,256]{2,1,0:T(8,128)(2,1)S(1)} collective-permute-done((bf16[2,256,256]{2,1,0:T(8,128)(2,1)S(1)}, bf16[2,256,256]{2,1,0:T(8,128)(2,1)S(1)}, u32[]{:S(2)}, u32[]{:S(2)}) %collective-permute-start.7) | collective-permute-done | bytes 262176 | tf_op jit(solution)/shard_map/ppermute | solution.py:35
  51.9 9.4 %collective-permute-done.15.refs_15_ = bf16[2,256,256]{2,1,0:T(8,128)(2,1)S(1)} collective-permute-done((bf16[2,256,256]{2,1,0:T(8,128)(2,1)S(1)}, bf16[2,256,256]{2,1,0:T(8,128)(2,1)S(1)}, u32[]{:S(2)}, u32[]{:S(2)}) %collective-permute-start.15) | collective-permute-done | bytes 262176 | tf_op jit(solution)/shard_map/ppermute | solution.py:35
  61.4 1.5 collective-permute-start.16
  62.8 1.3 collective-permute-start.17
  64.8 1.4 collective-permute-done.14.refs_9_
  66.2 0.7 slice.48
  67.6 2.7 %collective-permute-start.19 = (bf16[2,128,256]{2,1,0:T(8,128)(2,1)}, bf16[2,128,256]{2,1,0:T(8,128)(2,1)}, u32[]{:S(2)}, u32[]{:S(2)}) collective-permute-start(bf16[2,128,256]{2,1,0:T(8,128)(2,1)} %slice.49), channel_id=1, source_target_pairs={{0,192},{8,200},{16,208},{24,216},{32,224},{40,232},{48,240},{56,2... | collective-permute-start | bytes 393224 | tf_op jit(solution)/shard_map/ppermute | solution.py:35
  70.3 0.8 multiply_bitcast_fusion.refs_25_.amplitude
  71.1 0.7 constant_dynamic-slice_fusion.refs_23_
  71.9 4.2 %collective-permute-done.18.refs_13_ = bf16[2,128,256]{2,1,0:T(8,128)(2,1)S(1)} collective-permute-done((bf16[2,128,256]{2,1,0:T(8,128)(2,1)}, bf16[2,128,256]{2,1,0:T(8,128)(2,1)S(1)}, u32[]{:S(2)}, u32[]{:S(2)}) %collective-permute-start.18) | collective-permute-done | bytes 131104 | tf_op jit(solution)/shard_map/ppermute | solution.py:35
  76.1 4.0 %collective-permute-done.19.refs_14_ = bf16[2,128,256]{2,1,0:T(8,128)(2,1)} collective-permute-done((bf16[2,128,256]{2,1,0:T(8,128)(2,1)}, bf16[2,128,256]{2,1,0:T(8,128)(2,1)}, u32[]{:S(2)}, u32[]{:S(2)}) %collective-permute-start.19) | collective-permute-done | bytes 131104 | tf_op jit(solution)/shard_map/ppermute | solution.py:35
  80.2 2.7 %collective-permute-start.21 = (bf16[2,128,256]{2,1,0:T(8,128)(2,1)S(1)}, bf16[2,128,256]{2,1,0:T(8,128)(2,1)S(1)}, u32[]{:S(2)}, u32[]{:S(2)}) collective-permute-start(bf16[2,128,256]{2,1,0:T(8,128)(2,1)S(1)} %slice.51), channel_id=1, source_target_pairs={{0,192},{8,200},{16,208},{24,216},{32,224},{40,232},{48,240},{56,2... | collective-permute-start | bytes 393224 | tf_op jit(solution)/shard_map/ppermute | solution.py:35
  83.0 1.0 slice_select_fusion
  84.0 1.3 collective-permute-start.1
  85.4 0.8 pad_maximum_fusion.1.refs_26_
  86.1 1.1 collective-permute-done.1.refs_22_
  87.2 0.9 copy-done.4
  88.2 0.9 copy-done.6
  89.1 0.9 copy-done.8
  90.1 0.7 copy-done.9
  90.8 0.9 copy-done.12
  91.7 0.9 copy-done.14
  92.6 0.9 copy-done.16
  93.5 0.9 copy-done.18
  94.4 0.9 copy-done.20
  95.3 14.1 %signals.1 = (f32[128,8,256]{2,1,0:T(8,128)S(1)}, f32[128,8,256]{2,1,0:T(8,128)}, f32[16,8,256]{2,1,0:T(8,128)S(1)}, f32[16,256]{1,0:T(8,128)}) custom-call(s32[3]{0:T(128)S(1)} %pad_add_fusion.where, bf16[2,256,256]{2,1,0:T(8,128)(2,1)S(1)} %pad_maximum_fusion.refs_0_, bf16[2,256,256]{2,1,0:T(8,128)(2,1)S(1)} %collective-permute-done.4.refs_1_, ...), custom_call_target="tpu_custom_call" | custom-call | tf_op jit(solution)/shard_map/signals/pallas_call | solution.py:229
  110.1 1.9 %collective-permute-start.22 = (f32[16,256]{1,0:T(8,128)}, f32[16,256]{1,0:T(8,128)S(1)}, u32[]{:S(2)}, u32[]{:S(2)}) collective-permute-start(f32[16,256]{1,0:T(8,128)} %get-tuple-element.50), channel_id=1, source_target_pairs={{0,16},{8,24},{16,32},{24,40},{32,48},{40,56},{48,0},{56,8},{64,80... | collective-permute-start | bytes 49160 | tf_op jit(solution)/shard_map/ppermute | solution.py:35
  112.0 0.8 collective-permute-start.23
  112.8 1.3 collective-permute-start.24
  114.7 1.1 collective-permute-done.23
  115.8 0.8 multiply_add_fusion.1
  116.6 3.3 %collective-permute-start.25 = (f32[16,256]{1,0:T(8,128)S(1)}, f32[16,256]{1,0:T(8,128)S(1)}, u32[]{:S(2)}, u32[]{:S(2)}) collective-permute-start(f32[16,256]{1,0:T(8,128)S(1)} %multiply_add_fusion.1), channel_id=1, source_target_pairs={{0,64},{8,72},{16,80},{24,88},{32,96},{40,104},{48,112},{56,120},{... | collective-permute-start | bytes 49160 | tf_op jit(solution)/shard_map/ppermute | solution.py:35
  119.9 2.4 %collective-permute-start.26 = (f32[16,256]{1,0:T(8,128)S(1)}, f32[16,256]{1,0:T(8,128)S(1)}, u32[]{:S(2)}, u32[]{:S(2)}) collective-permute-start(f32[16,256]{1,0:T(8,128)S(1)} %multiply_add_fusion.1), channel_id=1, source_target_pairs={{0,128},{8,136},{16,144},{24,152},{32,160},{40,168},{48,176},{56,1... | collective-permute-start | bytes 49160 | tf_op jit(solution)/shard_map/ppermute | solution.py:35
  122.4 0.8 multiply_exponential_fusion.power
  123.2 0.8 dynamic_slice.15
  124.0 0.9 collective-permute-done.27
  124.9 0.7 multiply_add_fusion.carried
  125.6 1.2 copy-done.2
  126.8 0.7 copy-done.10
  127.6 0.9 copy-done.22
  129.1 2.2 %carries.1 = (f32[512,256]{1,0:T(8,128)S(1)}, f32[512,256]{1,0:T(8,128)S(1)}) custom-call(s32[3]{0:T(128)S(1)} %copy-done.25, f32[128,8,256]{2,1,0:T(8,128)S(1)} %get-tuple-element.47.signal, f32[128,8,256]{2,1,0:T(8,128)S(1)} %copy-done.2, f32[16,8,256]{2,1,0:T(8,128)S(1)} %copy-done.22, f32[16,256]{1,0:T(8,128)S(1)} %multiply_add_fusion.carried, ...), custom_call_target="tpu_custom_call" | custom-call | tf_op jit(solution)/shard_map/carries/pallas_call | solution.py:293
  131.3 7.1 %collective-permute-start.28 = (f32[512,256]{1,0:T(8,128)S(1)}, f32[512,256]{1,0:T(8,128)S(1)}, u32[]{:S(2)}, u32[]{:S(2)}) collective-permute-start(f32[512,256]{1,0:T(8,128)S(1)} %get-tuple-element.52), channel_id=1, source_target_pairs={{0,8},{8,0},{16,24},{24,16},{32,40},{40,32},{48,56},{56,48},{64,72... | collective-permute-start | bytes 1572872 | tf_op jit(solution)/shard_map/ppermute | solution.py:35
  138.4 0.9 broadcast_select_fusion.4.halo
  139.9 2.2 %copy-done = bf16[512,4096]{1,0:T(8,128)(2,1)S(1)} copy-done((bf16[512,4096]{1,0:T(8,128)(2,1)S(1)}, bf16[512,4096]{1,0:T(8,128)(2,1)}, u32[]{:S(2)}) %copy-start) | copy-done | bytes 4194328
  142.1 2.2 %copy-done.1 = bf16[1,4096,512]{2,1,0:T(8,128)(2,1)S(1)} copy-done((bf16[1,4096,512]{2,1,0:T(8,128)(2,1)S(1)}, bf16[1,4096,512]{2,1,0:T(8,128)(2,1)}, u32[]{:S(2)}) %copy-start.1) | copy-done | bytes 4194328
  144.3 0.8 copy-done.23
  145.7 6.5 %gated.1 = bf16[512,512]{1,0:T(8,128)(2,1)} custom-call(s32[3]{0:T(128)S(1)} %copy-done.26, bf16[512,4096]{1,0:T(8,128)(2,1)S(1)} %copy-done, bf16[16,4096]{1,0:T(8,128)(2,1)S(1)} %broadcast_select_fusion.4.halo, bf16[4096,512]{1,0:T(8,128)(2,1)S(1)} %bitcast.16, f32[3,7,512]{2,1,0:T(8,128)S(1)} %copy-done.23, f32[512,256]{1,0:T(8,128)S(1)} %get-tuple-element.51.keep, ...), custom_call_target="tpu_custom_call" | custom-call | tf_op jit(solution)/shard_map/gated/pallas_call | solution.py:354
  (81 shorter events, 5.8 us)
Async XLA Ops:
  6.5 133.4 %all-gather.3.cloned.1.call-start = ((), (), s32[]{:S(2)}) async-start(), calls=%async_computation | async-start | bytes 4325376 | tf_op jit(solution)/shard_map/all_gather | solution.py:397
  8.1 74.8 %collective-permute-start = (bf16[512,4096]{1,0:T(8,128)(2,1)}, bf16[512,4096]{1,0:T(8,128)(2,1)}, u32[]{:S(2)}, u32[]{:S(2)}) collective-permute-start(bf16[512,4096]{1,0:T(8,128)(2,1)} %tokens.1), channel_id=1, source_target_pairs={{0,8},{8,0},{16,24},{24,16},{32,40},{40,32},{48,56},{56,48},{64,72... | collective-permute-start | bytes 12582920 | tf_op jit(solution)/shard_map/ppermute | solution.py:35
  12.5 6.0 %collective-permute-start.2 = (bf16[2,128,256]{2,1,0:T(8,128)(2,1)S(1)}, bf16[2,128,256]{2,1,0:T(8,128)(2,1)S(1)}, u32[]{:S(2)}, u32[]{:S(2)}) collective-permute-start(bf16[2,128,256]{2,1,0:T(8,128)(2,1)S(1)} %broadcast_select_fusion.2), channel_id=1, source_target_pairs={{0,8},{8,0},{16,24},{24,16},{32,40},{40,32},{48,56},{56,48},{64,72... | collective-permute-start | bytes 393224 | tf_op jit(solution)/shard_map/ppermute | solution.py:35
  19.5 9.4 %collective-permute-start.3 = (bf16[2,256,256]{2,1,0:T(8,128)(2,1)S(1)}, bf16[2,256,256]{2,1,0:T(8,128)(2,1)S(1)}, u32[]{:S(2)}, u32[]{:S(2)}) collective-permute-start(bf16[2,256,256]{2,1,0:T(8,128)(2,1)S(1)} %pad_maximum_fusion.refs_0_), channel_id=1, source_target_pairs={{0,16},{8,24},{16,32},{24,40},{32,48},{40,56},{48,0},{56,8},{64,80... | collective-permute-start | bytes 786440 | tf_op jit(solution)/shard_map/ppermute | solution.py:35
  19.6 9.4 %collective-permute-start.4 = (bf16[2,256,256]{2,1,0:T(8,128)(2,1)S(1)}, bf16[2,256,256]{2,1,0:T(8,128)(2,1)S(1)}, u32[]{:S(2)}, u32[]{:S(2)}) collective-permute-start(bf16[2,256,256]{2,1,0:T(8,128)(2,1)S(1)} %pad_maximum_fusion.refs_0_), channel_id=1, source_target_pairs={{0,64},{8,72},{16,80},{24,88},{32,96},{40,104},{48,112},{56,120},{... | collective-permute-start | bytes 786440 | tf_op jit(solution)/shard_map/ppermute | solution.py:35
  20.7 8.3 %collective-permute-start.5 = (bf16[2,256,256]{2,1,0:T(8,128)(2,1)S(1)}, bf16[2,256,256]{2,1,0:T(8,128)(2,1)S(1)}, u32[]{:S(2)}, u32[]{:S(2)}) collective-permute-start(bf16[2,256,256]{2,1,0:T(8,128)(2,1)S(1)} %pad_maximum_fusion.refs_0_), channel_id=1, source_target_pairs={{0,192},{8,200},{16,208},{24,216},{32,224},{40,232},{48,240},{56,2... | collective-permute-start | bytes 786440 | tf_op jit(solution)/shard_map/ppermute | solution.py:35
  22.3 17.5 %collective-permute-start.10 = (bf16[2,256,256]{2,1,0:T(8,128)(2,1)S(1)}, bf16[2,256,256]{2,1,0:T(8,128)(2,1)S(1)}, u32[]{:S(2)}, u32[]{:S(2)}) collective-permute-start(bf16[2,256,256]{2,1,0:T(8,128)(2,1)S(1)} %pad_maximum_fusion.refs_0_), channel_id=1, source_target_pairs={{0,48},{8,56},{16,0},{24,8},{32,16},{40,24},{48,32},{56,40},{64,11... | collective-permute-start | bytes 786440 | tf_op jit(solution)/shard_map/ppermute | solution.py:35
  28.9 58.3 %copy-start.3 = (bf16[2,256,256]{2,1,0:T(8,128)(2,1)}, bf16[2,256,256]{2,1,0:T(8,128)(2,1)S(1)}, u32[]{:S(2)}) copy-start(bf16[2,256,256]{2,1,0:T(8,128)(2,1)S(1)} %collective-permute-done.3.refs_5_) | copy-start | bytes 786436
  28.9 15.5 %collective-permute-start.6 = (bf16[2,256,256]{2,1,0:T(8,128)(2,1)S(1)}, bf16[2,256,256]{2,1,0:T(8,128)(2,1)S(1)}, u32[]{:S(2)}, u32[]{:S(2)}) collective-permute-start(bf16[2,256,256]{2,1,0:T(8,128)(2,1)S(1)} %collective-permute-done.3.refs_5_), channel_id=1, source_target_pairs={{0,64},{8,72},{16,80},{24,88},{32,96},{40,104},{48,112},{56,120},{... | collective-permute-start | bytes 786440 | tf_op jit(solution)/shard_map/ppermute | solution.py:35
  29.9 12.3 %collective-permute-start.8 = (bf16[2,128,256]{2,1,0:T(8,128)(2,1)S(1)}, bf16[2,128,256]{2,1,0:T(8,128)(2,1)S(1)}, u32[]{:S(2)}, u32[]{:S(2)}) collective-permute-start(bf16[2,128,256]{2,1,0:T(8,128)(2,1)S(1)} %slice.44), channel_id=1, source_target_pairs={{0,64},{8,72},{16,80},{24,88},{32,96},{40,104},{48,112},{56,120},{... | collective-permute-start | bytes 393224 | tf_op jit(solution)/shard_map/ppermute | solution.py:35
  31.2 11.7 %collective-permute-start.9 = (bf16[2,128,256]{2,1,0:T(8,128)(2,1)S(1)}, bf16[2,128,256]{2,1,0:T(8,128)(2,1)S(1)}, u32[]{:S(2)}, u32[]{:S(2)}) collective-permute-start(bf16[2,128,256]{2,1,0:T(8,128)(2,1)S(1)} %slice.45), channel_id=1, source_target_pairs={{0,192},{8,200},{16,208},{24,216},{32,224},{40,232},{48,240},{56,2... | collective-permute-start | bytes 393224 | tf_op jit(solution)/shard_map/ppermute | solution.py:35
  39.8 47.4 %copy-start.5 = (bf16[2,256,256]{2,1,0:T(8,128)(2,1)}, bf16[2,256,256]{2,1,0:T(8,128)(2,1)S(1)}, u32[]{:S(2)}) copy-start(bf16[2,256,256]{2,1,0:T(8,128)(2,1)S(1)} %collective-permute-done.10.refs_10_) | copy-start | bytes 786436
  39.8 12.0 %collective-permute-start.7 = (bf16[2,256,256]{2,1,0:T(8,128)(2,1)S(1)}, bf16[2,256,256]{2,1,0:T(8,128)(2,1)S(1)}, u32[]{:S(2)}, u32[]{:S(2)}) collective-permute-start(bf16[2,256,256]{2,1,0:T(8,128)(2,1)S(1)} %collective-permute-done.3.refs_5_), channel_id=1, source_target_pairs={{0,192},{8,200},{16,208},{24,216},{32,224},{40,232},{48,240},{56,2... | collective-permute-start | bytes 786440 | tf_op jit(solution)/shard_map/ppermute | solution.py:35
  42.2 0.7 copy-start.11
  42.8 18.5 %collective-permute-start.15 = (bf16[2,256,256]{2,1,0:T(8,128)(2,1)S(1)}, bf16[2,256,256]{2,1,0:T(8,128)(2,1)S(1)}, u32[]{:S(2)}, u32[]{:S(2)}) collective-permute-start(bf16[2,256,256]{2,1,0:T(8,128)(2,1)S(1)} %pad_maximum_fusion.refs_0_), channel_id=1, source_target_pairs={{0,32},{8,40},{16,48},{24,56},{32,0},{40,8},{48,16},{56,24},{64,96... | collective-permute-start | bytes 786440 | tf_op jit(solution)/shard_map/ppermute | solution.py:35
  42.8 44.4 %copy-start.13 = (bf16[2,128,256]{2,1,0:T(8,128)(2,1)}, bf16[2,128,256]{2,1,0:T(8,128)(2,1)S(1)}, u32[]{:S(2)}) copy-start(bf16[2,128,256]{2,1,0:T(8,128)(2,1)S(1)} %collective-permute-done.9.refs_4_) | copy-start | bytes 393220
  42.8 18.5 %collective-permute-start.11 = (bf16[2,256,256]{2,1,0:T(8,128)(2,1)S(1)}, bf16[2,256,256]{2,1,0:T(8,128)(2,1)S(1)}, u32[]{:S(2)}, u32[]{:S(2)}) collective-permute-start(bf16[2,256,256]{2,1,0:T(8,128)(2,1)S(1)} %collective-permute-done.10.refs_10_), channel_id=1, source_target_pairs={{0,64},{8,72},{16,80},{24,88},{32,96},{40,104},{48,112},{56,120},{... | collective-permute-start | bytes 786440 | tf_op jit(solution)/shard_map/ppermute | solution.py:35
  44.4 18.5 %collective-permute-start.12 = (bf16[2,256,256]{2,1,0:T(8,128)(2,1)S(1)}, bf16[2,256,256]{2,1,0:T(8,128)(2,1)S(1)}, u32[]{:S(2)}, u32[]{:S(2)}) collective-permute-start(bf16[2,256,256]{2,1,0:T(8,128)(2,1)S(1)} %collective-permute-done.10.refs_10_), channel_id=1, source_target_pairs={{0,192},{8,200},{16,208},{24,216},{32,224},{40,232},{48,240},{56,2... | collective-permute-start | bytes 786440 | tf_op jit(solution)/shard_map/ppermute | solution.py:35
  46.9 23.4 %copy-start.27 = (f32[16,256]{1,0:T(8,128)}, f32[16,256]{1,0:T(8,128)S(1)}, u32[]{:S(2)}) copy-start(f32[16,256]{1,0:T(8,128)S(1)} %get-tuple-element.54) | copy-start | bytes 49156
  51.8 13.0 %collective-permute-start.13 = (bf16[2,128,256]{2,1,0:T(8,128)(2,1)S(1)}, bf16[2,128,256]{2,1,0:T(8,128)(2,1)S(1)}, u32[]{:S(2)}, u32[]{:S(2)}) collective-permute-start(bf16[2,128,256]{2,1,0:T(8,128)(2,1)S(1)} %slice.46), channel_id=1, source_target_pairs={{0,64},{8,72},{16,80},{24,88},{32,96},{40,104},{48,112},{56,120},{... | collective-permute-start | bytes 393224 | tf_op jit(solution)/shard_map/ppermute | solution.py:35
  61.4 25.8 %copy-start.7 = (bf16[2,256,256]{2,1,0:T(8,128)(2,1)}, bf16[2,256,256]{2,1,0:T(8,128)(2,1)S(1)}, u32[]{:S(2)}) copy-start(bf16[2,256,256]{2,1,0:T(8,128)(2,1)S(1)} %collective-permute-done.15.refs_15_) | copy-start | bytes 786436
  61.4 4.8 %collective-permute-start.14 = (bf16[2,128,256]{2,1,0:T(8,128)(2,1)S(1)}, bf16[2,128,256]{2,1,0:T(8,128)(2,1)S(1)}, u32[]{:S(2)}, u32[]{:S(2)}) collective-permute-start(bf16[2,128,256]{2,1,0:T(8,128)(2,1)S(1)} %slice.47), channel_id=1, source_target_pairs={{0,192},{8,200},{16,208},{24,216},{32,224},{40,232},{48,240},{56,2... | collective-permute-start | bytes 393224 | tf_op jit(solution)/shard_map/ppermute | solution.py:35
  61.4 18.7 %collective-permute-start.16 = (bf16[2,256,256]{2,1,0:T(8,128)(2,1)S(1)}, bf16[2,256,256]{2,1,0:T(8,128)(2,1)S(1)}, u32[]{:S(2)}, u32[]{:S(2)}) collective-permute-start(bf16[2,256,256]{2,1,0:T(8,128)(2,1)S(1)} %collective-permute-done.15.refs_15_), channel_id=1, source_target_pairs={{0,64},{8,72},{16,80},{24,88},{32,96},{40,104},{48,112},{56,120},{... | collective-permute-start | bytes 786440 | tf_op jit(solution)/shard_map/ppermute | solution.py:35
  62.8 17.3 %collective-permute-start.17 = (bf16[2,256,256]{2,1,0:T(8,128)(2,1)S(1)}, bf16[2,256,256]{2,1,0:T(8,128)(2,1)S(1)}, u32[]{:S(2)}, u32[]{:S(2)}) collective-permute-start(bf16[2,256,256]{2,1,0:T(8,128)(2,1)S(1)} %collective-permute-done.15.refs_15_), channel_id=1, source_target_pairs={{0,192},{8,200},{16,208},{24,216},{32,224},{40,232},{48,240},{56,2... | collective-permute-start | bytes 786440 | tf_op jit(solution)/shard_map/ppermute | solution.py:35
  64.8 22.4 %copy-start.15 = (bf16[2,128,256]{2,1,0:T(8,128)(2,1)}, bf16[2,128,256]{2,1,0:T(8,128)(2,1)S(1)}, u32[]{:S(2)}) copy-start(bf16[2,128,256]{2,1,0:T(8,128)(2,1)S(1)} %collective-permute-done.13.refs_8_) | copy-start | bytes 393220
  66.2 1.4 copy-start.17
  67.0 9.1 %collective-permute-start.18 = (bf16[2,128,256]{2,1,0:T(8,128)(2,1)}, bf16[2,128,256]{2,1,0:T(8,128)(2,1)S(1)}, u32[]{:S(2)}, u32[]{:S(2)}) collective-permute-start(bf16[2,128,256]{2,1,0:T(8,128)(2,1)} %slice.48), channel_id=1, source_target_pairs={{0,64},{8,72},{16,80},{24,88},{32,96},{40,104},{48,112},{56,120},{... | collective-permute-start | bytes 393224 | tf_op jit(solution)/shard_map/ppermute | solution.py:35
  67.6 12.5 %collective-permute-start.19 = (bf16[2,128,256]{2,1,0:T(8,128)(2,1)}, bf16[2,128,256]{2,1,0:T(8,128)(2,1)}, u32[]{:S(2)}, u32[]{:S(2)}) collective-permute-start(bf16[2,128,256]{2,1,0:T(8,128)(2,1)} %slice.49), channel_id=1, source_target_pairs={{0,192},{8,200},{16,208},{24,216},{32,224},{40,232},{48,240},{56,2... | collective-permute-start | bytes 393224 | tf_op jit(solution)/shard_map/ppermute | solution.py:35
  76.1 6.9 %copy-start.19 = (bf16[2,128,256]{2,1,0:T(8,128)(2,1)}, bf16[2,128,256]{2,1,0:T(8,128)(2,1)S(1)}, u32[]{:S(2)}) copy-start(bf16[2,128,256]{2,1,0:T(8,128)(2,1)S(1)} %collective-permute-done.18.refs_13_) | copy-start | bytes 393220
  80.1 6.0 %collective-permute-start.20 = (bf16[2,128,256]{2,1,0:T(8,128)(2,1)S(1)}, bf16[2,128,256]{2,1,0:T(8,128)(2,1)S(1)}, u32[]{:S(2)}, u32[]{:S(2)}) collective-permute-start(bf16[2,128,256]{2,1,0:T(8,128)(2,1)S(1)} %slice.50), channel_id=1, source_target_pairs={{0,64},{8,72},{16,80},{24,88},{32,96},{40,104},{48,112},{56,120},{... | collective-permute-start | bytes 393224 | tf_op jit(solution)/shard_map/ppermute | solution.py:35
  80.2 5.9 %collective-permute-start.21 = (bf16[2,128,256]{2,1,0:T(8,128)(2,1)S(1)}, bf16[2,128,256]{2,1,0:T(8,128)(2,1)S(1)}, u32[]{:S(2)}, u32[]{:S(2)}) collective-permute-start(bf16[2,128,256]{2,1,0:T(8,128)(2,1)S(1)} %slice.51), channel_id=1, source_target_pairs={{0,192},{8,200},{16,208},{24,216},{32,224},{40,232},{48,240},{56,2... | collective-permute-start | bytes 393224 | tf_op jit(solution)/shard_map/ppermute | solution.py:35
  84.0 3.2 %collective-permute-start.1 = (bf16[16,4096]{1,0:T(8,128)(2,1)S(1)}, bf16[16,4096]{1,0:T(8,128)(2,1)S(1)}, u32[]{:S(2)}, u32[]{:S(2)}) collective-permute-start(bf16[16,4096]{1,0:T(8,128)(2,1)S(1)} %slice_select_fusion), channel_id=1, source_target_pairs={{0,16},{8,24},{16,32},{24,40},{32,48},{40,56},{48,64},{56,72},{64,... | collective-permute-start | bytes 393224 | tf_op jit(solution)/shard_map/ppermute | solution.py:35
  85.4 24.1 %copy-start.24 = (s32[3]{0:T(128)}, s32[3]{0:T(128)S(1)}, u32[]{:S(2)}) copy-start(s32[3]{0:T(128)S(1)} %pad_add_fusion.where) | copy-start | bytes 40
  87.2 1.0 copy-start.4
  88.2 0.9 copy-start.6
  89.1 0.9 copy-start.8
  90.1 0.7 copy-start.9
  90.8 0.9 copy-start.12
  91.7 0.9 copy-start.14
  92.6 0.9 copy-start.16
  93.5 0.9 copy-start.18
  94.4 0.9 copy-start.20
  109.5 0.7 copy-start.21
  110.1 4.6 %collective-permute-start.22 = (f32[16,256]{1,0:T(8,128)}, f32[16,256]{1,0:T(8,128)S(1)}, u32[]{:S(2)}, u32[]{:S(2)}) collective-permute-start(f32[16,256]{1,0:T(8,128)} %get-tuple-element.50), channel_id=1, source_target_pairs={{0,16},{8,24},{16,32},{24,40},{32,48},{40,56},{48,0},{56,8},{64,80... | collective-permute-start | bytes 49160 | tf_op jit(solution)/shard_map/ppermute | solution.py:35
  112.0 3.8 %collective-permute-start.23 = (f32[16,256]{1,0:T(8,128)}, f32[16,256]{1,0:T(8,128)S(1)}, u32[]{:S(2)}, u32[]{:S(2)}) collective-permute-start(f32[16,256]{1,0:T(8,128)} %get-tuple-element.50), channel_id=1, source_target_pairs={{0,32},{8,40},{16,48},{24,56},{32,0},{40,8},{48,16},{56,24},{64,96... | collective-permute-start | bytes 49160 | tf_op jit(solution)/shard_map/ppermute | solution.py:35
  112.8 3.0 %collective-permute-start.24 = (f32[16,256]{1,0:T(8,128)}, f32[16,256]{1,0:T(8,128)S(1)}, u32[]{:S(2)}, u32[]{:S(2)}) collective-permute-start(f32[16,256]{1,0:T(8,128)} %get-tuple-element.50), channel_id=1, source_target_pairs={{0,48},{8,56},{16,0},{24,8},{32,16},{40,24},{48,32},{56,40},{64,11... | collective-permute-start | bytes 49160 | tf_op jit(solution)/shard_map/ppermute | solution.py:35
  116.6 7.4 %collective-permute-start.25 = (f32[16,256]{1,0:T(8,128)S(1)}, f32[16,256]{1,0:T(8,128)S(1)}, u32[]{:S(2)}, u32[]{:S(2)}) collective-permute-start(f32[16,256]{1,0:T(8,128)S(1)} %multiply_add_fusion.1), channel_id=1, source_target_pairs={{0,64},{8,72},{16,80},{24,88},{32,96},{40,104},{48,112},{56,120},{... | collective-permute-start | bytes 49160 | tf_op jit(solution)/shard_map/ppermute | solution.py:35
  119.9 4.1 %collective-permute-start.26 = (f32[16,256]{1,0:T(8,128)S(1)}, f32[16,256]{1,0:T(8,128)S(1)}, u32[]{:S(2)}, u32[]{:S(2)}) collective-permute-start(f32[16,256]{1,0:T(8,128)S(1)} %multiply_add_fusion.1), channel_id=1, source_target_pairs={{0,128},{8,136},{16,144},{24,152},{32,160},{40,168},{48,176},{56,1... | collective-permute-start | bytes 49160 | tf_op jit(solution)/shard_map/ppermute | solution.py:35
  122.3 2.6 %collective-permute-start.27 = (f32[16,256]{1,0:T(8,128)S(1)}, f32[16,256]{1,0:T(8,128)S(1)}, u32[]{:S(2)}, u32[]{:S(2)}) collective-permute-start(f32[16,256]{1,0:T(8,128)S(1)} %multiply_add_fusion.1), channel_id=1, source_target_pairs={{0,192},{8,200},{16,208},{24,216},{32,224},{40,232},{48,240},{56,2... | collective-permute-start | bytes 49160 | tf_op jit(solution)/shard_map/ppermute | solution.py:35
  125.6 1.2 copy-start.2
  126.8 0.7 copy-start.10
  127.6 0.9 copy-start.22
  128.5 0.6 copy-start.25
  131.3 8.7 %collective-permute-start.28 = (f32[512,256]{1,0:T(8,128)S(1)}, f32[512,256]{1,0:T(8,128)S(1)}, u32[]{:S(2)}, u32[]{:S(2)}) collective-permute-start(f32[512,256]{1,0:T(8,128)S(1)} %get-tuple-element.52), channel_id=1, source_target_pairs={{0,8},{8,0},{16,24},{24,16},{32,40},{40,32},{48,56},{56,48},{64,72... | collective-permute-start | bytes 1572872 | tf_op jit(solution)/shard_map/ppermute | solution.py:35
  139.9 2.2 %copy-start = (bf16[512,4096]{1,0:T(8,128)(2,1)S(1)}, bf16[512,4096]{1,0:T(8,128)(2,1)}, u32[]{:S(2)}) copy-start(bf16[512,4096]{1,0:T(8,128)(2,1)} %tokens.1) | copy-start | bytes 12582916
  142.1 2.2 %copy-start.1 = (bf16[1,4096,512]{2,1,0:T(8,128)(2,1)S(1)}, bf16[1,4096,512]{2,1,0:T(8,128)(2,1)}, u32[]{:S(2)}) copy-start(bf16[1,4096,512]{2,1,0:T(8,128)(2,1)} %all-gather.3.cloned.1.call-done) | copy-start | bytes 12582916
  144.3 0.8 copy-start.23
  145.1 0.6 copy-start.26
Sparse Core Ops, SparseCore 0:
  9.2 77.4 all-gather.2

commit v2 on v1

v2 whole, which is shorter than its diff:
```python
import functools
import math

import jax
import jax.numpy as jnp
from jax import lax
from jax.experimental import pallas as pl
from jax.experimental.pallas import tpu as pltpu
from jax.sharding import PartitionSpec as P

SHORT = 7
X, Z, CORES = 4, 4, 2
CHIPS = X * Z
HALO = 16
LANES = 128
SEGMENTS = 8

QUERY = pl.ds(0, 1)
KEY_VALUE = pl.ds(1, 2)

HBM = pl.BlockSpec(memory_space=pltpu.HBM)
VMEM = pl.BlockSpec(memory_space=pltpu.VMEM)
SMEM = pl.BlockSpec(memory_space=pltpu.SMEM)


def in_hbm(*arrays):
    return [pltpu.with_memory_space_constraint(array, pltpu.HBM) for array in arrays]


def in_vmem(*arrays):
    return [pltpu.with_memory_space_constraint(array, pltpu.VMEM) for array in arrays]


def place(x, z, core):
    return (x * Z + z) * CORES + core


def permute(value, target):
    pairs = []
    for x in range(X):
        for z in range(Z):
            for core in range(CORES):
                to = target(x, z, core)
                if to is not None:
                    pairs.append((place(x, z, core), place(*to)))
    return lax.ppermute(value, "seq", pairs)


def along_x(value, steps):
    return permute(value, lambda x, z, core: ((x + steps) % X, z, core))


def along_z(value, steps):
    return permute(value, lambda x, z, core: (x, (z + steps) % Z, core))


def swap_cores(value):
    return permute(value, lambda x, z, core: (x, z, 1 - core))


def next_chip(value, to_core):
    def target(x, z, core):
        chip = x * Z + z + 1
        if core != CORES - 1 or chip == CHIPS:
            return None
        return (chip // Z, chip % Z, to_core)

    return permute(value, target)


def together(*values):
    return lax.optimization_barrier(values)


def forwards(right, left):
    half = right.shape[1] // 2
    return along_x(right[:, :half], 1), along_x(left[:, half:], 3)


def sides(block):
    return along_x(block, 1), along_x(block, 3)


def with_sides(z_steps, block, right, left):
    height = block.shape[1]
    return [
        (x_steps, z_steps, 0, array, 0, height)
        for x_steps, array in ((0, block), (1, right), (3, left))
    ]


def with_far(z_steps, far_right, far_left):
    height = far_right.shape[1]
    return [(2, z_steps, 0, far_right, 0, height), (2, z_steps, height, far_left, 0, height)]


def rounded(value):
    return value.astype(jnp.bfloat16).astype(jnp.float32)


def start_copies(plan, streams, where, pieces, mine, other, halo, rows, weights, sems):
    x, z, core = where[0], where[1], where[2]
    length, depth = mine.shape
    groups = []
    offset = 0
    for at, (x_steps, z_steps, row, which, start, height) in enumerate(plan):
        chip = (x - x_steps + X) % X * Z + (z - z_steps + Z) % Z
        column = pl.multiple_of(chip * (depth // CHIPS) + row, LANES)
        copies = [
            pltpu.make_async_copy(
                pieces[which].at[streams, pl.ds(start, height), :],
                weights.at[:, pl.ds(offset, height), :],
                sems.at[at, 0],
            ),
            pltpu.make_async_copy(
                halo.at[:, pl.ds(column, height)],
                rows.at[pl.ds(0, HALO), pl.ds(offset, height)],
                sems.at[at, 1],
            ),
        ]
        for sem, array, block in ((2, mine, core), (3, other, 1 - core)):
            first = pl.multiple_of(HALO + block * length, HALO)
            copies.append(
                pltpu.make_async_copy(
                    array.at[:, pl.ds(column, height)],
                    rows.at[pl.ds(first, length), pl.ds(offset, height)],
                    sems.at[at, sem],
                )
            )
        for copy in copies:
            copy.start()
        groups.append((offset, height, copies))
        offset += height
    return groups


def multiply(groups, parts, rows, weights, before, totals, last):
    depth = rows.shape[1]
    streams, _, channels = weights.shape
    for part in range(parts):
        low, high = part * depth // parts, (part + 1) * depth // parts
        for offset, height, copies in groups:
            if low <= offset < high:
                for copy in copies:
                    copy.wait()
        for stream in range(streams):
            product = jnp.dot(
                rows[:, low:high], weights[stream, low:high, :], preferred_element_type=jnp.float32
            )
            source = before if part == 0 else totals
            for group in range(channels // LANES):
                share = product[:, group * LANES : (group + 1) * LANES]
                if source is not None:
                    share = source[stream, group] + share
                totals[stream, group] = rounded(share) if last and part == parts - 1 else share


def arrays_in(plan):
    return 1 + max(step[3] for step in plan)


def partial_kernel(plan, streams, parts, has_before, where, *refs):
    count = arrays_in(plan)
    pieces, refs = refs[:count], refs[count:]
    mine, other, halo = refs[:3]
    before, refs = (refs[3], refs[4:]) if has_before else (None, refs[3:])
    totals, rows, weights, sems = refs
    groups = start_copies(plan, streams, where, pieces, mine, other, halo, rows, weights, sems)
    multiply(groups, parts, rows, weights, before, totals, False)


def plan_of(pieces):
    arrays = []
    plan = []
    for x_steps, z_steps, row, array, start, height in pieces:
        which = next((at for at, seen in enumerate(arrays) if seen is array), len(arrays))
        if which == len(arrays):
            arrays.append(array)
        plan.append((x_steps, z_steps, row, which, start, height))
    return tuple(plan), arrays, sum(step[-1] for step in plan)


def copy_scratch(pieces, streams, mine):
    plan, arrays, depth = plan_of(pieces)
    channels = arrays[0].shape[2]
    return [
        pltpu.VMEM((HALO + 2 * mine.shape[0], depth), jnp.bfloat16),
        pltpu.VMEM((streams.size, depth, channels), jnp.bfloat16),
        pltpu.SemaphoreType.DMA((len(plan), 4)),
    ]


def partial_products(where, pieces, streams, mine, other, halo, before, parts, name):
    plan, arrays, _ = plan_of(pieces)
    channels = arrays[0].shape[2]
    more = [] if before is None else [before]
    shape = (streams.size, channels // LANES, HALO + 2 * mine.shape[0], LANES)
    return pl.pallas_call(
        functools.partial(partial_kernel, plan, streams, parts, before is not None),
        out_shape=pltpu.VMEM(shape, jnp.float32),
        in_specs=[SMEM] + [HBM] * (len(arrays) + 3) + [VMEM] * len(more),
        out_specs=VMEM,
        scratch_shapes=copy_scratch(pieces, streams, mine),
        compiler_params=pltpu.CompilerParams(vmem_limit_bytes=24 * 1024 * 1024),
        name=name,
    )(where, *in_hbm(*arrays, mine, other, halo), *in_vmem(*more))


def signal_kernel(plan, streams, where, *refs):
    count = arrays_in(plan)
    pieces, refs = refs[:count], refs[count:]
    mine, other, halo, products, taps, decay, amplitude, power = refs[:8]
    signal, start_conv, before, ends, rows, weights, sems, projected = refs[8:]
    channels = weights.shape[2]
    steps = 2 * mine.shape[0] // SEGMENTS
    groups = start_copies(plan, streams, where, pieces, mine, other, halo, rows, weights, sems)
    multiply(groups, 1, rows, weights, products, projected, True)
    for low in range(0, channels, LANES):
        lanes = pl.ds(low, LANES)
        group = low // LANES

        def spread(ref, *index):
            return jnp.broadcast_to(ref[(*index, lanes)].reshape(1, LANES), (SEGMENTS, LANES))

        def load(stream, step):
            return projected[stream, group, pl.ds(HALO + step, SEGMENTS, stride=steps), :]

        key_taps = [spread(taps, 1, offset) for offset in range(SHORT)]
        value_taps = [spread(taps, 2, offset) for offset in range(SHORT)]

        def featurize(step, carry):
            keys, values = carry
            keys = (load(0, step),) + keys
            values = (load(1, step),) + values
            total_key = key_taps[0] * keys[0]
            total_value = value_taps[0] * values[0]
            for offset in range(1, SHORT):
                total_key += key_taps[offset] * keys[offset]
                total_value += value_taps[offset] * values[offset]
            signal[step, :, lanes] = total_key * total_value
            return keys[:-1], values[:-1]

        lax.fori_loop(
            0,
            steps,
            featurize,
            (
                tuple(load(0, -offset) for offset in range(1, SHORT)),
                tuple(load(1, -offset) for offset in range(1, SHORT)),
            ),
            unroll=4,
        )
        modes = decay.shape[0]
        decays = [spread(decay, mode) for mode in range(modes)]
        amplitudes = [spread(amplitude, mode) for mode in range(modes)]

        def scan(step, states):
            here = signal[step, :, lanes]
            states = tuple(decays[mode] * states[mode] + here for mode in range(modes))
            terms = [amplitudes[mode] * states[mode] for mode in range(modes)]
            while len(terms) > 1:
                terms = [terms[at] + terms[at + 1] for at in range(0, len(terms), 2)]
            start_conv[step, :, lanes] = terms[0]
            return states

        empty = jnp.zeros((SEGMENTS, LANES), jnp.float32)
        states = lax.fori_loop(0, steps, scan, (empty,) * modes, unroll=2)
        segment = lax.broadcasted_iota(jnp.int32, (SEGMENTS, LANES), 0)
        for mode in range(modes):
            state = states[mode]
            for level, distance in enumerate((1, 2, 4)):
                moved = pltpu.roll(state, distance, 0)
                state = state + jnp.where(
                    segment >= distance, spread(power, level, mode) * moved, 0.0
                )
            before[mode, :, lanes] = jnp.where(segment >= 1, pltpu.roll(state, 1, 0), 0.0)
            ends[pl.ds(mode, 1), lanes] = state[SEGMENTS - 1 :, :]


def signals(where, pieces, mine, other, halo, products, taps, decay, amplitude, power):
    plan, arrays, _ = plan_of(pieces)
    modes, channels = decay.shape
    steps = 2 * mine.shape[0] // SEGMENTS
    return pl.pallas_call(
        functools.partial(signal_kernel, plan, KEY_VALUE),
        out_shape=(
            pltpu.VMEM((steps, SEGMENTS, channels), jnp.float32),
            pltpu.VMEM((steps, SEGMENTS, channels), jnp.float32),
            pltpu.VMEM((modes, SEGMENTS, channels), jnp.float32),
            jax.ShapeDtypeStruct((modes, channels), jnp.float32),
        ),
        in_specs=[SMEM] + [HBM] * (len(arrays) + 3) + [VMEM] * 5,
        out_specs=(VMEM,) * 4,
        scratch_shapes=copy_scratch(pieces, KEY_VALUE, mine) + [pltpu.VMEM(products.shape, jnp.float32)],
        compiler_params=pltpu.CompilerParams(vmem_limit_bytes=16 * 1024 * 1024),
        name="signals",
    )(
        where,
        *in_hbm(*arrays, mine, other, halo),
        *in_vmem(products),
        taps,
        decay,
        amplitude,
        power,
    )


def query_kernel(plan, streams, parts, where, *refs):
    count = arrays_in(plan)
    pieces, refs = refs[:count], refs[count:]
    mine, other, halo, taps, query, rows, weights, sems, projected = refs
    channels = weights.shape[2]
    steps = 2 * mine.shape[0] // SEGMENTS
    groups = start_copies(plan, streams, where, pieces, mine, other, halo, rows, weights, sems)
    multiply(groups, parts, rows, weights, None, projected, True)
    for group in range(channels // LANES):
        lanes = pl.ds(group * LANES, LANES)
        spread = [
            jnp.broadcast_to(taps[0, offset, lanes].reshape(1, LANES), (SEGMENTS, LANES))
            for offset in range(SHORT)
        ]

        def load(step):
            return projected[0, group, pl.ds(HALO + step, SEGMENTS, stride=steps), :]

        def featurize(step, held):
            held = (load(step),) + held
            total = spread[0] * held[0]
            for offset in range(1, SHORT):
                total += spread[offset] * held[offset]
            query[step, :, lanes] = total
            return held[:-1]

        held = tuple(load(-offset) for offset in range(1, SHORT))
        lax.fori_loop(0, steps, featurize, held, unroll=4)


def queries(where, pieces, mine, other, halo, taps):
    plan, arrays, _ = plan_of(pieces)
    channels = arrays[0].shape[2]
    rows = 2 * mine.shape[0]
    return pl.pallas_call(
        functools.partial(query_kernel, plan, QUERY, 4),
        out_shape=pltpu.VMEM((rows // SEGMENTS, SEGMENTS, channels), jnp.float32),
        in_specs=[SMEM] + [HBM] * (len(arrays) + 3) + [VMEM],
        out_specs=VMEM,
        scratch_shapes=copy_scratch(pieces, QUERY, mine)
        + [pltpu.VMEM((1, channels // LANES, HALO + rows, LANES), jnp.float32)],
        compiler_params=pltpu.CompilerParams(vmem_limit_bytes=24 * 1024 * 1024),
        name="queries",
    )(where, *in_hbm(*arrays, mine, other, halo), taps)


def gate_kernel(
    where,
    query,
    signal,
    start_conv,
    before,
    carried,
    decay,
    amplitude,
    power,
    skip,
    keep,
    send,
    whole,
):
    core = where[2]
    steps, _, channels = signal.shape
    length = keep.shape[0]
    modes = decay.shape[0]
    for low in range(0, channels, LANES):
        lanes = pl.ds(low, LANES)

        def spread(ref, *index):
            return jnp.broadcast_to(ref[(*index, lanes)].reshape(1, LANES), (SEGMENTS, LANES))

        direct = spread(skip, 0)
        decays = [spread(decay, mode) for mode in range(modes)]
        states = tuple(
            spread(amplitude, mode)
            * decays[mode]
            * (before[mode, :, lanes] + power[mode, :, lanes] * spread(carried, mode))
            for mode in range(modes)
        )

        def add(step, states):
            terms = list(states)
            while len(terms) > 1:
                terms = [terms[at] + terms[at + 1] for at in range(0, len(terms), 2)]
            total = start_conv[step, :, lanes] + terms[0] + direct * signal[step, :, lanes]
            whole[low // LANES, pl.ds(step, SEGMENTS, stride=steps), :] = (
                query[step, :, lanes] * total
            )
            return tuple(decays[mode] * states[mode] for mode in range(modes))

        lax.fori_loop(0, steps, add, states, unroll=4)
    for group in range(channels // LANES):
        lanes = pl.ds(group * LANES, LANES)
        for out, block in ((keep, core), (send, 1 - core)):
            first = pl.multiple_of(block * length, SEGMENTS)
            out[:, lanes] = whole[group, pl.ds(first, length), :].astype(jnp.bfloat16)


def gated(where, query, signal, start_conv, before, carried, decay, amplitude, power, skip):
    steps, _, channels = signal.shape
    length = steps * SEGMENTS // 2
    return pl.pallas_call(
        gate_kernel,
        out_shape=(jax.ShapeDtypeStruct((length, channels), jnp.bfloat16),) * 2,
        in_specs=[SMEM] + [VMEM] * 9,
        out_specs=(VMEM,) * 2,
        scratch_shapes=[pltpu.VMEM((channels // LANES, 2 * length, LANES), jnp.float32)],
        compiler_params=pltpu.CompilerParams(vmem_limit_bytes=16 * 1024 * 1024),
        name="gated",
    )(
        where,
        *in_vmem(query, signal, start_conv, before),
        carried,
        decay,
        amplitude,
        power,
        skip,
    )


def carried_states(ends, rate, x, z, span):
    others = [along_z(ends, steps) for steps in range(1, Z)]
    carry = jnp.zeros_like(ends)
    line = ends * jnp.exp(-rate * (span * (Z - 1 - z)))
    for steps, state in zip(range(1, Z), others):
        source = (z - steps) % Z
        line = line + state * jnp.exp(-rate * (span * (Z - 1 - source)))
        carry = carry + jnp.where(z >= steps, state, 0.0) * jnp.exp(-rate * (span * (steps - 1)))
    others = [along_x(line, steps) for steps in range(1, X)]
    far = jnp.zeros_like(ends)
    for steps, state in zip(range(1, X), others):
        far = far + jnp.where(x >= steps, state, 0.0) * jnp.exp(-rate * (Z * span * (steps - 1)))
    return carry + far * jnp.exp(-rate * (span * z))


def local(tokens, in_weight, short_filter, residues, rates, skip):
    index = lax.axis_index("seq")
    core = index % CORES
    z = index // CORES % Z
    x = index // (CORES * Z)
    where = jnp.stack([x, z, core]).astype(jnp.int32)
    length = tokens.shape[0]
    channels = skip.shape[0]
    half = channels // 2
    span = CORES * length
    first = core == 0

    def half_of(array, axis):
        return lax.dynamic_slice_in_dim(array, core * half, half, axis)

    low, high = in_weight[:, :, :half], in_weight[:, :, half:]
    own = jnp.where(first, low, high)
    received = swap_cores(jnp.where(first, high, low))
    block = jnp.concatenate(
        [jnp.where(first, own, received), jnp.where(first, received, own)], axis=1
    )
    up, down = along_z(block, 1), along_z(block, 3)
    right, left = sides(block)
    other = swap_cores(tokens)
    tail = tokens[length - HALO :]
    halo, other_halo = next_chip(tail, 0), next_chip(tail, 1)
    up, right, left, held, other, halo, other_halo = together(
        up, right, left, block, other, halo, other_halo
    )
    halo = halo + other_halo
    near = with_sides(0, block, right, left)

    across = along_z(held, 2)
    far = forwards(right, left)
    right, left = sides(up)
    right, left, far_right, far_left, down = together(right, left, *far, down)
    near += with_far(0, far_right, far_left) + with_sides(1, up, right, left)

    far = forwards(right, left)
    right, left = sides(down)
    right, left, far_right, far_left, across = together(right, left, *far, across)
    near += with_far(1, far_right, far_left) + with_sides(3, down, right, left)
    pieces = near

    far = forwards(right, left)
    right, left = sides(across)
    products = partial_products(where, near, KEY_VALUE, tokens, other, halo, None, 2, "early")
    right, left, far_right, far_left, products = together(right, left, *far, products)
    near = with_far(3, far_right, far_left) + with_sides(2, across, right, left)

    last = with_far(2, *forwards(right, left))

    rate = half_of(rates, 0).T
    residue = half_of(residues, 0).T
    decay = jnp.exp(-rate)
    amplitude = residue * jnp.sqrt(-jnp.expm1(-2.0 * rate))
    step = span // SEGMENTS
    power = jnp.stack([jnp.exp(-rate * (step * distance)) for distance in (1, 2, 4)])
    starts = jnp.arange(SEGMENTS, dtype=jnp.float32)[None, :, None] * step
    start_power = jnp.exp(-rate[:, None, :] * starts)
    taps = half_of(short_filter, 2)

    products = partial_products(where, near, KEY_VALUE, tokens, other, halo, products, 1, "near")
    signal, start_conv, before, ends = signals(
        where, last, tokens, other, halo, products, taps, decay, amplitude, power
    )
    query = queries(where, pieces + near + last, tokens, other, halo, taps)
    carried = carried_states(ends, rate, x, z, span)
    keep, send = gated(
        where,
        query,
        signal,
        start_conv,
        before,
        carried,
        decay,
        amplitude,
        start_power,
        half_of(skip, 0)[None, :],
    )
    taken = swap_cores(send)
    return jnp.concatenate(
        [jnp.where(first, keep, taken), jnp.where(first, taken, keep)], axis=1
    )


def solution(mesh):
    placed = (
        P("seq", None),
        P(None, "seq", "mp"),
        P(None, None, "mp"),
        P("mp", None),
        P("mp", None),
        P("mp"),
    )
    return jax.shard_map(
        local, mesh=mesh, in_specs=placed, out_specs=P("seq", "mp"), check_vma=False
    )
```

time: 160 us -> 120 us (0.75)
  local copies, waits for them, and re-layouts: 23.2 us -> 3.88 us
  waiting for transfers between devices: 44.7 us -> 31.3 us
  between operations: 13.7 us -> 0.42 us
  Pallas kernels: 22.8 us -> 30.3 us
  other arithmetic: 9.77 us -> 4.99 us
  starting transfers between devices: 44.9 us -> 48.7 us
    unnamed x56 -> x46, local copies, waits for them, and re-layouts: 18.7 us -> 1.42 us
    ppermute x29 -> x30, waiting for transfers between devices: 44.7 us -> 31.3 us  [permute(): return lax.ppermute(value, 'seq', pairs)]
    pallas_call x3 -> x5, Pallas kernels: 22.8 us -> 30.3 us  [the longest x2 11.1 us: partial_products(): pl.pallas_call(functools.partial(partial_kernel, plan, streams, parts, be...]
    ppermute x29 -> x30, starting transfers between devices: 44.9 us -> 48.7 us  [permute(): return lax.ppermute(value, 'seq', pairs)]
    another operation x3, other arithmetic: 2.71 us -> 0.03 us  [local(): jnp.stack([jnp.exp(-rate * (step * distance)) for distance in (1, 2, 4)])]
    select_n x2 -> x1, other arithmetic: 1.9 us -> 0.06 us  [local(): jnp.where(first, keep, taken)]
    add x0 -> x1, other arithmetic: none -> 1.67 us  [local(): halo = halo + other_halo]
  transfers between devices with their start and end apart: 30 -> 30, of which waited for: 13 -> 17; matrix products, arithmetic and copies ran while one was open for 8% -> 5% of each run, Pallas kernels for 10% -> 17%
where the time goes in v2:
time: 120 us
  starting transfers between devices  48.7 us (41%)
  waiting for transfers between devices  31.3 us (26%)
  Pallas kernels  30.3 us (25%)
  other arithmetic  4.99 us (4%)
  local copies, waits for them, and re-layouts  3.88 us (3%)
    ppermute x30, starting transfers between devices, permute(): return lax.ppermute(value, 'seq', pairs)  48.7 us
    ppermute x30, waiting for transfers between devices, permute(): return lax.ppermute(value, 'seq', pairs)  31.3 us
    pallas_call x2, Pallas kernels, partial_products(): pl.pallas_call(functools.partial(partial_kernel, plan, streams, parts, be...  11.1 us
    pallas_call x1, Pallas kernels, queries(): pl.pallas_call(functools.partial(query_kernel, plan, QUERY, 4), out_shape...  9.4 us
    pallas_call x1, Pallas kernels, signals(): pl.pallas_call(functools.partial(signal_kernel, plan, KEY_VALUE), out_sha...  7.63 us
  transfers between devices with their start and end apart: 30, of which 17 were waited for; matrix products, arithmetic and copies ran while one was open for 5% of the time, Pallas kernels for 17%

profile of v2, /device:TPU:1, one launch (start us, length us, event | category | flops | bytes accessed | tf_op | source)
XLA Modules:
  0.0 119.6 jit_solution(16266052154508030379)
XLA Ops:
  0.0 3.2 %collective-permute-start.4 = (bf16[512,4096]{1,0:T(8,128)(2,1)}, bf16[512,4096]{1,0:T(8,128)(2,1)}, u32[]{:S(2)}, u32[]{:S(2)}) collective-permute-start(bf16[512,4096]{1,0:T(8,128)(2,1)} %refs_2_.1), channel_id=1, source_target_pairs={{0,8},{8,0},{16,24},{24,16},{32,40},{40,32},{48,56},{56,48},{64,72... | collective-permute-start | bytes 12582920 | tf_op jit(solution)/shard_map/ppermute | solution.py:46
  3.2 1.0 broadcast_select_fusion.4
  4.3 0.1 collective-permute-start
  4.4 5.9 %collective-permute-done = bf16[3,128,256]{2,1,0:T(8,128)(2,1)S(1)} collective-permute-done((bf16[3,128,256]{2,1,0:T(8,128)(2,1)S(1)}, bf16[3,128,256]{2,1,0:T(8,128)(2,1)S(1)}, u32[]{:S(2)}, u32[]{:S(2)}) %collective-permute-start) | collective-permute-done | bytes 196640 | tf_op jit(solution)/shard_map/ppermute | solution.py:46
  10.3 1.1 broadcast_select_fusion.3
  11.4 0.1 collective-permute-start.1
  11.5 1.1 collective-permute-start.2
  12.6 1.7 %collective-permute-start.3 = (bf16[3,256,256]{2,1,0:T(8,128)(2,1)S(1)}, bf16[3,256,256]{2,1,0:T(8,128)(2,1)S(1)}, u32[]{:S(2)}, u32[]{:S(2)}) collective-permute-start(bf16[3,256,256]{2,1,0:T(8,128)(2,1)S(1)} %pad_maximum_fusion.1.refs_0_), channel_id=1, source_target_pairs={{0,192},{8,200},{16,208},{24,216},{32,224},{40,232},{48,240},{56,2... | collective-permute-start | bytes 1179656 | tf_op jit(solution)/shard_map/ppermute | solution.py:46
  14.3 0.9 slice.35
  15.2 4.5 %collective-permute-start.5 = (bf16[16,4096]{1,0:T(8,128)(2,1)S(1)}, bf16[16,4096]{1,0:T(8,128)(2,1)S(1)}, u32[]{:S(2)}, u32[]{:S(2)}) collective-permute-start(bf16[16,4096]{1,0:T(8,128)(2,1)S(1)} %slice.35), channel_id=1, source_target_pairs={{8,16},{24,32},{40,48},{56,64},{72,80},{88,96},{104,112},{120,128}... | collective-permute-start | bytes 393224 | tf_op jit(solution)/shard_map/ppermute | solution.py:46
  19.7 2.2 %collective-permute-done.5 = bf16[16,4096]{1,0:T(8,128)(2,1)S(1)} collective-permute-done((bf16[16,4096]{1,0:T(8,128)(2,1)S(1)}, bf16[16,4096]{1,0:T(8,128)(2,1)S(1)}, u32[]{:S(2)}, u32[]{:S(2)}) %collective-permute-start.5) | collective-permute-done | bytes 131104 | tf_op jit(solution)/shard_map/ppermute | solution.py:46
  21.9 3.4 %collective-permute-start.6 = (bf16[16,4096]{1,0:T(8,128)(2,1)S(1)}, bf16[16,4096]{1,0:T(8,128)(2,1)S(1)}, u32[]{:S(2)}, u32[]{:S(2)}) collective-permute-start(bf16[16,4096]{1,0:T(8,128)(2,1)S(1)} %slice.35), channel_id=1, source_target_pairs={{8,24},{24,40},{40,56},{56,72},{72,88},{88,104},{104,120},{120,136... | collective-permute-start | bytes 393224 | tf_op jit(solution)/shard_map/ppermute | solution.py:46
  25.3 1.9 %collective-permute-done.6 = bf16[16,4096]{1,0:T(8,128)(2,1)S(1)} collective-permute-done((bf16[16,4096]{1,0:T(8,128)(2,1)S(1)}, bf16[16,4096]{1,0:T(8,128)(2,1)S(1)}, u32[]{:S(2)}, u32[]{:S(2)}) %collective-permute-start.6) | collective-permute-done | bytes 131104 | tf_op jit(solution)/shard_map/ppermute | solution.py:46
  27.2 3.6 %collective-permute-start.11 = (bf16[3,256,256]{2,1,0:T(8,128)(2,1)S(1)}, bf16[3,256,256]{2,1,0:T(8,128)(2,1)S(1)}, u32[]{:S(2)}, u32[]{:S(2)}) collective-permute-start(bf16[3,256,256]{2,1,0:T(8,128)(2,1)S(1)} %pad_maximum_fusion.1.refs_0_), channel_id=1, source_target_pairs={{0,48},{8,56},{16,0},{24,8},{32,16},{40,24},{48,32},{56,40},{64,11... | collective-permute-start | bytes 1179656 | tf_op jit(solution)/shard_map/ppermute | solution.py:46
  30.9 2.2 %collective-permute-start.7 = (bf16[3,256,256]{2,1,0:T(8,128)(2,1)S(1)}, bf16[3,256,256]{2,1,0:T(8,128)(2,1)S(1)}, u32[]{:S(2)}, u32[]{:S(2)}) collective-permute-start(bf16[3,256,256]{2,1,0:T(8,128)(2,1)S(1)} %collective-permute-done.1.refs_5_), channel_id=1, source_target_pairs={{0,64},{8,72},{16,80},{24,88},{32,96},{40,104},{48,112},{56,120},{... | collective-permute-start | bytes 1179656 | tf_op jit(solution)/shard_map/ppermute | solution.py:46
  33.1 1.1 collective-permute-start.8
  34.3 0.4 collective-permute-start.9
  34.7 2.4 %collective-permute-start.10 = (bf16[3,128,256]{2,1,0:T(8,128)(2,1)S(1)}, bf16[3,128,256]{2,1,0:T(8,128)(2,1)S(1)}, u32[]{:S(2)}, u32[]{:S(2)}) collective-permute-start(bf16[3,128,256]{2,1,0:T(8,128)(2,1)S(1)} %slice.37), channel_id=1, source_target_pairs={{0,192},{8,200},{16,208},{24,216},{32,224},{40,232},{48,240},{56,2... | collective-permute-start | bytes 589832 | tf_op jit(solution)/shard_map/ppermute | solution.py:46
  37.1 0.1 collective-permute-done.11.refs_10_
  37.2 2.0 %collective-permute-start.16 = (bf16[3,256,256]{2,1,0:T(8,128)(2,1)S(1)}, bf16[3,256,256]{2,1,0:T(8,128)(2,1)}, u32[]{:S(2)}, u32[]{:S(2)}) collective-permute-start(bf16[3,256,256]{2,1,0:T(8,128)(2,1)S(1)} %pad_maximum_fusion.1.refs_0_), channel_id=1, source_target_pairs={{0,32},{8,40},{16,48},{24,56},{32,0},{40,8},{48,16},{56,24},{64,96... | collective-permute-start | bytes 1179656 | tf_op jit(solution)/shard_map/ppermute | solution.py:46
  39.2 6.0 %collective-permute-done.9.refs_3_ = bf16[3,128,256]{2,1,0:T(8,128)(2,1)S(1)} collective-permute-done((bf16[3,128,256]{2,1,0:T(8,128)(2,1)S(1)}, bf16[3,128,256]{2,1,0:T(8,128)(2,1)S(1)}, u32[]{:S(2)}, u32[]{:S(2)}) %collective-permute-start.9) | collective-permute-done | bytes 196640 | tf_op jit(solution)/shard_map/ppermute | solution.py:46
  45.2 0.4 collective-permute-done.10.refs_4_
  45.7 0.7 copy-done.13
  46.3 1.2 %collective-permute-start.12 = (bf16[3,256,256]{2,1,0:T(8,128)(2,1)S(1)}, bf16[3,256,256]{2,1,0:T(8,128)(2,1)S(1)}, u32[]{:S(2)}, u32[]{:S(2)}) collective-permute-start(bf16[3,256,256]{2,1,0:T(8,128)(2,1)S(1)} %collective-permute-done.11.refs_10_), channel_id=1, source_target_pairs={{0,64},{8,72},{16,80},{24,88},{32,96},{40,104},{48,112},{56,120},{... | collective-permute-start | bytes 1179656 | tf_op jit(solution)/shard_map/ppermute | solution.py:46
  47.5 1.5 %collective-permute-start.13 = (bf16[3,256,256]{2,1,0:T(8,128)(2,1)S(1)}, bf16[3,256,256]{2,1,0:T(8,128)(2,1)S(1)}, u32[]{:S(2)}, u32[]{:S(2)}) collective-permute-start(bf16[3,256,256]{2,1,0:T(8,128)(2,1)S(1)} %collective-permute-done.11.refs_10_), channel_id=1, source_target_pairs={{0,192},{8,200},{16,208},{24,216},{32,224},{40,232},{48,240},{56,2... | collective-permute-start | bytes 1179656 | tf_op jit(solution)/shard_map/ppermute | solution.py:46
  49.0 0.7 slice.38
  49.7 0.7 slice.39
  50.4 2.7 %collective-permute-start.15 = (bf16[3,128,256]{2,1,0:T(8,128)(2,1)}, bf16[3,128,256]{2,1,0:T(8,128)(2,1)}, u32[]{:S(2)}, u32[]{:S(2)}) collective-permute-start(bf16[3,128,256]{2,1,0:T(8,128)(2,1)} %slice.39), channel_id=1, source_target_pairs={{0,192},{8,200},{16,208},{24,216},{32,224},{40,232},{48,240},{56,2... | collective-permute-start | bytes 589832 | tf_op jit(solution)/shard_map/ppermute | solution.py:46
  53.1 2.9 %collective-permute-done.16.refs_15_.refs_2_ = bf16[3,256,256]{2,1,0:T(8,128)(2,1)} collective-permute-done((bf16[3,256,256]{2,1,0:T(8,128)(2,1)S(1)}, bf16[3,256,256]{2,1,0:T(8,128)(2,1)}, u32[]{:S(2)}, u32[]{:S(2)}) %collective-permute-start.16) | collective-permute-done | bytes 393248 | tf_op jit(solution)/shard_map/ppermute | solution.py:46
  56.0 4.5 %collective-permute-done.14.refs_8_ = bf16[3,128,256]{2,1,0:T(8,128)(2,1)} collective-permute-done((bf16[3,128,256]{2,1,0:T(8,128)(2,1)}, bf16[3,128,256]{2,1,0:T(8,128)(2,1)}, u32[]{:S(2)}, u32[]{:S(2)}) %collective-permute-start.14) | collective-permute-done | bytes 196640 | tf_op jit(solution)/shard_map/ppermute | solution.py:46
  60.5 0.2 collective-permute-done.15.refs_9_
  60.7 1.2 %collective-permute-start.17 = (bf16[3,256,256]{2,1,0:T(8,128)(2,1)}, bf16[3,256,256]{2,1,0:T(8,128)(2,1)S(1)}, u32[]{:S(2)}, u32[]{:S(2)}) collective-permute-start(bf16[3,256,256]{2,1,0:T(8,128)(2,1)} %collective-permute-done.16.refs_15_.refs_2_), channel_id=1, source_target_pairs={{0,64},{8,72},{16,80},{24,88},{32,96},{40,104},{48,112},{56,120},{... | collective-permute-start | bytes 1179656 | tf_op jit(solution)/shard_map/ppermute | solution.py:46
  62.0 1.9 %collective-permute-start.18 = (bf16[3,256,256]{2,1,0:T(8,128)(2,1)}, bf16[3,256,256]{2,1,0:T(8,128)(2,1)S(1)}, u32[]{:S(2)}, u32[]{:S(2)}) collective-permute-start(bf16[3,256,256]{2,1,0:T(8,128)(2,1)} %collective-permute-done.16.refs_15_.refs_2_), channel_id=1, source_target_pairs={{0,192},{8,200},{16,208},{24,216},{32,224},{40,232},{48,240},{56,2... | collective-permute-start | bytes 1179656 | tf_op jit(solution)/shard_map/ppermute | solution.py:46
  63.8 0.1 pad_add_fusion.where
  63.9 0.1 collective-permute-start.19
  64.0 2.7 %collective-permute-start.20 = (bf16[3,128,256]{2,1,0:T(8,128)(2,1)S(1)}, bf16[3,128,256]{2,1,0:T(8,128)(2,1)S(1)}, u32[]{:S(2)}, u32[]{:S(2)}) collective-permute-start(bf16[3,128,256]{2,1,0:T(8,128)(2,1)S(1)} %slice.41), channel_id=1, source_target_pairs={{0,192},{8,200},{16,208},{24,216},{32,224},{40,232},{48,240},{56,2... | collective-permute-start | bytes 589832 | tf_op jit(solution)/shard_map/ppermute | solution.py:46
  66.8 1.7 %add.56.refs_15_.refs_22_.refs_7_.refs_4_ = bf16[16,4096]{1,0:T(8,128)(2,1)} add(bf16[16,4096]{1,0:T(8,128)(2,1)} %copy-done.18, bf16[16,4096]{1,0:T(8,128)(2,1)} %copy-done.19) | non-fusion elementwise | flops 65536 | bytes 393216 | tf_op jit(solution)/shard_map/add | solution.py:472
  68.5 7.1 %early.1.refs_8_ = f32[2,2,1040,128]{3,2,1,0:T(8,128)S(1)} custom-call(s32[3]{0:T(128)S(1)} %pad_add_fusion.where, bf16[3,256,256]{2,1,0:T(8,128)(2,1)} %copy-done.1, bf16[3,256,256]{2,1,0:T(8,128)(2,1)} %copy-done.2, bf16[3,256,256]{2,1,0:T(8,128)(2,1)} %copy-done.3, bf16[3,128,256]{2,1,0:T(8,128)(2,1)} %copy-done.12, bf16[3,128,256]{2,1,0:T(8,128)(2,1)} %copy-done.13, ...), custom_call_target="tpu_custom_call" | custom-call | tf_op jit(solution)/shard_map/early/pallas_call | solution.py:198
  75.6 0.8 collective-permute-done.19.refs_13_.refs_0_
  76.4 0.5 collective-permute-done.20.refs_14_.refs_1_
  76.9 1.9 %collective-permute-start.21 = (bf16[3,128,256]{2,1,0:T(8,128)(2,1)S(1)}, bf16[3,128,256]{2,1,0:T(8,128)(2,1)S(1)}, u32[]{:S(2)}, u32[]{:S(2)}) collective-permute-start(bf16[3,128,256]{2,1,0:T(8,128)(2,1)S(1)} %slice.42), channel_id=1, source_target_pairs={{0,64},{8,72},{16,80},{24,88},{32,96},{40,104},{48,112},{56,120},{... | collective-permute-start | bytes 589832 | tf_op jit(solution)/shard_map/ppermute | solution.py:46
  78.9 0.9 collective-permute-start.22
  79.9 4.0 %near.1.refs_5_ = f32[2,2,1040,128]{3,2,1,0:T(8,128)S(1)} custom-call(s32[3]{0:T(128)S(1)} %pad_add_fusion.where, bf16[3,128,256]{2,1,0:T(8,128)(2,1)} %copy-done.14, bf16[3,128,256]{2,1,0:T(8,128)(2,1)} %copy-done.15, bf16[3,256,256]{2,1,0:T(8,128)(2,1)} %collective-permute-done.16.refs_15_.refs_2_, bf16[3,256,256]{2,1,0:T(8,128)(2,1)} %copy-done.8, ...), custom_call_target="tpu_custom_call" | custom-call | tf_op jit(solution)/shard_map/near/pallas_call | solution.py:198
  83.9 0.5 collective-permute-done.21.refs_18_.refs_0_
  84.4 0.4 collective-permute-done.22.refs_19_.refs_1_
  84.7 0.3 copy-done.16
  85.0 0.4 copy-done.17
  85.4 7.6 %signals.1 = (f32[128,8,256]{2,1,0:T(8,128)S(1)}, f32[128,8,256]{2,1,0:T(8,128)S(1)}, f32[16,8,256]{2,1,0:T(8,128)S(1)}, f32[16,256]{1,0:T(8,128)S(1)}) custom-call(s32[3]{0:T(128)S(1)} %pad_add_fusion.where, bf16[3,128,256]{2,1,0:T(8,128)(2,1)} %copy-done.16, bf16[3,128,256]{2,1,0:T(8,128)(2,1)} %copy-done.17, bf16[512,4096]{1,0:T(8,128)(2,1)} %refs_2_.1, ...), custom_call_target="tpu_custom_call" | custom-call | tf_op jit(solution)/shard_map/signals/pallas_call | solution.py:284
  93.1 0.3 collective-permute-start.25
  93.3 0.7 collective-permute-start.24
  94.0 0.6 collective-permute-start.23
  94.6 1.1 collective-permute-done.25
  95.7 1.1 collective-permute-done.24
  96.8 1.6 %collective-permute-done.23 = f32[16,256]{1,0:T(8,128)S(1)} collective-permute-done((f32[16,256]{1,0:T(8,128)S(1)}, f32[16,256]{1,0:T(8,128)S(1)}, u32[]{:S(2)}, u32[]{:S(2)}) %collective-permute-start.23) | collective-permute-done | bytes 16416 | tf_op jit(solution)/shard_map/ppermute | solution.py:46
  98.4 3.1 %collective-permute-start.28 = (f32[16,256]{1,0:T(8,128)S(1)}, f32[16,256]{1,0:T(8,128)S(1)}, u32[]{:S(2)}, u32[]{:S(2)}) collective-permute-start(f32[16,256]{1,0:T(8,128)S(1)} %multiply_add_fusion.1), channel_id=1, source_target_pairs={{0,192},{8,200},{16,208},{24,216},{32,224},{40,232},{48,240},{56,2... | collective-permute-start | bytes 49160 | tf_op jit(solution)/shard_map/ppermute | solution.py:46
  101.5 0.1 collective-permute-start.27
  101.6 0.8 collective-permute-start.26
  102.4 0.1 multiply_exponential_fusion.power
  102.5 0.1 dynamic_slice.15
  102.6 9.4 %queries.1.query = f32[128,8,256]{2,1,0:T(8,128)S(1)} custom-call(s32[3]{0:T(128)S(1)} %pad_add_fusion.where, bf16[3,256,256]{2,1,0:T(8,128)(2,1)} %copy-done.1, bf16[3,256,256]{2,1,0:T(8,128)(2,1)} %copy-done.2, bf16[3,256,256]{2,1,0:T(8,128)(2,1)} %copy-done.3, bf16[3,128,256]{2,1,0:T(8,128)(2,1)} %copy-done.12, bf16[3,128,256]{2,1,0:T(8,128)(2,1)} %copy-done.13, ...), custom_call_target="tpu_custom_call" | custom-call | tf_op jit(solution)/shard_map/queries/pallas_call | solution.py:342
  112.1 2.2 %gated.1 = (bf16[512,256]{1,0:T(8,128)(2,1)S(1)}, bf16[512,256]{1,0:T(8,128)(2,1)S(1)}) custom-call(s32[3]{0:T(128)S(1)} %pad_add_fusion.where, f32[128,8,256]{2,1,0:T(8,128)S(1)} %queries.1.query, f32[128,8,256]{2,1,0:T(8,128)S(1)} %get-tuple-element.55.signal, f32[128,8,256]{2,1,0:T(8,128)S(1)} %get-tuple-element.56.start_conv, ...), custom_call_target="tpu_custom_call" | custom-call | tf_op jit(solution)/shard_map/gated/pallas_call | solution.py:409
  114.3 3.2 %collective-permute-start.29 = (bf16[512,256]{1,0:T(8,128)(2,1)S(1)}, bf16[512,256]{1,0:T(8,128)(2,1)S(1)}, u32[]{:S(2)}, u32[]{:S(2)}) collective-permute-start(bf16[512,256]{1,0:T(8,128)(2,1)S(1)} %get-tuple-element.60), channel_id=1, source_target_pairs={{0,8},{8,0},{16,24},{24,16},{32,40},{40,32},{48,56},{56,48},{64,72... | collective-permute-start | bytes 786440 | tf_op jit(solution)/shard_map/ppermute | solution.py:46
  117.5 1.2 collective-permute-done.29
  118.8 0.8 pad_maximum_fusion
  (73 shorter events, 0.4 us)
Async XLA Ops:
  0.0 63.9 %copy-start = (f32[3,7,512]{2,1,0:T(8,128)S(1)}, f32[3,7,512]{2,1,0:T(8,128)}, u32[]{:S(2)}) copy-start(f32[3,7,512]{2,1,0:T(8,128)} %param.8) | copy-start | bytes 129028
  0.0 53.1 %copy-start.20 = (f32[512,16]{0,1:T(8,128)S(1)}, f32[512,16]{0,1:T(8,128)}, u32[]{:S(2)}) copy-start(f32[512,16]{0,1:T(8,128)} %param.10) | copy-start | bytes 98308
  0.0 30.9 %collective-permute-start.4 = (bf16[512,4096]{1,0:T(8,128)(2,1)}, bf16[512,4096]{1,0:T(8,128)(2,1)}, u32[]{:S(2)}, u32[]{:S(2)}) collective-permute-start(bf16[512,4096]{1,0:T(8,128)(2,1)} %refs_2_.1), channel_id=1, source_target_pairs={{0,8},{8,0},{16,24},{24,16},{32,40},{40,32},{48,56},{56,48},{64,72... | collective-permute-start | bytes 12582920 | tf_op jit(solution)/shard_map/ppermute | solution.py:46
  4.3 6.0 %collective-permute-start = (bf16[3,128,256]{2,1,0:T(8,128)(2,1)S(1)}, bf16[3,128,256]{2,1,0:T(8,128)(2,1)S(1)}, u32[]{:S(2)}, u32[]{:S(2)}) collective-permute-start(bf16[3,128,256]{2,1,0:T(8,128)(2,1)S(1)} %broadcast_select_fusion.4), channel_id=1, source_target_pairs={{0,8},{8,0},{16,24},{24,16},{32,40},{40,32},{48,56},{56,48},{64,72... | collective-permute-start | bytes 589832 | tf_op jit(solution)/shard_map/ppermute | solution.py:46
  11.4 57.0 %copy-start.1 = (bf16[3,256,256]{2,1,0:T(8,128)(2,1)}, bf16[3,256,256]{2,1,0:T(8,128)(2,1)S(1)}, u32[]{:S(2)}) copy-start(bf16[3,256,256]{2,1,0:T(8,128)(2,1)S(1)} %pad_maximum_fusion.1.refs_0_) | copy-start | bytes 1179652
  11.4 19.4 %collective-permute-start.1 = (bf16[3,256,256]{2,1,0:T(8,128)(2,1)S(1)}, bf16[3,256,256]{2,1,0:T(8,128)(2,1)S(1)}, u32[]{:S(2)}, u32[]{:S(2)}) collective-permute-start(bf16[3,256,256]{2,1,0:T(8,128)(2,1)S(1)} %pad_maximum_fusion.1.refs_0_), channel_id=1, source_target_pairs={{0,16},{8,24},{16,32},{24,40},{32,48},{40,56},{48,0},{56,8},{64,80... | collective-permute-start | bytes 1179656 | tf_op jit(solution)/shard_map/ppermute | solution.py:46
  11.5 19.3 %collective-permute-start.2 = (bf16[3,256,256]{2,1,0:T(8,128)(2,1)S(1)}, bf16[3,256,256]{2,1,0:T(8,128)(2,1)S(1)}, u32[]{:S(2)}, u32[]{:S(2)}) collective-permute-start(bf16[3,256,256]{2,1,0:T(8,128)(2,1)S(1)} %pad_maximum_fusion.1.refs_0_), channel_id=1, source_target_pairs={{0,64},{8,72},{16,80},{24,88},{32,96},{40,104},{48,112},{56,120},{... | collective-permute-start | bytes 1179656 | tf_op jit(solution)/shard_map/ppermute | solution.py:46
  12.6 18.3 %collective-permute-start.3 = (bf16[3,256,256]{2,1,0:T(8,128)(2,1)S(1)}, bf16[3,256,256]{2,1,0:T(8,128)(2,1)S(1)}, u32[]{:S(2)}, u32[]{:S(2)}) collective-permute-start(bf16[3,256,256]{2,1,0:T(8,128)(2,1)S(1)} %pad_maximum_fusion.1.refs_0_), channel_id=1, source_target_pairs={{0,192},{8,200},{16,208},{24,216},{32,224},{40,232},{48,240},{56,2... | collective-permute-start | bytes 1179656 | tf_op jit(solution)/shard_map/ppermute | solution.py:46
  15.2 6.7 %collective-permute-start.5 = (bf16[16,4096]{1,0:T(8,128)(2,1)S(1)}, bf16[16,4096]{1,0:T(8,128)(2,1)S(1)}, u32[]{:S(2)}, u32[]{:S(2)}) collective-permute-start(bf16[16,4096]{1,0:T(8,128)(2,1)S(1)} %slice.35), channel_id=1, source_target_pairs={{8,16},{24,32},{40,48},{56,64},{72,80},{88,96},{104,112},{120,128}... | collective-permute-start | bytes 393224 | tf_op jit(solution)/shard_map/ppermute | solution.py:46
  21.9 11.3 %copy-start.18 = (bf16[16,4096]{1,0:T(8,128)(2,1)}, bf16[16,4096]{1,0:T(8,128)(2,1)S(1)}, u32[]{:S(2)}) copy-start(bf16[16,4096]{1,0:T(8,128)(2,1)S(1)} %collective-permute-done.5) | copy-start | bytes 393220
  21.9 5.4 %collective-permute-start.6 = (bf16[16,4096]{1,0:T(8,128)(2,1)S(1)}, bf16[16,4096]{1,0:T(8,128)(2,1)S(1)}, u32[]{:S(2)}, u32[]{:S(2)}) collective-permute-start(bf16[16,4096]{1,0:T(8,128)(2,1)S(1)} %slice.35), channel_id=1, source_target_pairs={{8,24},{24,40},{40,56},{56,72},{72,88},{88,104},{104,120},{120,136... | collective-permute-start | bytes 393224 | tf_op jit(solution)/shard_map/ppermute | solution.py:46
  27.2 3.7 %copy-start.19 = (bf16[16,4096]{1,0:T(8,128)(2,1)}, bf16[16,4096]{1,0:T(8,128)(2,1)S(1)}, u32[]{:S(2)}) copy-start(bf16[16,4096]{1,0:T(8,128)(2,1)S(1)} %collective-permute-done.6) | copy-start | bytes 393220
  27.2 10.0 %collective-permute-start.11 = (bf16[3,256,256]{2,1,0:T(8,128)(2,1)S(1)}, bf16[3,256,256]{2,1,0:T(8,128)(2,1)S(1)}, u32[]{:S(2)}, u32[]{:S(2)}) collective-permute-start(bf16[3,256,256]{2,1,0:T(8,128)(2,1)S(1)} %pad_maximum_fusion.1.refs_0_), channel_id=1, source_target_pairs={{0,48},{8,56},{16,0},{24,8},{32,16},{40,24},{48,32},{56,40},{64,11... | collective-permute-start | bytes 1179656 | tf_op jit(solution)/shard_map/ppermute | solution.py:46
  30.9 14.8 %copy-start.10 = (bf16[3,256,256]{2,1,0:T(8,128)(2,1)}, bf16[3,256,256]{2,1,0:T(8,128)(2,1)S(1)}, u32[]{:S(2)}) copy-start(bf16[3,256,256]{2,1,0:T(8,128)(2,1)S(1)} %collective-permute-done.1.refs_5_) | copy-start | bytes 1179652
  30.9 37.6 %copy-start.2 = (bf16[3,256,256]{2,1,0:T(8,128)(2,1)}, bf16[3,256,256]{2,1,0:T(8,128)(2,1)S(1)}, u32[]{:S(2)}) copy-start(bf16[3,256,256]{2,1,0:T(8,128)(2,1)S(1)} %collective-permute-done.2.refs_1_) | copy-start | bytes 1179652
  30.9 37.6 %copy-start.3 = (bf16[3,256,256]{2,1,0:T(8,128)(2,1)}, bf16[3,256,256]{2,1,0:T(8,128)(2,1)S(1)}, u32[]{:S(2)}) copy-start(bf16[3,256,256]{2,1,0:T(8,128)(2,1)S(1)} %collective-permute-done.3.refs_2_) | copy-start | bytes 1179652
  30.9 14.7 %collective-permute-start.7 = (bf16[3,256,256]{2,1,0:T(8,128)(2,1)S(1)}, bf16[3,256,256]{2,1,0:T(8,128)(2,1)S(1)}, u32[]{:S(2)}, u32[]{:S(2)}) collective-permute-start(bf16[3,256,256]{2,1,0:T(8,128)(2,1)S(1)} %collective-permute-done.1.refs_5_), channel_id=1, source_target_pairs={{0,64},{8,72},{16,80},{24,88},{32,96},{40,104},{48,112},{56,120},{... | collective-permute-start | bytes 1179656 | tf_op jit(solution)/shard_map/ppermute | solution.py:46
  33.1 12.5 %collective-permute-start.8 = (bf16[3,256,256]{2,1,0:T(8,128)(2,1)S(1)}, bf16[3,256,256]{2,1,0:T(8,128)(2,1)S(1)}, u32[]{:S(2)}, u32[]{:S(2)}) collective-permute-start(bf16[3,256,256]{2,1,0:T(8,128)(2,1)S(1)} %collective-permute-done.1.refs_5_), channel_id=1, source_target_pairs={{0,192},{8,200},{16,208},{24,216},{32,224},{40,232},{48,240},{56,2... | collective-permute-start | bytes 1179656 | tf_op jit(solution)/shard_map/ppermute | solution.py:46
  34.3 10.9 %collective-permute-start.9 = (bf16[3,128,256]{2,1,0:T(8,128)(2,1)S(1)}, bf16[3,128,256]{2,1,0:T(8,128)(2,1)S(1)}, u32[]{:S(2)}, u32[]{:S(2)}) collective-permute-start(bf16[3,128,256]{2,1,0:T(8,128)(2,1)S(1)} %slice.36), channel_id=1, source_target_pairs={{0,64},{8,72},{16,80},{24,88},{32,96},{40,104},{48,112},{56,120},{... | collective-permute-start | bytes 589832 | tf_op jit(solution)/shard_map/ppermute | solution.py:46
  34.7 10.9 %collective-permute-start.10 = (bf16[3,128,256]{2,1,0:T(8,128)(2,1)S(1)}, bf16[3,128,256]{2,1,0:T(8,128)(2,1)S(1)}, u32[]{:S(2)}, u32[]{:S(2)}) collective-permute-start(bf16[3,128,256]{2,1,0:T(8,128)(2,1)S(1)} %slice.37), channel_id=1, source_target_pairs={{0,192},{8,200},{16,208},{24,216},{32,224},{40,232},{48,240},{56,2... | collective-permute-start | bytes 589832 | tf_op jit(solution)/shard_map/ppermute | solution.py:46
  37.2 23.5 %copy-start.11 = (bf16[3,256,256]{2,1,0:T(8,128)(2,1)}, bf16[3,256,256]{2,1,0:T(8,128)(2,1)S(1)}, u32[]{:S(2)}) copy-start(bf16[3,256,256]{2,1,0:T(8,128)(2,1)S(1)} %collective-permute-done.11.refs_10_) | copy-start | bytes 1179652
  37.2 18.8 %collective-permute-start.16 = (bf16[3,256,256]{2,1,0:T(8,128)(2,1)S(1)}, bf16[3,256,256]{2,1,0:T(8,128)(2,1)}, u32[]{:S(2)}, u32[]{:S(2)}) collective-permute-start(bf16[3,256,256]{2,1,0:T(8,128)(2,1)S(1)} %pad_maximum_fusion.1.refs_0_), channel_id=1, source_target_pairs={{0,32},{8,40},{16,48},{24,56},{32,0},{40,8},{48,16},{56,24},{64,96... | collective-permute-start | bytes 1179656 | tf_op jit(solution)/shard_map/ppermute | solution.py:46
  45.2 23.3 %copy-start.12 = (bf16[3,128,256]{2,1,0:T(8,128)(2,1)}, bf16[3,128,256]{2,1,0:T(8,128)(2,1)S(1)}, u32[]{:S(2)}) copy-start(bf16[3,128,256]{2,1,0:T(8,128)(2,1)S(1)} %collective-permute-done.9.refs_3_) | copy-start | bytes 589828
  45.6 0.7 copy-start.13
  45.7 22.8 %copy-start.4 = (bf16[3,256,256]{2,1,0:T(8,128)(2,1)}, bf16[3,256,256]{2,1,0:T(8,128)(2,1)S(1)}, u32[]{:S(2)}) copy-start(bf16[3,256,256]{2,1,0:T(8,128)(2,1)S(1)} %collective-permute-done.7.refs_6_) | copy-start | bytes 1179652
  46.3 22.2 %copy-start.5 = (bf16[3,256,256]{2,1,0:T(8,128)(2,1)}, bf16[3,256,256]{2,1,0:T(8,128)(2,1)S(1)}, u32[]{:S(2)}) copy-start(bf16[3,256,256]{2,1,0:T(8,128)(2,1)S(1)} %collective-permute-done.8.refs_7_) | copy-start | bytes 1179652
  46.3 14.4 %collective-permute-start.12 = (bf16[3,256,256]{2,1,0:T(8,128)(2,1)S(1)}, bf16[3,256,256]{2,1,0:T(8,128)(2,1)S(1)}, u32[]{:S(2)}, u32[]{:S(2)}) collective-permute-start(bf16[3,256,256]{2,1,0:T(8,128)(2,1)S(1)} %collective-permute-done.11.refs_10_), channel_id=1, source_target_pairs={{0,64},{8,72},{16,80},{24,88},{32,96},{40,104},{48,112},{56,120},{... | collective-permute-start | bytes 1179656 | tf_op jit(solution)/shard_map/ppermute | solution.py:46
  47.5 13.2 %collective-permute-start.13 = (bf16[3,256,256]{2,1,0:T(8,128)(2,1)S(1)}, bf16[3,256,256]{2,1,0:T(8,128)(2,1)S(1)}, u32[]{:S(2)}, u32[]{:S(2)}) collective-permute-start(bf16[3,256,256]{2,1,0:T(8,128)(2,1)S(1)} %collective-permute-done.11.refs_10_), channel_id=1, source_target_pairs={{0,192},{8,200},{16,208},{24,216},{32,224},{40,232},{48,240},{56,2... | collective-permute-start | bytes 1179656 | tf_op jit(solution)/shard_map/ppermute | solution.py:46
  49.7 10.8 %collective-permute-start.14 = (bf16[3,128,256]{2,1,0:T(8,128)(2,1)}, bf16[3,128,256]{2,1,0:T(8,128)(2,1)}, u32[]{:S(2)}, u32[]{:S(2)}) collective-permute-start(bf16[3,128,256]{2,1,0:T(8,128)(2,1)} %slice.38), channel_id=1, source_target_pairs={{0,64},{8,72},{16,80},{24,88},{32,96},{40,104},{48,112},{56,120},{... | collective-permute-start | bytes 589832 | tf_op jit(solution)/shard_map/ppermute | solution.py:46
  50.4 10.3 %collective-permute-start.15 = (bf16[3,128,256]{2,1,0:T(8,128)(2,1)}, bf16[3,128,256]{2,1,0:T(8,128)(2,1)}, u32[]{:S(2)}, u32[]{:S(2)}) collective-permute-start(bf16[3,128,256]{2,1,0:T(8,128)(2,1)} %slice.39), channel_id=1, source_target_pairs={{0,192},{8,200},{16,208},{24,216},{32,224},{40,232},{48,240},{56,2... | collective-permute-start | bytes 589832 | tf_op jit(solution)/shard_map/ppermute | solution.py:46
  60.7 7.8 %copy-start.6 = (bf16[3,256,256]{2,1,0:T(8,128)(2,1)}, bf16[3,256,256]{2,1,0:T(8,128)(2,1)S(1)}, u32[]{:S(2)}) copy-start(bf16[3,256,256]{2,1,0:T(8,128)(2,1)S(1)} %collective-permute-done.12.refs_11_) | copy-start | bytes 1179652
  60.7 7.8 %copy-start.7 = (bf16[3,256,256]{2,1,0:T(8,128)(2,1)}, bf16[3,256,256]{2,1,0:T(8,128)(2,1)S(1)}, u32[]{:S(2)}) copy-start(bf16[3,256,256]{2,1,0:T(8,128)(2,1)S(1)} %collective-permute-done.13.refs_12_) | copy-start | bytes 1179652
  60.7 16.2 %collective-permute-start.17 = (bf16[3,256,256]{2,1,0:T(8,128)(2,1)}, bf16[3,256,256]{2,1,0:T(8,128)(2,1)S(1)}, u32[]{:S(2)}, u32[]{:S(2)}) collective-permute-start(bf16[3,256,256]{2,1,0:T(8,128)(2,1)} %collective-permute-done.16.refs_15_.refs_2_), channel_id=1, source_target_pairs={{0,64},{8,72},{16,80},{24,88},{32,96},{40,104},{48,112},{56,120},{... | collective-permute-start | bytes 1179656 | tf_op jit(solution)/shard_map/ppermute | solution.py:46
  62.0 14.9 %collective-permute-start.18 = (bf16[3,256,256]{2,1,0:T(8,128)(2,1)}, bf16[3,256,256]{2,1,0:T(8,128)(2,1)S(1)}, u32[]{:S(2)}, u32[]{:S(2)}) collective-permute-start(bf16[3,256,256]{2,1,0:T(8,128)(2,1)} %collective-permute-done.16.refs_15_.refs_2_), channel_id=1, source_target_pairs={{0,192},{8,200},{16,208},{24,216},{32,224},{40,232},{48,240},{56,2... | collective-permute-start | bytes 1179656 | tf_op jit(solution)/shard_map/ppermute | solution.py:46
  63.9 12.4 %collective-permute-start.19 = (bf16[3,128,256]{2,1,0:T(8,128)(2,1)S(1)}, bf16[3,128,256]{2,1,0:T(8,128)(2,1)S(1)}, u32[]{:S(2)}, u32[]{:S(2)}) collective-permute-start(bf16[3,128,256]{2,1,0:T(8,128)(2,1)S(1)} %slice.40), channel_id=1, source_target_pairs={{0,64},{8,72},{16,80},{24,88},{32,96},{40,104},{48,112},{56,120},{... | collective-permute-start | bytes 589832 | tf_op jit(solution)/shard_map/ppermute | solution.py:46
  64.0 12.9 %collective-permute-start.20 = (bf16[3,128,256]{2,1,0:T(8,128)(2,1)S(1)}, bf16[3,128,256]{2,1,0:T(8,128)(2,1)S(1)}, u32[]{:S(2)}, u32[]{:S(2)}) collective-permute-start(bf16[3,128,256]{2,1,0:T(8,128)(2,1)S(1)} %slice.41), channel_id=1, source_target_pairs={{0,192},{8,200},{16,208},{24,216},{32,224},{40,232},{48,240},{56,2... | collective-permute-start | bytes 589832 | tf_op jit(solution)/shard_map/ppermute | solution.py:46
  68.5 11.3 %copy-start.21 = (f32[512,16]{0,1:T(8,128)S(1)}, f32[512,16]{0,1:T(8,128)}, u32[]{:S(2)}) copy-start(f32[512,16]{0,1:T(8,128)} %param.9) | copy-start | bytes 98308
  76.4 3.5 %copy-start.14 = (bf16[3,128,256]{2,1,0:T(8,128)(2,1)}, bf16[3,128,256]{2,1,0:T(8,128)(2,1)S(1)}, u32[]{:S(2)}) copy-start(bf16[3,128,256]{2,1,0:T(8,128)(2,1)S(1)} %collective-permute-done.19.refs_13_.refs_0_) | copy-start | bytes 589828
  76.9 3.0 %copy-start.15 = (bf16[3,128,256]{2,1,0:T(8,128)(2,1)}, bf16[3,128,256]{2,1,0:T(8,128)(2,1)S(1)}, u32[]{:S(2)}) copy-start(bf16[3,128,256]{2,1,0:T(8,128)(2,1)S(1)} %collective-permute-done.20.refs_14_.refs_1_) | copy-start | bytes 589828
  76.9 3.0 %copy-start.8 = (bf16[3,256,256]{2,1,0:T(8,128)(2,1)}, bf16[3,256,256]{2,1,0:T(8,128)(2,1)S(1)}, u32[]{:S(2)}) copy-start(bf16[3,256,256]{2,1,0:T(8,128)(2,1)S(1)} %collective-permute-done.17.refs_16_.refs_3_) | copy-start | bytes 1179652
  76.9 3.0 %copy-start.9 = (bf16[3,256,256]{2,1,0:T(8,128)(2,1)}, bf16[3,256,256]{2,1,0:T(8,128)(2,1)S(1)}, u32[]{:S(2)}) copy-start(bf16[3,256,256]{2,1,0:T(8,128)(2,1)S(1)} %collective-permute-done.18.refs_17_.refs_4_) | copy-start | bytes 1179652
  76.9 7.4 %collective-permute-start.21 = (bf16[3,128,256]{2,1,0:T(8,128)(2,1)S(1)}, bf16[3,128,256]{2,1,0:T(8,128)(2,1)S(1)}, u32[]{:S(2)}, u32[]{:S(2)}) collective-permute-start(bf16[3,128,256]{2,1,0:T(8,128)(2,1)S(1)} %slice.42), channel_id=1, source_target_pairs={{0,64},{8,72},{16,80},{24,88},{32,96},{40,104},{48,112},{56,120},{... | collective-permute-start | bytes 589832 | tf_op jit(solution)/shard_map/ppermute | solution.py:46
  78.9 5.8 %collective-permute-start.22 = (bf16[3,128,256]{2,1,0:T(8,128)(2,1)S(1)}, bf16[3,128,256]{2,1,0:T(8,128)(2,1)S(1)}, u32[]{:S(2)}, u32[]{:S(2)}) collective-permute-start(bf16[3,128,256]{2,1,0:T(8,128)(2,1)S(1)} %slice.43), channel_id=1, source_target_pairs={{0,192},{8,200},{16,208},{24,216},{32,224},{40,232},{48,240},{56,2... | collective-permute-start | bytes 589832 | tf_op jit(solution)/shard_map/ppermute | solution.py:46
  84.4 0.7 copy-start.16
  84.7 0.7 copy-start.17
  85.4 17.1 %copy-start.22 = (f32[512]{0:T(512)S(1)}, f32[512]{0:T(512)}, u32[]{:S(2)}) copy-start(f32[512]{0:T(512)} %param.11) | copy-start | bytes 6148
  93.1 2.7 %collective-permute-start.25 = (f32[16,256]{1,0:T(8,128)S(1)}, f32[16,256]{1,0:T(8,128)S(1)}, u32[]{:S(2)}, u32[]{:S(2)}) collective-permute-start(f32[16,256]{1,0:T(8,128)S(1)} %get-tuple-element.58), channel_id=1, source_target_pairs={{0,48},{8,56},{16,0},{24,8},{32,16},{40,24},{48,32},{56,40},{64,11... | collective-permute-start | bytes 49160 | tf_op jit(solution)/shard_map/ppermute | solution.py:46
  93.3 3.5 %collective-permute-start.24 = (f32[16,256]{1,0:T(8,128)S(1)}, f32[16,256]{1,0:T(8,128)S(1)}, u32[]{:S(2)}, u32[]{:S(2)}) collective-permute-start(f32[16,256]{1,0:T(8,128)S(1)} %get-tuple-element.58), channel_id=1, source_target_pairs={{0,32},{8,40},{16,48},{24,56},{32,0},{40,8},{48,16},{56,24},{64,96... | collective-permute-start | bytes 49160 | tf_op jit(solution)/shard_map/ppermute | solution.py:46
  94.0 4.4 %collective-permute-start.23 = (f32[16,256]{1,0:T(8,128)S(1)}, f32[16,256]{1,0:T(8,128)S(1)}, u32[]{:S(2)}, u32[]{:S(2)}) collective-permute-start(f32[16,256]{1,0:T(8,128)S(1)} %get-tuple-element.58), channel_id=1, source_target_pairs={{0,16},{8,24},{16,32},{24,40},{32,48},{40,56},{48,0},{56,8},{64,80... | collective-permute-start | bytes 49160 | tf_op jit(solution)/shard_map/ppermute | solution.py:46
  98.4 13.6 %collective-permute-start.28 = (f32[16,256]{1,0:T(8,128)S(1)}, f32[16,256]{1,0:T(8,128)S(1)}, u32[]{:S(2)}, u32[]{:S(2)}) collective-permute-start(f32[16,256]{1,0:T(8,128)S(1)} %multiply_add_fusion.1), channel_id=1, source_target_pairs={{0,192},{8,200},{16,208},{24,216},{32,224},{40,232},{48,240},{56,2... | collective-permute-start | bytes 49160 | tf_op jit(solution)/shard_map/ppermute | solution.py:46
  101.5 10.5 %collective-permute-start.27 = (f32[16,256]{1,0:T(8,128)S(1)}, f32[16,256]{1,0:T(8,128)S(1)}, u32[]{:S(2)}, u32[]{:S(2)}) collective-permute-start(f32[16,256]{1,0:T(8,128)S(1)} %multiply_add_fusion.1), channel_id=1, source_target_pairs={{0,128},{8,136},{16,144},{24,152},{32,160},{40,168},{48,176},{56,1... | collective-permute-start | bytes 49160 | tf_op jit(solution)/shard_map/ppermute | solution.py:46
  101.6 10.4 %collective-permute-start.26 = (f32[16,256]{1,0:T(8,128)S(1)}, f32[16,256]{1,0:T(8,128)S(1)}, u32[]{:S(2)}, u32[]{:S(2)}) collective-permute-start(f32[16,256]{1,0:T(8,128)S(1)} %multiply_add_fusion.1), channel_id=1, source_target_pairs={{0,64},{8,72},{16,80},{24,88},{32,96},{40,104},{48,112},{56,120},{... | collective-permute-start | bytes 49160 | tf_op jit(solution)/shard_map/ppermute | solution.py:46
  114.3 4.4 %collective-permute-start.29 = (bf16[512,256]{1,0:T(8,128)(2,1)S(1)}, bf16[512,256]{1,0:T(8,128)(2,1)S(1)}, u32[]{:S(2)}, u32[]{:S(2)}) collective-permute-start(bf16[512,256]{1,0:T(8,128)(2,1)S(1)} %get-tuple-element.60), channel_id=1, source_target_pairs={{0,8},{8,0},{16,24},{24,16},{32,40},{40,32},{48,56},{56,48},{64,72... | collective-permute-start | bytes 786440 | tf_op jit(solution)/shard_map/ppermute | solution.py:46

commit v3 on v2

v3 whole, which is shorter than its diff:
```python
import functools
import math

import jax
import jax.numpy as jnp
from jax import lax
from jax.experimental import pallas as pl
from jax.experimental.pallas import tpu as pltpu
from jax.sharding import PartitionSpec as P

SHORT = 7
X, Z, CORES = 4, 4, 2
CHIPS = X * Z
HALO = 16
LANES = 128
SEGMENTS = 8
BEFORE = 8

QUERY = pl.ds(0, 1)
KEY_VALUE = pl.ds(1, 2)
ALL = pl.ds(0, 3)

ANY = pl.BlockSpec(memory_space=pl.ANY)
HBM = pl.BlockSpec(memory_space=pltpu.HBM)
VMEM = pl.BlockSpec(memory_space=pltpu.VMEM)
SMEM = pl.BlockSpec(memory_space=pltpu.SMEM)


def in_hbm(*arrays):
    return [pltpu.with_memory_space_constraint(array, pltpu.HBM) for array in arrays]


def in_vmem(*arrays):
    return [pltpu.with_memory_space_constraint(array, pltpu.VMEM) for array in arrays]


def place(x, z, core):
    return (x * Z + z) * CORES + core


def permute(value, target):
    pairs = []
    for x in range(X):
        for z in range(Z):
            for core in range(CORES):
                to = target(x, z, core)
                if to is not None:
                    pairs.append((place(x, z, core), place(*to)))
    return lax.ppermute(value, "seq", pairs)


def along_x(value, steps):
    return permute(value, lambda x, z, core: ((x + steps) % X, z, core))


def along_z(value, steps):
    return permute(value, lambda x, z, core: (x, (z + steps) % Z, core))


def across_z(value, mask):
    return permute(value, lambda x, z, core: (x, z ^ mask, core))


def swap_cores(value):
    return permute(value, lambda x, z, core: (x, z, 1 - core))


def next_chip(value):
    def target(x, z, core):
        chip = x * Z + z + 1
        return (chip // Z, chip % Z, core) if chip < CHIPS else None

    return permute(value, target)


def together(*values):
    return lax.optimization_barrier(values)


def halves_kernel(right, left, right_half, left_half, sems):
    half = right_half.shape[1]
    copies = [
        pltpu.make_async_copy(right.at[:, pl.ds(0, half), :], right_half, sems.at[0]),
        pltpu.make_async_copy(left.at[:, pl.ds(half, half), :], left_half, sems.at[1]),
    ]
    for copy in copies:
        copy.start()
    for copy in copies:
        copy.wait()


def forwards(right, left):
    streams, height, channels = right.shape
    half = pltpu.VMEM((streams, height // 2, channels), right.dtype)
    right, left = pl.pallas_call(
        halves_kernel,
        out_shape=(half, half),
        in_specs=[ANY] * 2,
        out_specs=(VMEM,) * 2,
        scratch_shapes=[pltpu.SemaphoreType.DMA((2,))],
        compiler_params=pltpu.CompilerParams(vmem_limit_bytes=2 * 1024 * 1024),
        name="halves",
    )(right, left)
    return along_x(right, 1), along_x(left, 3)


def sides(block):
    return along_x(block, 1), along_x(block, 3)


def with_sides(z_mask, block, right, left):
    height = block.shape[1]
    return [
        (x_steps, z_mask, 0, array, 0, height)
        for x_steps, array in ((0, block), (1, right), (3, left))
    ]


def with_far(z_mask, far_right, far_left):
    height = far_right.shape[1]
    return [(2, z_mask, 0, far_right, 0, height), (2, z_mask, height, far_left, 0, height)]


def rounded(value):
    return value.astype(jnp.bfloat16).astype(jnp.float32)


def start_copies(plan, streams, where, pieces, mine, other, halo, rows, weights, sems):
    x, z, core = where[0], where[1], where[2]
    parts = []
    if halo is not None:
        parts.append((1, halo, 0))
    if mine is not None:
        base = HALO if halo is not None else 0
        length = mine.shape[0]
        parts += [(2, mine, base + core * length), (3, other, base + (1 - core) * length)]
    depth = CHIPS * 2 * LANES
    copies = []
    offset = 0
    for at, (x_steps, z_mask, row, which, start, height) in enumerate(plan):
        chip = (x - x_steps + X) % X * Z + (z ^ z_mask)
        column = pl.multiple_of(chip * (depth // CHIPS) + row, LANES)
        copies.append(
            pltpu.make_async_copy(
                pieces[which].at[streams, pl.ds(start, height), :],
                weights.at[:, pl.ds(offset, height), :],
                sems.at[at, 0],
            )
        )
        for sem, array, first in parts:
            if array is not halo:
                first = pl.multiple_of(first, HALO)
            copies.append(
                pltpu.make_async_copy(
                    array.at[:, pl.ds(column, height)],
                    rows.at[pl.ds(first, array.shape[0]), pl.ds(offset, height)],
                    sems.at[at, sem],
                )
            )
        offset += height
    for copy in copies:
        copy.start()
    return copies


def multiply(copies, rows, weights, finish):
    for copy in copies:
        copy.wait()
    streams, _, channels = weights.shape
    for stream in range(streams):
        product = jnp.dot(rows[...], weights[stream], preferred_element_type=jnp.float32)
        for group in range(channels // LANES):
            finish(stream, group, product[:, group * LANES : (group + 1) * LANES])


def segmented(ref, before, halo_before, first_stream):
    stride = ref.shape[2] // SEGMENTS
    steps = stride - BEFORE

    def finish(stream, group, share):
        main = rounded(before[first_stream + stream, group] + share[HALO:])
        head = rounded(halo_before[first_stream + stream, group] + share[:HALO])
        ref[stream, group, 0:BEFORE, :] = head[HALO - BEFORE :]
        ref[stream, group, BEFORE:stride, :] = main[:steps]
        for segment in range(1, SEGMENTS):
            first = segment * steps - BEFORE
            ref[stream, group, segment * stride : (segment + 1) * stride, :] = main[
                first : first + stride
            ]

    def load(stream, group, step):
        return ref[stream, group, pl.ds(BEFORE + step, SEGMENTS, stride=stride), :]

    return finish, load


def segment_scratch(streams, rows, channels):
    return pltpu.VMEM((streams.size, channels // LANES, rows + SEGMENTS * BEFORE, LANES), jnp.float32)


def arrays_in(plan):
    return 1 + max(step[3] for step in plan)


def partial_kernel(plan, has_main, has_halo, has_before, where, *refs):
    count = arrays_in(plan)
    pieces, refs = refs[:count], list(refs[count:])
    mine, other = (refs.pop(0), refs.pop(0)) if has_main else (None, None)
    halo = refs.pop(0) if has_halo else None
    before = refs.pop(0) if has_main and has_before else None
    halo_before = refs.pop(0) if has_halo and has_before else None
    totals = refs.pop(0) if has_main else None
    halo_totals = refs.pop(0) if has_halo else None
    rows, weights, sems = refs
    copies = start_copies(plan, ALL, where, pieces, mine, other, halo, rows, weights, sems)

    def finish(stream, group, share):
        if has_halo:
            head = share[:HALO]
            halo_totals[stream, group] = (
                head if halo_before is None else halo_before[stream, group] + head
            )
            share = share[HALO:]
        if has_main:
            totals[stream, group] = share if before is None else before[stream, group] + share

    multiply(copies, rows, weights, finish)


def plan_of(pieces):
    arrays = []
    plan = []
    for x_steps, z_mask, row, array, start, height in pieces:
        which = next((at for at, seen in enumerate(arrays) if seen is array), len(arrays))
        if which == len(arrays):
            arrays.append(array)
        plan.append((x_steps, z_mask, row, which, start, height))
    return tuple(plan), arrays, sum(step[-1] for step in plan)


def copy_scratch(pieces, streams, rows):
    plan, arrays, depth = plan_of(pieces)
    channels = arrays[0].shape[2]
    return [
        pltpu.VMEM((rows, depth), jnp.bfloat16),
        pltpu.VMEM((streams.size, depth, channels), jnp.bfloat16),
        pltpu.SemaphoreType.DMA((len(plan), 4)),
    ]


def partial_products(where, pieces, tokens, halo, before, name):
    plan, arrays, _ = plan_of(pieces)
    channels = arrays[0].shape[2]
    heights = [sum(array.shape[0] for array in tokens)] if tokens else []
    heights += [HALO] if halo else []
    shapes = [
        pltpu.VMEM((ALL.size, channels // LANES, height, LANES), jnp.float32) for height in heights
    ]
    inputs = [*arrays, *tokens, *halo]
    return pl.pallas_call(
        functools.partial(partial_kernel, plan, bool(tokens), bool(halo), bool(before)),
        out_shape=shapes,
        in_specs=[SMEM] + [HBM] * len(inputs) + [VMEM] * len(before),
        out_specs=[VMEM] * len(shapes),
        scratch_shapes=copy_scratch(pieces, ALL, sum(heights)),
        compiler_params=pltpu.CompilerParams(vmem_limit_bytes=8 * 1024 * 1024),
        name=name,
    )(where, *in_hbm(*inputs), *in_vmem(*before))


def signal_kernel(plan, streams, where, *refs):
    count = arrays_in(plan)
    pieces, refs = refs[:count], refs[count:]
    mine, other, halo, products, halo_products = refs[:5]
    taps, decay, amplitude, power, skip = refs[5:10]
    signal, before, ends, rows, weights, sems, projected = refs[10:]
    channels = weights.shape[2]
    steps = 2 * mine.shape[0] // SEGMENTS
    copies = start_copies(plan, streams, where, pieces, mine, other, halo, rows, weights, sems)
    finish, load = segmented(projected, products, halo_products, streams.start)
    multiply(copies, rows, weights, finish)
    for low in range(0, channels, LANES):
        lanes = pl.ds(low, LANES)
        group = low // LANES

        def spread(ref, *index):
            return jnp.broadcast_to(ref[(*index, lanes)].reshape(1, LANES), (SEGMENTS, LANES))

        key_taps = [spread(taps, 1, offset) for offset in range(SHORT)]
        value_taps = [spread(taps, 2, offset) for offset in range(SHORT)]

        def featurize(step, carry):
            keys, values = carry
            keys = (load(0, group, step),) + keys
            values = (load(1, group, step),) + values
            total_key = key_taps[0] * keys[0]
            total_value = value_taps[0] * values[0]
            for offset in range(1, SHORT):
                total_key += key_taps[offset] * keys[offset]
                total_value += value_taps[offset] * values[offset]
            signal[step, :, lanes] = total_key * total_value
            return keys[:-1], values[:-1]

        lax.fori_loop(
            0,
            steps,
            featurize,
            (
                tuple(load(0, group, -offset) for offset in range(1, SHORT)),
                tuple(load(1, group, -offset) for offset in range(1, SHORT)),
            ),
            unroll=8,
        )
        modes = decay.shape[0]
        decays = [spread(decay, mode) for mode in range(modes)]
        amplitudes = [spread(amplitude, mode) for mode in range(modes)]
        direct = spread(skip, 0)

        def scan(step, states):
            here = signal[step, :, lanes]
            states = tuple(decays[mode] * states[mode] + here for mode in range(modes))
            terms = [amplitudes[mode] * states[mode] for mode in range(modes)]
            while len(terms) > 1:
                terms = [terms[at] + terms[at + 1] for at in range(0, len(terms), 2)]
            signal[step, :, lanes] = terms[0] + direct * here
            return states

        empty = jnp.zeros((SEGMENTS, LANES), jnp.float32)
        states = lax.fori_loop(0, steps, scan, (empty,) * modes, unroll=8)
        segment = lax.broadcasted_iota(jnp.int32, (SEGMENTS, LANES), 0)
        for mode in range(modes):
            state = states[mode]
            for level, distance in enumerate((1, 2, 4)):
                moved = pltpu.roll(state, distance, 0)
                state = state + jnp.where(
                    segment >= distance, spread(power, level, mode) * moved, 0.0
                )
            before[mode, :, lanes] = jnp.where(segment >= 1, pltpu.roll(state, 1, 0), 0.0)
            ends[pl.ds(mode, 1), lanes] = state[SEGMENTS - 1 :, :]


def signals(where, pieces, tokens, halo, products, taps, decay, amplitude, power, skip):
    plan, arrays, _ = plan_of(pieces)
    modes, channels = decay.shape
    rows = sum(array.shape[0] for array in tokens)
    inputs = [*arrays, *tokens, halo]
    return pl.pallas_call(
        functools.partial(signal_kernel, plan, KEY_VALUE),
        out_shape=(
            pltpu.VMEM((rows // SEGMENTS, SEGMENTS, channels), jnp.float32),
            pltpu.VMEM((modes, SEGMENTS, channels), jnp.float32),
            jax.ShapeDtypeStruct((modes, channels), jnp.float32),
        ),
        in_specs=[SMEM] + [HBM] * len(inputs) + [VMEM] * 7,
        out_specs=(VMEM,) * 3,
        scratch_shapes=copy_scratch(pieces, KEY_VALUE, HALO + rows)
        + [segment_scratch(KEY_VALUE, rows, channels)],
        compiler_params=pltpu.CompilerParams(vmem_limit_bytes=8 * 1024 * 1024),
        name="signals",
    )(where, *in_hbm(*inputs), *in_vmem(*products), taps, decay, amplitude, power, skip)


def query_kernel(plan, streams, where, *refs):
    count = arrays_in(plan)
    pieces, refs = refs[:count], refs[count:]
    mine, other, halo, products, halo_products, conv, taps = refs[:7]
    query, gated, rows, weights, sems, projected = refs[7:]
    channels = weights.shape[2]
    steps = 2 * mine.shape[0] // SEGMENTS
    copies = start_copies(plan, streams, where, pieces, mine, other, halo, rows, weights, sems)
    finish, load = segmented(projected, products, halo_products, streams.start)
    multiply(copies, rows, weights, finish)
    for group in range(channels // LANES):
        lanes = pl.ds(group * LANES, LANES)
        spread = [
            jnp.broadcast_to(taps[0, offset, lanes].reshape(1, LANES), (SEGMENTS, LANES))
            for offset in range(SHORT)
        ]

        def featurize(step, held):
            held = (load(0, group, step),) + held
            total = spread[0] * held[0]
            for offset in range(1, SHORT):
                total += spread[offset] * held[offset]
            query[step, :, lanes] = total
            gated[step, :, lanes] = total * conv[step, :, lanes]
            return held[:-1]

        held = tuple(load(0, group, -offset) for offset in range(1, SHORT))
        lax.fori_loop(0, steps, featurize, held, unroll=8)


def queries(where, pieces, tokens, halo, products, conv, taps):
    plan, arrays, _ = plan_of(pieces)
    channels = arrays[0].shape[2]
    rows = sum(array.shape[0] for array in tokens)
    inputs = [*arrays, *tokens, halo]
    return pl.pallas_call(
        functools.partial(query_kernel, plan, QUERY),
        out_shape=(pltpu.VMEM((rows // SEGMENTS, SEGMENTS, channels), jnp.float32),) * 2,
        in_specs=[SMEM] + [HBM] * len(inputs) + [VMEM] * 4,
        out_specs=(VMEM,) * 2,
        scratch_shapes=copy_scratch(pieces, QUERY, HALO + rows)
        + [segment_scratch(QUERY, rows, channels)],
        compiler_params=pltpu.CompilerParams(vmem_limit_bytes=8 * 1024 * 1024),
        name="queries",
    )(where, *in_hbm(*inputs), *in_vmem(*products, conv), taps)


def gate_kernel(
    where,
    query,
    gated,
    before,
    carried,
    decay,
    amplitude,
    power,
    keep,
    send,
    whole,
):
    core = where[2]
    steps, _, channels = query.shape
    length = keep.shape[0]
    modes = decay.shape[0]
    for low in range(0, channels, LANES):
        lanes = pl.ds(low, LANES)

        def spread(ref, *index):
            return jnp.broadcast_to(ref[(*index, lanes)].reshape(1, LANES), (SEGMENTS, LANES))

        decays = [spread(decay, mode) for mode in range(modes)]
        states = tuple(
            spread(amplitude, mode)
            * decays[mode]
            * (before[mode, :, lanes] + power[mode, :, lanes] * spread(carried, mode))
            for mode in range(modes)
        )

        def add(step, states):
            terms = list(states)
            while len(terms) > 1:
                terms = [terms[at] + terms[at + 1] for at in range(0, len(terms), 2)]
            whole[0, low // LANES, pl.ds(step, SEGMENTS, stride=steps + BEFORE), :] = (
                gated[step, :, lanes] + query[step, :, lanes] * terms[0]
            )
            return tuple(decays[mode] * states[mode] for mode in range(modes))

        lax.fori_loop(0, steps, add, states, unroll=8)
    for group in range(channels // LANES):
        lanes = pl.ds(group * LANES, LANES)
        for out, block in ((keep, core), (send, 1 - core)):
            for segment in range(SEGMENTS // CORES):
                first = (block * (SEGMENTS // CORES) + segment) * (steps + BEFORE)
                first = pl.multiple_of(first, SEGMENTS)
                out[pl.ds(segment * steps, steps), lanes] = whole[
                    0, group, pl.ds(first, steps), :
                ].astype(jnp.bfloat16)


def carry_gated(where, query, gated, before, carried, decay, amplitude, power):
    steps, _, channels = query.shape
    length = steps * SEGMENTS // 2
    return pl.pallas_call(
        gate_kernel,
        out_shape=(jax.ShapeDtypeStruct((length, channels), jnp.bfloat16),) * 2,
        in_specs=[SMEM] + [VMEM] * 7,
        out_specs=(VMEM,) * 2,
        scratch_shapes=[segment_scratch(QUERY, 2 * length, channels)],
        compiler_params=pltpu.CompilerParams(vmem_limit_bytes=8 * 1024 * 1024),
        name="gated",
    )(where, *in_vmem(query, gated, before), carried, decay, amplitude, power)


def carry_factors(rate, x, z, span):
    x, z = x.astype(jnp.float32), z.astype(jnp.float32)

    def after(tokens):
        return jnp.exp(-rate * tokens)

    def if_before(position, steps):
        return jnp.where(position >= steps, 1.0, 0.0)

    line = [after(span * (Z - 1 - z))]
    for steps in range(1, Z):
        source = jnp.where(z >= steps, z - steps, z - steps + Z)
        line.append(after(span * (Z - 1 - source)))
    near = [if_before(z, steps) * after(float(span * (steps - 1))) for steps in range(1, Z)]
    far = [
        if_before(x, steps) * after(span * (Z * (steps - 1) + z)) for steps in range(1, X)
    ]
    return jnp.stack(line + near + far)


def carried_states(ends, factors):
    line, near, far = factors[:Z], factors[Z : 2 * Z - 1], factors[2 * Z - 1 :]
    others = [along_z(ends, steps) for steps in range(1, Z)]
    total, carry = line[0] * ends, 0.0
    for at, state in enumerate(others):
        total = total + line[at + 1] * state
        carry = carry + near[at] * state
    for at, state in enumerate([along_x(total, steps) for steps in range(1, X)]):
        carry = carry + far[at] * state
    return carry


def local(tokens, in_weight, short_filter, residues, rates, skip):
    index = lax.axis_index("seq")
    core = index % CORES
    z = index // CORES % Z
    x = index // (CORES * Z)
    where = jnp.stack([x, z, core]).astype(jnp.int32)
    length = tokens.shape[0]
    channels = skip.shape[0]
    half = channels // 2
    span = CORES * length
    first = core == 0

    def half_of(array, axis):
        return lax.dynamic_slice_in_dim(array, core * half, half, axis)

    low, high = in_weight[:, :, :half], in_weight[:, :, half:]
    own = jnp.where(first, low, high)
    received = swap_cores(jnp.where(first, high, low))
    tail = tokens[length - HALO :]
    tail = jnp.where(first, swap_cores(tail), tail)
    block = jnp.concatenate(
        [jnp.where(first, own, received), jnp.where(first, received, own)], axis=1
    )
    rate = half_of(rates, 0).T
    residue = half_of(residues, 0).T
    decay = jnp.exp(-rate)
    amplitude = residue * jnp.sqrt(-jnp.expm1(-2.0 * rate))
    step = span // SEGMENTS
    power = jnp.stack([jnp.exp(-rate * (step * distance)) for distance in (1, 2, 4)])
    starts = jnp.arange(SEGMENTS, dtype=jnp.float32)[None, :, None] * step
    start_power = jnp.exp(-rate[:, None, :] * starts)
    factors = carry_factors(rate, x, z, span)
    taps = half_of(short_filter, 2)
    direct = half_of(skip, 0)[None, :]

    beside = across_z(block, 1)
    right, left = sides(block)
    other = swap_cores(tokens)
    halo = next_chip(tail)
    held, other = together(block, other)
    over = across_z(held, 2)
    beside, right, left, held = together(beside, right, left, held)
    both = (tokens, other)

    far = forwards(right, left)
    pieces = with_sides(0, block, right, left)
    products = partial_products(where, pieces, both, (), (), "first")
    right, left = sides(beside)
    right, left, *far, over, products, halo = together(right, left, *far, over, *products, halo)
    so_far = pieces

    pieces = with_sides(1, beside, right, left) + with_far(0, *far)
    products = partial_products(where, pieces, both, (), (products,), "second")
    so_far += pieces
    halo_products = partial_products(where, so_far, (), (halo,), (), "halo")
    far = forwards(right, left)
    opposite = across_z(over, 1)
    right, left = sides(over)
    right, left, far_right, far_left, opposite, products, halo_products = together(
        right, left, *far, opposite, *products, *halo_products
    )

    pieces = with_sides(2, over, right, left) + with_far(1, far_right, far_left)
    products = partial_products(where, pieces, both, (halo,), (products, halo_products), "third")
    far = forwards(right, left)
    right, left = sides(opposite)
    small = (power, start_power, factors, decay, amplitude, taps, direct)
    right, left, far_right, far_left, products, halo_products, *small = together(
        right, left, *far, *products, *small
    )
    power, start_power, factors, decay, amplitude, taps, direct = small

    pieces = with_sides(3, opposite, right, left) + with_far(2, far_right, far_left)
    last = with_far(3, *forwards(right, left))
    products = partial_products(where, pieces, both, (halo,), (products, halo_products), "fourth")

    conv, before, ends = signals(
        where, last, both, halo, products, taps, decay, amplitude, power, direct
    )
    query, product = queries(where, last, both, halo, products, conv, taps)
    carried = carried_states(ends, factors)
    keep, send = carry_gated(
        where, query, product, before, carried, decay, amplitude, start_power
    )
    taken = swap_cores(send)
    return jnp.concatenate(
        [jnp.where(first, keep, taken), jnp.where(first, taken, keep)], axis=1
    )


def solution(mesh):
    placed = (
        P("seq", None),
        P(None, "seq", "mp"),
        P(None, None, "mp"),
        P("mp", None),
        P("mp", None),
        P("mp"),
    )
    return jax.shard_map(
        local, mesh=mesh, in_specs=placed, out_specs=P("seq", "mp"), check_vma=False
    )
```

time: 120 us -> 115 us (0.958)
  waiting for transfers between devices: 31.3 us -> 17 us
  other arithmetic: 4.99 us -> 13.2 us
  Pallas kernels: 30.3 us -> 34 us
  starting transfers between devices: 48.7 us -> 45.5 us
    ppermute x30, waiting for transfers between devices: 31.3 us -> 17 us  [permute(): return lax.ppermute(value, 'seq', pairs)]
    unnamed x0 -> x9, other arithmetic: none -> 5.49 us
    pallas_call x4 -> x11, Pallas kernels: 22.7 us -> 27.9 us  [the longest x5 20.7 us: partial_products(): pl.pallas_call(functools.partial(partial_kernel, plan, bool(tokens), bool...]
    ppermute x30, starting transfers between devices: 48.7 us -> 45.5 us  [permute(): return lax.ppermute(value, 'seq', pairs)]
    pallas_call x1, Pallas kernels: 7.63 us -> 6.04 us  [signals(): pl.pallas_call(functools.partial(signal_kernel, plan, KEY_VALUE), out_sha...]
    unnamed x46 -> x42, local copies, waits for them, and re-layouts: 1.42 us -> 2.99 us
    select_n x0 -> x1, other arithmetic: none -> 1.56 us  [local(): tail = jnp.where(first, swap_cores(tail), tail)]
    slice x8 -> x0, local copies, waits for them, and re-layouts: 1.47 us -> none  [forwards(): return (along_x(right[:, :half], 1), along_x(left[:, half:], 3))]
  transfers between devices with their start and end apart: 30 -> 30, of which waited for: 17 -> 9; matrix products, arithmetic and copies ran while one was open for 5% -> 10% of each run, Pallas kernels for 17% -> 22%
where the time goes in v3:
time: 115 us; the launch traced here: 114 us
  starting transfers between devices  45.5 us (40%)
  Pallas kernels  34 us (30%)
  waiting for transfers between devices  17 us (15%)
  other arithmetic  13.2 us (11%)
  local copies, waits for them, and re-layouts  3.98 us (3%)
    ppermute x30, starting transfers between devices, permute(): return lax.ppermute(value, 'seq', pairs)  45.5 us
    pallas_call x5, Pallas kernels, partial_products(): pl.pallas_call(functools.partial(partial_kernel, plan, bool(tokens), bool...  20.7 us
    ppermute x30, waiting for transfers between devices, permute(): return lax.ppermute(value, 'seq', pairs)  17 us
    pallas_call x1, Pallas kernels, signals(): pl.pallas_call(functools.partial(signal_kernel, plan, KEY_VALUE), out_sha...  6.04 us
    unnamed x9, other arithmetic  5.49 us
    unnamed x42, local copies, waits for them, and re-layouts  2.99 us
    pallas_call x1, Pallas kernels, queries(): pl.pallas_call(functools.partial(query_kernel, plan, QUERY), out_shape=(p...  2.81 us
    pallas_call x4, Pallas kernels, forwards(): pl.pallas_call(halves_kernel, out_shape=(half, half), in_specs=[ANY] * 2,...  2.58 us
  transfers between devices with their start and end apart: 30, of which 9 were waited for; matrix products, arithmetic and copies ran while one was open for 10% of the time, Pallas kernels for 22%

profile of v3, /device:TPU:1, one launch (start us, length us, event | category | flops | bytes accessed | tf_op | source)
XLA Modules:
  0.0 114.2 jit_solution(1562648044506148561)
XLA Ops:
  0.0 3.2 %collective-permute-start.4 = (bf16[512,4096]{1,0:T(8,128)(2,1)}, bf16[512,4096]{1,0:T(8,128)(2,1)}, u32[]{:S(2)}, u32[]{:S(2)}) collective-permute-start(bf16[512,4096]{1,0:T(8,128)(2,1)} %refs_2_.3), channel_id=1, source_target_pairs={{0,8},{8,0},{16,24},{24,16},{32,40},{40,32},{48,56},{56,48},{64,72... | collective-permute-start | bytes 12582920 | tf_op jit(solution)/shard_map/ppermute | solution.py:49
  3.2 1.0 broadcast_select_fusion.4
  4.4 0.9 slice.54
  5.3 0.6 collective-permute-start.10
  5.9 0.7 fusion.8
  6.6 0.6 constant_dynamic-update-slice_fusion.9
  7.2 0.6 constant_dynamic-update-slice_fusion.8
  7.8 0.6 constant_dynamic-update-slice_fusion.7
  8.4 0.6 constant_dynamic-update-slice_fusion.6
  9.2 0.6 constant_dynamic-update-slice_fusion.5
  9.8 0.5 collective-permute-done
  10.3 1.1 broadcast_select_fusion.3
  11.5 1.1 collective-permute-start.2
  12.6 1.7 %collective-permute-start.3 = (bf16[3,256,256]{2,1,0:T(8,128)(2,1)S(1)}, bf16[3,256,256]{2,1,0:T(8,128)(2,1)S(1)}, u32[]{:S(2)}, u32[]{:S(2)}) collective-permute-start(bf16[3,256,256]{2,1,0:T(8,128)(2,1)S(1)} %pad_maximum_fusion.1.refs_0_), channel_id=1, source_target_pairs={{0,192},{8,200},{16,208},{24,216},{32,224},{40,232},{48,240},{56,2... | collective-permute-start | bytes 1179656 | tf_op jit(solution)/shard_map/ppermute | solution.py:49
  14.3 1.6 %broadcast_select_fusion.6 = bf16[16,4096]{1,0:T(8,128)(2,1)} fusion(bf16[16,4096]{1,0:T(8,128)(2,1)S(1)} %collective-permute-done.10, pred[]{:T(512)S(6)} %eq.6, bf16[512,4096]{1,0:T(8,128)(2,1)} %refs_2_.3), kind=kLoop, calls=%fused_computation.9 | loop fusion | flops 65536 | bytes 393217 | tf_op jit(solution)/shard_map/jit(_where)/select_n | solution.py:527
  15.8 3.3 %collective-permute-start.11 = (bf16[16,4096]{1,0:T(8,128)(2,1)}, bf16[16,4096]{1,0:T(8,128)(2,1)S(1)}, u32[]{:S(2)}, u32[]{:S(2)}) collective-permute-start(bf16[16,4096]{1,0:T(8,128)(2,1)} %broadcast_select_fusion.6), channel_id=1, source_target_pairs={{0,16},{8,24},{16,32},{24,40},{32,48},{40,56},{48,64},{56,72},{64,... | collective-permute-start | bytes 393224 | tf_op jit(solution)/shard_map/ppermute | solution.py:49
  19.1 2.7 %collective-permute-done.1.refs_0_.refs_3_ = bf16[3,256,256]{2,1,0:T(8,128)(2,1)S(1)} collective-permute-done((bf16[3,256,256]{2,1,0:T(8,128)(2,1)S(1)}, bf16[3,256,256]{2,1,0:T(8,128)(2,1)S(1)}, u32[]{:S(2)}, u32[]{:S(2)}) %collective-permute-start.1) | collective-permute-done | bytes 393248 | tf_op jit(solution)/shard_map/ppermute | solution.py:49
  21.8 1.2 %collective-permute-done.2.right.refs_1_ = bf16[3,256,256]{2,1,0:T(8,128)(2,1)S(1)} collective-permute-done((bf16[3,256,256]{2,1,0:T(8,128)(2,1)S(1)}, bf16[3,256,256]{2,1,0:T(8,128)(2,1)S(1)}, u32[]{:S(2)}, u32[]{:S(2)}) %collective-permute-start.2) | collective-permute-done | bytes 393248 | tf_op jit(solution)/shard_map/ppermute | solution.py:49
  23.0 0.5 collective-permute-start.5
  23.5 2.3 %collective-permute-start.6 = (bf16[3,256,256]{2,1,0:T(8,128)(2,1)S(1)}, bf16[3,256,256]{2,1,0:T(8,128)(2,1)S(1)}, u32[]{:S(2)}, u32[]{:S(2)}) collective-permute-start(bf16[3,256,256]{2,1,0:T(8,128)(2,1)S(1)} %collective-permute-done.1.refs_0_.refs_3_), channel_id=1, source_target_pairs={{0,192},{8,200},{16,208},{24,216},{32,224},{40,232},{48,240},{56,2... | collective-permute-start | bytes 1179656 | tf_op jit(solution)/shard_map/ppermute | solution.py:49
  25.8 2.6 %collective-permute-start.9 = (bf16[3,256,256]{2,1,0:T(8,128)(2,1)S(1)}, bf16[3,256,256]{2,1,0:T(8,128)(2,1)}, u32[]{:S(2)}, u32[]{:S(2)}) collective-permute-start(bf16[3,256,256]{2,1,0:T(8,128)(2,1)S(1)} %pad_maximum_fusion.1.refs_0_), channel_id=1, source_target_pairs={{0,32},{8,40},{16,48},{24,56},{32,0},{40,8},{48,16},{56,24},{64,96... | collective-permute-start | bytes 1179656 | tf_op jit(solution)/shard_map/ppermute | solution.py:49
  28.4 0.6 constant_dynamic-update-slice_fusion.4
  29.1 0.2 halves.4
  29.4 2.6 %collective-permute-start.8 = (bf16[3,128,256]{2,1,0:T(8,128)(2,1)S(1)}, bf16[3,128,256]{2,1,0:T(8,128)(2,1)S(1)}, u32[]{:S(2)}, u32[]{:S(2)}) collective-permute-start(bf16[3,128,256]{2,1,0:T(8,128)(2,1)S(1)} %get-tuple-element.61), channel_id=1, source_target_pairs={{0,192},{8,200},{16,208},{24,216},{32,224},{40,232},{48,240},{56,2... | collective-permute-start | bytes 589832 | tf_op jit(solution)/shard_map/ppermute | solution.py:49
  32.0 0.6 constant_dynamic-update-slice_fusion.3
  32.6 3.8 %first.1.refs_7_ = f32[3,2,1024,128]{3,2,1,0:T(8,128)S(1)} custom-call(s32[3]{0:T(128)S(1)} %pad_add_fusion.where, bf16[3,256,256]{2,1,0:T(8,128)(2,1)} %copy-done.7, bf16[3,256,256]{2,1,0:T(8,128)(2,1)} %copy-done.3, bf16[3,256,256]{2,1,0:T(8,128)(2,1)} %copy-done.4, bf16[512,4096]{1,0:T(8,128)(2,1)} %refs_2_.3, ...), custom_call_target="tpu_custom_call" | custom-call | tf_op jit(solution)/shard_map/first/pallas_call | solution.py:260
  36.5 1.6 %copy-done.1 = f32[3,2,1024,128]{3,2,1,0:T(8,128)} copy-done((f32[3,2,1024,128]{3,2,1,0:T(8,128)}, f32[3,2,1024,128]{3,2,1,0:T(8,128)S(1)}, u32[]{:S(2)}) %copy-start.1) | copy-done | bytes 3145752
  38.2 7.6 %collective-permute-done.9.refs_0_ = bf16[3,256,256]{2,1,0:T(8,128)(2,1)} collective-permute-done((bf16[3,256,256]{2,1,0:T(8,128)(2,1)S(1)}, bf16[3,256,256]{2,1,0:T(8,128)(2,1)}, u32[]{:S(2)}, u32[]{:S(2)}) %collective-permute-start.9) | collective-permute-done | bytes 393248 | tf_op jit(solution)/shard_map/ppermute | solution.py:49
  45.8 0.2 collective-permute-start.12
  46.0 2.5 %collective-permute-start.13 = (bf16[3,256,256]{2,1,0:T(8,128)(2,1)}, bf16[3,256,256]{2,1,0:T(8,128)(2,1)}, u32[]{:S(2)}, u32[]{:S(2)}) collective-permute-start(bf16[3,256,256]{2,1,0:T(8,128)(2,1)} %collective-permute-done.9.refs_0_), channel_id=1, source_target_pairs={{0,192},{8,200},{16,208},{24,216},{32,224},{40,232},{48,240},{56,2... | collective-permute-start | bytes 1179656 | tf_op jit(solution)/shard_map/ppermute | solution.py:49
  48.4 0.6 constant_dynamic-update-slice_fusion.2
  49.1 0.2 halves.5
  49.3 2.7 %collective-permute-start.15 = (bf16[3,128,256]{2,1,0:T(8,128)(2,1)S(1)}, bf16[3,128,256]{2,1,0:T(8,128)(2,1)S(1)}, u32[]{:S(2)}, u32[]{:S(2)}) collective-permute-start(bf16[3,128,256]{2,1,0:T(8,128)(2,1)S(1)} %get-tuple-element.67), channel_id=1, source_target_pairs={{0,192},{8,200},{16,208},{24,216},{32,224},{40,232},{48,240},{56,2... | collective-permute-start | bytes 589832 | tf_op jit(solution)/shard_map/ppermute | solution.py:49
  52.0 0.6 constant_dynamic-update-slice_fusion.1
  52.6 3.1 %halo.1.refs_9_ = f32[3,2,16,128]{3,2,1,0:T(8,128)S(1)} custom-call(s32[3]{0:T(128)S(1)} %pad_add_fusion.where, bf16[3,256,256]{2,1,0:T(8,128)(2,1)} %copy-done.7, bf16[3,256,256]{2,1,0:T(8,128)(2,1)} %copy-done.3, bf16[3,256,256]{2,1,0:T(8,128)(2,1)} %copy-done.4, bf16[3,256,256]{2,1,0:T(8,128)(2,1)} %copy-done.9, bf16[3,256,256]{2,1,0:T(8,128)(2,1)} %copy-done.5, ...), custom_call_target="tpu_custom_call" | custom-call | tf_op jit(solution)/shard_map/halo/pallas_call | solution.py:260
  55.8 4.5 %second.1.refs_8_ = f32[3,2,1024,128]{3,2,1,0:T(8,128)S(1)} custom-call(s32[3]{0:T(128)S(1)} %pad_add_fusion.where, bf16[3,256,256]{2,1,0:T(8,128)(2,1)} %copy-done.9, bf16[3,256,256]{2,1,0:T(8,128)(2,1)} %copy-done.5, bf16[3,256,256]{2,1,0:T(8,128)(2,1)} %copy-done.6, bf16[3,128,256]{2,1,0:T(8,128)(2,1)} %copy-done.10, bf16[3,128,256]{2,1,0:T(8,128)(2,1)} %copy-done.11, ...), custom_call_target="tpu_custom_call" | custom-call | tf_op jit(solution)/shard_map/second/pallas_call | solution.py:260
  60.3 0.5 collective-permute-done.14.refs_3_
  60.9 0.6 copy-done.14
  61.5 2.1 %collective-permute-start.18 = (bf16[3,256,256]{2,1,0:T(8,128)(2,1)}, bf16[3,256,256]{2,1,0:T(8,128)(2,1)}, u32[]{:S(2)}, u32[]{:S(2)}) collective-permute-start(bf16[3,256,256]{2,1,0:T(8,128)(2,1)} %collective-permute-done.16.refs_0_), channel_id=1, source_target_pairs={{0,192},{8,200},{16,208},{24,216},{32,224},{40,232},{48,240},{56,2... | collective-permute-start | bytes 1179656 | tf_op jit(solution)/shard_map/ppermute | solution.py:49
  63.7 1.0 halves.6
  64.9 2.7 %collective-permute-start.20 = (bf16[3,128,256]{2,1,0:T(8,128)(2,1)S(1)}, bf16[3,128,256]{2,1,0:T(8,128)(2,1)S(1)}, u32[]{:S(2)}, u32[]{:S(2)}) collective-permute-start(bf16[3,128,256]{2,1,0:T(8,128)(2,1)S(1)} %get-tuple-element.76), channel_id=1, source_target_pairs={{0,192},{8,200},{16,208},{24,216},{32,224},{40,232},{48,240},{56,2... | collective-permute-start | bytes 589832 | tf_op jit(solution)/shard_map/ppermute | solution.py:49
  67.5 0.6 constant_dynamic-update-slice_fusion
  68.1 4.6 %third.1 = (f32[3,2,1024,128]{3,2,1,0:T(8,128)S(1)}, f32[3,2,16,128]{3,2,1,0:T(8,128)S(1)}) custom-call(s32[3]{0:T(128)S(1)} %pad_add_fusion.where, bf16[3,256,256]{2,1,0:T(8,128)(2,1)} %collective-permute-done.9.refs_0_, bf16[3,256,256]{2,1,0:T(8,128)(2,1)} %collective-permute-done.12.right.refs_1_, ...), custom_call_target="tpu_custom_call" | custom-call | tf_op jit(solution)/shard_map/third/pallas_call | solution.py:260
  72.7 2.4 %collective-permute-done.19.refs_3_ = bf16[3,128,256]{2,1,0:T(8,128)(2,1)S(1)} collective-permute-done((bf16[3,128,256]{2,1,0:T(8,128)(2,1)S(1)}, bf16[3,128,256]{2,1,0:T(8,128)(2,1)S(1)}, u32[]{:S(2)}, u32[]{:S(2)}) %collective-permute-start.19) | collective-permute-done | bytes 196640 | tf_op jit(solution)/shard_map/ppermute | solution.py:49
  75.1 1.2 %halves.7 = (bf16[3,128,256]{2,1,0:T(8,128)(2,1)S(1)}, bf16[3,128,256]{2,1,0:T(8,128)(2,1)S(1)}) custom-call(bf16[3,256,256]{2,1,0:T(8,128)(2,1)} %collective-permute-done.17.right.refs_1_, bf16[3,256,256]{2,1,0:T(8,128)(2,1)} %collective-permute-done.18.left.refs_2_), custom_call_target="tpu_custom_call" | custom-call | tf_op jit(solution)/shard_map/halves/pallas_call | solution.py:95
  76.3 0.3 collective-permute-start.21
  76.7 2.4 %collective-permute-start.22 = (bf16[3,128,256]{2,1,0:T(8,128)(2,1)S(1)}, bf16[3,128,256]{2,1,0:T(8,128)(2,1)S(1)}, u32[]{:S(2)}, u32[]{:S(2)}) collective-permute-start(bf16[3,128,256]{2,1,0:T(8,128)(2,1)S(1)} %get-tuple-element.86), channel_id=1, source_target_pairs={{0,192},{8,200},{16,208},{24,216},{32,224},{40,232},{48,240},{56,2... | collective-permute-start | bytes 589832 | tf_op jit(solution)/shard_map/ppermute | solution.py:49
  79.1 4.6 %fourth.1 = (f32[3,2,1024,128]{3,2,1,0:T(8,128)S(1)}, f32[3,2,16,128]{3,2,1,0:T(8,128)S(1)}) custom-call(s32[3]{0:T(128)S(1)} %pad_add_fusion.where, bf16[3,256,256]{2,1,0:T(8,128)(2,1)} %collective-permute-done.16.refs_0_, bf16[3,256,256]{2,1,0:T(8,128)(2,1)} %collective-permute-done.17.right.refs_1_, ...), custom_call_target="tpu_custom_call" | custom-call | tf_op jit(solution)/shard_map/fourth/pallas_call | solution.py:260
  83.8 0.6 copy-done.12
  84.5 6.0 %signals.1 = (f32[128,8,256]{2,1,0:T(8,128)S(1)}, f32[16,8,256]{2,1,0:T(8,128)S(1)}, f32[16,256]{1,0:T(8,128)S(1)}) custom-call(s32[3]{0:T(128)S(1)} %pad_add_fusion.where, bf16[3,128,256]{2,1,0:T(8,128)(2,1)} %copy-done.12, bf16[3,128,256]{2,1,0:T(8,128)(2,1)} %copy-done.13, bf16[512,4096]{1,0:T(8,128)(2,1)} %refs_2_.3, ...), custom_call_target="tpu_custom_call" | custom-call | tf_op jit(solution)/shard_map/signals/pallas_call | solution.py:347
  90.5 0.7 collective-permute-start.23
  91.2 1.8 %collective-permute-start.24 = (f32[16,256]{1,0:T(8,128)S(1)}, f32[16,256]{1,0:T(8,128)S(1)}, u32[]{:S(2)}, u32[]{:S(2)}) collective-permute-start(f32[16,256]{1,0:T(8,128)S(1)} %get-tuple-element.103), channel_id=1, source_target_pairs={{0,32},{8,40},{16,48},{24,56},{32,0},{40,8},{48,16},{56,24},{64,96... | collective-permute-start | bytes 49160 | tf_op jit(solution)/shard_map/ppermute | solution.py:49
  92.9 1.6 %collective-permute-start.25 = (f32[16,256]{1,0:T(8,128)S(1)}, f32[16,256]{1,0:T(8,128)S(1)}, u32[]{:S(2)}, u32[]{:S(2)}) collective-permute-start(f32[16,256]{1,0:T(8,128)S(1)} %get-tuple-element.103), channel_id=1, source_target_pairs={{0,48},{8,56},{16,0},{24,8},{32,16},{40,24},{48,32},{56,40},{64,11... | collective-permute-start | bytes 49160 | tf_op jit(solution)/shard_map/ppermute | solution.py:49
  94.5 0.5 collective-permute-done.23
  95.0 0.5 collective-permute-done.25
  95.5 0.8 fusion.2
  96.4 2.2 %collective-permute-start.27 = (f32[16,256]{1,0:T(8,128)S(1)}, f32[16,256]{1,0:T(8,128)S(1)}, u32[]{:S(2)}, u32[]{:S(2)}) collective-permute-start(f32[16,256]{1,0:T(8,128)S(1)} %fusion.2), channel_id=1, source_target_pairs={{0,128},{8,136},{16,144},{24,152},{32,160},{40,168},{48,176},{56,1... | collective-permute-start | bytes 49160 | tf_op jit(solution)/shard_map/ppermute | solution.py:49
  98.6 0.6 collective-permute-start.28
  99.3 2.8 %queries.1 = (f32[128,8,256]{2,1,0:T(8,128)S(1)}, f32[128,8,256]{2,1,0:T(8,128)S(1)}) custom-call(s32[3]{0:T(128)S(1)} %pad_add_fusion.where, bf16[3,128,256]{2,1,0:T(8,128)(2,1)} %copy-done.12, bf16[3,128,256]{2,1,0:T(8,128)(2,1)} %copy-done.13, bf16[512,4096]{1,0:T(8,128)(2,1)} %refs_2_.3, ...), custom_call_target="tpu_custom_call" | custom-call | tf_op jit(solution)/shard_map/queries/pallas_call | solution.py:398
  102.1 0.8 fusion.carried
  102.9 1.9 %gated.1 = (bf16[512,256]{1,0:T(8,128)(2,1)S(1)}, bf16[512,256]{1,0:T(8,128)(2,1)S(1)}) custom-call(s32[3]{0:T(128)S(1)} %pad_add_fusion.where, f32[128,8,256]{2,1,0:T(8,128)S(1)} %get-tuple-element.99.query, f32[128,8,256]{2,1,0:T(8,128)S(1)} %get-tuple-element.100.gated, f32[16,8,256]{2,1,0:T(8,128)S(1)} %get-tuple-element.101.before, ...), custom_call_target="tpu_custom_call" | custom-call | tf_op jit(solution)/shard_map/gated/pallas_call | solution.py:465
  104.8 7.3 %collective-permute-start.29 = (bf16[512,256]{1,0:T(8,128)(2,1)S(1)}, bf16[512,256]{1,0:T(8,128)(2,1)S(1)}, u32[]{:S(2)}, u32[]{:S(2)}) collective-permute-start(bf16[512,256]{1,0:T(8,128)(2,1)S(1)} %get-tuple-element.106), channel_id=1, source_target_pairs={{0,8},{8,0},{16,24},{24,16},{32,40},{40,32},{48,56},{56,48},{64,72... | collective-permute-start | bytes 786440 | tf_op jit(solution)/shard_map/ppermute | solution.py:49
  112.1 1.2 %collective-permute-done.29 = bf16[512,256]{1,0:T(8,128)(2,1)S(1)} collective-permute-done((bf16[512,256]{1,0:T(8,128)(2,1)S(1)}, bf16[512,256]{1,0:T(8,128)(2,1)S(1)}, u32[]{:S(2)}, u32[]{:S(2)}) %collective-permute-start.29) | collective-permute-done | bytes 262176 | tf_op jit(solution)/shard_map/ppermute | solution.py:49
  113.4 0.8 pad_maximum_fusion
  (78 shorter events, 1.2 us)
Async XLA Ops:
  0.0 49.0 %copy-start = (f32[3,7,512]{2,1,0:T(8,128)S(1)}, f32[3,7,512]{2,1,0:T(8,128)}, u32[]{:S(2)}) copy-start(f32[3,7,512]{2,1,0:T(8,128)} %param.8) | copy-start | bytes 129028
  0.0 19.1 %collective-permute-start.4 = (bf16[512,4096]{1,0:T(8,128)(2,1)}, bf16[512,4096]{1,0:T(8,128)(2,1)}, u32[]{:S(2)}, u32[]{:S(2)}) collective-permute-start(bf16[512,4096]{1,0:T(8,128)(2,1)} %refs_2_.3), channel_id=1, source_target_pairs={{0,8},{8,0},{16,24},{24,16},{32,40},{40,32},{48,56},{56,48},{64,72... | collective-permute-start | bytes 12582920 | tf_op jit(solution)/shard_map/ppermute | solution.py:49
  4.3 6.0 %collective-permute-start = (bf16[3,128,256]{2,1,0:T(8,128)(2,1)S(1)}, bf16[3,128,256]{2,1,0:T(8,128)(2,1)S(1)}, u32[]{:S(2)}, u32[]{:S(2)}) collective-permute-start(bf16[3,128,256]{2,1,0:T(8,128)(2,1)S(1)} %broadcast_select_fusion.4), channel_id=1, source_target_pairs={{0,8},{8,0},{16,24},{24,16},{32,40},{40,32},{48,56},{56,48},{64,72... | collective-permute-start | bytes 589832 | tf_op jit(solution)/shard_map/ppermute | solution.py:49
  5.3 9.0 %collective-permute-start.10 = (bf16[16,4096]{1,0:T(8,128)(2,1)S(1)}, bf16[16,4096]{1,0:T(8,128)(2,1)S(1)}, u32[]{:S(2)}, u32[]{:S(2)}) collective-permute-start(bf16[16,4096]{1,0:T(8,128)(2,1)S(1)} %slice.54), channel_id=1, source_target_pairs={{0,8},{8,0},{16,24},{24,16},{32,40},{40,32},{48,56},{56,48},{64,72... | collective-permute-start | bytes 393224 | tf_op jit(solution)/shard_map/ppermute | solution.py:49
  11.4 21.2 %copy-start.7 = (bf16[3,256,256]{2,1,0:T(8,128)(2,1)}, bf16[3,256,256]{2,1,0:T(8,128)(2,1)S(1)}, u32[]{:S(2)}) copy-start(bf16[3,256,256]{2,1,0:T(8,128)(2,1)S(1)} %pad_maximum_fusion.1.refs_0_) | copy-start | bytes 1179652
  11.4 10.4 %collective-permute-start.1 = (bf16[3,256,256]{2,1,0:T(8,128)(2,1)S(1)}, bf16[3,256,256]{2,1,0:T(8,128)(2,1)S(1)}, u32[]{:S(2)}, u32[]{:S(2)}) collective-permute-start(bf16[3,256,256]{2,1,0:T(8,128)(2,1)S(1)} %pad_maximum_fusion.1.refs_0_), channel_id=1, source_target_pairs={{0,16},{8,24},{16,0},{24,8},{32,48},{40,56},{48,32},{56,40},{64,80... | collective-permute-start | bytes 1179656 | tf_op jit(solution)/shard_map/ppermute | solution.py:49
  11.5 11.5 %collective-permute-start.2 = (bf16[3,256,256]{2,1,0:T(8,128)(2,1)S(1)}, bf16[3,256,256]{2,1,0:T(8,128)(2,1)S(1)}, u32[]{:S(2)}, u32[]{:S(2)}) collective-permute-start(bf16[3,256,256]{2,1,0:T(8,128)(2,1)S(1)} %pad_maximum_fusion.1.refs_0_), channel_id=1, source_target_pairs={{0,64},{8,72},{16,80},{24,88},{32,96},{40,104},{48,112},{56,120},{... | collective-permute-start | bytes 1179656 | tf_op jit(solution)/shard_map/ppermute | solution.py:49
  12.6 10.4 %collective-permute-start.3 = (bf16[3,256,256]{2,1,0:T(8,128)(2,1)S(1)}, bf16[3,256,256]{2,1,0:T(8,128)(2,1)S(1)}, u32[]{:S(2)}, u32[]{:S(2)}) collective-permute-start(bf16[3,256,256]{2,1,0:T(8,128)(2,1)S(1)} %pad_maximum_fusion.1.refs_0_), channel_id=1, source_target_pairs={{0,192},{8,200},{16,208},{24,216},{32,224},{40,232},{48,240},{56,2... | collective-permute-start | bytes 1179656 | tf_op jit(solution)/shard_map/ppermute | solution.py:49
  15.8 13.5 %collective-permute-start.11 = (bf16[16,4096]{1,0:T(8,128)(2,1)}, bf16[16,4096]{1,0:T(8,128)(2,1)S(1)}, u32[]{:S(2)}, u32[]{:S(2)}) collective-permute-start(bf16[16,4096]{1,0:T(8,128)(2,1)} %broadcast_select_fusion.6), channel_id=1, source_target_pairs={{0,16},{8,24},{16,32},{24,40},{32,48},{40,56},{48,64},{56,72},{64,... | collective-permute-start | bytes 393224 | tf_op jit(solution)/shard_map/ppermute | solution.py:49
  21.8 30.8 %copy-start.9 = (bf16[3,256,256]{2,1,0:T(8,128)(2,1)}, bf16[3,256,256]{2,1,0:T(8,128)(2,1)S(1)}, u32[]{:S(2)}) copy-start(bf16[3,256,256]{2,1,0:T(8,128)(2,1)S(1)} %collective-permute-done.1.refs_0_.refs_3_) | copy-start | bytes 1179652
  23.0 9.6 %copy-start.3 = (bf16[3,256,256]{2,1,0:T(8,128)(2,1)}, bf16[3,256,256]{2,1,0:T(8,128)(2,1)S(1)}, u32[]{:S(2)}) copy-start(bf16[3,256,256]{2,1,0:T(8,128)(2,1)S(1)} %collective-permute-done.2.right.refs_1_) | copy-start | bytes 1179652
  23.0 9.6 %copy-start.4 = (bf16[3,256,256]{2,1,0:T(8,128)(2,1)}, bf16[3,256,256]{2,1,0:T(8,128)(2,1)S(1)}, u32[]{:S(2)}) copy-start(bf16[3,256,256]{2,1,0:T(8,128)(2,1)S(1)} %collective-permute-done.3.left.refs_2_) | copy-start | bytes 1179652
  23.0 15.1 %collective-permute-start.5 = (bf16[3,256,256]{2,1,0:T(8,128)(2,1)S(1)}, bf16[3,256,256]{2,1,0:T(8,128)(2,1)S(1)}, u32[]{:S(2)}, u32[]{:S(2)}) collective-permute-start(bf16[3,256,256]{2,1,0:T(8,128)(2,1)S(1)} %collective-permute-done.1.refs_0_.refs_3_), channel_id=1, source_target_pairs={{0,64},{8,72},{16,80},{24,88},{32,96},{40,104},{48,112},{56,120},{... | collective-permute-start | bytes 1179656 | tf_op jit(solution)/shard_map/ppermute | solution.py:49
  23.5 14.6 %collective-permute-start.6 = (bf16[3,256,256]{2,1,0:T(8,128)(2,1)S(1)}, bf16[3,256,256]{2,1,0:T(8,128)(2,1)S(1)}, u32[]{:S(2)}, u32[]{:S(2)}) collective-permute-start(bf16[3,256,256]{2,1,0:T(8,128)(2,1)S(1)} %collective-permute-done.1.refs_0_.refs_3_), channel_id=1, source_target_pairs={{0,192},{8,200},{16,208},{24,216},{32,224},{40,232},{48,240},{56,2... | collective-permute-start | bytes 1179656 | tf_op jit(solution)/shard_map/ppermute | solution.py:49
  25.8 20.0 %collective-permute-start.9 = (bf16[3,256,256]{2,1,0:T(8,128)(2,1)S(1)}, bf16[3,256,256]{2,1,0:T(8,128)(2,1)}, u32[]{:S(2)}, u32[]{:S(2)}) collective-permute-start(bf16[3,256,256]{2,1,0:T(8,128)(2,1)S(1)} %pad_maximum_fusion.1.refs_0_), channel_id=1, source_target_pairs={{0,32},{8,40},{16,48},{24,56},{32,0},{40,8},{48,16},{56,24},{64,96... | collective-permute-start | bytes 1179656 | tf_op jit(solution)/shard_map/ppermute | solution.py:49
  29.2 8.9 %collective-permute-start.7 = (bf16[3,128,256]{2,1,0:T(8,128)(2,1)S(1)}, bf16[3,128,256]{2,1,0:T(8,128)(2,1)S(1)}, u32[]{:S(2)}, u32[]{:S(2)}) collective-permute-start(bf16[3,128,256]{2,1,0:T(8,128)(2,1)S(1)} %get-tuple-element.60), channel_id=1, source_target_pairs={{0,64},{8,72},{16,80},{24,88},{32,96},{40,104},{48,112},{56,120},{... | collective-permute-start | bytes 589832 | tf_op jit(solution)/shard_map/ppermute | solution.py:49
  29.3 7.1 %copy-start.8 = (bf16[16,4096]{1,0:T(8,128)(2,1)}, bf16[16,4096]{1,0:T(8,128)(2,1)S(1)}, u32[]{:S(2)}) copy-start(bf16[16,4096]{1,0:T(8,128)(2,1)S(1)} %collective-permute-done.11.refs_8_.refs_7_.refs_4_) | copy-start | bytes 393220
  29.4 8.8 %collective-permute-start.8 = (bf16[3,128,256]{2,1,0:T(8,128)(2,1)S(1)}, bf16[3,128,256]{2,1,0:T(8,128)(2,1)S(1)}, u32[]{:S(2)}, u32[]{:S(2)}) collective-permute-start(bf16[3,128,256]{2,1,0:T(8,128)(2,1)S(1)} %get-tuple-element.61), channel_id=1, source_target_pairs={{0,192},{8,200},{16,208},{24,216},{32,224},{40,232},{48,240},{56,2... | collective-permute-start | bytes 589832 | tf_op jit(solution)/shard_map/ppermute | solution.py:49
  36.4 1.7 %copy-start.1 = (f32[3,2,1024,128]{3,2,1,0:T(8,128)}, f32[3,2,1024,128]{3,2,1,0:T(8,128)S(1)}, u32[]{:S(2)}) copy-start(f32[3,2,1024,128]{3,2,1,0:T(8,128)S(1)} %first.1.refs_7_) | copy-start | bytes 9437188
  38.1 14.5 %copy-start.10 = (bf16[3,128,256]{2,1,0:T(8,128)(2,1)}, bf16[3,128,256]{2,1,0:T(8,128)(2,1)S(1)}, u32[]{:S(2)}) copy-start(bf16[3,128,256]{2,1,0:T(8,128)(2,1)S(1)} %collective-permute-done.7.refs_3_.refs_6_) | copy-start | bytes 589828
  38.1 7.6 %copy-start.11 = (bf16[3,128,256]{2,1,0:T(8,128)(2,1)}, bf16[3,128,256]{2,1,0:T(8,128)(2,1)S(1)}, u32[]{:S(2)}) copy-start(bf16[3,128,256]{2,1,0:T(8,128)(2,1)S(1)} %collective-permute-done.8.refs_4_.refs_7_) | copy-start | bytes 589828
  38.1 14.5 %copy-start.5 = (bf16[3,256,256]{2,1,0:T(8,128)(2,1)}, bf16[3,256,256]{2,1,0:T(8,128)(2,1)S(1)}, u32[]{:S(2)}) copy-start(bf16[3,256,256]{2,1,0:T(8,128)(2,1)S(1)} %collective-permute-done.5.right.refs_1_.refs_4_) | copy-start | bytes 1179652
  38.2 14.5 %copy-start.6 = (bf16[3,256,256]{2,1,0:T(8,128)(2,1)}, bf16[3,256,256]{2,1,0:T(8,128)(2,1)S(1)}, u32[]{:S(2)}) copy-start(bf16[3,256,256]{2,1,0:T(8,128)(2,1)S(1)} %collective-permute-done.6.left.refs_2_.refs_5_) | copy-start | bytes 1179652
  45.8 15.0 %collective-permute-start.12 = (bf16[3,256,256]{2,1,0:T(8,128)(2,1)}, bf16[3,256,256]{2,1,0:T(8,128)(2,1)}, u32[]{:S(2)}, u32[]{:S(2)}) collective-permute-start(bf16[3,256,256]{2,1,0:T(8,128)(2,1)} %collective-permute-done.9.refs_0_), channel_id=1, source_target_pairs={{0,64},{8,72},{16,80},{24,88},{32,96},{40,104},{48,112},{56,120},{... | collective-permute-start | bytes 1179656 | tf_op jit(solution)/shard_map/ppermute | solution.py:49
  46.0 14.8 %collective-permute-start.13 = (bf16[3,256,256]{2,1,0:T(8,128)(2,1)}, bf16[3,256,256]{2,1,0:T(8,128)(2,1)}, u32[]{:S(2)}, u32[]{:S(2)}) collective-permute-start(bf16[3,256,256]{2,1,0:T(8,128)(2,1)} %collective-permute-done.9.refs_0_), channel_id=1, source_target_pairs={{0,192},{8,200},{16,208},{24,216},{32,224},{40,232},{48,240},{56,2... | collective-permute-start | bytes 1179656 | tf_op jit(solution)/shard_map/ppermute | solution.py:49
  48.4 12.4 %collective-permute-start.16 = (bf16[3,256,256]{2,1,0:T(8,128)(2,1)}, bf16[3,256,256]{2,1,0:T(8,128)(2,1)}, u32[]{:S(2)}, u32[]{:S(2)}) collective-permute-start(bf16[3,256,256]{2,1,0:T(8,128)(2,1)} %collective-permute-done.9.refs_0_), channel_id=1, source_target_pairs={{0,16},{8,24},{16,0},{24,8},{32,48},{40,56},{48,32},{56,40},{64,80... | collective-permute-start | bytes 1179656 | tf_op jit(solution)/shard_map/ppermute | solution.py:49
  49.1 6.7 %copy-start.2 = (f32[3,2,1024,128]{3,2,1,0:T(8,128)S(1)}, f32[3,2,1024,128]{3,2,1,0:T(8,128)}, u32[]{:S(2)}) copy-start(f32[3,2,1024,128]{3,2,1,0:T(8,128)} %copy-done.1) | copy-start | bytes 9437188
  49.3 11.5 %collective-permute-start.14 = (bf16[3,128,256]{2,1,0:T(8,128)(2,1)S(1)}, bf16[3,128,256]{2,1,0:T(8,128)(2,1)S(1)}, u32[]{:S(2)}, u32[]{:S(2)}) collective-permute-start(bf16[3,128,256]{2,1,0:T(8,128)(2,1)S(1)} %get-tuple-element.66), channel_id=1, source_target_pairs={{0,64},{8,72},{16,80},{24,88},{32,96},{40,104},{48,112},{56,120},{... | collective-permute-start | bytes 589832 | tf_op jit(solution)/shard_map/ppermute | solution.py:49
  49.3 11.5 %collective-permute-start.15 = (bf16[3,128,256]{2,1,0:T(8,128)(2,1)S(1)}, bf16[3,128,256]{2,1,0:T(8,128)(2,1)S(1)}, u32[]{:S(2)}, u32[]{:S(2)}) collective-permute-start(bf16[3,128,256]{2,1,0:T(8,128)(2,1)S(1)} %get-tuple-element.67), channel_id=1, source_target_pairs={{0,192},{8,200},{16,208},{24,216},{32,224},{40,232},{48,240},{56,2... | collective-permute-start | bytes 589832 | tf_op jit(solution)/shard_map/ppermute | solution.py:49
  55.7 7.8 %copy-start.18 = (f32[512,16]{0,1:T(8,128)S(1)}, f32[512,16]{0,1:T(8,128)}, u32[]{:S(2)}) copy-start(f32[512,16]{0,1:T(8,128)} %param.10) | copy-start | bytes 98308
  55.8 7.8 %copy-start.19 = (f32[512,16]{0,1:T(8,128)S(1)}, f32[512,16]{0,1:T(8,128)}, u32[]{:S(2)}) copy-start(f32[512,16]{0,1:T(8,128)} %param.9) | copy-start | bytes 98308
  55.8 7.9 %copy-start.20 = (f32[512]{0:T(512)S(1)}, f32[512]{0:T(512)}, u32[]{:S(2)}) copy-start(f32[512]{0:T(512)} %param.11) | copy-start | bytes 6148
  60.8 0.7 copy-start.14
  60.8 2.8 %copy-start.15 = (bf16[3,128,256]{2,1,0:T(8,128)(2,1)}, bf16[3,128,256]{2,1,0:T(8,128)(2,1)S(1)}, u32[]{:S(2)}) copy-start(bf16[3,128,256]{2,1,0:T(8,128)(2,1)S(1)} %collective-permute-done.15.refs_4_) | copy-start | bytes 589828
  60.8 14.3 %collective-permute-start.17 = (bf16[3,256,256]{2,1,0:T(8,128)(2,1)}, bf16[3,256,256]{2,1,0:T(8,128)(2,1)}, u32[]{:S(2)}, u32[]{:S(2)}) collective-permute-start(bf16[3,256,256]{2,1,0:T(8,128)(2,1)} %collective-permute-done.16.refs_0_), channel_id=1, source_target_pairs={{0,64},{8,72},{16,80},{24,88},{32,96},{40,104},{48,112},{56,120},{... | collective-permute-start | bytes 1179656 | tf_op jit(solution)/shard_map/ppermute | solution.py:49
  61.5 13.7 %collective-permute-start.18 = (bf16[3,256,256]{2,1,0:T(8,128)(2,1)}, bf16[3,256,256]{2,1,0:T(8,128)(2,1)}, u32[]{:S(2)}, u32[]{:S(2)}) collective-permute-start(bf16[3,256,256]{2,1,0:T(8,128)(2,1)} %collective-permute-done.16.refs_0_), channel_id=1, source_target_pairs={{0,192},{8,200},{16,208},{24,216},{32,224},{40,232},{48,240},{56,2... | collective-permute-start | bytes 1179656 | tf_op jit(solution)/shard_map/ppermute | solution.py:49
  64.8 10.3 %collective-permute-start.19 = (bf16[3,128,256]{2,1,0:T(8,128)(2,1)S(1)}, bf16[3,128,256]{2,1,0:T(8,128)(2,1)S(1)}, u32[]{:S(2)}, u32[]{:S(2)}) collective-permute-start(bf16[3,128,256]{2,1,0:T(8,128)(2,1)S(1)} %get-tuple-element.75), channel_id=1, source_target_pairs={{0,64},{8,72},{16,80},{24,88},{32,96},{40,104},{48,112},{56,120},{... | collective-permute-start | bytes 589832 | tf_op jit(solution)/shard_map/ppermute | solution.py:49
  64.9 10.3 %collective-permute-start.20 = (bf16[3,128,256]{2,1,0:T(8,128)(2,1)S(1)}, bf16[3,128,256]{2,1,0:T(8,128)(2,1)S(1)}, u32[]{:S(2)}, u32[]{:S(2)}) collective-permute-start(bf16[3,128,256]{2,1,0:T(8,128)(2,1)S(1)} %get-tuple-element.76), channel_id=1, source_target_pairs={{0,192},{8,200},{16,208},{24,216},{32,224},{40,232},{48,240},{56,2... | collective-permute-start | bytes 589832 | tf_op jit(solution)/shard_map/ppermute | solution.py:49
  75.1 4.0 %copy-start.16 = (bf16[3,128,256]{2,1,0:T(8,128)(2,1)}, bf16[3,128,256]{2,1,0:T(8,128)(2,1)S(1)}, u32[]{:S(2)}) copy-start(bf16[3,128,256]{2,1,0:T(8,128)(2,1)S(1)} %collective-permute-done.19.refs_3_) | copy-start | bytes 589828
  75.1 4.0 %copy-start.17 = (bf16[3,128,256]{2,1,0:T(8,128)(2,1)}, bf16[3,128,256]{2,1,0:T(8,128)(2,1)S(1)}, u32[]{:S(2)}) copy-start(bf16[3,128,256]{2,1,0:T(8,128)(2,1)S(1)} %collective-permute-done.20.refs_4_) | copy-start | bytes 589828
  76.3 7.4 %collective-permute-start.21 = (bf16[3,128,256]{2,1,0:T(8,128)(2,1)S(1)}, bf16[3,128,256]{2,1,0:T(8,128)(2,1)S(1)}, u32[]{:S(2)}, u32[]{:S(2)}) collective-permute-start(bf16[3,128,256]{2,1,0:T(8,128)(2,1)S(1)} %get-tuple-element.85), channel_id=1, source_target_pairs={{0,64},{8,72},{16,80},{24,88},{32,96},{40,104},{48,112},{56,120},{... | collective-permute-start | bytes 589832 | tf_op jit(solution)/shard_map/ppermute | solution.py:49
  76.7 7.1 %collective-permute-start.22 = (bf16[3,128,256]{2,1,0:T(8,128)(2,1)S(1)}, bf16[3,128,256]{2,1,0:T(8,128)(2,1)S(1)}, u32[]{:S(2)}, u32[]{:S(2)}) collective-permute-start(bf16[3,128,256]{2,1,0:T(8,128)(2,1)S(1)} %get-tuple-element.86), channel_id=1, source_target_pairs={{0,192},{8,200},{16,208},{24,216},{32,224},{40,232},{48,240},{56,2... | collective-permute-start | bytes 589832 | tf_op jit(solution)/shard_map/ppermute | solution.py:49
  83.7 0.7 copy-start.12
  83.7 0.7 copy-start.13
  90.5 4.5 %collective-permute-start.23 = (f32[16,256]{1,0:T(8,128)S(1)}, f32[16,256]{1,0:T(8,128)S(1)}, u32[]{:S(2)}, u32[]{:S(2)}) collective-permute-start(f32[16,256]{1,0:T(8,128)S(1)} %get-tuple-element.103), channel_id=1, source_target_pairs={{0,16},{8,24},{16,32},{24,40},{32,48},{40,56},{48,0},{56,8},{64,80... | collective-permute-start | bytes 49160 | tf_op jit(solution)/shard_map/ppermute | solution.py:49
  91.2 3.8 %collective-permute-start.24 = (f32[16,256]{1,0:T(8,128)S(1)}, f32[16,256]{1,0:T(8,128)S(1)}, u32[]{:S(2)}, u32[]{:S(2)}) collective-permute-start(f32[16,256]{1,0:T(8,128)S(1)} %get-tuple-element.103), channel_id=1, source_target_pairs={{0,32},{8,40},{16,48},{24,56},{32,0},{40,8},{48,16},{56,24},{64,96... | collective-permute-start | bytes 49160 | tf_op jit(solution)/shard_map/ppermute | solution.py:49
  92.9 2.6 %collective-permute-start.25 = (f32[16,256]{1,0:T(8,128)S(1)}, f32[16,256]{1,0:T(8,128)S(1)}, u32[]{:S(2)}, u32[]{:S(2)}) collective-permute-start(f32[16,256]{1,0:T(8,128)S(1)} %get-tuple-element.103), channel_id=1, source_target_pairs={{0,48},{8,56},{16,0},{24,8},{32,16},{40,24},{48,32},{56,40},{64,11... | collective-permute-start | bytes 49160 | tf_op jit(solution)/shard_map/ppermute | solution.py:49
  96.3 5.8 %collective-permute-start.26 = (f32[16,256]{1,0:T(8,128)S(1)}, f32[16,256]{1,0:T(8,128)S(1)}, u32[]{:S(2)}, u32[]{:S(2)}) collective-permute-start(f32[16,256]{1,0:T(8,128)S(1)} %fusion.2), channel_id=1, source_target_pairs={{0,64},{8,72},{16,80},{24,88},{32,96},{40,104},{48,112},{56,120},{... | collective-permute-start | bytes 49160 | tf_op jit(solution)/shard_map/ppermute | solution.py:49
  96.4 5.7 %collective-permute-start.27 = (f32[16,256]{1,0:T(8,128)S(1)}, f32[16,256]{1,0:T(8,128)S(1)}, u32[]{:S(2)}, u32[]{:S(2)}) collective-permute-start(f32[16,256]{1,0:T(8,128)S(1)} %fusion.2), channel_id=1, source_target_pairs={{0,128},{8,136},{16,144},{24,152},{32,160},{40,168},{48,176},{56,1... | collective-permute-start | bytes 49160 | tf_op jit(solution)/shard_map/ppermute | solution.py:49
  98.6 3.5 %collective-permute-start.28 = (f32[16,256]{1,0:T(8,128)S(1)}, f32[16,256]{1,0:T(8,128)S(1)}, u32[]{:S(2)}, u32[]{:S(2)}) collective-permute-start(f32[16,256]{1,0:T(8,128)S(1)} %fusion.2), channel_id=1, source_target_pairs={{0,192},{8,200},{16,208},{24,216},{32,224},{40,232},{48,240},{56,2... | collective-permute-start | bytes 49160 | tf_op jit(solution)/shard_map/ppermute | solution.py:49
  104.8 8.5 %collective-permute-start.29 = (bf16[512,256]{1,0:T(8,128)(2,1)S(1)}, bf16[512,256]{1,0:T(8,128)(2,1)S(1)}, u32[]{:S(2)}, u32[]{:S(2)}) collective-permute-start(bf16[512,256]{1,0:T(8,128)(2,1)S(1)} %get-tuple-element.106), channel_id=1, source_target_pairs={{0,8},{8,0},{16,24},{24,16},{32,40},{40,32},{48,56},{56,48},{64,72... | collective-permute-start | bytes 786440 | tf_op jit(solution)/shard_map/ppermute | solution.py:49

commit v4 on v3

--- a/solution.py
+++ b/solution.py
@@ -163,12 +163,28 @@
     return copies
 
 
-def multiply(copies, rows, weights, finish):
+def columns_to(rows, where, x_steps, z_mask, mine, other, halo, sems):
+    x, z, core = where[0], where[1], where[2]
+    length, width = mine.shape[0], rows.shape[1]
+    chip = (x - x_steps + X) % X * Z + (z ^ z_mask)
+    span = pl.ds(pl.multiple_of(chip * width, LANES), width)
+    copies = [pltpu.make_async_copy(halo.at[:, span], rows.at[pl.ds(0, HALO), :], sems.at[0])]
+    for sem, array, block in ((1, mine, core), (2, other, 1 - core)):
+        first = pl.multiple_of(HALO + block * length, HALO)
+        copies.append(
+            pltpu.make_async_copy(
+                array.at[:, span], rows.at[pl.ds(first, length), :], sems.at[sem]
+            )
+        )
     for copy in copies:
-        copy.wait()
-    streams, _, channels = weights.shape
-    for stream in range(streams):
-        product = jnp.dot(rows[...], weights[stream], preferred_element_type=jnp.float32)
+        copy.start()
+    return copies
+
+
+def multiply(rows, weights, finish):
+    for stream, weight in enumerate(weights):
+        channels = weight.shape[1]
+        product = jnp.dot(rows[...], weight, preferred_element_type=jnp.float32)
         for group in range(channels // LANES):
             finish(stream, group, product[:, group * LANES : (group + 1) * LANES])
 
@@ -202,7 +218,7 @@
     return 1 + max(step[3] for step in plan)
 
 
-def partial_kernel(plan, has_main, has_halo, has_before, where, *refs):
+def partial_kernel(plan, has_main, has_halo, has_before, kept_from, where, *refs):
     count = arrays_in(plan)
     pieces, refs = refs[:count], list(refs[count:])
     mine, other = (refs.pop(0), refs.pop(0)) if has_main else (None, None)
@@ -211,8 +227,12 @@
     halo_before = refs.pop(0) if has_halo and has_before else None
     totals = refs.pop(0) if has_main else None
     halo_totals = refs.pop(0) if has_halo else None
-    rows, weights, sems = refs
+    kept = refs.pop(0) if kept_from else None
+    rows, weights, sems, kept_sems = refs
     copies = start_copies(plan, ALL, where, pieces, mine, other, halo, rows, weights, sems)
+    kept_copies = (
+        columns_to(kept, where, *kept_from, mine, other, halo, kept_sems) if kept_from else []
+    )
 
     def finish(stream, group, share):
         if has_halo:
@@ -224,7 +244,11 @@
         if has_main:
             totals[stream, group] = share if before is None else before[stream, group] + share
 
-    multiply(copies, rows, weights, finish)
+    for copy in copies:
+        copy.wait()
+    multiply(rows, [weights[stream] for stream in range(ALL.size)], finish)
+    for copy in kept_copies:
+        copy.wait()
 
 
 def plan_of(pieces):
@@ -245,10 +269,11 @@
         pltpu.VMEM((rows, depth), jnp.bfloat16),
         pltpu.VMEM((streams.size, depth, channels), jnp.bfloat16),
         pltpu.SemaphoreType.DMA((len(plan), 4)),
+        pltpu.SemaphoreType.DMA((3,)),
     ]
 
 
-def partial_products(where, pieces, tokens, halo, before, name):
+def partial_products(where, pieces, tokens, halo, before, name, kept_from=None):
     plan, arrays, _ = plan_of(pieces)
     channels = arrays[0].shape[2]
     heights = [sum(array.shape[0] for array in tokens)] if tokens else []
@@ -256,9 +281,13 @@
     shapes = [
         pltpu.VMEM((ALL.size, channels // LANES, height, LANES), jnp.float32) for height in heights
     ]
+    if kept_from:
+        shapes.append(pltpu.VMEM((sum(heights), 2 * LANES), jnp.bfloat16))
     inputs = [*arrays, *tokens, *halo]
     return pl.pallas_call(
-        functools.partial(partial_kernel, plan, bool(tokens), bool(halo), bool(before)),
+        functools.partial(
+            partial_kernel, plan, bool(tokens), bool(halo), bool(before), kept_from
+        ),
         out_shape=shapes,
         in_specs=[SMEM] + [HBM] * len(inputs) + [VMEM] * len(before),
         out_specs=[VMEM] * len(shapes),
@@ -268,17 +297,33 @@
     )(where, *in_hbm(*inputs), *in_vmem(*before))
 
 
-def signal_kernel(plan, streams, where, *refs):
-    count = arrays_in(plan)
-    pieces, refs = refs[:count], refs[count:]
-    mine, other, halo, products, halo_products = refs[:5]
-    taps, decay, amplitude, power, skip = refs[5:10]
-    signal, before, ends, rows, weights, sems, projected = refs[10:]
-    channels = weights.shape[2]
-    steps = 2 * mine.shape[0] // SEGMENTS
-    copies = start_copies(plan, streams, where, pieces, mine, other, halo, rows, weights, sems)
-    finish, load = segmented(projected, products, halo_products, streams.start)
-    multiply(copies, rows, weights, finish)
+def last_weights(upper, lower, streams):
+    return [
+        jnp.concatenate([upper[stream], lower[stream]], axis=0)
+        for stream in range(streams.start, streams.start + streams.size)
+    ]
+
+
+def signal_kernel(
+    rows,
+    upper,
+    lower,
+    products,
+    halo_products,
+    taps,
+    decay,
+    amplitude,
+    power,
+    skip,
+    signal,
+    before,
+    ends,
+    projected,
+):
+    channels = upper.shape[2]
+    steps = signal.shape[0]
+    finish, load = segmented(projected, products, halo_products, KEY_VALUE.start)
+    multiply(rows, last_weights(upper, lower, KEY_VALUE), finish)
     for low in range(0, channels, LANES):
         lanes = pl.ds(low, LANES)
         group = low // LANES
@@ -339,37 +384,31 @@
             ends[pl.ds(mode, 1), lanes] = state[SEGMENTS - 1 :, :]
 
 
-def signals(where, pieces, tokens, halo, products, taps, decay, amplitude, power, skip):
-    plan, arrays, _ = plan_of(pieces)
+def signals(rows, last, products, taps, decay, amplitude, power, skip):
     modes, channels = decay.shape
-    rows = sum(array.shape[0] for array in tokens)
-    inputs = [*arrays, *tokens, halo]
+    length = rows.shape[0] - HALO
     return pl.pallas_call(
-        functools.partial(signal_kernel, plan, KEY_VALUE),
+        signal_kernel,
         out_shape=(
-            pltpu.VMEM((rows // SEGMENTS, SEGMENTS, channels), jnp.float32),
+            pltpu.VMEM((length // SEGMENTS, SEGMENTS, channels), jnp.float32),
             pltpu.VMEM((modes, SEGMENTS, channels), jnp.float32),
             jax.ShapeDtypeStruct((modes, channels), jnp.float32),
         ),
-        in_specs=[SMEM] + [HBM] * len(inputs) + [VMEM] * 7,
+        in_specs=[VMEM] * 10,
         out_specs=(VMEM,) * 3,
-        scratch_shapes=copy_scratch(pieces, KEY_VALUE, HALO + rows)
-        + [segment_scratch(KEY_VALUE, rows, channels)],
+        scratch_shapes=[segment_scratch(KEY_VALUE, length, channels)],
         compiler_params=pltpu.CompilerParams(vmem_limit_bytes=8 * 1024 * 1024),
         name="signals",
-    )(where, *in_hbm(*inputs), *in_vmem(*products), taps, decay, amplitude, power, skip)
-
-
-def query_kernel(plan, streams, where, *refs):
-    count = arrays_in(plan)
-    pieces, refs = refs[:count], refs[count:]
-    mine, other, halo, products, halo_products, conv, taps = refs[:7]
-    query, gated, rows, weights, sems, projected = refs[7:]
-    channels = weights.shape[2]
-    steps = 2 * mine.shape[0] // SEGMENTS
-    copies = start_copies(plan, streams, where, pieces, mine, other, halo, rows, weights, sems)
-    finish, load = segmented(projected, products, halo_products, streams.start)
-    multiply(copies, rows, weights, finish)
+    )(*in_vmem(rows, *last, *products), taps, decay, amplitude, power, skip)
+
+
+def query_kernel(
+    rows, upper, lower, products, halo_products, conv, taps, query, gated, projected
+):
+    channels = upper.shape[2]
+    steps = conv.shape[0]
+    finish, load = segmented(projected, products, halo_products, QUERY.start)
+    multiply(rows, last_weights(upper, lower, QUERY), finish)
     for group in range(channels // LANES):
         lanes = pl.ds(group * LANES, LANES)
         spread = [
@@ -390,21 +429,17 @@
         lax.fori_loop(0, steps, featurize, held, unroll=8)
 
 
-def queries(where, pieces, tokens, halo, products, conv, taps):
-    plan, arrays, _ = plan_of(pieces)
-    channels = arrays[0].shape[2]
-    rows = sum(array.shape[0] for array in tokens)
-    inputs = [*arrays, *tokens, halo]
+def queries(rows, last, products, conv, taps):
+    steps, _, channels = conv.shape
     return pl.pallas_call(
-        functools.partial(query_kernel, plan, QUERY),
-        out_shape=(pltpu.VMEM((rows // SEGMENTS, SEGMENTS, channels), jnp.float32),) * 2,
-        in_specs=[SMEM] + [HBM] * len(inputs) + [VMEM] * 4,
+        query_kernel,
+        out_shape=(pltpu.VMEM(conv.shape, jnp.float32),) * 2,
+        in_specs=[VMEM] * 7,
         out_specs=(VMEM,) * 2,
-        scratch_shapes=copy_scratch(pieces, QUERY, HALO + rows)
-        + [segment_scratch(QUERY, rows, channels)],
+        scratch_shapes=[segment_scratch(QUERY, steps * SEGMENTS, channels)],
         compiler_params=pltpu.CompilerParams(vmem_limit_bytes=8 * 1024 * 1024),
         name="queries",
-    )(where, *in_hbm(*inputs), *in_vmem(*products, conv), taps)
+    )(*in_vmem(rows, *last, *products, conv), taps)
 
 
 def gate_kernel(
@@ -522,12 +557,23 @@
 
     low, high = in_weight[:, :, :half], in_weight[:, :, half:]
     own = jnp.where(first, low, high)
-    received = swap_cores(jnp.where(first, high, low))
-    tail = tokens[length - HALO :]
-    tail = jnp.where(first, swap_cores(tail), tail)
+    received, later_tokens = together(swap_cores(jnp.where(first, high, low)), tokens)
     block = jnp.concatenate(
         [jnp.where(first, own, received), jnp.where(first, received, own)], axis=1
     )
+    beside = across_z(block, 1)
+    right, left = sides(block)
+    other = swap_cores(later_tokens)
+    held, tail = together(block, later_tokens[length - HALO :])
+    held, other_tail = together(held, swap_cores(tail))
+    over = across_z(held, 2)
+    halo = next_chip(jnp.where(first, other_tail, tail))
+    beside, right, left, other, *parameters = together(
+        beside, right, left, other, rates, residues, short_filter, skip
+    )
+    rates, residues, short_filter, skip = parameters
+    both = (tokens, other)
+
     rate = half_of(rates, 0).T
     residue = half_of(residues, 0).T
     decay = jnp.exp(-rate)
@@ -540,51 +586,45 @@
     taps = half_of(short_filter, 2)
     direct = half_of(skip, 0)[None, :]
 
-    beside = across_z(block, 1)
-    right, left = sides(block)
-    other = swap_cores(tokens)
-    halo = next_chip(tail)
-    held, other = together(block, other)
-    over = across_z(held, 2)
-    beside, right, left, held = together(beside, right, left, held)
-    both = (tokens, other)
-
     far = forwards(right, left)
     pieces = with_sides(0, block, right, left)
     products = partial_products(where, pieces, both, (), (), "first")
     right, left = sides(beside)
-    right, left, *far, over, products, halo = together(right, left, *far, over, *products, halo)
+    far_beside = forwards(right, left)
+    right, left, *far, over, products, halo, far_right, far_left = together(
+        right, left, *far, over, *products, halo, *far_beside
+    )
     so_far = pieces
 
+    opposite = across_z(over, 1)
     pieces = with_sides(1, beside, right, left) + with_far(0, *far)
     products = partial_products(where, pieces, both, (), (products,), "second")
     so_far += pieces
+    right, left = sides(over)
+    right, left, opposite, products = together(right, left, opposite, *products)
+
+    pieces = with_sides(2, over, right, left) + with_far(1, far_right, far_left)
+    products = partial_products(where, pieces, both, (), (products,), "third")
+    so_far += pieces
     halo_products = partial_products(where, so_far, (), (halo,), (), "halo")
-    far = forwards(right, left)
-    opposite = across_z(over, 1)
-    right, left = sides(over)
-    right, left, far_right, far_left, opposite, products, halo_products = together(
-        right, left, *far, opposite, *products, *halo_products
-    )
-
-    pieces = with_sides(2, over, right, left) + with_far(1, far_right, far_left)
-    products = partial_products(where, pieces, both, (halo,), (products, halo_products), "third")
     far = forwards(right, left)
     right, left = sides(opposite)
     small = (power, start_power, factors, decay, amplitude, taps, direct)
     right, left, far_right, far_left, products, halo_products, *small = together(
-        right, left, *far, *products, *small
+        right, left, *far, *products, *halo_products, *small
     )
     power, start_power, factors, decay, amplitude, taps, direct = small
 
     pieces = with_sides(3, opposite, right, left) + with_far(2, far_right, far_left)
-    last = with_far(3, *forwards(right, left))
-    products = partial_products(where, pieces, both, (halo,), (products, halo_products), "fourth")
+    last = forwards(right, left)
+    *products, rows = partial_products(
+        where, pieces, both, (halo,), (products, halo_products), "fourth", (2, 3)
+    )
 
     conv, before, ends = signals(
-        where, last, both, halo, products, taps, decay, amplitude, power, direct
-    )
-    query, product = queries(where, last, both, halo, products, conv, taps)
+        rows, last, products, taps, decay, amplitude, power, direct
+    )
+    query, product = queries(rows, last, products, conv, taps)
     carried = carried_states(ends, factors)
     keep, send = carry_gated(
         where, query, product, before, carried, decay, amplitude, start_power

time: 115 us -> 103 us (0.90)
  other arithmetic: 13.2 us -> 3.41 us
  Pallas kernels: 34 us -> 29.4 us
  starting transfers between devices: 45.5 us -> 48.6 us
  waiting for transfers between devices: 17 us -> 19.9 us
  local copies, waits for them, and re-layouts: 3.98 us -> 1.1 us
    unnamed x9, other arithmetic: 5.49 us -> 0.1 us
    pallas_call x2, Pallas kernels: 8.85 us -> 5.19 us  [the longest x1 4.17 us: signals(): pl.pallas_call(signal_kernel, out_shape=(pltpu.VMEM((length // SEGMENTS,...]
    ppermute x30, starting transfers between devices: 45.5 us -> 48.6 us  [permute(): return lax.ppermute(value, 'seq', pairs)]
    unnamed x42 -> x46, local copies, waits for them, and re-layouts: 2.99 us -> 0.1 us
    ppermute x30, waiting for transfers between devices: 17 us -> 19.9 us  [permute(): return lax.ppermute(value, 'seq', pairs)]
    pallas_call x4, Pallas kernels: 2.58 us -> 0.75 us  [forwards(): pl.pallas_call(halves_kernel, out_shape=(half, half), in_specs=[ANY] * 2,...]
    select_n x2, other arithmetic: 2.61 us -> 1.07 us  [the longest x1 1.06 us: local(): jnp.where(first, high, low)]
  transfers between devices with their start and end apart: 30 -> 30, of which waited for: 9 -> 14; matrix products, arithmetic and copies ran while one was open for 10% -> 2% of each run, Pallas kernels for 22% -> 23%
where the time goes in v4:
time: 103 us
  starting transfers between devices  48.6 us (47%)
  Pallas kernels  29.4 us (29%)
  waiting for transfers between devices  19.9 us (19%)
  other arithmetic  3.41 us (3%)
  local copies, waits for them, and re-layouts  1.1 us (1%)
    ppermute x30, starting transfers between devices, permute(): return lax.ppermute(value, 'seq', pairs)  48.6 us
    pallas_call x5, Pallas kernels, partial_products(): pl.pallas_call(functools.partial(partial_kernel, plan, bool(tokens), bool...  21.6 us
    ppermute x30, waiting for transfers between devices, permute(): return lax.ppermute(value, 'seq', pairs)  19.9 us
    pallas_call x1, Pallas kernels, signals(): pl.pallas_call(signal_kernel, out_shape=(pltpu.VMEM((length // SEGMENTS,...  4.17 us
  transfers between devices with their start and end apart: 30, of which 14 were waited for; matrix products, arithmetic and copies ran while one was open for 2% of the time, Pallas kernels for 23%

profile of v4, /device:TPU:1, one launch (start us, length us, event | category | flops | bytes accessed | tf_op | source)
XLA Modules:
  0.0 103.0 jit_solution(17672448430497057656)
XLA Ops:
  0.0 1.1 %broadcast_select_fusion.4 = bf16[3,128,256]{2,1,0:T(8,128)(2,1)S(1)} fusion(pred[]{:T(512)S(6)} %eq.6, bf16[3,128,512]{2,1,0:T(8,128)(2,1)} %param.7), kind=kLoop, calls=%fused_computation.6 | loop fusion | flops 98304 | bytes 589825 | tf_op jit(solution)/shard_map/jit(_where)/select_n | solution.py:560
  1.1 3.3 %collective-permute-start = (bf16[3,128,256]{2,1,0:T(8,128)(2,1)S(1)}, bf16[3,128,256]{2,1,0:T(8,128)(2,1)S(1)}, u32[]{:S(2)}, u32[]{:S(2)}) collective-permute-start(bf16[3,128,256]{2,1,0:T(8,128)(2,1)S(1)} %broadcast_select_fusion.4), channel_id=1, source_target_pairs={{0,8},{8,0},{16,24},{24,16},{32,40},{40,32},{48,56},{56,48},{64,72... | collective-permute-start | bytes 589832 | tf_op jit(solution)/shard_map/ppermute | solution.py:49
  4.4 1.1 %collective-permute-done = bf16[3,128,256]{2,1,0:T(8,128)(2,1)S(1)} collective-permute-done((bf16[3,128,256]{2,1,0:T(8,128)(2,1)S(1)}, bf16[3,128,256]{2,1,0:T(8,128)(2,1)S(1)}, u32[]{:S(2)}, u32[]{:S(2)}) %collective-permute-start) | collective-permute-done | bytes 196640 | tf_op jit(solution)/shard_map/ppermute | solution.py:49
  5.5 0.4 collective-permute-start.4
  5.8 0.9 slice.54
  6.8 1.1 %broadcast_select_fusion.3 = (bf16[3,128,256]{2,1,0:T(8,128)(2,1)S(1)}, bf16[3,128,256]{2,1,0:T(8,128)(2,1)S(1)}) fusion(bf16[3,128,256]{2,1,0:T(8,128)(2,1)S(1)} %collective-permute-done, pred[]{:T(512)S(6)} %eq.6, bf16[3,128,512]{2,1,0:T(8,128)(2,1)} %param.7), kind=kLoop, calls=%fused_computation.5 | loop fusion | flops 294912 | bytes 983041 | tf_op jit(solution)/shard_map/jit(_where)/select_n | solution.py:562
  7.9 0.2 collective-permute-start.9
  8.1 0.1 pad_add_fusion.where
  8.2 0.0 collective-permute-start.1
  8.2 1.1 %collective-permute-start.2 = (bf16[3,256,256]{2,1,0:T(8,128)(2,1)S(1)}, bf16[3,256,256]{2,1,0:T(8,128)(2,1)S(1)}, u32[]{:S(2)}, u32[]{:S(2)}) collective-permute-start(bf16[3,256,256]{2,1,0:T(8,128)(2,1)S(1)} %pad_maximum_fusion.1.refs_0_), channel_id=1, source_target_pairs={{0,64},{8,72},{16,80},{24,88},{32,96},{40,104},{48,112},{56,120},{... | collective-permute-start | bytes 1179656 | tf_op jit(solution)/shard_map/ppermute | solution.py:49
  9.3 1.7 %collective-permute-start.3 = (bf16[3,256,256]{2,1,0:T(8,128)(2,1)S(1)}, bf16[3,256,256]{2,1,0:T(8,128)(2,1)S(1)}, u32[]{:S(2)}, u32[]{:S(2)}) collective-permute-start(bf16[3,256,256]{2,1,0:T(8,128)(2,1)S(1)} %pad_maximum_fusion.1.refs_0_), channel_id=1, source_target_pairs={{0,192},{8,200},{16,208},{24,216},{32,224},{40,232},{48,240},{56,2... | collective-permute-start | bytes 1179656 | tf_op jit(solution)/shard_map/ppermute | solution.py:49
  11.0 1.8 %collective-permute-done.9 = bf16[16,4096]{1,0:T(8,128)(2,1)S(1)} collective-permute-done((bf16[16,4096]{1,0:T(8,128)(2,1)S(1)}, bf16[16,4096]{1,0:T(8,128)(2,1)S(1)}, u32[]{:S(2)}, u32[]{:S(2)}) %collective-permute-start.9) | collective-permute-done | bytes 131104 | tf_op jit(solution)/shard_map/ppermute | solution.py:49
  12.8 1.8 %collective-permute-start.11 = (bf16[16,4096]{1,0:T(8,128)(2,1)S(1)}, bf16[16,4096]{1,0:T(8,128)(2,1)S(1)}, u32[]{:S(2)}, u32[]{:S(2)}) collective-permute-start(bf16[16,4096]{1,0:T(8,128)(2,1)S(1)} %broadcast_select_fusion.6), channel_id=1, source_target_pairs={{0,16},{8,24},{16,32},{24,40},{32,48},{40,56},{48,64},{56,72},{64,... | collective-permute-start | bytes 393224 | tf_op jit(solution)/shard_map/ppermute | solution.py:49
  14.7 3.9 %collective-permute-done.1.refs_0_.refs_3_ = bf16[3,256,256]{2,1,0:T(8,128)(2,1)S(1)} collective-permute-done((bf16[3,256,256]{2,1,0:T(8,128)(2,1)S(1)}, bf16[3,256,256]{2,1,0:T(8,128)(2,1)S(1)}, u32[]{:S(2)}, u32[]{:S(2)}) %collective-permute-start.1) | collective-permute-done | bytes 393248 | tf_op jit(solution)/shard_map/ppermute | solution.py:49
  18.5 1.6 %collective-permute-start.10 = (bf16[3,256,256]{2,1,0:T(8,128)(2,1)S(1)}, bf16[3,256,256]{2,1,0:T(8,128)(2,1)S(1)}, u32[]{:S(2)}, u32[]{:S(2)}) collective-permute-start(bf16[3,256,256]{2,1,0:T(8,128)(2,1)S(1)} %pad_maximum_fusion.1.refs_0_), channel_id=1, source_target_pairs={{0,32},{8,40},{16,48},{24,56},{32,0},{40,8},{48,16},{56,24},{64,96... | collective-permute-start | bytes 1179656 | tf_op jit(solution)/shard_map/ppermute | solution.py:49
  20.2 1.3 %collective-permute-start.5 = (bf16[3,256,256]{2,1,0:T(8,128)(2,1)S(1)}, bf16[3,256,256]{2,1,0:T(8,128)(2,1)S(1)}, u32[]{:S(2)}, u32[]{:S(2)}) collective-permute-start(bf16[3,256,256]{2,1,0:T(8,128)(2,1)S(1)} %collective-permute-done.1.refs_0_.refs_3_), channel_id=1, source_target_pairs={{0,64},{8,72},{16,80},{24,88},{32,96},{40,104},{48,112},{56,120},{... | collective-permute-start | bytes 1179656 | tf_op jit(solution)/shard_map/ppermute | solution.py:49
  21.5 1.5 %collective-permute-start.6 = (bf16[3,256,256]{2,1,0:T(8,128)(2,1)S(1)}, bf16[3,256,256]{2,1,0:T(8,128)(2,1)S(1)}, u32[]{:S(2)}, u32[]{:S(2)}) collective-permute-start(bf16[3,256,256]{2,1,0:T(8,128)(2,1)S(1)} %collective-permute-done.1.refs_0_.refs_3_), channel_id=1, source_target_pairs={{0,192},{8,200},{16,208},{24,216},{32,224},{40,232},{48,240},{56,2... | collective-permute-start | bytes 1179656 | tf_op jit(solution)/shard_map/ppermute | solution.py:49
  23.0 0.2 halves.4
  23.2 0.1 collective-permute-start.7
  23.4 3.8 %first.1.refs_7_ = f32[3,2,1024,128]{3,2,1,0:T(8,128)S(1)} custom-call(s32[3]{0:T(128)S(1)} %pad_add_fusion.where, bf16[3,256,256]{2,1,0:T(8,128)(2,1)} %copy-done.9, bf16[3,256,256]{2,1,0:T(8,128)(2,1)} %copy-done.1, bf16[3,256,256]{2,1,0:T(8,128)(2,1)} %copy-done.2, bf16[512,4096]{1,0:T(8,128)(2,1)} %refs_5_.5, ...), custom_call_target="tpu_custom_call" | custom-call | tf_op jit(solution)/shard_map/first/pallas_call | solution.py:287
  27.2 3.0 %collective-permute-done.5.right.refs_1_.refs_4_ = bf16[3,256,256]{2,1,0:T(8,128)(2,1)S(1)} collective-permute-done((bf16[3,256,256]{2,1,0:T(8,128)(2,1)S(1)}, bf16[3,256,256]{2,1,0:T(8,128)(2,1)S(1)}, u32[]{:S(2)}, u32[]{:S(2)}) %collective-permute-start.5) | collective-permute-done | bytes 393248 | tf_op jit(solution)/shard_map/ppermute | solution.py:49
  30.2 3.2 %collective-permute-start.8 = (bf16[3,128,256]{2,1,0:T(8,128)(2,1)S(1)}, bf16[3,128,256]{2,1,0:T(8,128)(2,1)S(1)}, u32[]{:S(2)}, u32[]{:S(2)}) collective-permute-start(bf16[3,128,256]{2,1,0:T(8,128)(2,1)S(1)} %get-tuple-element.69), channel_id=1, source_target_pairs={{0,192},{8,200},{16,208},{24,216},{32,224},{40,232},{48,240},{56,2... | collective-permute-start | bytes 589832 | tf_op jit(solution)/shard_map/ppermute | solution.py:49
  33.4 0.2 halves.5
  33.6 0.1 collective-permute-start.12
  33.7 2.6 %collective-permute-start.13 = (bf16[3,128,256]{2,1,0:T(8,128)(2,1)S(1)}, bf16[3,128,256]{2,1,0:T(8,128)(2,1)S(1)}, u32[]{:S(2)}, u32[]{:S(2)}) collective-permute-start(bf16[3,128,256]{2,1,0:T(8,128)(2,1)S(1)} %get-tuple-element.76), channel_id=1, source_target_pairs={{0,192},{8,200},{16,208},{24,216},{32,224},{40,232},{48,240},{56,2... | collective-permute-start | bytes 589832 | tf_op jit(solution)/shard_map/ppermute | solution.py:49
  36.3 3.7 %collective-permute-done.10.refs_0_.refs_8_ = bf16[3,256,256]{2,1,0:T(8,128)(2,1)S(1)} collective-permute-done((bf16[3,256,256]{2,1,0:T(8,128)(2,1)S(1)}, bf16[3,256,256]{2,1,0:T(8,128)(2,1)S(1)}, u32[]{:S(2)}, u32[]{:S(2)}) %collective-permute-start.10) | collective-permute-done | bytes 393248 | tf_op jit(solution)/shard_map/ppermute | solution.py:49
  40.1 0.7 collective-permute-done.13.refs_4_.refs_12_
  40.8 0.6 collective-permute-start.14
  41.4 2.8 %collective-permute-start.15 = (bf16[3,256,256]{2,1,0:T(8,128)(2,1)S(1)}, bf16[3,256,256]{2,1,0:T(8,128)(2,1)S(1)}, u32[]{:S(2)}, u32[]{:S(2)}) collective-permute-start(bf16[3,256,256]{2,1,0:T(8,128)(2,1)S(1)} %collective-permute-done.10.refs_0_.refs_8_), channel_id=1, source_target_pairs={{0,192},{8,200},{16,208},{24,216},{32,224},{40,232},{48,240},{56,2... | collective-permute-start | bytes 1179656 | tf_op jit(solution)/shard_map/ppermute | solution.py:49
  44.2 0.1 multiply_exponential_fusion.power
  44.4 0.0 copy-start.21
  44.4 0.0 copy-start.22
  44.4 4.5 %second.1.refs_7_ = f32[3,2,1024,128]{3,2,1,0:T(8,128)S(1)} custom-call(s32[3]{0:T(128)S(1)} %pad_add_fusion.where, bf16[3,256,256]{2,1,0:T(8,128)(2,1)} %copy-done.10, bf16[3,256,256]{2,1,0:T(8,128)(2,1)} %copy-done.3, bf16[3,256,256]{2,1,0:T(8,128)(2,1)} %copy-done.4, bf16[3,128,256]{2,1,0:T(8,128)(2,1)} %copy-done.12, bf16[3,128,256]{2,1,0:T(8,128)(2,1)} %copy-done.13, ...), custom_call_target="tpu_custom_call" | custom-call | tf_op jit(solution)/shard_map/second/pallas_call | solution.py:287
  49.0 1.8 %collective-permute-done.14.right.refs_1_.refs_9_ = bf16[3,256,256]{2,1,0:T(8,128)(2,1)S(1)} collective-permute-done((bf16[3,256,256]{2,1,0:T(8,128)(2,1)S(1)}, bf16[3,256,256]{2,1,0:T(8,128)(2,1)S(1)}, u32[]{:S(2)}, u32[]{:S(2)}) %collective-permute-start.14) | collective-permute-done | bytes 393248 | tf_op jit(solution)/shard_map/ppermute | solution.py:49
  50.8 0.3 collective-permute-done.16.refs_0_
  51.1 0.4 collective-permute-start.17
  51.5 2.3 %collective-permute-start.18 = (bf16[3,256,256]{2,1,0:T(8,128)(2,1)S(1)}, bf16[3,256,256]{2,1,0:T(8,128)(2,1)S(1)}, u32[]{:S(2)}, u32[]{:S(2)}) collective-permute-start(bf16[3,256,256]{2,1,0:T(8,128)(2,1)S(1)} %collective-permute-done.16.refs_0_), channel_id=1, source_target_pairs={{0,192},{8,200},{16,208},{24,216},{32,224},{40,232},{48,240},{56,2... | collective-permute-start | bytes 1179656 | tf_op jit(solution)/shard_map/ppermute | solution.py:49
  53.8 0.1 dynamic_slice.15
  53.9 0.2 halves.6
  54.1 0.1 collective-permute-start.19
  54.2 2.7 %collective-permute-start.20 = (bf16[3,128,256]{2,1,0:T(8,128)(2,1)S(1)}, bf16[3,128,256]{2,1,0:T(8,128)(2,1)S(1)}, u32[]{:S(2)}, u32[]{:S(2)}) collective-permute-start(bf16[3,128,256]{2,1,0:T(8,128)(2,1)S(1)} %get-tuple-element.87), channel_id=1, source_target_pairs={{0,192},{8,200},{16,208},{24,216},{32,224},{40,232},{48,240},{56,2... | collective-permute-start | bytes 589832 | tf_op jit(solution)/shard_map/ppermute | solution.py:49
  56.9 4.0 %halo.1.refs_9_ = f32[3,2,16,128]{3,2,1,0:T(8,128)S(1)} custom-call(s32[3]{0:T(128)S(1)} %pad_add_fusion.where, bf16[3,256,256]{2,1,0:T(8,128)(2,1)} %copy-done.9, bf16[3,256,256]{2,1,0:T(8,128)(2,1)} %copy-done.1, bf16[3,256,256]{2,1,0:T(8,128)(2,1)} %copy-done.2, bf16[3,256,256]{2,1,0:T(8,128)(2,1)} %copy-done.10, bf16[3,256,256]{2,1,0:T(8,128)(2,1)} %copy-done.3, ...), custom_call_target="tpu_custom_call" | custom-call | tf_op jit(solution)/shard_map/halo/pallas_call | solution.py:287
  60.9 4.5 %third.1.refs_8_ = f32[3,2,1024,128]{3,2,1,0:T(8,128)S(1)} custom-call(s32[3]{0:T(128)S(1)} %pad_add_fusion.where, bf16[3,256,256]{2,1,0:T(8,128)(2,1)} %copy-done.11, bf16[3,256,256]{2,1,0:T(8,128)(2,1)} %copy-done.5, bf16[3,256,256]{2,1,0:T(8,128)(2,1)} %copy-done.6, bf16[3,128,256]{2,1,0:T(8,128)(2,1)} %copy-done.14, bf16[3,128,256]{2,1,0:T(8,128)(2,1)} %copy-done.15, ...), custom_call_target="tpu_custom_call" | custom-call | tf_op jit(solution)/shard_map/third/pallas_call | solution.py:287
  65.5 0.2 halves.7
  65.7 0.1 collective-permute-start.21
  65.8 2.7 %collective-permute-start.22 = (bf16[3,128,256]{2,1,0:T(8,128)(2,1)S(1)}, bf16[3,128,256]{2,1,0:T(8,128)(2,1)S(1)}, u32[]{:S(2)}, u32[]{:S(2)}) collective-permute-start(bf16[3,128,256]{2,1,0:T(8,128)(2,1)S(1)} %get-tuple-element.104), channel_id=1, source_target_pairs={{0,192},{8,200},{16,208},{24,216},{32,224},{40,232},{48,240},{56,2... | collective-permute-start | bytes 589832 | tf_op jit(solution)/shard_map/ppermute | solution.py:49
  68.5 4.7 %fourth.1 = (f32[3,2,1024,128]{3,2,1,0:T(8,128)S(1)}, f32[3,2,16,128]{3,2,1,0:T(8,128)S(1)}, bf16[1040,256]{1,0:T(8,128)(2,1)S(1)}) custom-call(s32[3]{0:T(128)S(1)} %pad_add_fusion.where, bf16[3,256,256]{2,1,0:T(8,128)(2,1)} %copy-done.17, bf16[3,256,256]{2,1,0:T(8,128)(2,1)} %copy-done.7, bf16[3,256,256]{2,1,0:T(8,128)(2,1)} %copy-done.8, ...), custom_call_target="tpu_custom_call" | custom-call | tf_op jit(solution)/shard_map/fourth/pallas_call | solution.py:287
  73.3 4.2 %signals.1 = (f32[128,8,256]{2,1,0:T(8,128)S(1)}, f32[16,8,256]{2,1,0:T(8,128)S(1)}, f32[16,256]{1,0:T(8,128)S(1)}) custom-call(bf16[1040,256]{1,0:T(8,128)(2,1)S(1)} %get-tuple-element.102.rows, bf16[3,128,256]{2,1,0:T(8,128)(2,1)S(1)} %collective-permute-done.21.upper, bf16[3,128,256]{2,1,0:T(8,128)(2,1)S(1)} %collective-permute-done.22.lower, ...), custom_call_target="tpu_custom_call" | custom-call | tf_op jit(solution)/shard_map/signals/pallas_call | solution.py:390
  77.4 0.1 collective-permute-start.23
  77.5 0.3 collective-permute-start.24
  77.9 2.9 %collective-permute-start.25 = (f32[16,256]{1,0:T(8,128)S(1)}, f32[16,256]{1,0:T(8,128)S(1)}, u32[]{:S(2)}, u32[]{:S(2)}) collective-permute-start(f32[16,256]{1,0:T(8,128)S(1)} %get-tuple-element.117), channel_id=1, source_target_pairs={{0,48},{8,56},{16,0},{24,8},{32,16},{40,24},{48,32},{56,40},{64,11... | collective-permute-start | bytes 49160 | tf_op jit(solution)/shard_map/ppermute | solution.py:49
  80.8 1.1 %collective-permute-done.23 = f32[16,256]{1,0:T(8,128)S(1)} collective-permute-done((f32[16,256]{1,0:T(8,128)S(1)}, f32[16,256]{1,0:T(8,128)S(1)}, u32[]{:S(2)}, u32[]{:S(2)}) %collective-permute-start.23) | collective-permute-done | bytes 16416 | tf_op jit(solution)/shard_map/ppermute | solution.py:49
  81.9 0.3 collective-permute-done.25
  82.2 0.1 collective-permute-start.26
  82.3 2.1 %collective-permute-start.27 = (f32[16,256]{1,0:T(8,128)S(1)}, f32[16,256]{1,0:T(8,128)S(1)}, u32[]{:S(2)}, u32[]{:S(2)}) collective-permute-start(f32[16,256]{1,0:T(8,128)S(1)} %fusion.2), channel_id=1, source_target_pairs={{0,128},{8,136},{16,144},{24,152},{32,160},{40,168},{48,176},{56,1... | collective-permute-start | bytes 49160 | tf_op jit(solution)/shard_map/ppermute | solution.py:49
  84.4 0.5 collective-permute-start.28
  85.0 1.0 queries.1
  86.0 0.1 collective-permute-done.26
  86.1 0.4 collective-permute-done.27
  86.5 0.5 collective-permute-done.28
  87.0 1.9 %gated.1 = (bf16[512,256]{1,0:T(8,128)(2,1)S(1)}, bf16[512,256]{1,0:T(8,128)(2,1)S(1)}) custom-call(s32[3]{0:T(128)S(1)} %pad_add_fusion.where, f32[128,8,256]{2,1,0:T(8,128)S(1)} %get-tuple-element.113.query, f32[128,8,256]{2,1,0:T(8,128)S(1)} %get-tuple-element.114.gated, f32[16,8,256]{2,1,0:T(8,128)S(1)} %get-tuple-element.115.before, ...), custom_call_target="tpu_custom_call" | custom-call | tf_op jit(solution)/shard_map/gated/pallas_call | solution.py:500
  88.9 12.1 %collective-permute-start.29 = (bf16[512,256]{1,0:T(8,128)(2,1)S(1)}, bf16[512,256]{1,0:T(8,128)(2,1)S(1)}, u32[]{:S(2)}, u32[]{:S(2)}) collective-permute-start(bf16[512,256]{1,0:T(8,128)(2,1)S(1)} %get-tuple-element.120), channel_id=1, source_target_pairs={{0,8},{8,0},{16,24},{24,16},{32,40},{40,32},{48,56},{56,48},{64,72... | collective-permute-start | bytes 786440 | tf_op jit(solution)/shard_map/ppermute | solution.py:49
  101.0 1.2 %collective-permute-done.29 = bf16[512,256]{1,0:T(8,128)(2,1)S(1)} collective-permute-done((bf16[512,256]{1,0:T(8,128)(2,1)S(1)}, bf16[512,256]{1,0:T(8,128)(2,1)S(1)}, u32[]{:S(2)}, u32[]{:S(2)}) %collective-permute-start.29) | collective-permute-done | bytes 262176 | tf_op jit(solution)/shard_map/ppermute | solution.py:49
  102.2 0.8 pad_maximum_fusion
  (82 shorter events, 0.4 us)
Async XLA Ops:
  0.0 44.2 %copy-start = (f32[3,7,512]{2,1,0:T(8,128)S(1)}, f32[3,7,512]{2,1,0:T(8,128)}, u32[]{:S(2)}) copy-start(f32[3,7,512]{2,1,0:T(8,128)} %param.8) | copy-start | bytes 129028
  0.0 22.9 %copy-start.20 = (f32[512,16]{0,1:T(8,128)S(1)}, f32[512,16]{0,1:T(8,128)}, u32[]{:S(2)}) copy-start(f32[512,16]{0,1:T(8,128)} %param.10) | copy-start | bytes 98308
  1.1 4.4 %collective-permute-start = (bf16[3,128,256]{2,1,0:T(8,128)(2,1)S(1)}, bf16[3,128,256]{2,1,0:T(8,128)(2,1)S(1)}, u32[]{:S(2)}, u32[]{:S(2)}) collective-permute-start(bf16[3,128,256]{2,1,0:T(8,128)(2,1)S(1)} %broadcast_select_fusion.4), channel_id=1, source_target_pairs={{0,8},{8,0},{16,24},{24,16},{32,40},{40,32},{48,56},{56,48},{64,72... | collective-permute-start | bytes 589832 | tf_op jit(solution)/shard_map/ppermute | solution.py:49
  5.5 14.7 %collective-permute-start.4 = (bf16[512,4096]{1,0:T(8,128)(2,1)}, bf16[512,4096]{1,0:T(8,128)(2,1)}, u32[]{:S(2)}, u32[]{:S(2)}) collective-permute-start(bf16[512,4096]{1,0:T(8,128)(2,1)} %refs_5_.5), channel_id=1, source_target_pairs={{0,8},{8,0},{16,24},{24,16},{32,40},{40,32},{48,56},{56,48},{64,72... | collective-permute-start | bytes 12582920 | tf_op jit(solution)/shard_map/ppermute | solution.py:49
  7.9 15.5 %copy-start.9 = (bf16[3,256,256]{2,1,0:T(8,128)(2,1)}, bf16[3,256,256]{2,1,0:T(8,128)(2,1)S(1)}, u32[]{:S(2)}) copy-start(bf16[3,256,256]{2,1,0:T(8,128)(2,1)S(1)} %pad_maximum_fusion.1.refs_0_) | copy-start | bytes 1179652
  7.9 4.9 %collective-permute-start.9 = (bf16[16,4096]{1,0:T(8,128)(2,1)S(1)}, bf16[16,4096]{1,0:T(8,128)(2,1)S(1)}, u32[]{:S(2)}, u32[]{:S(2)}) collective-permute-start(bf16[16,4096]{1,0:T(8,128)(2,1)S(1)} %slice.54), channel_id=1, source_target_pairs={{0,8},{8,0},{16,24},{24,16},{32,40},{40,32},{48,56},{56,48},{64,72... | collective-permute-start | bytes 393224 | tf_op jit(solution)/shard_map/ppermute | solution.py:49
  8.2 10.4 %collective-permute-start.1 = (bf16[3,256,256]{2,1,0:T(8,128)(2,1)S(1)}, bf16[3,256,256]{2,1,0:T(8,128)(2,1)S(1)}, u32[]{:S(2)}, u32[]{:S(2)}) collective-permute-start(bf16[3,256,256]{2,1,0:T(8,128)(2,1)S(1)} %pad_maximum_fusion.1.refs_0_), channel_id=1, source_target_pairs={{0,16},{8,24},{16,0},{24,8},{32,48},{40,56},{48,32},{56,40},{64,80... | collective-permute-start | bytes 1179656 | tf_op jit(solution)/shard_map/ppermute | solution.py:49
  8.2 11.9 %collective-permute-start.2 = (bf16[3,256,256]{2,1,0:T(8,128)(2,1)S(1)}, bf16[3,256,256]{2,1,0:T(8,128)(2,1)S(1)}, u32[]{:S(2)}, u32[]{:S(2)}) collective-permute-start(bf16[3,256,256]{2,1,0:T(8,128)(2,1)S(1)} %pad_maximum_fusion.1.refs_0_), channel_id=1, source_target_pairs={{0,64},{8,72},{16,80},{24,88},{32,96},{40,104},{48,112},{56,120},{... | collective-permute-start | bytes 1179656 | tf_op jit(solution)/shard_map/ppermute | solution.py:49
  9.3 10.9 %collective-permute-start.3 = (bf16[3,256,256]{2,1,0:T(8,128)(2,1)S(1)}, bf16[3,256,256]{2,1,0:T(8,128)(2,1)S(1)}, u32[]{:S(2)}, u32[]{:S(2)}) collective-permute-start(bf16[3,256,256]{2,1,0:T(8,128)(2,1)S(1)} %pad_maximum_fusion.1.refs_0_), channel_id=1, source_target_pairs={{0,192},{8,200},{16,208},{24,216},{32,224},{40,232},{48,240},{56,2... | collective-permute-start | bytes 1179656 | tf_op jit(solution)/shard_map/ppermute | solution.py:49
  12.8 20.8 %collective-permute-start.11 = (bf16[16,4096]{1,0:T(8,128)(2,1)S(1)}, bf16[16,4096]{1,0:T(8,128)(2,1)S(1)}, u32[]{:S(2)}, u32[]{:S(2)}) collective-permute-start(bf16[16,4096]{1,0:T(8,128)(2,1)S(1)} %broadcast_select_fusion.6), channel_id=1, source_target_pairs={{0,16},{8,24},{16,32},{24,40},{32,48},{40,56},{48,64},{56,72},{64,... | collective-permute-start | bytes 393224 | tf_op jit(solution)/shard_map/ppermute | solution.py:49
  18.5 25.8 %copy-start.10 = (bf16[3,256,256]{2,1,0:T(8,128)(2,1)}, bf16[3,256,256]{2,1,0:T(8,128)(2,1)S(1)}, u32[]{:S(2)}) copy-start(bf16[3,256,256]{2,1,0:T(8,128)(2,1)S(1)} %collective-permute-done.1.refs_0_.refs_3_) | copy-start | bytes 1179652
  18.5 21.5 %collective-permute-start.10 = (bf16[3,256,256]{2,1,0:T(8,128)(2,1)S(1)}, bf16[3,256,256]{2,1,0:T(8,128)(2,1)S(1)}, u32[]{:S(2)}, u32[]{:S(2)}) collective-permute-start(bf16[3,256,256]{2,1,0:T(8,128)(2,1)S(1)} %pad_maximum_fusion.1.refs_0_), channel_id=1, source_target_pairs={{0,32},{8,40},{16,48},{24,56},{32,0},{40,8},{48,16},{56,24},{64,96... | collective-permute-start | bytes 1179656 | tf_op jit(solution)/shard_map/ppermute | solution.py:49
  20.2 3.2 %copy-start.1 = (bf16[3,256,256]{2,1,0:T(8,128)(2,1)}, bf16[3,256,256]{2,1,0:T(8,128)(2,1)S(1)}, u32[]{:S(2)}) copy-start(bf16[3,256,256]{2,1,0:T(8,128)(2,1)S(1)} %collective-permute-done.2.right.refs_1_) | copy-start | bytes 1179652
  20.2 3.2 %copy-start.2 = (bf16[3,256,256]{2,1,0:T(8,128)(2,1)}, bf16[3,256,256]{2,1,0:T(8,128)(2,1)S(1)}, u32[]{:S(2)}) copy-start(bf16[3,256,256]{2,1,0:T(8,128)(2,1)S(1)} %collective-permute-done.3.left.refs_2_) | copy-start | bytes 1179652
  20.2 10.0 %collective-permute-start.5 = (bf16[3,256,256]{2,1,0:T(8,128)(2,1)S(1)}, bf16[3,256,256]{2,1,0:T(8,128)(2,1)S(1)}, u32[]{:S(2)}, u32[]{:S(2)}) collective-permute-start(bf16[3,256,256]{2,1,0:T(8,128)(2,1)S(1)} %collective-permute-done.1.refs_0_.refs_3_), channel_id=1, source_target_pairs={{0,64},{8,72},{16,80},{24,88},{32,96},{40,104},{48,112},{56,120},{... | collective-permute-start | bytes 1179656 | tf_op jit(solution)/shard_map/ppermute | solution.py:49
  21.5 11.9 %collective-permute-start.6 = (bf16[3,256,256]{2,1,0:T(8,128)(2,1)S(1)}, bf16[3,256,256]{2,1,0:T(8,128)(2,1)S(1)}, u32[]{:S(2)}, u32[]{:S(2)}) collective-permute-start(bf16[3,256,256]{2,1,0:T(8,128)(2,1)S(1)} %collective-permute-done.1.refs_0_.refs_3_), channel_id=1, source_target_pairs={{0,192},{8,200},{16,208},{24,216},{32,224},{40,232},{48,240},{56,2... | collective-permute-start | bytes 1179656 | tf_op jit(solution)/shard_map/ppermute | solution.py:49
  23.2 16.8 %collective-permute-start.7 = (bf16[3,128,256]{2,1,0:T(8,128)(2,1)S(1)}, bf16[3,128,256]{2,1,0:T(8,128)(2,1)S(1)}, u32[]{:S(2)}, u32[]{:S(2)}) collective-permute-start(bf16[3,128,256]{2,1,0:T(8,128)(2,1)S(1)} %get-tuple-element.68), channel_id=1, source_target_pairs={{0,64},{8,72},{16,80},{24,88},{32,96},{40,104},{48,112},{56,120},{... | collective-permute-start | bytes 589832 | tf_op jit(solution)/shard_map/ppermute | solution.py:49
  30.2 14.1 %copy-start.3 = (bf16[3,256,256]{2,1,0:T(8,128)(2,1)}, bf16[3,256,256]{2,1,0:T(8,128)(2,1)S(1)}, u32[]{:S(2)}) copy-start(bf16[3,256,256]{2,1,0:T(8,128)(2,1)S(1)} %collective-permute-done.5.right.refs_1_.refs_4_) | copy-start | bytes 1179652
  30.2 9.9 %collective-permute-start.8 = (bf16[3,128,256]{2,1,0:T(8,128)(2,1)S(1)}, bf16[3,128,256]{2,1,0:T(8,128)(2,1)S(1)}, u32[]{:S(2)}, u32[]{:S(2)}) collective-permute-start(bf16[3,128,256]{2,1,0:T(8,128)(2,1)S(1)} %get-tuple-element.69), channel_id=1, source_target_pairs={{0,192},{8,200},{16,208},{24,216},{32,224},{40,232},{48,240},{56,2... | collective-permute-start | bytes 589832 | tf_op jit(solution)/shard_map/ppermute | solution.py:49
  33.4 11.0 %copy-start.4 = (bf16[3,256,256]{2,1,0:T(8,128)(2,1)}, bf16[3,256,256]{2,1,0:T(8,128)(2,1)S(1)}, u32[]{:S(2)}) copy-start(bf16[3,256,256]{2,1,0:T(8,128)(2,1)S(1)} %collective-permute-done.6.left.refs_2_.refs_5_) | copy-start | bytes 1179652
  33.6 6.5 %collective-permute-start.12 = (bf16[3,128,256]{2,1,0:T(8,128)(2,1)S(1)}, bf16[3,128,256]{2,1,0:T(8,128)(2,1)S(1)}, u32[]{:S(2)}, u32[]{:S(2)}) collective-permute-start(bf16[3,128,256]{2,1,0:T(8,128)(2,1)S(1)} %get-tuple-element.75), channel_id=1, source_target_pairs={{0,64},{8,72},{16,80},{24,88},{32,96},{40,104},{48,112},{56,120},{... | collective-permute-start | bytes 589832 | tf_op jit(solution)/shard_map/ppermute | solution.py:49
  33.7 23.2 %copy-start.16 = (bf16[16,4096]{1,0:T(8,128)(2,1)}, bf16[16,4096]{1,0:T(8,128)(2,1)S(1)}, u32[]{:S(2)}) copy-start(bf16[16,4096]{1,0:T(8,128)(2,1)S(1)} %collective-permute-done.11.refs_13_.refs_7_) | copy-start | bytes 393220
  33.7 7.1 %collective-permute-start.13 = (bf16[3,128,256]{2,1,0:T(8,128)(2,1)S(1)}, bf16[3,128,256]{2,1,0:T(8,128)(2,1)S(1)}, u32[]{:S(2)}, u32[]{:S(2)}) collective-permute-start(bf16[3,128,256]{2,1,0:T(8,128)(2,1)S(1)} %get-tuple-element.76), channel_id=1, source_target_pairs={{0,192},{8,200},{16,208},{24,216},{32,224},{40,232},{48,240},{56,2... | collective-permute-start | bytes 589832 | tf_op jit(solution)/shard_map/ppermute | solution.py:49
  40.0 8.9 %copy-start.11 = (bf16[3,256,256]{2,1,0:T(8,128)(2,1)}, bf16[3,256,256]{2,1,0:T(8,128)(2,1)S(1)}, u32[]{:S(2)}) copy-start(bf16[3,256,256]{2,1,0:T(8,128)(2,1)S(1)} %collective-permute-done.10.refs_0_.refs_8_) | copy-start | bytes 1179652
  40.1 4.3 %copy-start.12 = (bf16[3,128,256]{2,1,0:T(8,128)(2,1)}, bf16[3,128,256]{2,1,0:T(8,128)(2,1)S(1)}, u32[]{:S(2)}) copy-start(bf16[3,128,256]{2,1,0:T(8,128)(2,1)S(1)} %collective-permute-done.7.refs_3_.refs_6_) | copy-start | bytes 589828
  40.1 4.3 %copy-start.13 = (bf16[3,128,256]{2,1,0:T(8,128)(2,1)}, bf16[3,128,256]{2,1,0:T(8,128)(2,1)S(1)}, u32[]{:S(2)}) copy-start(bf16[3,128,256]{2,1,0:T(8,128)(2,1)S(1)} %collective-permute-done.8.refs_4_.refs_7_) | copy-start | bytes 589828
  40.1 8.9 %copy-start.14 = (bf16[3,128,256]{2,1,0:T(8,128)(2,1)}, bf16[3,128,256]{2,1,0:T(8,128)(2,1)S(1)}, u32[]{:S(2)}) copy-start(bf16[3,128,256]{2,1,0:T(8,128)(2,1)S(1)} %collective-permute-done.12.refs_3_.refs_11_) | copy-start | bytes 589828
  40.8 8.2 %copy-start.15 = (bf16[3,128,256]{2,1,0:T(8,128)(2,1)}, bf16[3,128,256]{2,1,0:T(8,128)(2,1)S(1)}, u32[]{:S(2)}) copy-start(bf16[3,128,256]{2,1,0:T(8,128)(2,1)S(1)} %collective-permute-done.13.refs_4_.refs_12_) | copy-start | bytes 589828
  40.8 10.0 %collective-permute-start.14 = (bf16[3,256,256]{2,1,0:T(8,128)(2,1)S(1)}, bf16[3,256,256]{2,1,0:T(8,128)(2,1)S(1)}, u32[]{:S(2)}, u32[]{:S(2)}) collective-permute-start(bf16[3,256,256]{2,1,0:T(8,128)(2,1)S(1)} %collective-permute-done.10.refs_0_.refs_8_), channel_id=1, source_target_pairs={{0,64},{8,72},{16,80},{24,88},{32,96},{40,104},{48,112},{56,120},{... | collective-permute-start | bytes 1179656 | tf_op jit(solution)/shard_map/ppermute | solution.py:49
  41.4 9.4 %collective-permute-start.15 = (bf16[3,256,256]{2,1,0:T(8,128)(2,1)S(1)}, bf16[3,256,256]{2,1,0:T(8,128)(2,1)S(1)}, u32[]{:S(2)}, u32[]{:S(2)}) collective-permute-start(bf16[3,256,256]{2,1,0:T(8,128)(2,1)S(1)} %collective-permute-done.10.refs_0_.refs_8_), channel_id=1, source_target_pairs={{0,192},{8,200},{16,208},{24,216},{32,224},{40,232},{48,240},{56,2... | collective-permute-start | bytes 1179656 | tf_op jit(solution)/shard_map/ppermute | solution.py:49
  44.2 6.9 %collective-permute-start.16 = (bf16[3,256,256]{2,1,0:T(8,128)(2,1)S(1)}, bf16[3,256,256]{2,1,0:T(8,128)(2,1)S(1)}, u32[]{:S(2)}, u32[]{:S(2)}) collective-permute-start(bf16[3,256,256]{2,1,0:T(8,128)(2,1)S(1)} %collective-permute-done.10.refs_0_.refs_8_), channel_id=1, source_target_pairs={{0,16},{8,24},{16,0},{24,8},{32,48},{40,56},{48,32},{56,40},{64,80... | collective-permute-start | bytes 1179656 | tf_op jit(solution)/shard_map/ppermute | solution.py:49
  44.4 9.4 %copy-start.21 = (f32[512,16]{0,1:T(8,128)S(1)}, f32[512,16]{0,1:T(8,128)}, u32[]{:S(2)}) copy-start(f32[512,16]{0,1:T(8,128)} %param.9) | copy-start | bytes 98308
  44.4 9.4 %copy-start.22 = (f32[512]{0:T(512)S(1)}, f32[512]{0:T(512)}, u32[]{:S(2)}) copy-start(f32[512]{0:T(512)} %param.11) | copy-start | bytes 6148
  50.8 6.1 %copy-start.5 = (bf16[3,256,256]{2,1,0:T(8,128)(2,1)}, bf16[3,256,256]{2,1,0:T(8,128)(2,1)S(1)}, u32[]{:S(2)}) copy-start(bf16[3,256,256]{2,1,0:T(8,128)(2,1)S(1)} %collective-permute-done.14.right.refs_1_.refs_9_) | copy-start | bytes 1179652
  50.8 6.1 %copy-start.6 = (bf16[3,256,256]{2,1,0:T(8,128)(2,1)}, bf16[3,256,256]{2,1,0:T(8,128)(2,1)S(1)}, u32[]{:S(2)}) copy-start(bf16[3,256,256]{2,1,0:T(8,128)(2,1)S(1)} %collective-permute-done.15.left.refs_2_.refs_10_) | copy-start | bytes 1179652
  51.1 14.4 %copy-start.17 = (bf16[3,256,256]{2,1,0:T(8,128)(2,1)}, bf16[3,256,256]{2,1,0:T(8,128)(2,1)S(1)}, u32[]{:S(2)}) copy-start(bf16[3,256,256]{2,1,0:T(8,128)(2,1)S(1)} %collective-permute-done.16.refs_0_) | copy-start | bytes 1179652
  51.1 14.4 %collective-permute-start.17 = (bf16[3,256,256]{2,1,0:T(8,128)(2,1)S(1)}, bf16[3,256,256]{2,1,0:T(8,128)(2,1)S(1)}, u32[]{:S(2)}, u32[]{:S(2)}) collective-permute-start(bf16[3,256,256]{2,1,0:T(8,128)(2,1)S(1)} %collective-permute-done.16.refs_0_), channel_id=1, source_target_pairs={{0,64},{8,72},{16,80},{24,88},{32,96},{40,104},{48,112},{56,120},{... | collective-permute-start | bytes 1179656 | tf_op jit(solution)/shard_map/ppermute | solution.py:49
  51.5 14.1 %collective-permute-start.18 = (bf16[3,256,256]{2,1,0:T(8,128)(2,1)S(1)}, bf16[3,256,256]{2,1,0:T(8,128)(2,1)S(1)}, u32[]{:S(2)}, u32[]{:S(2)}) collective-permute-start(bf16[3,256,256]{2,1,0:T(8,128)(2,1)S(1)} %collective-permute-done.16.refs_0_), channel_id=1, source_target_pairs={{0,192},{8,200},{16,208},{24,216},{32,224},{40,232},{48,240},{56,2... | collective-permute-start | bytes 1179656 | tf_op jit(solution)/shard_map/ppermute | solution.py:49
  54.1 11.4 %collective-permute-start.19 = (bf16[3,128,256]{2,1,0:T(8,128)(2,1)S(1)}, bf16[3,128,256]{2,1,0:T(8,128)(2,1)S(1)}, u32[]{:S(2)}, u32[]{:S(2)}) collective-permute-start(bf16[3,128,256]{2,1,0:T(8,128)(2,1)S(1)} %get-tuple-element.86), channel_id=1, source_target_pairs={{0,64},{8,72},{16,80},{24,88},{32,96},{40,104},{48,112},{56,120},{... | collective-permute-start | bytes 589832 | tf_op jit(solution)/shard_map/ppermute | solution.py:49
  54.2 11.3 %collective-permute-start.20 = (bf16[3,128,256]{2,1,0:T(8,128)(2,1)S(1)}, bf16[3,128,256]{2,1,0:T(8,128)(2,1)S(1)}, u32[]{:S(2)}, u32[]{:S(2)}) collective-permute-start(bf16[3,128,256]{2,1,0:T(8,128)(2,1)S(1)} %get-tuple-element.87), channel_id=1, source_target_pairs={{0,192},{8,200},{16,208},{24,216},{32,224},{40,232},{48,240},{56,2... | collective-permute-start | bytes 589832 | tf_op jit(solution)/shard_map/ppermute | solution.py:49
  65.5 3.0 %copy-start.18 = (bf16[3,128,256]{2,1,0:T(8,128)(2,1)}, bf16[3,128,256]{2,1,0:T(8,128)(2,1)S(1)}, u32[]{:S(2)}) copy-start(bf16[3,128,256]{2,1,0:T(8,128)(2,1)S(1)} %collective-permute-done.19.refs_3_) | copy-start | bytes 589828
  65.5 3.0 %copy-start.19 = (bf16[3,128,256]{2,1,0:T(8,128)(2,1)}, bf16[3,128,256]{2,1,0:T(8,128)(2,1)S(1)}, u32[]{:S(2)}) copy-start(bf16[3,128,256]{2,1,0:T(8,128)(2,1)S(1)} %collective-permute-done.20.refs_4_) | copy-start | bytes 589828
  65.5 3.0 %copy-start.7 = (bf16[3,256,256]{2,1,0:T(8,128)(2,1)}, bf16[3,256,256]{2,1,0:T(8,128)(2,1)S(1)}, u32[]{:S(2)}) copy-start(bf16[3,256,256]{2,1,0:T(8,128)(2,1)S(1)} %collective-permute-done.17.refs_1_.right) | copy-start | bytes 1179652
  65.5 3.0 %copy-start.8 = (bf16[3,256,256]{2,1,0:T(8,128)(2,1)}, bf16[3,256,256]{2,1,0:T(8,128)(2,1)S(1)}, u32[]{:S(2)}) copy-start(bf16[3,256,256]{2,1,0:T(8,128)(2,1)S(1)} %collective-permute-done.18.refs_2_.left) | copy-start | bytes 1179652
  65.7 7.5 %collective-permute-start.21 = (bf16[3,128,256]{2,1,0:T(8,128)(2,1)S(1)}, bf16[3,128,256]{2,1,0:T(8,128)(2,1)S(1)}, u32[]{:S(2)}, u32[]{:S(2)}) collective-permute-start(bf16[3,128,256]{2,1,0:T(8,128)(2,1)S(1)} %get-tuple-element.103), channel_id=1, source_target_pairs={{0,64},{8,72},{16,80},{24,88},{32,96},{40,104},{48,112},{56,120},{... | collective-permute-start | bytes 589832 | tf_op jit(solution)/shard_map/ppermute | solution.py:49
  65.8 7.4 %collective-permute-start.22 = (bf16[3,128,256]{2,1,0:T(8,128)(2,1)S(1)}, bf16[3,128,256]{2,1,0:T(8,128)(2,1)S(1)}, u32[]{:S(2)}, u32[]{:S(2)}) collective-permute-start(bf16[3,128,256]{2,1,0:T(8,128)(2,1)S(1)} %get-tuple-element.104), channel_id=1, source_target_pairs={{0,192},{8,200},{16,208},{24,216},{32,224},{40,232},{48,240},{56,2... | collective-permute-start | bytes 589832 | tf_op jit(solution)/shard_map/ppermute | solution.py:49
  77.4 4.5 %collective-permute-start.23 = (f32[16,256]{1,0:T(8,128)S(1)}, f32[16,256]{1,0:T(8,128)S(1)}, u32[]{:S(2)}, u32[]{:S(2)}) collective-permute-start(f32[16,256]{1,0:T(8,128)S(1)} %get-tuple-element.117), channel_id=1, source_target_pairs={{0,16},{8,24},{16,32},{24,40},{32,48},{40,56},{48,0},{56,8},{64,80... | collective-permute-start | bytes 49160 | tf_op jit(solution)/shard_map/ppermute | solution.py:49
  77.5 4.4 %collective-permute-start.24 = (f32[16,256]{1,0:T(8,128)S(1)}, f32[16,256]{1,0:T(8,128)S(1)}, u32[]{:S(2)}, u32[]{:S(2)}) collective-permute-start(f32[16,256]{1,0:T(8,128)S(1)} %get-tuple-element.117), channel_id=1, source_target_pairs={{0,32},{8,40},{16,48},{24,56},{32,0},{40,8},{48,16},{56,24},{64,96... | collective-permute-start | bytes 49160 | tf_op jit(solution)/shard_map/ppermute | solution.py:49
  77.9 4.3 %collective-permute-start.25 = (f32[16,256]{1,0:T(8,128)S(1)}, f32[16,256]{1,0:T(8,128)S(1)}, u32[]{:S(2)}, u32[]{:S(2)}) collective-permute-start(f32[16,256]{1,0:T(8,128)S(1)} %get-tuple-element.117), channel_id=1, source_target_pairs={{0,48},{8,56},{16,0},{24,8},{32,16},{40,24},{48,32},{56,40},{64,11... | collective-permute-start | bytes 49160 | tf_op jit(solution)/shard_map/ppermute | solution.py:49
  82.2 3.9 %collective-permute-start.26 = (f32[16,256]{1,0:T(8,128)S(1)}, f32[16,256]{1,0:T(8,128)S(1)}, u32[]{:S(2)}, u32[]{:S(2)}) collective-permute-start(f32[16,256]{1,0:T(8,128)S(1)} %fusion.2), channel_id=1, source_target_pairs={{0,64},{8,72},{16,80},{24,88},{32,96},{40,104},{48,112},{56,120},{... | collective-permute-start | bytes 49160 | tf_op jit(solution)/shard_map/ppermute | solution.py:49
  82.3 4.2 %collective-permute-start.27 = (f32[16,256]{1,0:T(8,128)S(1)}, f32[16,256]{1,0:T(8,128)S(1)}, u32[]{:S(2)}, u32[]{:S(2)}) collective-permute-start(f32[16,256]{1,0:T(8,128)S(1)} %fusion.2), channel_id=1, source_target_pairs={{0,128},{8,136},{16,144},{24,152},{32,160},{40,168},{48,176},{56,1... | collective-permute-start | bytes 49160 | tf_op jit(solution)/shard_map/ppermute | solution.py:49
  84.4 2.6 %collective-permute-start.28 = (f32[16,256]{1,0:T(8,128)S(1)}, f32[16,256]{1,0:T(8,128)S(1)}, u32[]{:S(2)}, u32[]{:S(2)}) collective-permute-start(f32[16,256]{1,0:T(8,128)S(1)} %fusion.2), channel_id=1, source_target_pairs={{0,192},{8,200},{16,208},{24,216},{32,224},{40,232},{48,240},{56,2... | collective-permute-start | bytes 49160 | tf_op jit(solution)/shard_map/ppermute | solution.py:49
  88.9 13.2 %collective-permute-start.29 = (bf16[512,256]{1,0:T(8,128)(2,1)S(1)}, bf16[512,256]{1,0:T(8,128)(2,1)S(1)}, u32[]{:S(2)}, u32[]{:S(2)}) collective-permute-start(bf16[512,256]{1,0:T(8,128)(2,1)S(1)} %get-tuple-element.120), channel_id=1, source_target_pairs={{0,8},{8,0},{16,24},{24,16},{32,40},{40,32},{48,56},{56,48},{64,72... | collective-permute-start | bytes 786440 | tf_op jit(solution)/shard_map/ppermute | solution.py:49

commit v5 on v4

--- a/solution.py
+++ b/solution.py
@@ -108,11 +108,11 @@
     return along_x(block, 1), along_x(block, 3)
 
 
-def with_sides(z_mask, block, right, left):
+def with_sides(z_mask, block, *both_sides):
     height = block.shape[1]
     return [
         (x_steps, z_mask, 0, array, 0, height)
-        for x_steps, array in ((0, block), (1, right), (3, left))
+        for x_steps, array in zip((0, 1, 3), (block, *both_sides))
     ]
 
 
@@ -163,19 +163,27 @@
     return copies
 
 
-def columns_to(rows, where, x_steps, z_mask, mine, other, halo, sems):
+def columns_to(rows, where, chips, mine, other, halo, sems):
     x, z, core = where[0], where[1], where[2]
-    length, width = mine.shape[0], rows.shape[1]
-    chip = (x - x_steps + X) % X * Z + (z ^ z_mask)
-    span = pl.ds(pl.multiple_of(chip * width, LANES), width)
-    copies = [pltpu.make_async_copy(halo.at[:, span], rows.at[pl.ds(0, HALO), :], sems.at[0])]
-    for sem, array, block in ((1, mine, core), (2, other, 1 - core)):
-        first = pl.multiple_of(HALO + block * length, HALO)
-        copies.append(
-            pltpu.make_async_copy(
-                array.at[:, span], rows.at[pl.ds(first, length), :], sems.at[sem]
+    length, width = mine.shape[0], 2 * LANES
+    copies = []
+    for at, (x_steps, z_mask) in enumerate(chips):
+        chip = (x - x_steps + X) % X * Z + (z ^ z_mask)
+        span = pl.ds(pl.multiple_of(chip * width, LANES), width)
+        into = pl.ds(at * width, width)
+        for sem, array, first in (
+            (0, halo, 0),
+            (1, mine, HALO + core * length),
+            (2, other, HALO + (1 - core) * length),
+        ):
+            first = first if sem == 0 else pl.multiple_of(first, HALO)
+            copies.append(
+                pltpu.make_async_copy(
+                    array.at[:, span],
+                    rows.at[pl.ds(first, array.shape[0]), into],
+                    sems.at[at, sem],
+                )
             )
-        )
     for copy in copies:
         copy.start()
     return copies
@@ -231,7 +239,7 @@
     rows, weights, sems, kept_sems = refs
     copies = start_copies(plan, ALL, where, pieces, mine, other, halo, rows, weights, sems)
     kept_copies = (
-        columns_to(kept, where, *kept_from, mine, other, halo, kept_sems) if kept_from else []
+        columns_to(kept, where, kept_from, mine, other, halo, kept_sems) if kept_from else []
     )
 
     def finish(stream, group, share):
@@ -269,7 +277,7 @@
         pltpu.VMEM((rows, depth), jnp.bfloat16),
         pltpu.VMEM((streams.size, depth, channels), jnp.bfloat16),
         pltpu.SemaphoreType.DMA((len(plan), 4)),
-        pltpu.SemaphoreType.DMA((3,)),
+        pltpu.SemaphoreType.DMA((3, 3)),
     ]
 
 
@@ -282,7 +290,7 @@
         pltpu.VMEM((ALL.size, channels // LANES, height, LANES), jnp.float32) for height in heights
     ]
     if kept_from:
-        shapes.append(pltpu.VMEM((sum(heights), 2 * LANES), jnp.bfloat16))
+        shapes.append(pltpu.VMEM((sum(heights), len(kept_from) * 2 * LANES), jnp.bfloat16))
     inputs = [*arrays, *tokens, *halo]
     return pl.pallas_call(
         functools.partial(
@@ -297,33 +305,21 @@
     )(where, *in_hbm(*inputs), *in_vmem(*before))
 
 
-def last_weights(upper, lower, streams):
+def last_weights(last, streams):
     return [
-        jnp.concatenate([upper[stream], lower[stream]], axis=0)
+        jnp.concatenate([array[stream] for array in last], axis=0)
         for stream in range(streams.start, streams.start + streams.size)
     ]
 
 
-def signal_kernel(
-    rows,
-    upper,
-    lower,
-    products,
-    halo_products,
-    taps,
-    decay,
-    amplitude,
-    power,
-    skip,
-    signal,
-    before,
-    ends,
-    projected,
-):
-    channels = upper.shape[2]
+def signal_kernel(count, rows, *refs):
+    last, refs = refs[:count], refs[count:]
+    products, halo_products, taps, decay, amplitude, power, skip = refs[:7]
+    signal, before, ends, projected = refs[7:]
+    channels = last[0].shape[2]
     steps = signal.shape[0]
     finish, load = segmented(projected, products, halo_products, KEY_VALUE.start)
-    multiply(rows, last_weights(upper, lower, KEY_VALUE), finish)
+    multiply(rows, last_weights(last, KEY_VALUE), finish)
     for low in range(0, channels, LANES):
         lanes = pl.ds(low, LANES)
         group = low // LANES
@@ -388,13 +384,13 @@
     modes, channels = decay.shape
     length = rows.shape[0] - HALO
     return pl.pallas_call(
-        signal_kernel,
+        functools.partial(signal_kernel, len(last)),
         out_shape=(
             pltpu.VMEM((length // SEGMENTS, SEGMENTS, channels), jnp.float32),
             pltpu.VMEM((modes, SEGMENTS, channels), jnp.float32),
             jax.ShapeDtypeStruct((modes, channels), jnp.float32),
         ),
-        in_specs=[VMEM] * 10,
+        in_specs=[VMEM] * (len(last) + 8),
         out_specs=(VMEM,) * 3,
         scratch_shapes=[segment_scratch(KEY_VALUE, length, channels)],
         compiler_params=pltpu.CompilerParams(vmem_limit_bytes=8 * 1024 * 1024),
@@ -402,13 +398,13 @@
     )(*in_vmem(rows, *last, *products), taps, decay, amplitude, power, skip)
 
 
-def query_kernel(
-    rows, upper, lower, products, halo_products, conv, taps, query, gated, projected
-):
-    channels = upper.shape[2]
+def query_kernel(count, rows, *refs):
+    last, refs = refs[:count], refs[count:]
+    products, halo_products, conv, taps, query, gated, projected = refs
+    channels = last[0].shape[2]
     steps = conv.shape[0]
     finish, load = segmented(projected, products, halo_products, QUERY.start)
-    multiply(rows, last_weights(upper, lower, QUERY), finish)
+    multiply(rows, last_weights(last, QUERY), finish)
     for group in range(channels // LANES):
         lanes = pl.ds(group * LANES, LANES)
         spread = [
@@ -432,9 +428,9 @@
 def queries(rows, last, products, conv, taps):
     steps, _, channels = conv.shape
     return pl.pallas_call(
-        query_kernel,
+        functools.partial(query_kernel, len(last)),
         out_shape=(pltpu.VMEM(conv.shape, jnp.float32),) * 2,
-        in_specs=[VMEM] * 7,
+        in_specs=[VMEM] * (len(last) + 5),
         out_specs=(VMEM,) * 2,
         scratch_shapes=[segment_scratch(QUERY, steps * SEGMENTS, channels)],
         compiler_params=pltpu.CompilerParams(vmem_limit_bytes=8 * 1024 * 1024),
@@ -588,38 +584,45 @@
 
     far = forwards(right, left)
     pieces = with_sides(0, block, right, left)
-    products = partial_products(where, pieces, both, (), (), "first")
+    products = partial_products(where, pieces, both, (halo,), (), "first")
     right, left = sides(beside)
-    far_beside = forwards(right, left)
-    right, left, *far, over, products, halo, far_right, far_left = together(
-        right, left, *far, over, *products, halo, *far_beside
-    )
-    so_far = pieces
+    right, left, *far, over, products, halo_products = together(
+        right, left, *far, over, *products
+    )
 
     opposite = across_z(over, 1)
+    far_beside = across_z(far[0], 1), across_z(far[1], 1)
     pieces = with_sides(1, beside, right, left) + with_far(0, *far)
-    products = partial_products(where, pieces, both, (), (products,), "second")
-    so_far += pieces
+    products = partial_products(
+        where, pieces, both, (halo,), (products, halo_products), "second"
+    )
     right, left = sides(over)
-    right, left, opposite, products = together(right, left, opposite, *products)
-
-    pieces = with_sides(2, over, right, left) + with_far(1, far_right, far_left)
-    products = partial_products(where, pieces, both, (), (products,), "third")
-    so_far += pieces
-    halo_products = partial_products(where, so_far, (), (halo,), (), "halo")
+    right, left, products, halo_products = together(right, left, *products)
+
     far = forwards(right, left)
+    pieces = with_sides(2, over, right, left)
+    products = partial_products(where, pieces, both, (halo,), (products, halo_products), "third")
+    far_right, far_left, opposite, *far_beside, products, halo_products = together(
+        *far, opposite, *far_beside, *products
+    )
+
     right, left = sides(opposite)
+    far_opposite = across_z(far_right, 1), across_z(far_left, 1)
+    pieces = with_sides(3, opposite) + with_far(1, *far_beside) + with_far(2, far_right, far_left)
+    *products, rows = partial_products(
+        where,
+        pieces,
+        both,
+        (halo,),
+        (products, halo_products),
+        "fourth",
+        ((1, 3), (3, 3), (2, 3)),
+    )
     small = (power, start_power, factors, decay, amplitude, taps, direct)
-    right, left, far_right, far_left, products, halo_products, *small = together(
-        right, left, *far, *products, *halo_products, *small
-    )
-    power, start_power, factors, decay, amplitude, taps, direct = small
-
-    pieces = with_sides(3, opposite, right, left) + with_far(2, far_right, far_left)
-    last = forwards(right, left)
-    *products, rows = partial_products(
-        where, pieces, both, (halo,), (products, halo_products), "fourth", (2, 3)
-    )
+    *last, products, halo_products, rows, power, start_power, factors, decay, amplitude, taps, direct = (
+        together(right, left, *far_opposite, *products, rows, *small)
+    )
+    products = products, halo_products
 
     conv, before, ends = signals(
         rows, last, products, taps, decay, amplitude, power, direct

time: 103 us -> 97.3 us (0.945)
  starting transfers between devices: 48.6 us -> 39.9 us
  waiting for transfers between devices: 19.9 us -> 26.7 us
  Pallas kernels: 29.4 us -> 25.4 us
    ppermute x30, starting transfers between devices: 48.6 us -> 39.9 us  [permute(): return lax.ppermute(value, 'seq', pairs)]
    ppermute x30, waiting for transfers between devices: 19.9 us -> 26.7 us  [permute(): return lax.ppermute(value, 'seq', pairs)]
    pallas_call x5 -> x4, Pallas kernels: 21.6 us -> 17 us  [partial_products(): pl.pallas_call(functools.partial(partial_kernel, plan, bool(tokens), bool...]
  transfers between devices with their start and end apart: 30 -> 30, of which waited for: 14 -> 12; matrix products, arithmetic and copies ran while one was open for 2% -> 3% of each run, Pallas kernels for 23% -> 19%
where the time goes in v5:
time: 97.3 us; the launch traced here: 97 us
  starting transfers between devices  39.9 us (41%)
  waiting for transfers between devices  26.7 us (27%)
  Pallas kernels  25.4 us (26%)
  other arithmetic  3.41 us (4%)
  local copies, waits for them, and re-layouts  1.09 us (1%)
    ppermute x30, starting transfers between devices, permute(): return lax.ppermute(value, 'seq', pairs)  39.9 us
    ppermute x30, waiting for transfers between devices, permute(): return lax.ppermute(value, 'seq', pairs)  26.7 us
    pallas_call x4, Pallas kernels, partial_products(): pl.pallas_call(functools.partial(partial_kernel, plan, bool(tokens), bool...  17 us
    pallas_call x1, Pallas kernels, signals(): pl.pallas_call(functools.partial(signal_kernel, len(last)), out_shape=(pl...  4.74 us
  transfers between devices with their start and end apart: 30, of which 12 were waited for; matrix products, arithmetic and copies ran while one was open for 3% of the time, Pallas kernels for 19%

profile of v5, /device:TPU:1, one launch (start us, length us, event | category | flops | bytes accessed | tf_op | source)
XLA Modules:
  0.0 97.0 jit_solution(8098540991378678857)
XLA Ops:
  0.0 1.1 %broadcast_select_fusion.4 = bf16[3,128,256]{2,1,0:T(8,128)(2,1)S(1)} fusion(pred[]{:T(512)S(6)} %eq.6, bf16[3,128,512]{2,1,0:T(8,128)(2,1)} %param.7), kind=kLoop, calls=%fused_computation.6 | loop fusion | flops 98304 | bytes 589825 | tf_op jit(solution)/shard_map/jit(_where)/select_n | solution.py:556
  1.1 3.3 %collective-permute-start = (bf16[3,128,256]{2,1,0:T(8,128)(2,1)S(1)}, bf16[3,128,256]{2,1,0:T(8,128)(2,1)S(1)}, u32[]{:S(2)}, u32[]{:S(2)}) collective-permute-start(bf16[3,128,256]{2,1,0:T(8,128)(2,1)S(1)} %broadcast_select_fusion.4), channel_id=1, source_target_pairs={{0,8},{8,0},{16,24},{24,16},{32,40},{40,32},{48,56},{56,48},{64,72... | collective-permute-start | bytes 589832 | tf_op jit(solution)/shard_map/ppermute | solution.py:49
  4.4 1.1 %collective-permute-done = bf16[3,128,256]{2,1,0:T(8,128)(2,1)S(1)} collective-permute-done((bf16[3,128,256]{2,1,0:T(8,128)(2,1)S(1)}, bf16[3,128,256]{2,1,0:T(8,128)(2,1)S(1)}, u32[]{:S(2)}, u32[]{:S(2)}) %collective-permute-start) | collective-permute-done | bytes 196640 | tf_op jit(solution)/shard_map/ppermute | solution.py:49
  5.5 0.4 collective-permute-start.4
  5.8 0.9 slice.54
  6.8 1.1 %broadcast_select_fusion.3 = (bf16[3,128,256]{2,1,0:T(8,128)(2,1)S(1)}, bf16[3,128,256]{2,1,0:T(8,128)(2,1)S(1)}) fusion(bf16[3,128,256]{2,1,0:T(8,128)(2,1)S(1)} %collective-permute-done, pred[]{:T(512)S(6)} %eq.6, bf16[3,128,512]{2,1,0:T(8,128)(2,1)} %param.7), kind=kLoop, calls=%fused_computation.5 | loop fusion | flops 294912 | bytes 983041 | tf_op jit(solution)/shard_map/jit(_where)/select_n | solution.py:558
  7.9 0.0 copy-start.6
  7.9 0.2 collective-permute-start.9
  8.1 0.1 pad_add_fusion.where
  8.2 0.0 collective-permute-start.1
  8.2 1.1 %collective-permute-start.2 = (bf16[3,256,256]{2,1,0:T(8,128)(2,1)S(1)}, bf16[3,256,256]{2,1,0:T(8,128)(2,1)S(1)}, u32[]{:S(2)}, u32[]{:S(2)}) collective-permute-start(bf16[3,256,256]{2,1,0:T(8,128)(2,1)S(1)} %pad_maximum_fusion.1.refs_0_), channel_id=1, source_target_pairs={{0,64},{8,72},{16,80},{24,88},{32,96},{40,104},{48,112},{56,120},{... | collective-permute-start | bytes 1179656 | tf_op jit(solution)/shard_map/ppermute | solution.py:49
  9.3 1.7 %collective-permute-start.3 = (bf16[3,256,256]{2,1,0:T(8,128)(2,1)S(1)}, bf16[3,256,256]{2,1,0:T(8,128)(2,1)S(1)}, u32[]{:S(2)}, u32[]{:S(2)}) collective-permute-start(bf16[3,256,256]{2,1,0:T(8,128)(2,1)S(1)} %pad_maximum_fusion.1.refs_0_), channel_id=1, source_target_pairs={{0,192},{8,200},{16,208},{24,216},{32,224},{40,232},{48,240},{56,2... | collective-permute-start | bytes 1179656 | tf_op jit(solution)/shard_map/ppermute | solution.py:49
  11.0 1.8 %collective-permute-done.9 = bf16[16,4096]{1,0:T(8,128)(2,1)S(1)} collective-permute-done((bf16[16,4096]{1,0:T(8,128)(2,1)S(1)}, bf16[16,4096]{1,0:T(8,128)(2,1)S(1)}, u32[]{:S(2)}, u32[]{:S(2)}) %collective-permute-start.9) | collective-permute-done | bytes 131104 | tf_op jit(solution)/shard_map/ppermute | solution.py:49
  12.8 1.8 %collective-permute-start.11 = (bf16[16,4096]{1,0:T(8,128)(2,1)S(1)}, bf16[16,4096]{1,0:T(8,128)(2,1)S(1)}, u32[]{:S(2)}, u32[]{:S(2)}) collective-permute-start(bf16[16,4096]{1,0:T(8,128)(2,1)S(1)} %broadcast_select_fusion.6), channel_id=1, source_target_pairs={{0,16},{8,24},{16,32},{24,40},{32,48},{40,56},{48,64},{56,72},{64,... | collective-permute-start | bytes 393224 | tf_op jit(solution)/shard_map/ppermute | solution.py:49
  14.7 3.9 %collective-permute-done.1.refs_0_ = bf16[3,256,256]{2,1,0:T(8,128)(2,1)S(1)} collective-permute-done((bf16[3,256,256]{2,1,0:T(8,128)(2,1)S(1)}, bf16[3,256,256]{2,1,0:T(8,128)(2,1)S(1)}, u32[]{:S(2)}, u32[]{:S(2)}) %collective-permute-start.1) | collective-permute-done | bytes 393248 | tf_op jit(solution)/shard_map/ppermute | solution.py:49
  18.5 1.6 %collective-permute-start.10 = (bf16[3,256,256]{2,1,0:T(8,128)(2,1)S(1)}, bf16[3,256,256]{2,1,0:T(8,128)(2,1)S(1)}, u32[]{:S(2)}, u32[]{:S(2)}) collective-permute-start(bf16[3,256,256]{2,1,0:T(8,128)(2,1)S(1)} %pad_maximum_fusion.1.refs_0_), channel_id=1, source_target_pairs={{0,32},{8,40},{16,48},{24,56},{32,0},{40,8},{48,16},{56,24},{64,96... | collective-permute-start | bytes 1179656 | tf_op jit(solution)/shard_map/ppermute | solution.py:49
  20.2 0.0 collective-permute-done.2.right.refs_1_
  20.2 0.0 collective-permute-done.3.left.refs_2_
  20.2 1.3 %collective-permute-start.5 = (bf16[3,256,256]{2,1,0:T(8,128)(2,1)S(1)}, bf16[3,256,256]{2,1,0:T(8,128)(2,1)S(1)}, u32[]{:S(2)}, u32[]{:S(2)}) collective-permute-start(bf16[3,256,256]{2,1,0:T(8,128)(2,1)S(1)} %collective-permute-done.1.refs_0_), channel_id=1, source_target_pairs={{0,64},{8,72},{16,80},{24,88},{32,96},{40,104},{48,112},{56,120},{... | collective-permute-start | bytes 1179656 | tf_op jit(solution)/shard_map/ppermute | solution.py:49
  21.5 1.5 %collective-permute-start.6 = (bf16[3,256,256]{2,1,0:T(8,128)(2,1)S(1)}, bf16[3,256,256]{2,1,0:T(8,128)(2,1)S(1)}, u32[]{:S(2)}, u32[]{:S(2)}) collective-permute-start(bf16[3,256,256]{2,1,0:T(8,128)(2,1)S(1)} %collective-permute-done.1.refs_0_), channel_id=1, source_target_pairs={{0,192},{8,200},{16,208},{24,216},{32,224},{40,232},{48,240},{56,2... | collective-permute-start | bytes 1179656 | tf_op jit(solution)/shard_map/ppermute | solution.py:49
  23.0 0.2 halves.2
  23.2 0.1 collective-permute-start.7
  23.3 0.1 multiply_exponential_fusion.power
  23.4 0.0 collective-permute-done.11.refs_5_.refs_7_
  23.5 2.7 %collective-permute-start.8 = (bf16[3,128,256]{2,1,0:T(8,128)(2,1)S(1)}, bf16[3,128,256]{2,1,0:T(8,128)(2,1)S(1)}, u32[]{:S(2)}, u32[]{:S(2)}) collective-permute-start(bf16[3,128,256]{2,1,0:T(8,128)(2,1)S(1)} %get-tuple-element.77), channel_id=1, source_target_pairs={{0,192},{8,200},{16,208},{24,216},{32,224},{40,232},{48,240},{56,2... | collective-permute-start | bytes 589832 | tf_op jit(solution)/shard_map/ppermute | solution.py:49
  26.2 3.9 %first.1 = (f32[3,2,1024,128]{3,2,1,0:T(8,128)S(1)}, f32[3,2,16,128]{3,2,1,0:T(8,128)S(1)}) custom-call(s32[3]{0:T(128)S(1)} %pad_add_fusion.where, bf16[3,256,256]{2,1,0:T(8,128)(2,1)} %copy-done.6, bf16[3,256,256]{2,1,0:T(8,128)(2,1)} %copy-done.1, bf16[3,256,256]{2,1,0:T(8,128)(2,1)} %copy-done.2, bf16[512,4096]{1,0:T(8,128)(2,1)} %refs_5_.3, ...), custom_call_target="tpu_custom_call" | custom-call | tf_op jit(solution)/shard_map/first/pallas_call | solution.py:295
  30.2 9.9 %collective-permute-done.10.refs_0_ = bf16[3,256,256]{2,1,0:T(8,128)(2,1)S(1)} collective-permute-done((bf16[3,256,256]{2,1,0:T(8,128)(2,1)S(1)}, bf16[3,256,256]{2,1,0:T(8,128)(2,1)S(1)}, u32[]{:S(2)}, u32[]{:S(2)}) %collective-permute-start.10) | collective-permute-done | bytes 393248 | tf_op jit(solution)/shard_map/ppermute | solution.py:49
  40.1 1.3 %collective-permute-start.12 = (bf16[3,256,256]{2,1,0:T(8,128)(2,1)S(1)}, bf16[3,256,256]{2,1,0:T(8,128)(2,1)S(1)}, u32[]{:S(2)}, u32[]{:S(2)}) collective-permute-start(bf16[3,256,256]{2,1,0:T(8,128)(2,1)S(1)} %collective-permute-done.10.refs_0_), channel_id=1, source_target_pairs={{0,64},{8,72},{16,80},{24,88},{32,96},{40,104},{48,112},{56,120},{... | collective-permute-start | bytes 1179656 | tf_op jit(solution)/shard_map/ppermute | solution.py:49
  41.4 1.5 %collective-permute-start.13 = (bf16[3,256,256]{2,1,0:T(8,128)(2,1)S(1)}, bf16[3,256,256]{2,1,0:T(8,128)(2,1)S(1)}, u32[]{:S(2)}, u32[]{:S(2)}) collective-permute-start(bf16[3,256,256]{2,1,0:T(8,128)(2,1)S(1)} %collective-permute-done.10.refs_0_), channel_id=1, source_target_pairs={{0,192},{8,200},{16,208},{24,216},{32,224},{40,232},{48,240},{56,2... | collective-permute-start | bytes 1179656 | tf_op jit(solution)/shard_map/ppermute | solution.py:49
  42.9 0.1 collective-permute-start.16
  43.0 1.5 %collective-permute-start.17 = (bf16[3,128,256]{2,1,0:T(8,128)(2,1)S(1)}, bf16[3,128,256]{2,1,0:T(8,128)(2,1)S(1)}, u32[]{:S(2)}, u32[]{:S(2)}) collective-permute-start(bf16[3,128,256]{2,1,0:T(8,128)(2,1)S(1)} %collective-permute-done.7.refs_3_), channel_id=1, source_target_pairs={{0,16},{8,24},{16,0},{24,8},{32,48},{40,56},{48,32},{56,40},{64,80... | collective-permute-start | bytes 589832 | tf_op jit(solution)/shard_map/ppermute | solution.py:49
  44.6 0.3 collective-permute-start.18
  44.9 4.7 %second.1 = (f32[3,2,1024,128]{3,2,1,0:T(8,128)S(1)}, f32[3,2,16,128]{3,2,1,0:T(8,128)S(1)}) custom-call(s32[3]{0:T(128)S(1)} %pad_add_fusion.where, bf16[3,256,256]{2,1,0:T(8,128)(2,1)} %copy-done.8, bf16[3,256,256]{2,1,0:T(8,128)(2,1)} %copy-done.10, bf16[3,256,256]{2,1,0:T(8,128)(2,1)} %copy-done.11, bf16[3,128,256]{2,1,0:T(8,128)(2,1)} %copy-done.12, ...), custom_call_target="tpu_custom_call" | custom-call | tf_op jit(solution)/shard_map/second/pallas_call | solution.py:295
  49.6 2.0 %collective-permute-done.12.right.refs_1_ = bf16[3,256,256]{2,1,0:T(8,128)(2,1)S(1)} collective-permute-done((bf16[3,256,256]{2,1,0:T(8,128)(2,1)S(1)}, bf16[3,256,256]{2,1,0:T(8,128)(2,1)S(1)}, u32[]{:S(2)}, u32[]{:S(2)}) %collective-permute-start.12) | collective-permute-done | bytes 393248 | tf_op jit(solution)/shard_map/ppermute | solution.py:49
  51.6 0.2 halves.3
  51.8 1.0 collective-permute-start.14
  52.8 1.8 %collective-permute-start.15 = (bf16[3,128,256]{2,1,0:T(8,128)(2,1)S(1)}, bf16[3,128,256]{2,1,0:T(8,128)(2,1)S(1)}, u32[]{:S(2)}, u32[]{:S(2)}) collective-permute-start(bf16[3,128,256]{2,1,0:T(8,128)(2,1)S(1)} %get-tuple-element.97), channel_id=1, source_target_pairs={{0,192},{8,200},{16,208},{24,216},{32,224},{40,232},{48,240},{56,2... | collective-permute-start | bytes 589832 | tf_op jit(solution)/shard_map/ppermute | solution.py:49
  54.6 0.0 copy-start.19
  54.6 0.0 copy-start.20
  54.6 4.0 %third.1 = (f32[3,2,1024,128]{3,2,1,0:T(8,128)S(1)}, f32[3,2,16,128]{3,2,1,0:T(8,128)S(1)}) custom-call(s32[3]{0:T(128)S(1)} %pad_add_fusion.where, bf16[3,256,256]{2,1,0:T(8,128)(2,1)} %copy-done.7, bf16[3,256,256]{2,1,0:T(8,128)(2,1)} %copy-done.3, bf16[3,256,256]{2,1,0:T(8,128)(2,1)} %copy-done.4, bf16[512,4096]{1,0:T(8,128)(2,1)} %refs_5_.3, ...), custom_call_target="tpu_custom_call" | custom-call | tf_op jit(solution)/shard_map/third/pallas_call | solution.py:295
  58.6 2.4 %collective-permute-done.18.refs_2_ = bf16[3,128,256]{2,1,0:T(8,128)(2,1)S(1)} collective-permute-done((bf16[3,128,256]{2,1,0:T(8,128)(2,1)S(1)}, bf16[3,128,256]{2,1,0:T(8,128)(2,1)S(1)}, u32[]{:S(2)}, u32[]{:S(2)}) %collective-permute-start.18) | collective-permute-done | bytes 196640 | tf_op jit(solution)/shard_map/ppermute | solution.py:49
  61.0 0.1 collective-permute-start.19
  61.1 2.7 %collective-permute-start.20 = (bf16[3,256,256]{2,1,0:T(8,128)(2,1)S(1)}, bf16[3,256,256]{2,1,0:T(8,128)(2,1)S(1)}, u32[]{:S(2)}, u32[]{:S(2)}) collective-permute-start(bf16[3,256,256]{2,1,0:T(8,128)(2,1)S(1)} %collective-permute-done.16.refs_0_), channel_id=1, source_target_pairs={{0,192},{8,200},{16,208},{24,216},{32,224},{40,232},{48,240},{56,2... | collective-permute-start | bytes 1179656 | tf_op jit(solution)/shard_map/ppermute | solution.py:49
  63.8 0.1 dynamic_slice.15
  63.9 0.4 collective-permute-start.21
  64.2 1.1 %collective-permute-start.22 = (bf16[3,128,256]{2,1,0:T(8,128)(2,1)S(1)}, bf16[3,128,256]{2,1,0:T(8,128)(2,1)S(1)}, u32[]{:S(2)}, u32[]{:S(2)}) collective-permute-start(bf16[3,128,256]{2,1,0:T(8,128)(2,1)S(1)} %collective-permute-done.15.refs_4_), channel_id=1, source_target_pairs={{0,16},{8,24},{16,0},{24,8},{32,48},{40,56},{48,32},{56,40},{64,80... | collective-permute-start | bytes 589832 | tf_op jit(solution)/shard_map/ppermute | solution.py:49
  65.4 4.5 %fourth.1 = (f32[3,2,1024,128]{3,2,1,0:T(8,128)S(1)}, f32[3,2,16,128]{3,2,1,0:T(8,128)S(1)}, bf16[1040,768]{1,0:T(8,128)(2,1)S(1)}) custom-call(s32[3]{0:T(128)S(1)} %pad_add_fusion.where, bf16[3,256,256]{2,1,0:T(8,128)(2,1)} %copy-done.9, bf16[3,128,256]{2,1,0:T(8,128)(2,1)} %copy-done.14, bf16[3,128,256]{2,1,0:T(8,128)(2,1)} %copy-done.15, ...), custom_call_target="tpu_custom_call" | custom-call | tf_op jit(solution)/shard_map/fourth/pallas_call | solution.py:295
  69.9 2.1 %collective-permute-done.22.refs_3_ = bf16[3,128,256]{2,1,0:T(8,128)(2,1)S(1)} collective-permute-done((bf16[3,128,256]{2,1,0:T(8,128)(2,1)S(1)}, bf16[3,128,256]{2,1,0:T(8,128)(2,1)S(1)}, u32[]{:S(2)}, u32[]{:S(2)}) %collective-permute-start.22) | collective-permute-done | bytes 196640 | tf_op jit(solution)/shard_map/ppermute | solution.py:49
  72.0 4.7 %signals.1 = (f32[128,8,256]{2,1,0:T(8,128)S(1)}, f32[16,8,256]{2,1,0:T(8,128)S(1)}, f32[16,256]{1,0:T(8,128)S(1)}) custom-call(bf16[1040,768]{1,0:T(8,128)(2,1)S(1)} %get-tuple-element.116.rows, bf16[3,256,256]{2,1,0:T(8,128)(2,1)S(1)} %collective-permute-done.19.refs_0_, bf16[3,256,256]{2,1,0:T(8,128)(2,1)S(1)} %collective-permute-done.20.refs_1_, ...), custom_call_target="tpu_custom_call" | custom-call | tf_op jit(solution)/shard_map/signals/pallas_call | solution.py:386
  76.7 0.7 collective-permute-start.23
  77.4 1.0 %collective-permute-start.24 = (f32[16,256]{1,0:T(8,128)S(1)}, f32[16,256]{1,0:T(8,128)S(1)}, u32[]{:S(2)}, u32[]{:S(2)}) collective-permute-start(f32[16,256]{1,0:T(8,128)S(1)} %get-tuple-element.133), channel_id=1, source_target_pairs={{0,32},{8,40},{16,48},{24,56},{32,0},{40,8},{48,16},{56,24},{64,96... | collective-permute-start | bytes 49160 | tf_op jit(solution)/shard_map/ppermute | solution.py:49
  78.5 1.6 %collective-permute-start.25 = (f32[16,256]{1,0:T(8,128)S(1)}, f32[16,256]{1,0:T(8,128)S(1)}, u32[]{:S(2)}, u32[]{:S(2)}) collective-permute-start(f32[16,256]{1,0:T(8,128)S(1)} %get-tuple-element.133), channel_id=1, source_target_pairs={{0,48},{8,56},{16,0},{24,8},{32,16},{40,24},{48,32},{56,40},{64,11... | collective-permute-start | bytes 49160 | tf_op jit(solution)/shard_map/ppermute | solution.py:49
  80.1 1.1 %collective-permute-done.23 = f32[16,256]{1,0:T(8,128)S(1)} collective-permute-done((f32[16,256]{1,0:T(8,128)S(1)}, f32[16,256]{1,0:T(8,128)S(1)}, u32[]{:S(2)}, u32[]{:S(2)}) %collective-permute-start.23) | collective-permute-done | bytes 16416 | tf_op jit(solution)/shard_map/ppermute | solution.py:49
  81.2 0.3 collective-permute-done.25
  81.5 0.1 collective-permute-start.26
  81.6 2.5 %collective-permute-start.27 = (f32[16,256]{1,0:T(8,128)S(1)}, f32[16,256]{1,0:T(8,128)S(1)}, u32[]{:S(2)}, u32[]{:S(2)}) collective-permute-start(f32[16,256]{1,0:T(8,128)S(1)} %fusion.2), channel_id=1, source_target_pairs={{0,128},{8,136},{16,144},{24,152},{32,160},{40,168},{48,176},{56,1... | collective-permute-start | bytes 49160 | tf_op jit(solution)/shard_map/ppermute | solution.py:49
  84.1 0.2 collective-permute-start.28
  84.3 1.3 %queries.1 = (f32[128,8,256]{2,1,0:T(8,128)S(1)}, f32[128,8,256]{2,1,0:T(8,128)S(1)}) custom-call(bf16[1040,768]{1,0:T(8,128)(2,1)S(1)} %get-tuple-element.116.rows, bf16[3,256,256]{2,1,0:T(8,128)(2,1)S(1)} %collective-permute-done.19.refs_0_, bf16[3,256,256]{2,1,0:T(8,128)(2,1)S(1)} %collective-permute-done.20.refs_1_, ...), custom_call_target="tpu_custom_call" | custom-call | tf_op jit(solution)/shard_map/queries/pallas_call | solution.py:430
  85.6 0.4 collective-permute-done.27
  86.0 0.7 collective-permute-done.28
  86.7 1.9 %gated.1 = (bf16[512,256]{1,0:T(8,128)(2,1)S(1)}, bf16[512,256]{1,0:T(8,128)(2,1)S(1)}) custom-call(s32[3]{0:T(128)S(1)} %pad_add_fusion.where, f32[128,8,256]{2,1,0:T(8,128)S(1)} %get-tuple-element.129.query, f32[128,8,256]{2,1,0:T(8,128)S(1)} %get-tuple-element.130.gated, f32[16,8,256]{2,1,0:T(8,128)S(1)} %get-tuple-element.131.before, ...), custom_call_target="tpu_custom_call" | custom-call | tf_op jit(solution)/shard_map/gated/pallas_call | solution.py:496
  88.6 6.4 %collective-permute-start.29 = (bf16[512,256]{1,0:T(8,128)(2,1)S(1)}, bf16[512,256]{1,0:T(8,128)(2,1)S(1)}, u32[]{:S(2)}, u32[]{:S(2)}) collective-permute-start(bf16[512,256]{1,0:T(8,128)(2,1)S(1)} %get-tuple-element.136), channel_id=1, source_target_pairs={{0,8},{8,0},{16,24},{24,16},{32,40},{40,32},{48,56},{56,48},{64,72... | collective-permute-start | bytes 786440 | tf_op jit(solution)/shard_map/ppermute | solution.py:49
  95.0 1.2 %collective-permute-done.29 = bf16[512,256]{1,0:T(8,128)(2,1)S(1)} collective-permute-done((bf16[512,256]{1,0:T(8,128)(2,1)S(1)}, bf16[512,256]{1,0:T(8,128)(2,1)S(1)}, u32[]{:S(2)}, u32[]{:S(2)}) %collective-permute-start.29) | collective-permute-done | bytes 262176 | tf_op jit(solution)/shard_map/ppermute | solution.py:49
  96.2 0.8 pad_maximum_fusion
  (75 shorter events, 0.4 us)
Async XLA Ops:
  0.0 43.0 %copy-start = (f32[3,7,512]{2,1,0:T(8,128)S(1)}, f32[3,7,512]{2,1,0:T(8,128)}, u32[]{:S(2)}) copy-start(f32[3,7,512]{2,1,0:T(8,128)} %param.8) | copy-start | bytes 129028
  0.0 22.9 %copy-start.18 = (f32[512,16]{0,1:T(8,128)S(1)}, f32[512,16]{0,1:T(8,128)}, u32[]{:S(2)}) copy-start(f32[512,16]{0,1:T(8,128)} %param.10) | copy-start | bytes 98308
  1.1 4.4 %collective-permute-start = (bf16[3,128,256]{2,1,0:T(8,128)(2,1)S(1)}, bf16[3,128,256]{2,1,0:T(8,128)(2,1)S(1)}, u32[]{:S(2)}, u32[]{:S(2)}) collective-permute-start(bf16[3,128,256]{2,1,0:T(8,128)(2,1)S(1)} %broadcast_select_fusion.4), channel_id=1, source_target_pairs={{0,8},{8,0},{16,24},{24,16},{32,40},{40,32},{48,56},{56,48},{64,72... | collective-permute-start | bytes 589832 | tf_op jit(solution)/shard_map/ppermute | solution.py:49
  5.5 14.7 %collective-permute-start.4 = (bf16[512,4096]{1,0:T(8,128)(2,1)}, bf16[512,4096]{1,0:T(8,128)(2,1)}, u32[]{:S(2)}, u32[]{:S(2)}) collective-permute-start(bf16[512,4096]{1,0:T(8,128)(2,1)} %refs_5_.3), channel_id=1, source_target_pairs={{0,8},{8,0},{16,24},{24,16},{32,40},{40,32},{48,56},{56,48},{64,72... | collective-permute-start | bytes 12582920 | tf_op jit(solution)/shard_map/ppermute | solution.py:49
  7.9 18.4 %copy-start.6 = (bf16[3,256,256]{2,1,0:T(8,128)(2,1)}, bf16[3,256,256]{2,1,0:T(8,128)(2,1)S(1)}, u32[]{:S(2)}) copy-start(bf16[3,256,256]{2,1,0:T(8,128)(2,1)S(1)} %pad_maximum_fusion.1.refs_0_) | copy-start | bytes 1179652
  7.9 4.9 %collective-permute-start.9 = (bf16[16,4096]{1,0:T(8,128)(2,1)S(1)}, bf16[16,4096]{1,0:T(8,128)(2,1)S(1)}, u32[]{:S(2)}, u32[]{:S(2)}) collective-permute-start(bf16[16,4096]{1,0:T(8,128)(2,1)S(1)} %slice.54), channel_id=1, source_target_pairs={{0,8},{8,0},{16,24},{24,16},{32,40},{40,32},{48,56},{56,48},{64,72... | collective-permute-start | bytes 393224 | tf_op jit(solution)/shard_map/ppermute | solution.py:49
  8.2 10.4 %collective-permute-start.1 = (bf16[3,256,256]{2,1,0:T(8,128)(2,1)S(1)}, bf16[3,256,256]{2,1,0:T(8,128)(2,1)S(1)}, u32[]{:S(2)}, u32[]{:S(2)}) collective-permute-start(bf16[3,256,256]{2,1,0:T(8,128)(2,1)S(1)} %pad_maximum_fusion.1.refs_0_), channel_id=1, source_target_pairs={{0,16},{8,24},{16,0},{24,8},{32,48},{40,56},{48,32},{56,40},{64,80... | collective-permute-start | bytes 1179656 | tf_op jit(solution)/shard_map/ppermute | solution.py:49
  8.2 11.9 %collective-permute-start.2 = (bf16[3,256,256]{2,1,0:T(8,128)(2,1)S(1)}, bf16[3,256,256]{2,1,0:T(8,128)(2,1)S(1)}, u32[]{:S(2)}, u32[]{:S(2)}) collective-permute-start(bf16[3,256,256]{2,1,0:T(8,128)(2,1)S(1)} %pad_maximum_fusion.1.refs_0_), channel_id=1, source_target_pairs={{0,64},{8,72},{16,80},{24,88},{32,96},{40,104},{48,112},{56,120},{... | collective-permute-start | bytes 1179656 | tf_op jit(solution)/shard_map/ppermute | solution.py:49
  9.3 10.9 %collective-permute-start.3 = (bf16[3,256,256]{2,1,0:T(8,128)(2,1)S(1)}, bf16[3,256,256]{2,1,0:T(8,128)(2,1)S(1)}, u32[]{:S(2)}, u32[]{:S(2)}) collective-permute-start(bf16[3,256,256]{2,1,0:T(8,128)(2,1)S(1)} %pad_maximum_fusion.1.refs_0_), channel_id=1, source_target_pairs={{0,192},{8,200},{16,208},{24,216},{32,224},{40,232},{48,240},{56,2... | collective-permute-start | bytes 1179656 | tf_op jit(solution)/shard_map/ppermute | solution.py:49
  12.8 10.6 %collective-permute-start.11 = (bf16[16,4096]{1,0:T(8,128)(2,1)S(1)}, bf16[16,4096]{1,0:T(8,128)(2,1)S(1)}, u32[]{:S(2)}, u32[]{:S(2)}) collective-permute-start(bf16[16,4096]{1,0:T(8,128)(2,1)S(1)} %broadcast_select_fusion.6), channel_id=1, source_target_pairs={{0,16},{8,24},{16,32},{24,40},{32,48},{40,56},{48,64},{56,72},{64,... | collective-permute-start | bytes 393224 | tf_op jit(solution)/shard_map/ppermute | solution.py:49
  18.5 11.6 %copy-start.8 = (bf16[3,256,256]{2,1,0:T(8,128)(2,1)}, bf16[3,256,256]{2,1,0:T(8,128)(2,1)S(1)}, u32[]{:S(2)}) copy-start(bf16[3,256,256]{2,1,0:T(8,128)(2,1)S(1)} %collective-permute-done.1.refs_0_) | copy-start | bytes 1179652
  18.5 21.5 %collective-permute-start.10 = (bf16[3,256,256]{2,1,0:T(8,128)(2,1)S(1)}, bf16[3,256,256]{2,1,0:T(8,128)(2,1)S(1)}, u32[]{:S(2)}, u32[]{:S(2)}) collective-permute-start(bf16[3,256,256]{2,1,0:T(8,128)(2,1)S(1)} %pad_maximum_fusion.1.refs_0_), channel_id=1, source_target_pairs={{0,32},{8,40},{16,48},{24,56},{32,0},{40,8},{48,16},{56,24},{64,96... | collective-permute-start | bytes 1179656 | tf_op jit(solution)/shard_map/ppermute | solution.py:49
  20.2 6.0 %copy-start.1 = (bf16[3,256,256]{2,1,0:T(8,128)(2,1)}, bf16[3,256,256]{2,1,0:T(8,128)(2,1)S(1)}, u32[]{:S(2)}) copy-start(bf16[3,256,256]{2,1,0:T(8,128)(2,1)S(1)} %collective-permute-done.2.right.refs_1_) | copy-start | bytes 1179652
  20.2 6.0 %copy-start.2 = (bf16[3,256,256]{2,1,0:T(8,128)(2,1)}, bf16[3,256,256]{2,1,0:T(8,128)(2,1)S(1)}, u32[]{:S(2)}) copy-start(bf16[3,256,256]{2,1,0:T(8,128)(2,1)S(1)} %collective-permute-done.3.left.refs_2_) | copy-start | bytes 1179652
  20.2 19.9 %collective-permute-start.5 = (bf16[3,256,256]{2,1,0:T(8,128)(2,1)S(1)}, bf16[3,256,256]{2,1,0:T(8,128)(2,1)S(1)}, u32[]{:S(2)}, u32[]{:S(2)}) collective-permute-start(bf16[3,256,256]{2,1,0:T(8,128)(2,1)S(1)} %collective-permute-done.1.refs_0_), channel_id=1, source_target_pairs={{0,64},{8,72},{16,80},{24,88},{32,96},{40,104},{48,112},{56,120},{... | collective-permute-start | bytes 1179656 | tf_op jit(solution)/shard_map/ppermute | solution.py:49
  21.5 18.6 %collective-permute-start.6 = (bf16[3,256,256]{2,1,0:T(8,128)(2,1)S(1)}, bf16[3,256,256]{2,1,0:T(8,128)(2,1)S(1)}, u32[]{:S(2)}, u32[]{:S(2)}) collective-permute-start(bf16[3,256,256]{2,1,0:T(8,128)(2,1)S(1)} %collective-permute-done.1.refs_0_), channel_id=1, source_target_pairs={{0,192},{8,200},{16,208},{24,216},{32,224},{40,232},{48,240},{56,2... | collective-permute-start | bytes 1179656 | tf_op jit(solution)/shard_map/ppermute | solution.py:49
  23.2 16.8 %collective-permute-start.7 = (bf16[3,128,256]{2,1,0:T(8,128)(2,1)S(1)}, bf16[3,128,256]{2,1,0:T(8,128)(2,1)S(1)}, u32[]{:S(2)}, u32[]{:S(2)}) collective-permute-start(bf16[3,128,256]{2,1,0:T(8,128)(2,1)S(1)} %get-tuple-element.76), channel_id=1, source_target_pairs={{0,64},{8,72},{16,80},{24,88},{32,96},{40,104},{48,112},{56,120},{... | collective-permute-start | bytes 589832 | tf_op jit(solution)/shard_map/ppermute | solution.py:49
  23.5 2.8 %copy-start.5 = (bf16[16,4096]{1,0:T(8,128)(2,1)}, bf16[16,4096]{1,0:T(8,128)(2,1)S(1)}, u32[]{:S(2)}) copy-start(bf16[16,4096]{1,0:T(8,128)(2,1)S(1)} %collective-permute-done.11.refs_5_.refs_7_) | copy-start | bytes 393220
  23.5 16.6 %collective-permute-start.8 = (bf16[3,128,256]{2,1,0:T(8,128)(2,1)S(1)}, bf16[3,128,256]{2,1,0:T(8,128)(2,1)S(1)}, u32[]{:S(2)}, u32[]{:S(2)}) collective-permute-start(bf16[3,128,256]{2,1,0:T(8,128)(2,1)S(1)} %get-tuple-element.77), channel_id=1, source_target_pairs={{0,192},{8,200},{16,208},{24,216},{32,224},{40,232},{48,240},{56,2... | collective-permute-start | bytes 589832 | tf_op jit(solution)/shard_map/ppermute | solution.py:49
  40.1 9.5 %copy-start.7 = (bf16[3,256,256]{2,1,0:T(8,128)(2,1)}, bf16[3,256,256]{2,1,0:T(8,128)(2,1)S(1)}, u32[]{:S(2)}) copy-start(bf16[3,256,256]{2,1,0:T(8,128)(2,1)S(1)} %collective-permute-done.10.refs_0_) | copy-start | bytes 1179652
  40.1 4.8 %copy-start.12 = (bf16[3,128,256]{2,1,0:T(8,128)(2,1)}, bf16[3,128,256]{2,1,0:T(8,128)(2,1)S(1)}, u32[]{:S(2)}) copy-start(bf16[3,128,256]{2,1,0:T(8,128)(2,1)S(1)} %collective-permute-done.7.refs_3_) | copy-start | bytes 589828
  40.1 4.8 %copy-start.13 = (bf16[3,128,256]{2,1,0:T(8,128)(2,1)}, bf16[3,128,256]{2,1,0:T(8,128)(2,1)S(1)}, u32[]{:S(2)}) copy-start(bf16[3,128,256]{2,1,0:T(8,128)(2,1)S(1)} %collective-permute-done.8.refs_4_) | copy-start | bytes 589828
  40.1 4.8 %copy-start.10 = (bf16[3,256,256]{2,1,0:T(8,128)(2,1)}, bf16[3,256,256]{2,1,0:T(8,128)(2,1)S(1)}, u32[]{:S(2)}) copy-start(bf16[3,256,256]{2,1,0:T(8,128)(2,1)S(1)} %collective-permute-done.5.refs_1_) | copy-start | bytes 1179652
  40.1 4.8 %copy-start.11 = (bf16[3,256,256]{2,1,0:T(8,128)(2,1)}, bf16[3,256,256]{2,1,0:T(8,128)(2,1)S(1)}, u32[]{:S(2)}) copy-start(bf16[3,256,256]{2,1,0:T(8,128)(2,1)S(1)} %collective-permute-done.6.refs_2_) | copy-start | bytes 1179652
  40.1 11.5 %collective-permute-start.12 = (bf16[3,256,256]{2,1,0:T(8,128)(2,1)S(1)}, bf16[3,256,256]{2,1,0:T(8,128)(2,1)S(1)}, u32[]{:S(2)}, u32[]{:S(2)}) collective-permute-start(bf16[3,256,256]{2,1,0:T(8,128)(2,1)S(1)} %collective-permute-done.10.refs_0_), channel_id=1, source_target_pairs={{0,64},{8,72},{16,80},{24,88},{32,96},{40,104},{48,112},{56,120},{... | collective-permute-start | bytes 1179656 | tf_op jit(solution)/shard_map/ppermute | solution.py:49
  41.4 10.2 %collective-permute-start.13 = (bf16[3,256,256]{2,1,0:T(8,128)(2,1)S(1)}, bf16[3,256,256]{2,1,0:T(8,128)(2,1)S(1)}, u32[]{:S(2)}, u32[]{:S(2)}) collective-permute-start(bf16[3,256,256]{2,1,0:T(8,128)(2,1)S(1)} %collective-permute-done.10.refs_0_), channel_id=1, source_target_pairs={{0,192},{8,200},{16,208},{24,216},{32,224},{40,232},{48,240},{56,2... | collective-permute-start | bytes 1179656 | tf_op jit(solution)/shard_map/ppermute | solution.py:49
  42.9 18.1 %collective-permute-start.16 = (bf16[3,256,256]{2,1,0:T(8,128)(2,1)S(1)}, bf16[3,256,256]{2,1,0:T(8,128)(2,1)S(1)}, u32[]{:S(2)}, u32[]{:S(2)}) collective-permute-start(bf16[3,256,256]{2,1,0:T(8,128)(2,1)S(1)} %collective-permute-done.10.refs_0_), channel_id=1, source_target_pairs={{0,16},{8,24},{16,0},{24,8},{32,48},{40,56},{48,32},{56,40},{64,80... | collective-permute-start | bytes 1179656 | tf_op jit(solution)/shard_map/ppermute | solution.py:49
  43.0 15.5 %collective-permute-start.17 = (bf16[3,128,256]{2,1,0:T(8,128)(2,1)S(1)}, bf16[3,128,256]{2,1,0:T(8,128)(2,1)S(1)}, u32[]{:S(2)}, u32[]{:S(2)}) collective-permute-start(bf16[3,128,256]{2,1,0:T(8,128)(2,1)S(1)} %collective-permute-done.7.refs_3_), channel_id=1, source_target_pairs={{0,16},{8,24},{16,0},{24,8},{32,48},{40,56},{48,32},{56,40},{64,80... | collective-permute-start | bytes 589832 | tf_op jit(solution)/shard_map/ppermute | solution.py:49
  44.6 16.4 %collective-permute-start.18 = (bf16[3,128,256]{2,1,0:T(8,128)(2,1)S(1)}, bf16[3,128,256]{2,1,0:T(8,128)(2,1)S(1)}, u32[]{:S(2)}, u32[]{:S(2)}) collective-permute-start(bf16[3,128,256]{2,1,0:T(8,128)(2,1)S(1)} %collective-permute-done.8.refs_4_), channel_id=1, source_target_pairs={{0,16},{8,24},{16,0},{24,8},{32,48},{40,56},{48,32},{56,40},{64,80... | collective-permute-start | bytes 589832 | tf_op jit(solution)/shard_map/ppermute | solution.py:49
  51.6 3.0 %copy-start.3 = (bf16[3,256,256]{2,1,0:T(8,128)(2,1)}, bf16[3,256,256]{2,1,0:T(8,128)(2,1)S(1)}, u32[]{:S(2)}) copy-start(bf16[3,256,256]{2,1,0:T(8,128)(2,1)S(1)} %collective-permute-done.12.right.refs_1_) | copy-start | bytes 1179652
  51.6 3.0 %copy-start.4 = (bf16[3,256,256]{2,1,0:T(8,128)(2,1)}, bf16[3,256,256]{2,1,0:T(8,128)(2,1)S(1)}, u32[]{:S(2)}) copy-start(bf16[3,256,256]{2,1,0:T(8,128)(2,1)S(1)} %collective-permute-done.13.left.refs_2_) | copy-start | bytes 1179652
  51.8 9.2 %collective-permute-start.14 = (bf16[3,128,256]{2,1,0:T(8,128)(2,1)S(1)}, bf16[3,128,256]{2,1,0:T(8,128)(2,1)S(1)}, u32[]{:S(2)}, u32[]{:S(2)}) collective-permute-start(bf16[3,128,256]{2,1,0:T(8,128)(2,1)S(1)} %get-tuple-element.96), channel_id=1, source_target_pairs={{0,64},{8,72},{16,80},{24,88},{32,96},{40,104},{48,112},{56,120},{... | collective-permute-start | bytes 589832 | tf_op jit(solution)/shard_map/ppermute | solution.py:49
  52.8 8.2 %collective-permute-start.15 = (bf16[3,128,256]{2,1,0:T(8,128)(2,1)S(1)}, bf16[3,128,256]{2,1,0:T(8,128)(2,1)S(1)}, u32[]{:S(2)}, u32[]{:S(2)}) collective-permute-start(bf16[3,128,256]{2,1,0:T(8,128)(2,1)S(1)} %get-tuple-element.97), channel_id=1, source_target_pairs={{0,192},{8,200},{16,208},{24,216},{32,224},{40,232},{48,240},{56,2... | collective-permute-start | bytes 589832 | tf_op jit(solution)/shard_map/ppermute | solution.py:49
  54.6 9.2 %copy-start.19 = (f32[512,16]{0,1:T(8,128)S(1)}, f32[512,16]{0,1:T(8,128)}, u32[]{:S(2)}) copy-start(f32[512,16]{0,1:T(8,128)} %param.9) | copy-start | bytes 98308
  54.6 9.2 %copy-start.20 = (f32[512]{0:T(512)S(1)}, f32[512]{0:T(512)}, u32[]{:S(2)}) copy-start(f32[512]{0:T(512)} %param.11) | copy-start | bytes 6148
  58.6 6.8 %copy-start.14 = (bf16[3,128,256]{2,1,0:T(8,128)(2,1)}, bf16[3,128,256]{2,1,0:T(8,128)(2,1)S(1)}, u32[]{:S(2)}) copy-start(bf16[3,128,256]{2,1,0:T(8,128)(2,1)S(1)} %collective-permute-done.17.refs_1_) | copy-start | bytes 589828
  61.0 4.5 %copy-start.15 = (bf16[3,128,256]{2,1,0:T(8,128)(2,1)}, bf16[3,128,256]{2,1,0:T(8,128)(2,1)S(1)}, u32[]{:S(2)}) copy-start(bf16[3,128,256]{2,1,0:T(8,128)(2,1)S(1)} %collective-permute-done.18.refs_2_) | copy-start | bytes 589828
  61.0 4.5 %copy-start.9 = (bf16[3,256,256]{2,1,0:T(8,128)(2,1)}, bf16[3,256,256]{2,1,0:T(8,128)(2,1)S(1)}, u32[]{:S(2)}) copy-start(bf16[3,256,256]{2,1,0:T(8,128)(2,1)S(1)} %collective-permute-done.16.refs_0_) | copy-start | bytes 1179652
  61.0 4.5 %copy-start.16 = (bf16[3,128,256]{2,1,0:T(8,128)(2,1)}, bf16[3,128,256]{2,1,0:T(8,128)(2,1)S(1)}, u32[]{:S(2)}) copy-start(bf16[3,128,256]{2,1,0:T(8,128)(2,1)S(1)} %collective-permute-done.14.refs_3_) | copy-start | bytes 589828
  61.0 4.4 %copy-start.17 = (bf16[3,128,256]{2,1,0:T(8,128)(2,1)}, bf16[3,128,256]{2,1,0:T(8,128)(2,1)S(1)}, u32[]{:S(2)}) copy-start(bf16[3,128,256]{2,1,0:T(8,128)(2,1)S(1)} %collective-permute-done.15.refs_4_) | copy-start | bytes 589828
  61.0 11.0 %collective-permute-start.19 = (bf16[3,256,256]{2,1,0:T(8,128)(2,1)S(1)}, bf16[3,256,256]{2,1,0:T(8,128)(2,1)S(1)}, u32[]{:S(2)}, u32[]{:S(2)}) collective-permute-start(bf16[3,256,256]{2,1,0:T(8,128)(2,1)S(1)} %collective-permute-done.16.refs_0_), channel_id=1, source_target_pairs={{0,64},{8,72},{16,80},{24,88},{32,96},{40,104},{48,112},{56,120},{... | collective-permute-start | bytes 1179656 | tf_op jit(solution)/shard_map/ppermute | solution.py:49
  61.1 10.9 %collective-permute-start.20 = (bf16[3,256,256]{2,1,0:T(8,128)(2,1)S(1)}, bf16[3,256,256]{2,1,0:T(8,128)(2,1)S(1)}, u32[]{:S(2)}, u32[]{:S(2)}) collective-permute-start(bf16[3,256,256]{2,1,0:T(8,128)(2,1)S(1)} %collective-permute-done.16.refs_0_), channel_id=1, source_target_pairs={{0,192},{8,200},{16,208},{24,216},{32,224},{40,232},{48,240},{56,2... | collective-permute-start | bytes 1179656 | tf_op jit(solution)/shard_map/ppermute | solution.py:49
  63.9 6.1 %collective-permute-start.21 = (bf16[3,128,256]{2,1,0:T(8,128)(2,1)S(1)}, bf16[3,128,256]{2,1,0:T(8,128)(2,1)S(1)}, u32[]{:S(2)}, u32[]{:S(2)}) collective-permute-start(bf16[3,128,256]{2,1,0:T(8,128)(2,1)S(1)} %collective-permute-done.14.refs_3_), channel_id=1, source_target_pairs={{0,16},{8,24},{16,0},{24,8},{32,48},{40,56},{48,32},{56,40},{64,80... | collective-permute-start | bytes 589832 | tf_op jit(solution)/shard_map/ppermute | solution.py:49
  64.2 7.8 %collective-permute-start.22 = (bf16[3,128,256]{2,1,0:T(8,128)(2,1)S(1)}, bf16[3,128,256]{2,1,0:T(8,128)(2,1)S(1)}, u32[]{:S(2)}, u32[]{:S(2)}) collective-permute-start(bf16[3,128,256]{2,1,0:T(8,128)(2,1)S(1)} %collective-permute-done.15.refs_4_), channel_id=1, source_target_pairs={{0,16},{8,24},{16,0},{24,8},{32,48},{40,56},{48,32},{56,40},{64,80... | collective-permute-start | bytes 589832 | tf_op jit(solution)/shard_map/ppermute | solution.py:49
  76.7 4.5 %collective-permute-start.23 = (f32[16,256]{1,0:T(8,128)S(1)}, f32[16,256]{1,0:T(8,128)S(1)}, u32[]{:S(2)}, u32[]{:S(2)}) collective-permute-start(f32[16,256]{1,0:T(8,128)S(1)} %get-tuple-element.133), channel_id=1, source_target_pairs={{0,16},{8,24},{16,32},{24,40},{32,48},{40,56},{48,0},{56,8},{64,80... | collective-permute-start | bytes 49160 | tf_op jit(solution)/shard_map/ppermute | solution.py:49
  77.4 3.8 %collective-permute-start.24 = (f32[16,256]{1,0:T(8,128)S(1)}, f32[16,256]{1,0:T(8,128)S(1)}, u32[]{:S(2)}, u32[]{:S(2)}) collective-permute-start(f32[16,256]{1,0:T(8,128)S(1)} %get-tuple-element.133), channel_id=1, source_target_pairs={{0,32},{8,40},{16,48},{24,56},{32,0},{40,8},{48,16},{56,24},{64,96... | collective-permute-start | bytes 49160 | tf_op jit(solution)/shard_map/ppermute | solution.py:49
  78.5 3.0 %collective-permute-start.25 = (f32[16,256]{1,0:T(8,128)S(1)}, f32[16,256]{1,0:T(8,128)S(1)}, u32[]{:S(2)}, u32[]{:S(2)}) collective-permute-start(f32[16,256]{1,0:T(8,128)S(1)} %get-tuple-element.133), channel_id=1, source_target_pairs={{0,48},{8,56},{16,0},{24,8},{32,16},{40,24},{48,32},{56,40},{64,11... | collective-permute-start | bytes 49160 | tf_op jit(solution)/shard_map/ppermute | solution.py:49
  81.5 4.1 %collective-permute-start.26 = (f32[16,256]{1,0:T(8,128)S(1)}, f32[16,256]{1,0:T(8,128)S(1)}, u32[]{:S(2)}, u32[]{:S(2)}) collective-permute-start(f32[16,256]{1,0:T(8,128)S(1)} %fusion.2), channel_id=1, source_target_pairs={{0,64},{8,72},{16,80},{24,88},{32,96},{40,104},{48,112},{56,120},{... | collective-permute-start | bytes 49160 | tf_op jit(solution)/shard_map/ppermute | solution.py:49
  81.6 4.4 %collective-permute-start.27 = (f32[16,256]{1,0:T(8,128)S(1)}, f32[16,256]{1,0:T(8,128)S(1)}, u32[]{:S(2)}, u32[]{:S(2)}) collective-permute-start(f32[16,256]{1,0:T(8,128)S(1)} %fusion.2), channel_id=1, source_target_pairs={{0,128},{8,136},{16,144},{24,152},{32,160},{40,168},{48,176},{56,1... | collective-permute-start | bytes 49160 | tf_op jit(solution)/shard_map/ppermute | solution.py:49
  84.1 2.6 %collective-permute-start.28 = (f32[16,256]{1,0:T(8,128)S(1)}, f32[16,256]{1,0:T(8,128)S(1)}, u32[]{:S(2)}, u32[]{:S(2)}) collective-permute-start(f32[16,256]{1,0:T(8,128)S(1)} %fusion.2), channel_id=1, source_target_pairs={{0,192},{8,200},{16,208},{24,216},{32,224},{40,232},{48,240},{56,2... | collective-permute-start | bytes 49160 | tf_op jit(solution)/shard_map/ppermute | solution.py:49
  88.6 7.6 %collective-permute-start.29 = (bf16[512,256]{1,0:T(8,128)(2,1)S(1)}, bf16[512,256]{1,0:T(8,128)(2,1)S(1)}, u32[]{:S(2)}, u32[]{:S(2)}) collective-permute-start(bf16[512,256]{1,0:T(8,128)(2,1)S(1)} %get-tuple-element.136), channel_id=1, source_target_pairs={{0,8},{8,0},{16,24},{24,16},{32,40},{40,32},{48,56},{56,48},{64,72... | collective-permute-start | bytes 786440 | tf_op jit(solution)/shard_map/ppermute | solution.py:49

commit v6 on v5

--- a/solution.py
+++ b/solution.py
@@ -277,7 +277,7 @@
         pltpu.VMEM((rows, depth), jnp.bfloat16),
         pltpu.VMEM((streams.size, depth, channels), jnp.bfloat16),
         pltpu.SemaphoreType.DMA((len(plan), 4)),
-        pltpu.SemaphoreType.DMA((3, 3)),
+        pltpu.SemaphoreType.DMA((4, 3)),
     ]
 
 
@@ -300,7 +300,7 @@
         in_specs=[SMEM] + [HBM] * len(inputs) + [VMEM] * len(before),
         out_specs=[VMEM] * len(shapes),
         scratch_shapes=copy_scratch(pieces, ALL, sum(heights)),
-        compiler_params=pltpu.CompilerParams(vmem_limit_bytes=8 * 1024 * 1024),
+        compiler_params=pltpu.CompilerParams(vmem_limit_bytes=12 * 1024 * 1024),
         name=name,
     )(where, *in_hbm(*inputs), *in_vmem(*before))
 
@@ -552,15 +552,16 @@
         return lax.dynamic_slice_in_dim(array, core * half, half, axis)
 
     low, high = in_weight[:, :, :half], in_weight[:, :, half:]
-    own = jnp.where(first, low, high)
     received, later_tokens = together(swap_cores(jnp.where(first, high, low)), tokens)
     block = jnp.concatenate(
-        [jnp.where(first, own, received), jnp.where(first, received, own)], axis=1
-    )
+        [jnp.where(first, low, received), jnp.where(first, received, high)], axis=1
+    )
+
     beside = across_z(block, 1)
     right, left = sides(block)
     other = swap_cores(later_tokens)
-    held, tail = together(block, later_tokens[length - HALO :])
+    held, late_tokens = together(block, later_tokens)
+    tail = late_tokens[length - HALO :]
     held, other_tail = together(held, swap_cores(tail))
     over = across_z(held, 2)
     halo = next_chip(jnp.where(first, other_tail, tail))
@@ -599,28 +600,23 @@
     right, left = sides(over)
     right, left, products, halo_products = together(right, left, *products)
 
+    pieces = with_sides(2, over, right, left)
     far = forwards(right, left)
-    pieces = with_sides(2, over, right, left)
-    products = partial_products(where, pieces, both, (halo,), (products, halo_products), "third")
-    far_right, far_left, opposite, *far_beside, products, halo_products = together(
-        *far, opposite, *far_beside, *products
-    )
-
     right, left = sides(opposite)
-    far_opposite = across_z(far_right, 1), across_z(far_left, 1)
-    pieces = with_sides(3, opposite) + with_far(1, *far_beside) + with_far(2, far_right, far_left)
+    far_opposite = across_z(far[0], 1), across_z(far[1], 1)
+    pieces += with_sides(3, opposite) + with_far(2, *far)
     *products, rows = partial_products(
         where,
         pieces,
         both,
         (halo,),
         (products, halo_products),
-        "fourth",
-        ((1, 3), (3, 3), (2, 3)),
+        "third",
+        ((1, 3), (3, 3), (2, 3), (2, 1)),
     )
     small = (power, start_power, factors, decay, amplitude, taps, direct)
     *last, products, halo_products, rows, power, start_power, factors, decay, amplitude, taps, direct = (
-        together(right, left, *far_opposite, *products, rows, *small)
+        together(right, left, *far_opposite, *far_beside, *products, rows, *small)
     )
     products = products, halo_products
 

time: 97.3 us -> 95.1 us (0.977)
  Pallas kernels: 25.4 us -> 23.5 us
  waiting for transfers between devices: 26.7 us -> 25.4 us
    pallas_call x4 -> x3, Pallas kernels: 17 us -> 14.8 us  [partial_products(): pl.pallas_call(functools.partial(partial_kernel, plan, bool(tokens), bool...]
    ppermute x30, waiting for transfers between devices: 26.7 us -> 25.4 us  [permute(): return lax.ppermute(value, 'seq', pairs)]
  transfers between devices with their start and end apart: 30 -> 30, of which waited for: 12 -> 10; matrix products, arithmetic and copies ran while one was open for 3% -> 4% of each run, Pallas kernels for 19% -> 18%
where the time goes in v6:
time: 95.1 us; the launch traced here: 94.8 us
  starting transfers between devices  40 us (42%)
  waiting for transfers between devices  25.4 us (27%)
  Pallas kernels  23.5 us (25%)
  other arithmetic  4.31 us (5%)
  local copies, waits for them, and re-layouts  1.23 us (1%)
    ppermute x30, starting transfers between devices, permute(): return lax.ppermute(value, 'seq', pairs)  40 us
    ppermute x30, waiting for transfers between devices, permute(): return lax.ppermute(value, 'seq', pairs)  25.4 us
    pallas_call x3, Pallas kernels, partial_products(): pl.pallas_call(functools.partial(partial_kernel, plan, bool(tokens), bool...  14.8 us
    pallas_call x1, Pallas kernels, signals(): pl.pallas_call(functools.partial(signal_kernel, len(last)), out_shape=(pl...  5 us
  transfers between devices with their start and end apart: 30, of which 10 were waited for; matrix products, arithmetic and copies ran while one was open for 4% of the time, Pallas kernels for 18%

profile of v6, /device:TPU:1, one launch (start us, length us, event | category | flops | bytes accessed | tf_op | source)
XLA Modules:
  0.0 94.8 jit_solution(5760084400577357203)
XLA Ops:
  0.0 1.1 %broadcast_select_fusion.4 = bf16[3,128,256]{2,1,0:T(8,128)(2,1)S(1)} fusion(pred[]{:T(512)S(6)} %eq.6, bf16[3,128,512]{2,1,0:T(8,128)(2,1)} %param.7), kind=kLoop, calls=%fused_computation.6 | loop fusion | flops 98304 | bytes 589825 | tf_op jit(solution)/shard_map/jit(_where)/select_n | solution.py:555
  1.1 3.3 %collective-permute-start = (bf16[3,128,256]{2,1,0:T(8,128)(2,1)S(1)}, bf16[3,128,256]{2,1,0:T(8,128)(2,1)S(1)}, u32[]{:S(2)}, u32[]{:S(2)}) collective-permute-start(bf16[3,128,256]{2,1,0:T(8,128)(2,1)S(1)} %broadcast_select_fusion.4), channel_id=1, source_target_pairs={{0,8},{8,0},{16,24},{24,16},{32,40},{40,32},{48,56},{56,48},{64,72... | collective-permute-start | bytes 589832 | tf_op jit(solution)/shard_map/ppermute | solution.py:49
  4.4 1.1 %collective-permute-done = bf16[3,128,256]{2,1,0:T(8,128)(2,1)S(1)} collective-permute-done((bf16[3,128,256]{2,1,0:T(8,128)(2,1)S(1)}, bf16[3,128,256]{2,1,0:T(8,128)(2,1)S(1)}, u32[]{:S(2)}, u32[]{:S(2)}) %collective-permute-start) | collective-permute-done | bytes 196640 | tf_op jit(solution)/shard_map/ppermute | solution.py:49
  5.5 0.4 collective-permute-start.4
  5.8 1.1 %broadcast_select_fusion.3 = (bf16[3,128,256]{2,1,0:T(8,128)(2,1)S(1)}, bf16[3,128,256]{2,1,0:T(8,128)(2,1)S(1)}) fusion(bf16[3,128,256]{2,1,0:T(8,128)(2,1)S(1)} %collective-permute-done, pred[]{:T(512)S(6)} %eq.6, bf16[3,128,512]{2,1,0:T(8,128)(2,1)} %param.7), kind=kLoop, calls=%fused_computation.5 | loop fusion | flops 196608 | bytes 983041 | tf_op jit(solution)/shard_map/jit(_where)/select_n | solution.py:557
  6.9 0.0 copy-start.5
  6.9 1.1 %slice.54 = bf16[16,4096]{1,0:T(8,128)(2,1)S(1)} slice(bf16[512,4096]{1,0:T(8,128)(2,1)} %refs_6_.1), slice={[496:512], [0:4096]} | slice | bytes 262144 | tf_op jit(solution)/shard_map/slice | solution.py:564
  8.0 0.2 collective-permute-start.9
  8.2 0.1 pad_add_fusion.where
  8.3 0.0 collective-permute-start.1
  8.4 1.1 %collective-permute-start.2 = (bf16[3,256,256]{2,1,0:T(8,128)(2,1)S(1)}, bf16[3,256,256]{2,1,0:T(8,128)(2,1)S(1)}, u32[]{:S(2)}, u32[]{:S(2)}) collective-permute-start(bf16[3,256,256]{2,1,0:T(8,128)(2,1)S(1)} %pad_maximum_fusion.1.refs_0_), channel_id=1, source_target_pairs={{0,64},{8,72},{16,80},{24,88},{32,96},{40,104},{48,112},{56,120},{... | collective-permute-start | bytes 1179656 | tf_op jit(solution)/shard_map/ppermute | solution.py:49
  9.5 1.7 %collective-permute-start.3 = (bf16[3,256,256]{2,1,0:T(8,128)(2,1)S(1)}, bf16[3,256,256]{2,1,0:T(8,128)(2,1)S(1)}, u32[]{:S(2)}, u32[]{:S(2)}) collective-permute-start(bf16[3,256,256]{2,1,0:T(8,128)(2,1)S(1)} %pad_maximum_fusion.1.refs_0_), channel_id=1, source_target_pairs={{0,192},{8,200},{16,208},{24,216},{32,224},{40,232},{48,240},{56,2... | collective-permute-start | bytes 1179656 | tf_op jit(solution)/shard_map/ppermute | solution.py:49
  11.1 1.7 %collective-permute-done.9 = bf16[16,4096]{1,0:T(8,128)(2,1)S(1)} collective-permute-done((bf16[16,4096]{1,0:T(8,128)(2,1)S(1)}, bf16[16,4096]{1,0:T(8,128)(2,1)S(1)}, u32[]{:S(2)}, u32[]{:S(2)}) %collective-permute-start.9) | collective-permute-done | bytes 131104 | tf_op jit(solution)/shard_map/ppermute | solution.py:49
  12.8 0.9 broadcast_select_fusion.5
  13.7 1.8 %collective-permute-start.11 = (bf16[16,4096]{1,0:T(8,128)(2,1)S(1)}, bf16[16,4096]{1,0:T(8,128)(2,1)S(1)}, u32[]{:S(2)}, u32[]{:S(2)}) collective-permute-start(bf16[16,4096]{1,0:T(8,128)(2,1)S(1)} %broadcast_select_fusion.5), channel_id=1, source_target_pairs={{0,16},{8,24},{16,32},{24,40},{32,48},{40,56},{48,64},{56,72},{64,... | collective-permute-start | bytes 393224 | tf_op jit(solution)/shard_map/ppermute | solution.py:49
  15.6 3.1 %collective-permute-done.1.refs_0_ = bf16[3,256,256]{2,1,0:T(8,128)(2,1)S(1)} collective-permute-done((bf16[3,256,256]{2,1,0:T(8,128)(2,1)S(1)}, bf16[3,256,256]{2,1,0:T(8,128)(2,1)S(1)}, u32[]{:S(2)}, u32[]{:S(2)}) %collective-permute-start.1) | collective-permute-done | bytes 393248 | tf_op jit(solution)/shard_map/ppermute | solution.py:49
  18.7 1.6 %collective-permute-start.10 = (bf16[3,256,256]{2,1,0:T(8,128)(2,1)S(1)}, bf16[3,256,256]{2,1,0:T(8,128)(2,1)S(1)}, u32[]{:S(2)}, u32[]{:S(2)}) collective-permute-start(bf16[3,256,256]{2,1,0:T(8,128)(2,1)S(1)} %pad_maximum_fusion.1.refs_0_), channel_id=1, source_target_pairs={{0,32},{8,40},{16,48},{24,56},{32,0},{40,8},{48,16},{56,24},{64,96... | collective-permute-start | bytes 1179656 | tf_op jit(solution)/shard_map/ppermute | solution.py:49
  20.3 0.0 collective-permute-done.2.right.refs_1_
  20.3 0.0 collective-permute-done.3.left.refs_2_
  20.3 1.3 %collective-permute-start.5 = (bf16[3,256,256]{2,1,0:T(8,128)(2,1)S(1)}, bf16[3,256,256]{2,1,0:T(8,128)(2,1)S(1)}, u32[]{:S(2)}, u32[]{:S(2)}) collective-permute-start(bf16[3,256,256]{2,1,0:T(8,128)(2,1)S(1)} %collective-permute-done.1.refs_0_), channel_id=1, source_target_pairs={{0,64},{8,72},{16,80},{24,88},{32,96},{40,104},{48,112},{56,120},{... | collective-permute-start | bytes 1179656 | tf_op jit(solution)/shard_map/ppermute | solution.py:49
  21.6 1.5 %collective-permute-start.6 = (bf16[3,256,256]{2,1,0:T(8,128)(2,1)S(1)}, bf16[3,256,256]{2,1,0:T(8,128)(2,1)S(1)}, u32[]{:S(2)}, u32[]{:S(2)}) collective-permute-start(bf16[3,256,256]{2,1,0:T(8,128)(2,1)S(1)} %collective-permute-done.1.refs_0_), channel_id=1, source_target_pairs={{0,192},{8,200},{16,208},{24,216},{32,224},{40,232},{48,240},{56,2... | collective-permute-start | bytes 1179656 | tf_op jit(solution)/shard_map/ppermute | solution.py:49
  23.1 0.2 halves.2
  23.3 0.1 collective-permute-start.7
  23.5 0.0 collective-permute-done.11.refs_5_.refs_7_.refs_8_
  23.6 2.7 %collective-permute-start.8 = (bf16[3,128,256]{2,1,0:T(8,128)(2,1)S(1)}, bf16[3,128,256]{2,1,0:T(8,128)(2,1)S(1)}, u32[]{:S(2)}, u32[]{:S(2)}) collective-permute-start(bf16[3,128,256]{2,1,0:T(8,128)(2,1)S(1)} %get-tuple-element.70), channel_id=1, source_target_pairs={{0,192},{8,200},{16,208},{24,216},{32,224},{40,232},{48,240},{56,2... | collective-permute-start | bytes 589832 | tf_op jit(solution)/shard_map/ppermute | solution.py:49
  26.3 3.9 %first.1 = (f32[3,2,1024,128]{3,2,1,0:T(8,128)S(1)}, f32[3,2,16,128]{3,2,1,0:T(8,128)S(1)}) custom-call(s32[3]{0:T(128)S(1)} %pad_add_fusion.where, bf16[3,256,256]{2,1,0:T(8,128)(2,1)} %copy-done.5, bf16[3,256,256]{2,1,0:T(8,128)(2,1)} %copy-done.1, bf16[3,256,256]{2,1,0:T(8,128)(2,1)} %copy-done.2, bf16[512,4096]{1,0:T(8,128)(2,1)} %refs_6_.1, ...), custom_call_target="tpu_custom_call" | custom-call | tf_op jit(solution)/shard_map/first/pallas_call | solution.py:295
  30.3 9.9 %collective-permute-done.10.refs_0_ = bf16[3,256,256]{2,1,0:T(8,128)(2,1)S(1)} collective-permute-done((bf16[3,256,256]{2,1,0:T(8,128)(2,1)S(1)}, bf16[3,256,256]{2,1,0:T(8,128)(2,1)S(1)}, u32[]{:S(2)}, u32[]{:S(2)}) %collective-permute-start.10) | collective-permute-done | bytes 393248 | tf_op jit(solution)/shard_map/ppermute | solution.py:49
  40.2 0.0 collective-permute-done.6.refs_2_
  40.3 1.3 %collective-permute-start.15 = (bf16[3,256,256]{2,1,0:T(8,128)(2,1)S(1)}, bf16[3,256,256]{2,1,0:T(8,128)(2,1)S(1)}, u32[]{:S(2)}, u32[]{:S(2)}) collective-permute-start(bf16[3,256,256]{2,1,0:T(8,128)(2,1)S(1)} %collective-permute-done.10.refs_0_), channel_id=1, source_target_pairs={{0,64},{8,72},{16,80},{24,88},{32,96},{40,104},{48,112},{56,120},{... | collective-permute-start | bytes 1179656 | tf_op jit(solution)/shard_map/ppermute | solution.py:49
  41.5 1.5 %collective-permute-start.16 = (bf16[3,256,256]{2,1,0:T(8,128)(2,1)S(1)}, bf16[3,256,256]{2,1,0:T(8,128)(2,1)S(1)}, u32[]{:S(2)}, u32[]{:S(2)}) collective-permute-start(bf16[3,256,256]{2,1,0:T(8,128)(2,1)S(1)} %collective-permute-done.10.refs_0_), channel_id=1, source_target_pairs={{0,192},{8,200},{16,208},{24,216},{32,224},{40,232},{48,240},{56,2... | collective-permute-start | bytes 1179656 | tf_op jit(solution)/shard_map/ppermute | solution.py:49
  43.0 0.0 collective-permute-start.12
  43.1 0.1 multiply_exponential_fusion.power
  43.2 0.0 copy-start.17
  43.2 0.0 copy-start.18
  43.2 1.7 %collective-permute-start.21 = (bf16[3,128,256]{2,1,0:T(8,128)(2,1)S(1)}, bf16[3,128,256]{2,1,0:T(8,128)(2,1)S(1)}, u32[]{:S(2)}, u32[]{:S(2)}) collective-permute-start(bf16[3,128,256]{2,1,0:T(8,128)(2,1)S(1)} %collective-permute-done.7.refs_3_), channel_id=1, source_target_pairs={{0,16},{8,24},{16,0},{24,8},{32,48},{40,56},{48,32},{56,40},{64,80... | collective-permute-start | bytes 589832 | tf_op jit(solution)/shard_map/ppermute | solution.py:49
  44.9 4.7 %second.1 = (f32[3,2,1024,128]{3,2,1,0:T(8,128)S(1)}, f32[3,2,16,128]{3,2,1,0:T(8,128)S(1)}) custom-call(s32[3]{0:T(128)S(1)} %pad_add_fusion.where, bf16[3,256,256]{2,1,0:T(8,128)(2,1)} %copy-done.7, bf16[3,256,256]{2,1,0:T(8,128)(2,1)} %copy-done.8, bf16[3,256,256]{2,1,0:T(8,128)(2,1)} %copy-done.9, bf16[3,128,256]{2,1,0:T(8,128)(2,1)} %copy-done.13, ...), custom_call_target="tpu_custom_call" | custom-call | tf_op jit(solution)/shard_map/second/pallas_call | solution.py:295
  49.7 2.1 %collective-permute-done.15.right.refs_1_ = bf16[3,256,256]{2,1,0:T(8,128)(2,1)S(1)} collective-permute-done((bf16[3,256,256]{2,1,0:T(8,128)(2,1)S(1)}, bf16[3,256,256]{2,1,0:T(8,128)(2,1)S(1)}, u32[]{:S(2)}, u32[]{:S(2)}) %collective-permute-start.15) | collective-permute-done | bytes 393248 | tf_op jit(solution)/shard_map/ppermute | solution.py:49
  51.7 0.2 halves.3
  51.9 1.0 %collective-permute-start.17 = (bf16[3,128,256]{2,1,0:T(8,128)(2,1)S(1)}, bf16[3,128,256]{2,1,0:T(8,128)(2,1)S(1)}, u32[]{:S(2)}, u32[]{:S(2)}) collective-permute-start(bf16[3,128,256]{2,1,0:T(8,128)(2,1)S(1)} %get-tuple-element.89), channel_id=1, source_target_pairs={{0,64},{8,72},{16,80},{24,88},{32,96},{40,104},{48,112},{56,120},{... | collective-permute-start | bytes 589832 | tf_op jit(solution)/shard_map/ppermute | solution.py:49
  52.9 1.8 %collective-permute-start.19 = (bf16[3,128,256]{2,1,0:T(8,128)(2,1)S(1)}, bf16[3,128,256]{2,1,0:T(8,128)(2,1)S(1)}, u32[]{:S(2)}, u32[]{:S(2)}) collective-permute-start(bf16[3,128,256]{2,1,0:T(8,128)(2,1)S(1)} %get-tuple-element.90), channel_id=1, source_target_pairs={{0,192},{8,200},{16,208},{24,216},{32,224},{40,232},{48,240},{56,2... | collective-permute-start | bytes 589832 | tf_op jit(solution)/shard_map/ppermute | solution.py:49
  54.7 2.7 %collective-permute-start.14 = (bf16[3,256,256]{2,1,0:T(8,128)(2,1)S(1)}, bf16[3,256,256]{2,1,0:T(8,128)(2,1)S(1)}, u32[]{:S(2)}, u32[]{:S(2)}) collective-permute-start(bf16[3,256,256]{2,1,0:T(8,128)(2,1)S(1)} %collective-permute-done.12.refs_3_), channel_id=1, source_target_pairs={{0,192},{8,200},{16,208},{24,216},{32,224},{40,232},{48,240},{56,2... | collective-permute-start | bytes 1179656 | tf_op jit(solution)/shard_map/ppermute | solution.py:49
  57.4 0.1 dynamic_slice.15
  57.5 0.1 collective-permute-start.22
  57.6 0.7 collective-permute-done.17.refs_4_
  58.3 0.8 collective-permute-start.18
  59.1 0.7 collective-permute-start.20
  59.8 6.1 %third.1 = (f32[3,2,1024,128]{3,2,1,0:T(8,128)S(1)}, f32[3,2,16,128]{3,2,1,0:T(8,128)S(1)}, bf16[1040,1024]{1,0:T(8,128)(2,1)S(1)}) custom-call(s32[3]{0:T(128)S(1)} %pad_add_fusion.where, bf16[3,256,256]{2,1,0:T(8,128)(2,1)} %copy-done.10, bf16[3,256,256]{2,1,0:T(8,128)(2,1)} %copy-done.3, bf16[3,256,256]{2,1,0:T(8,128)(2,1)} %copy-done.4, ...), custom_call_target="tpu_custom_call" | custom-call | tf_op jit(solution)/shard_map/third/pallas_call | solution.py:295
  65.9 0.0 collective-permute-done.22.refs_5_
  65.9 0.0 collective-permute-done.18.refs_2_
  66.0 4.2 %collective-permute-done.20.refs_3_ = bf16[3,128,256]{2,1,0:T(8,128)(2,1)S(1)} collective-permute-done((bf16[3,128,256]{2,1,0:T(8,128)(2,1)S(1)}, bf16[3,128,256]{2,1,0:T(8,128)(2,1)S(1)}, u32[]{:S(2)}, u32[]{:S(2)}) %collective-permute-start.20) | collective-permute-done | bytes 196640 | tf_op jit(solution)/shard_map/ppermute | solution.py:49
  70.2 5.0 %signals.1 = (f32[128,8,256]{2,1,0:T(8,128)S(1)}, f32[16,8,256]{2,1,0:T(8,128)S(1)}, f32[16,256]{1,0:T(8,128)S(1)}) custom-call(bf16[1040,1024]{1,0:T(8,128)(2,1)S(1)} %get-tuple-element.100.rows, bf16[3,256,256]{2,1,0:T(8,128)(2,1)S(1)} %collective-permute-done.13.refs_0_, bf16[3,256,256]{2,1,0:T(8,128)(2,1)S(1)} %collective-permute-done.14.refs_1_, ...), custom_call_target="tpu_custom_call" | custom-call | tf_op jit(solution)/shard_map/signals/pallas_call | solution.py:386
  75.2 0.4 collective-permute-start.23
  75.5 1.4 %collective-permute-start.24 = (f32[16,256]{1,0:T(8,128)S(1)}, f32[16,256]{1,0:T(8,128)S(1)}, u32[]{:S(2)}, u32[]{:S(2)}) collective-permute-start(f32[16,256]{1,0:T(8,128)S(1)} %get-tuple-element.119), channel_id=1, source_target_pairs={{0,32},{8,40},{16,48},{24,56},{32,0},{40,8},{48,16},{56,24},{64,96... | collective-permute-start | bytes 49160 | tf_op jit(solution)/shard_map/ppermute | solution.py:49
  76.9 1.6 %collective-permute-start.25 = (f32[16,256]{1,0:T(8,128)S(1)}, f32[16,256]{1,0:T(8,128)S(1)}, u32[]{:S(2)}, u32[]{:S(2)}) collective-permute-start(f32[16,256]{1,0:T(8,128)S(1)} %get-tuple-element.119), channel_id=1, source_target_pairs={{0,48},{8,56},{16,0},{24,8},{32,16},{40,24},{48,32},{56,40},{64,11... | collective-permute-start | bytes 49160 | tf_op jit(solution)/shard_map/ppermute | solution.py:49
  78.5 1.1 %collective-permute-done.23 = f32[16,256]{1,0:T(8,128)S(1)} collective-permute-done((f32[16,256]{1,0:T(8,128)S(1)}, f32[16,256]{1,0:T(8,128)S(1)}, u32[]{:S(2)}, u32[]{:S(2)}) %collective-permute-start.23) | collective-permute-done | bytes 16416 | tf_op jit(solution)/shard_map/ppermute | solution.py:49
  79.6 0.3 collective-permute-done.25
  79.9 0.1 collective-permute-start.26
  80.0 1.5 %collective-permute-start.27 = (f32[16,256]{1,0:T(8,128)S(1)}, f32[16,256]{1,0:T(8,128)S(1)}, u32[]{:S(2)}, u32[]{:S(2)}) collective-permute-start(f32[16,256]{1,0:T(8,128)S(1)} %fusion.2), channel_id=1, source_target_pairs={{0,128},{8,136},{16,144},{24,152},{32,160},{40,168},{48,176},{56,1... | collective-permute-start | bytes 49160 | tf_op jit(solution)/shard_map/ppermute | solution.py:49
  81.5 1.8 %collective-permute-start.28 = (f32[16,256]{1,0:T(8,128)S(1)}, f32[16,256]{1,0:T(8,128)S(1)}, u32[]{:S(2)}, u32[]{:S(2)}) collective-permute-start(f32[16,256]{1,0:T(8,128)S(1)} %fusion.2), channel_id=1, source_target_pairs={{0,192},{8,200},{16,208},{24,216},{32,224},{40,232},{48,240},{56,2... | collective-permute-start | bytes 49160 | tf_op jit(solution)/shard_map/ppermute | solution.py:49
  83.3 1.5 %queries.1 = (f32[128,8,256]{2,1,0:T(8,128)S(1)}, f32[128,8,256]{2,1,0:T(8,128)S(1)}) custom-call(bf16[1040,1024]{1,0:T(8,128)(2,1)S(1)} %get-tuple-element.100.rows, bf16[3,256,256]{2,1,0:T(8,128)(2,1)S(1)} %collective-permute-done.13.refs_0_, bf16[3,256,256]{2,1,0:T(8,128)(2,1)S(1)} %collective-permute-done.14.refs_1_, ...), custom_call_target="tpu_custom_call" | custom-call | tf_op jit(solution)/shard_map/queries/pallas_call | solution.py:430
  84.8 1.9 %gated.1 = (bf16[512,256]{1,0:T(8,128)(2,1)S(1)}, bf16[512,256]{1,0:T(8,128)(2,1)S(1)}) custom-call(s32[3]{0:T(128)S(1)} %pad_add_fusion.where, f32[128,8,256]{2,1,0:T(8,128)S(1)} %get-tuple-element.115.query, f32[128,8,256]{2,1,0:T(8,128)S(1)} %get-tuple-element.116.gated, f32[16,8,256]{2,1,0:T(8,128)S(1)} %get-tuple-element.117.before, ...), custom_call_target="tpu_custom_call" | custom-call | tf_op jit(solution)/shard_map/gated/pallas_call | solution.py:496
  86.7 6.1 %collective-permute-start.29 = (bf16[512,256]{1,0:T(8,128)(2,1)S(1)}, bf16[512,256]{1,0:T(8,128)(2,1)S(1)}, u32[]{:S(2)}, u32[]{:S(2)}) collective-permute-start(bf16[512,256]{1,0:T(8,128)(2,1)S(1)} %get-tuple-element.122), channel_id=1, source_target_pairs={{0,8},{8,0},{16,24},{24,16},{32,40},{40,32},{48,56},{56,48},{64,72... | collective-permute-start | bytes 786440 | tf_op jit(solution)/shard_map/ppermute | solution.py:49
  92.8 1.2 %collective-permute-done.29 = bf16[512,256]{1,0:T(8,128)(2,1)S(1)} collective-permute-done((bf16[512,256]{1,0:T(8,128)(2,1)S(1)}, bf16[512,256]{1,0:T(8,128)(2,1)S(1)}, u32[]{:S(2)}, u32[]{:S(2)}) %collective-permute-start.29) | collective-permute-done | bytes 262176 | tf_op jit(solution)/shard_map/ppermute | solution.py:49
  94.0 0.8 pad_maximum_fusion
  (70 shorter events, 0.4 us)
Async XLA Ops:
  0.0 43.0 %copy-start = (f32[3,7,512]{2,1,0:T(8,128)S(1)}, f32[3,7,512]{2,1,0:T(8,128)}, u32[]{:S(2)}) copy-start(f32[3,7,512]{2,1,0:T(8,128)} %param.8) | copy-start | bytes 129028
  0.0 23.1 %copy-start.16 = (f32[512,16]{0,1:T(8,128)S(1)}, f32[512,16]{0,1:T(8,128)}, u32[]{:S(2)}) copy-start(f32[512,16]{0,1:T(8,128)} %param.10) | copy-start | bytes 98308
  1.1 4.4 %collective-permute-start = (bf16[3,128,256]{2,1,0:T(8,128)(2,1)S(1)}, bf16[3,128,256]{2,1,0:T(8,128)(2,1)S(1)}, u32[]{:S(2)}, u32[]{:S(2)}) collective-permute-start(bf16[3,128,256]{2,1,0:T(8,128)(2,1)S(1)} %broadcast_select_fusion.4), channel_id=1, source_target_pairs={{0,8},{8,0},{16,24},{24,16},{32,40},{40,32},{48,56},{56,48},{64,72... | collective-permute-start | bytes 589832 | tf_op jit(solution)/shard_map/ppermute | solution.py:49
  5.5 14.9 %collective-permute-start.4 = (bf16[512,4096]{1,0:T(8,128)(2,1)}, bf16[512,4096]{1,0:T(8,128)(2,1)}, u32[]{:S(2)}, u32[]{:S(2)}) collective-permute-start(bf16[512,4096]{1,0:T(8,128)(2,1)} %refs_6_.1), channel_id=1, source_target_pairs={{0,8},{8,0},{16,24},{24,16},{32,40},{40,32},{48,56},{56,48},{64,72... | collective-permute-start | bytes 12582920 | tf_op jit(solution)/shard_map/ppermute | solution.py:49
  6.9 19.4 %copy-start.5 = (bf16[3,256,256]{2,1,0:T(8,128)(2,1)}, bf16[3,256,256]{2,1,0:T(8,128)(2,1)S(1)}, u32[]{:S(2)}) copy-start(bf16[3,256,256]{2,1,0:T(8,128)(2,1)S(1)} %pad_maximum_fusion.1.refs_0_) | copy-start | bytes 1179652
  8.0 4.8 %collective-permute-start.9 = (bf16[16,4096]{1,0:T(8,128)(2,1)S(1)}, bf16[16,4096]{1,0:T(8,128)(2,1)S(1)}, u32[]{:S(2)}, u32[]{:S(2)}) collective-permute-start(bf16[16,4096]{1,0:T(8,128)(2,1)S(1)} %slice.54), channel_id=1, source_target_pairs={{0,8},{8,0},{16,24},{24,16},{32,40},{40,32},{48,56},{56,48},{64,72... | collective-permute-start | bytes 393224 | tf_op jit(solution)/shard_map/ppermute | solution.py:49
  8.3 10.4 %collective-permute-start.1 = (bf16[3,256,256]{2,1,0:T(8,128)(2,1)S(1)}, bf16[3,256,256]{2,1,0:T(8,128)(2,1)S(1)}, u32[]{:S(2)}, u32[]{:S(2)}) collective-permute-start(bf16[3,256,256]{2,1,0:T(8,128)(2,1)S(1)} %pad_maximum_fusion.1.refs_0_), channel_id=1, source_target_pairs={{0,16},{8,24},{16,0},{24,8},{32,48},{40,56},{48,32},{56,40},{64,80... | collective-permute-start | bytes 1179656 | tf_op jit(solution)/shard_map/ppermute | solution.py:49
  8.4 11.9 %collective-permute-start.2 = (bf16[3,256,256]{2,1,0:T(8,128)(2,1)S(1)}, bf16[3,256,256]{2,1,0:T(8,128)(2,1)S(1)}, u32[]{:S(2)}, u32[]{:S(2)}) collective-permute-start(bf16[3,256,256]{2,1,0:T(8,128)(2,1)S(1)} %pad_maximum_fusion.1.refs_0_), channel_id=1, source_target_pairs={{0,64},{8,72},{16,80},{24,88},{32,96},{40,104},{48,112},{56,120},{... | collective-permute-start | bytes 1179656 | tf_op jit(solution)/shard_map/ppermute | solution.py:49
  9.5 10.9 %collective-permute-start.3 = (bf16[3,256,256]{2,1,0:T(8,128)(2,1)S(1)}, bf16[3,256,256]{2,1,0:T(8,128)(2,1)S(1)}, u32[]{:S(2)}, u32[]{:S(2)}) collective-permute-start(bf16[3,256,256]{2,1,0:T(8,128)(2,1)S(1)} %pad_maximum_fusion.1.refs_0_), channel_id=1, source_target_pairs={{0,192},{8,200},{16,208},{24,216},{32,224},{40,232},{48,240},{56,2... | collective-permute-start | bytes 1179656 | tf_op jit(solution)/shard_map/ppermute | solution.py:49
  13.7 9.8 %collective-permute-start.11 = (bf16[16,4096]{1,0:T(8,128)(2,1)S(1)}, bf16[16,4096]{1,0:T(8,128)(2,1)S(1)}, u32[]{:S(2)}, u32[]{:S(2)}) collective-permute-start(bf16[16,4096]{1,0:T(8,128)(2,1)S(1)} %broadcast_select_fusion.5), channel_id=1, source_target_pairs={{0,16},{8,24},{16,32},{24,40},{32,48},{40,56},{48,64},{56,72},{64,... | collective-permute-start | bytes 393224 | tf_op jit(solution)/shard_map/ppermute | solution.py:49
  18.7 26.2 %copy-start.7 = (bf16[3,256,256]{2,1,0:T(8,128)(2,1)}, bf16[3,256,256]{2,1,0:T(8,128)(2,1)S(1)}, u32[]{:S(2)}) copy-start(bf16[3,256,256]{2,1,0:T(8,128)(2,1)S(1)} %collective-permute-done.1.refs_0_) | copy-start | bytes 1179652
  18.7 21.5 %collective-permute-start.10 = (bf16[3,256,256]{2,1,0:T(8,128)(2,1)S(1)}, bf16[3,256,256]{2,1,0:T(8,128)(2,1)S(1)}, u32[]{:S(2)}, u32[]{:S(2)}) collective-permute-start(bf16[3,256,256]{2,1,0:T(8,128)(2,1)S(1)} %pad_maximum_fusion.1.refs_0_), channel_id=1, source_target_pairs={{0,32},{8,40},{16,48},{24,56},{32,0},{40,8},{48,16},{56,24},{64,96... | collective-permute-start | bytes 1179656 | tf_op jit(solution)/shard_map/ppermute | solution.py:49
  20.3 6.0 %copy-start.1 = (bf16[3,256,256]{2,1,0:T(8,128)(2,1)}, bf16[3,256,256]{2,1,0:T(8,128)(2,1)S(1)}, u32[]{:S(2)}) copy-start(bf16[3,256,256]{2,1,0:T(8,128)(2,1)S(1)} %collective-permute-done.2.right.refs_1_) | copy-start | bytes 1179652
  20.3 6.0 %copy-start.2 = (bf16[3,256,256]{2,1,0:T(8,128)(2,1)}, bf16[3,256,256]{2,1,0:T(8,128)(2,1)S(1)}, u32[]{:S(2)}) copy-start(bf16[3,256,256]{2,1,0:T(8,128)(2,1)S(1)} %collective-permute-done.3.left.refs_2_) | copy-start | bytes 1179652
  20.3 19.9 %collective-permute-start.5 = (bf16[3,256,256]{2,1,0:T(8,128)(2,1)S(1)}, bf16[3,256,256]{2,1,0:T(8,128)(2,1)S(1)}, u32[]{:S(2)}, u32[]{:S(2)}) collective-permute-start(bf16[3,256,256]{2,1,0:T(8,128)(2,1)S(1)} %collective-permute-done.1.refs_0_), channel_id=1, source_target_pairs={{0,64},{8,72},{16,80},{24,88},{32,96},{40,104},{48,112},{56,120},{... | collective-permute-start | bytes 1179656 | tf_op jit(solution)/shard_map/ppermute | solution.py:49
  21.6 18.6 %collective-permute-start.6 = (bf16[3,256,256]{2,1,0:T(8,128)(2,1)S(1)}, bf16[3,256,256]{2,1,0:T(8,128)(2,1)S(1)}, u32[]{:S(2)}, u32[]{:S(2)}) collective-permute-start(bf16[3,256,256]{2,1,0:T(8,128)(2,1)S(1)} %collective-permute-done.1.refs_0_), channel_id=1, source_target_pairs={{0,192},{8,200},{16,208},{24,216},{32,224},{40,232},{48,240},{56,2... | collective-permute-start | bytes 1179656 | tf_op jit(solution)/shard_map/ppermute | solution.py:49
  23.3 16.8 %collective-permute-start.7 = (bf16[3,128,256]{2,1,0:T(8,128)(2,1)S(1)}, bf16[3,128,256]{2,1,0:T(8,128)(2,1)S(1)}, u32[]{:S(2)}, u32[]{:S(2)}) collective-permute-start(bf16[3,128,256]{2,1,0:T(8,128)(2,1)S(1)} %get-tuple-element.69), channel_id=1, source_target_pairs={{0,64},{8,72},{16,80},{24,88},{32,96},{40,104},{48,112},{56,120},{... | collective-permute-start | bytes 589832 | tf_op jit(solution)/shard_map/ppermute | solution.py:49
  23.5 2.8 %copy-start.6 = (bf16[16,4096]{1,0:T(8,128)(2,1)}, bf16[16,4096]{1,0:T(8,128)(2,1)S(1)}, u32[]{:S(2)}) copy-start(bf16[16,4096]{1,0:T(8,128)(2,1)S(1)} %collective-permute-done.11.refs_5_.refs_7_.refs_8_) | copy-start | bytes 393220
  23.6 16.6 %collective-permute-start.8 = (bf16[3,128,256]{2,1,0:T(8,128)(2,1)S(1)}, bf16[3,128,256]{2,1,0:T(8,128)(2,1)S(1)}, u32[]{:S(2)}, u32[]{:S(2)}) collective-permute-start(bf16[3,128,256]{2,1,0:T(8,128)(2,1)S(1)} %get-tuple-element.70), channel_id=1, source_target_pairs={{0,192},{8,200},{16,208},{24,216},{32,224},{40,232},{48,240},{56,2... | collective-permute-start | bytes 589832 | tf_op jit(solution)/shard_map/ppermute | solution.py:49
  40.2 19.6 %copy-start.10 = (bf16[3,256,256]{2,1,0:T(8,128)(2,1)}, bf16[3,256,256]{2,1,0:T(8,128)(2,1)S(1)}, u32[]{:S(2)}) copy-start(bf16[3,256,256]{2,1,0:T(8,128)(2,1)S(1)} %collective-permute-done.10.refs_0_) | copy-start | bytes 1179652
  40.2 4.7 %copy-start.13 = (bf16[3,128,256]{2,1,0:T(8,128)(2,1)}, bf16[3,128,256]{2,1,0:T(8,128)(2,1)S(1)}, u32[]{:S(2)}) copy-start(bf16[3,128,256]{2,1,0:T(8,128)(2,1)S(1)} %collective-permute-done.7.refs_3_) | copy-start | bytes 589828
  40.2 4.7 %copy-start.12 = (bf16[3,128,256]{2,1,0:T(8,128)(2,1)}, bf16[3,128,256]{2,1,0:T(8,128)(2,1)S(1)}, u32[]{:S(2)}) copy-start(bf16[3,128,256]{2,1,0:T(8,128)(2,1)S(1)} %collective-permute-done.8.refs_4_) | copy-start | bytes 589828
  40.2 4.7 %copy-start.8 = (bf16[3,256,256]{2,1,0:T(8,128)(2,1)}, bf16[3,256,256]{2,1,0:T(8,128)(2,1)S(1)}, u32[]{:S(2)}) copy-start(bf16[3,256,256]{2,1,0:T(8,128)(2,1)S(1)} %collective-permute-done.5.refs_1_) | copy-start | bytes 1179652
  40.2 4.7 %copy-start.9 = (bf16[3,256,256]{2,1,0:T(8,128)(2,1)}, bf16[3,256,256]{2,1,0:T(8,128)(2,1)S(1)}, u32[]{:S(2)}) copy-start(bf16[3,256,256]{2,1,0:T(8,128)(2,1)S(1)} %collective-permute-done.6.refs_2_) | copy-start | bytes 1179652
  40.3 11.5 %collective-permute-start.15 = (bf16[3,256,256]{2,1,0:T(8,128)(2,1)S(1)}, bf16[3,256,256]{2,1,0:T(8,128)(2,1)S(1)}, u32[]{:S(2)}, u32[]{:S(2)}) collective-permute-start(bf16[3,256,256]{2,1,0:T(8,128)(2,1)S(1)} %collective-permute-done.10.refs_0_), channel_id=1, source_target_pairs={{0,64},{8,72},{16,80},{24,88},{32,96},{40,104},{48,112},{56,120},{... | collective-permute-start | bytes 1179656 | tf_op jit(solution)/shard_map/ppermute | solution.py:49
  41.5 10.2 %collective-permute-start.16 = (bf16[3,256,256]{2,1,0:T(8,128)(2,1)S(1)}, bf16[3,256,256]{2,1,0:T(8,128)(2,1)S(1)}, u32[]{:S(2)}, u32[]{:S(2)}) collective-permute-start(bf16[3,256,256]{2,1,0:T(8,128)(2,1)S(1)} %collective-permute-done.10.refs_0_), channel_id=1, source_target_pairs={{0,192},{8,200},{16,208},{24,216},{32,224},{40,232},{48,240},{56,2... | collective-permute-start | bytes 1179656 | tf_op jit(solution)/shard_map/ppermute | solution.py:49
  43.0 11.7 %collective-permute-start.12 = (bf16[3,256,256]{2,1,0:T(8,128)(2,1)S(1)}, bf16[3,256,256]{2,1,0:T(8,128)(2,1)S(1)}, u32[]{:S(2)}, u32[]{:S(2)}) collective-permute-start(bf16[3,256,256]{2,1,0:T(8,128)(2,1)S(1)} %collective-permute-done.10.refs_0_), channel_id=1, source_target_pairs={{0,16},{8,24},{16,0},{24,8},{32,48},{40,56},{48,32},{56,40},{64,80... | collective-permute-start | bytes 1179656 | tf_op jit(solution)/shard_map/ppermute | solution.py:49
  43.2 14.2 %copy-start.17 = (f32[512,16]{0,1:T(8,128)S(1)}, f32[512,16]{0,1:T(8,128)}, u32[]{:S(2)}) copy-start(f32[512,16]{0,1:T(8,128)} %param.9) | copy-start | bytes 98308
  43.2 14.2 %copy-start.18 = (f32[512]{0:T(512)S(1)}, f32[512]{0:T(512)}, u32[]{:S(2)}) copy-start(f32[512]{0:T(512)} %param.11) | copy-start | bytes 6148
  43.2 14.3 %collective-permute-start.21 = (bf16[3,128,256]{2,1,0:T(8,128)(2,1)S(1)}, bf16[3,128,256]{2,1,0:T(8,128)(2,1)S(1)}, u32[]{:S(2)}, u32[]{:S(2)}) collective-permute-start(bf16[3,128,256]{2,1,0:T(8,128)(2,1)S(1)} %collective-permute-done.7.refs_3_), channel_id=1, source_target_pairs={{0,16},{8,24},{16,0},{24,8},{32,48},{40,56},{48,32},{56,40},{64,80... | collective-permute-start | bytes 589832 | tf_op jit(solution)/shard_map/ppermute | solution.py:49
  51.7 8.0 %copy-start.3 = (bf16[3,256,256]{2,1,0:T(8,128)(2,1)}, bf16[3,256,256]{2,1,0:T(8,128)(2,1)S(1)}, u32[]{:S(2)}) copy-start(bf16[3,256,256]{2,1,0:T(8,128)(2,1)S(1)} %collective-permute-done.15.right.refs_1_) | copy-start | bytes 1179652
  51.7 8.1 %copy-start.4 = (bf16[3,256,256]{2,1,0:T(8,128)(2,1)}, bf16[3,256,256]{2,1,0:T(8,128)(2,1)S(1)}, u32[]{:S(2)}) copy-start(bf16[3,256,256]{2,1,0:T(8,128)(2,1)S(1)} %collective-permute-done.16.left.refs_2_) | copy-start | bytes 1179652
  51.9 6.3 %collective-permute-start.17 = (bf16[3,128,256]{2,1,0:T(8,128)(2,1)S(1)}, bf16[3,128,256]{2,1,0:T(8,128)(2,1)S(1)}, u32[]{:S(2)}, u32[]{:S(2)}) collective-permute-start(bf16[3,128,256]{2,1,0:T(8,128)(2,1)S(1)} %get-tuple-element.89), channel_id=1, source_target_pairs={{0,64},{8,72},{16,80},{24,88},{32,96},{40,104},{48,112},{56,120},{... | collective-permute-start | bytes 589832 | tf_op jit(solution)/shard_map/ppermute | solution.py:49
  52.9 6.2 %collective-permute-start.19 = (bf16[3,128,256]{2,1,0:T(8,128)(2,1)S(1)}, bf16[3,128,256]{2,1,0:T(8,128)(2,1)S(1)}, u32[]{:S(2)}, u32[]{:S(2)}) collective-permute-start(bf16[3,128,256]{2,1,0:T(8,128)(2,1)S(1)} %get-tuple-element.90), channel_id=1, source_target_pairs={{0,192},{8,200},{16,208},{24,216},{32,224},{40,232},{48,240},{56,2... | collective-permute-start | bytes 589832 | tf_op jit(solution)/shard_map/ppermute | solution.py:49
  54.7 5.1 %copy-start.11 = (bf16[3,256,256]{2,1,0:T(8,128)(2,1)}, bf16[3,256,256]{2,1,0:T(8,128)(2,1)S(1)}, u32[]{:S(2)}) copy-start(bf16[3,256,256]{2,1,0:T(8,128)(2,1)S(1)} %collective-permute-done.12.refs_3_) | copy-start | bytes 1179652
  54.7 15.5 %collective-permute-start.13 = (bf16[3,256,256]{2,1,0:T(8,128)(2,1)S(1)}, bf16[3,256,256]{2,1,0:T(8,128)(2,1)S(1)}, u32[]{:S(2)}, u32[]{:S(2)}) collective-permute-start(bf16[3,256,256]{2,1,0:T(8,128)(2,1)S(1)} %collective-permute-done.12.refs_3_), channel_id=1, source_target_pairs={{0,64},{8,72},{16,80},{24,88},{32,96},{40,104},{48,112},{56,120},{... | collective-permute-start | bytes 1179656 | tf_op jit(solution)/shard_map/ppermute | solution.py:49
  54.7 15.5 %collective-permute-start.14 = (bf16[3,256,256]{2,1,0:T(8,128)(2,1)S(1)}, bf16[3,256,256]{2,1,0:T(8,128)(2,1)S(1)}, u32[]{:S(2)}, u32[]{:S(2)}) collective-permute-start(bf16[3,256,256]{2,1,0:T(8,128)(2,1)S(1)} %collective-permute-done.12.refs_3_), channel_id=1, source_target_pairs={{0,192},{8,200},{16,208},{24,216},{32,224},{40,232},{48,240},{56,2... | collective-permute-start | bytes 1179656 | tf_op jit(solution)/shard_map/ppermute | solution.py:49
  57.5 8.4 %collective-permute-start.22 = (bf16[3,128,256]{2,1,0:T(8,128)(2,1)}, bf16[3,128,256]{2,1,0:T(8,128)(2,1)S(1)}, u32[]{:S(2)}, u32[]{:S(2)}) collective-permute-start(bf16[3,128,256]{2,1,0:T(8,128)(2,1)} %copy-done.12), channel_id=1, source_target_pairs={{0,16},{8,24},{16,0},{24,8},{32,48},{40,56},{48,32},{56,40},{64,80... | collective-permute-start | bytes 589832 | tf_op jit(solution)/shard_map/ppermute | solution.py:49
  58.3 1.5 %copy-start.14 = (bf16[3,128,256]{2,1,0:T(8,128)(2,1)}, bf16[3,128,256]{2,1,0:T(8,128)(2,1)S(1)}, u32[]{:S(2)}) copy-start(bf16[3,128,256]{2,1,0:T(8,128)(2,1)S(1)} %collective-permute-done.17.refs_4_) | copy-start | bytes 589828
  58.3 7.7 %collective-permute-start.18 = (bf16[3,128,256]{2,1,0:T(8,128)(2,1)S(1)}, bf16[3,128,256]{2,1,0:T(8,128)(2,1)S(1)}, u32[]{:S(2)}, u32[]{:S(2)}) collective-permute-start(bf16[3,128,256]{2,1,0:T(8,128)(2,1)S(1)} %collective-permute-done.17.refs_4_), channel_id=1, source_target_pairs={{0,16},{8,24},{16,0},{24,8},{32,48},{40,56},{48,32},{56,40},{64,80... | collective-permute-start | bytes 589832 | tf_op jit(solution)/shard_map/ppermute | solution.py:49
  59.0 0.8 copy-start.15
  59.1 11.1 %collective-permute-start.20 = (bf16[3,128,256]{2,1,0:T(8,128)(2,1)S(1)}, bf16[3,128,256]{2,1,0:T(8,128)(2,1)S(1)}, u32[]{:S(2)}, u32[]{:S(2)}) collective-permute-start(bf16[3,128,256]{2,1,0:T(8,128)(2,1)S(1)} %collective-permute-done.19.refs_5_), channel_id=1, source_target_pairs={{0,16},{8,24},{16,0},{24,8},{32,48},{40,56},{48,32},{56,40},{64,80... | collective-permute-start | bytes 589832 | tf_op jit(solution)/shard_map/ppermute | solution.py:49
  75.2 4.5 %collective-permute-start.23 = (f32[16,256]{1,0:T(8,128)S(1)}, f32[16,256]{1,0:T(8,128)S(1)}, u32[]{:S(2)}, u32[]{:S(2)}) collective-permute-start(f32[16,256]{1,0:T(8,128)S(1)} %get-tuple-element.119), channel_id=1, source_target_pairs={{0,16},{8,24},{16,32},{24,40},{32,48},{40,56},{48,0},{56,8},{64,80... | collective-permute-start | bytes 49160 | tf_op jit(solution)/shard_map/ppermute | solution.py:49
  75.5 4.1 %collective-permute-start.24 = (f32[16,256]{1,0:T(8,128)S(1)}, f32[16,256]{1,0:T(8,128)S(1)}, u32[]{:S(2)}, u32[]{:S(2)}) collective-permute-start(f32[16,256]{1,0:T(8,128)S(1)} %get-tuple-element.119), channel_id=1, source_target_pairs={{0,32},{8,40},{16,48},{24,56},{32,0},{40,8},{48,16},{56,24},{64,96... | collective-permute-start | bytes 49160 | tf_op jit(solution)/shard_map/ppermute | solution.py:49
  76.9 3.0 %collective-permute-start.25 = (f32[16,256]{1,0:T(8,128)S(1)}, f32[16,256]{1,0:T(8,128)S(1)}, u32[]{:S(2)}, u32[]{:S(2)}) collective-permute-start(f32[16,256]{1,0:T(8,128)S(1)} %get-tuple-element.119), channel_id=1, source_target_pairs={{0,48},{8,56},{16,0},{24,8},{32,16},{40,24},{48,32},{56,40},{64,11... | collective-permute-start | bytes 49160 | tf_op jit(solution)/shard_map/ppermute | solution.py:49
  79.9 4.8 %collective-permute-start.26 = (f32[16,256]{1,0:T(8,128)S(1)}, f32[16,256]{1,0:T(8,128)S(1)}, u32[]{:S(2)}, u32[]{:S(2)}) collective-permute-start(f32[16,256]{1,0:T(8,128)S(1)} %fusion.2), channel_id=1, source_target_pairs={{0,64},{8,72},{16,80},{24,88},{32,96},{40,104},{48,112},{56,120},{... | collective-permute-start | bytes 49160 | tf_op jit(solution)/shard_map/ppermute | solution.py:49
  80.0 4.8 %collective-permute-start.27 = (f32[16,256]{1,0:T(8,128)S(1)}, f32[16,256]{1,0:T(8,128)S(1)}, u32[]{:S(2)}, u32[]{:S(2)}) collective-permute-start(f32[16,256]{1,0:T(8,128)S(1)} %fusion.2), channel_id=1, source_target_pairs={{0,128},{8,136},{16,144},{24,152},{32,160},{40,168},{48,176},{56,1... | collective-permute-start | bytes 49160 | tf_op jit(solution)/shard_map/ppermute | solution.py:49
  81.5 3.2 %collective-permute-start.28 = (f32[16,256]{1,0:T(8,128)S(1)}, f32[16,256]{1,0:T(8,128)S(1)}, u32[]{:S(2)}, u32[]{:S(2)}) collective-permute-start(f32[16,256]{1,0:T(8,128)S(1)} %fusion.2), channel_id=1, source_target_pairs={{0,192},{8,200},{16,208},{24,216},{32,224},{40,232},{48,240},{56,2... | collective-permute-start | bytes 49160 | tf_op jit(solution)/shard_map/ppermute | solution.py:49
  86.7 7.2 %collective-permute-start.29 = (bf16[512,256]{1,0:T(8,128)(2,1)S(1)}, bf16[512,256]{1,0:T(8,128)(2,1)S(1)}, u32[]{:S(2)}, u32[]{:S(2)}) collective-permute-start(bf16[512,256]{1,0:T(8,128)(2,1)S(1)} %get-tuple-element.122), channel_id=1, source_target_pairs={{0,8},{8,0},{16,24},{24,16},{32,40},{40,32},{48,56},{56,48},{64,72... | collective-permute-start | bytes 786440 | tf_op jit(solution)/shard_map/ppermute | solution.py:49

commit v7 on v6

--- a/solution.py
+++ b/solution.py
@@ -587,9 +587,7 @@
     pieces = with_sides(0, block, right, left)
     products = partial_products(where, pieces, both, (halo,), (), "first")
     right, left = sides(beside)
-    right, left, *far, over, products, halo_products = together(
-        right, left, *far, over, *products
-    )
+    *far, over, products, halo_products = together(*far, over, *products)
 
     opposite = across_z(over, 1)
     far_beside = across_z(far[0], 1), across_z(far[1], 1)

time: 95.1 us -> 95 us (level)
  no operation moved by 1% of the time
where the time goes in v7:
time: 95 us; the launch traced here: 94.8 us
  starting transfers between devices  40 us (42%)
  waiting for transfers between devices  24.6 us (26%)
  Pallas kernels  23.5 us (25%)
  other arithmetic  4.31 us (5%)
  local copies, waits for them, and re-layouts  1.96 us (2%)
    ppermute x30, starting transfers between devices, permute(): return lax.ppermute(value, 'seq', pairs)  40 us
    ppermute x30, waiting for transfers between devices, permute(): return lax.ppermute(value, 'seq', pairs)  24.6 us
    pallas_call x3, Pallas kernels, partial_products(): pl.pallas_call(functools.partial(partial_kernel, plan, bool(tokens), bool...  14.8 us
    pallas_call x1, Pallas kernels, signals(): pl.pallas_call(functools.partial(signal_kernel, len(last)), out_shape=(pl...  5 us
  transfers between devices with their start and end apart: 30, of which 10 were waited for; matrix products, arithmetic and copies ran while one was open for 4% of the time, Pallas kernels for 18%

profile of v7, /device:TPU:1, one launch (start us, length us, event | category | flops | bytes accessed | tf_op | source)
XLA Modules:
  0.0 94.8 jit_solution(7198655703289940188)
XLA Ops:
  0.0 1.1 %broadcast_select_fusion.4 = bf16[3,128,256]{2,1,0:T(8,128)(2,1)S(1)} fusion(pred[]{:T(512)S(6)} %eq.6, bf16[3,128,512]{2,1,0:T(8,128)(2,1)} %param.7), kind=kLoop, calls=%fused_computation.6 | loop fusion | flops 98304 | bytes 589825 | tf_op jit(solution)/shard_map/jit(_where)/select_n | solution.py:555
  1.1 3.3 %collective-permute-start = (bf16[3,128,256]{2,1,0:T(8,128)(2,1)S(1)}, bf16[3,128,256]{2,1,0:T(8,128)(2,1)S(1)}, u32[]{:S(2)}, u32[]{:S(2)}) collective-permute-start(bf16[3,128,256]{2,1,0:T(8,128)(2,1)S(1)} %broadcast_select_fusion.4), channel_id=1, source_target_pairs={{0,8},{8,0},{16,24},{24,16},{32,40},{40,32},{48,56},{56,48},{64,72... | collective-permute-start | bytes 589832 | tf_op jit(solution)/shard_map/ppermute | solution.py:49
  4.4 1.1 %collective-permute-done = bf16[3,128,256]{2,1,0:T(8,128)(2,1)S(1)} collective-permute-done((bf16[3,128,256]{2,1,0:T(8,128)(2,1)S(1)}, bf16[3,128,256]{2,1,0:T(8,128)(2,1)S(1)}, u32[]{:S(2)}, u32[]{:S(2)}) %collective-permute-start) | collective-permute-done | bytes 196640 | tf_op jit(solution)/shard_map/ppermute | solution.py:49
  5.5 0.4 collective-permute-start.4
  5.8 1.1 %broadcast_select_fusion.3 = (bf16[3,128,256]{2,1,0:T(8,128)(2,1)S(1)}, bf16[3,128,256]{2,1,0:T(8,128)(2,1)S(1)}) fusion(bf16[3,128,256]{2,1,0:T(8,128)(2,1)S(1)} %collective-permute-done, pred[]{:T(512)S(6)} %eq.6, bf16[3,128,512]{2,1,0:T(8,128)(2,1)} %param.7), kind=kLoop, calls=%fused_computation.5 | loop fusion | flops 196608 | bytes 983041 | tf_op jit(solution)/shard_map/jit(_where)/select_n | solution.py:557
  6.9 0.0 copy-start.5
  6.9 1.1 %slice.54 = bf16[16,4096]{1,0:T(8,128)(2,1)S(1)} slice(bf16[512,4096]{1,0:T(8,128)(2,1)} %refs_6_.1), slice={[496:512], [0:4096]} | slice | bytes 262144 | tf_op jit(solution)/shard_map/slice | solution.py:564
  8.0 0.2 collective-permute-start.7
  8.2 0.1 pad_add_fusion.where
  8.3 0.0 collective-permute-start.1
  8.4 1.1 %collective-permute-start.2 = (bf16[3,256,256]{2,1,0:T(8,128)(2,1)S(1)}, bf16[3,256,256]{2,1,0:T(8,128)(2,1)S(1)}, u32[]{:S(2)}, u32[]{:S(2)}) collective-permute-start(bf16[3,256,256]{2,1,0:T(8,128)(2,1)S(1)} %pad_maximum_fusion.1.refs_0_), channel_id=1, source_target_pairs={{0,64},{8,72},{16,80},{24,88},{32,96},{40,104},{48,112},{56,120},{... | collective-permute-start | bytes 1179656 | tf_op jit(solution)/shard_map/ppermute | solution.py:49
  9.5 1.7 %collective-permute-start.3 = (bf16[3,256,256]{2,1,0:T(8,128)(2,1)S(1)}, bf16[3,256,256]{2,1,0:T(8,128)(2,1)S(1)}, u32[]{:S(2)}, u32[]{:S(2)}) collective-permute-start(bf16[3,256,256]{2,1,0:T(8,128)(2,1)S(1)} %pad_maximum_fusion.1.refs_0_), channel_id=1, source_target_pairs={{0,192},{8,200},{16,208},{24,216},{32,224},{40,232},{48,240},{56,2... | collective-permute-start | bytes 1179656 | tf_op jit(solution)/shard_map/ppermute | solution.py:49
  11.1 1.7 %collective-permute-done.7 = bf16[16,4096]{1,0:T(8,128)(2,1)S(1)} collective-permute-done((bf16[16,4096]{1,0:T(8,128)(2,1)S(1)}, bf16[16,4096]{1,0:T(8,128)(2,1)S(1)}, u32[]{:S(2)}, u32[]{:S(2)}) %collective-permute-start.7) | collective-permute-done | bytes 131104 | tf_op jit(solution)/shard_map/ppermute | solution.py:49
  12.8 0.9 broadcast_select_fusion.5
  13.7 1.8 %collective-permute-start.9 = (bf16[16,4096]{1,0:T(8,128)(2,1)S(1)}, bf16[16,4096]{1,0:T(8,128)(2,1)S(1)}, u32[]{:S(2)}, u32[]{:S(2)}) collective-permute-start(bf16[16,4096]{1,0:T(8,128)(2,1)S(1)} %broadcast_select_fusion.5), channel_id=1, source_target_pairs={{0,16},{8,24},{16,32},{24,40},{32,48},{40,56},{48,64},{56,72},{64,... | collective-permute-start | bytes 393224 | tf_op jit(solution)/shard_map/ppermute | solution.py:49
  15.6 3.1 %collective-permute-done.1.refs_0_ = bf16[3,256,256]{2,1,0:T(8,128)(2,1)S(1)} collective-permute-done((bf16[3,256,256]{2,1,0:T(8,128)(2,1)S(1)}, bf16[3,256,256]{2,1,0:T(8,128)(2,1)S(1)}, u32[]{:S(2)}, u32[]{:S(2)}) %collective-permute-start.1) | collective-permute-done | bytes 393248 | tf_op jit(solution)/shard_map/ppermute | solution.py:49
  18.7 1.6 %collective-permute-start.8 = (bf16[3,256,256]{2,1,0:T(8,128)(2,1)S(1)}, bf16[3,256,256]{2,1,0:T(8,128)(2,1)S(1)}, u32[]{:S(2)}, u32[]{:S(2)}) collective-permute-start(bf16[3,256,256]{2,1,0:T(8,128)(2,1)S(1)} %pad_maximum_fusion.1.refs_0_), channel_id=1, source_target_pairs={{0,32},{8,40},{16,48},{24,56},{32,0},{40,8},{48,16},{56,24},{64,96... | collective-permute-start | bytes 1179656 | tf_op jit(solution)/shard_map/ppermute | solution.py:49
  20.3 0.0 collective-permute-done.2.right.refs_1_
  20.3 0.0 collective-permute-done.3.left.refs_2_
  20.3 1.3 %collective-permute-start.15 = (bf16[3,256,256]{2,1,0:T(8,128)(2,1)S(1)}, bf16[3,256,256]{2,1,0:T(8,128)(2,1)S(1)}, u32[]{:S(2)}, u32[]{:S(2)}) collective-permute-start(bf16[3,256,256]{2,1,0:T(8,128)(2,1)S(1)} %collective-permute-done.1.refs_0_), channel_id=1, source_target_pairs={{0,64},{8,72},{16,80},{24,88},{32,96},{40,104},{48,112},{56,120},{... | collective-permute-start | bytes 1179656 | tf_op jit(solution)/shard_map/ppermute | solution.py:49
  21.6 1.5 %collective-permute-start.16 = (bf16[3,256,256]{2,1,0:T(8,128)(2,1)S(1)}, bf16[3,256,256]{2,1,0:T(8,128)(2,1)S(1)}, u32[]{:S(2)}, u32[]{:S(2)}) collective-permute-start(bf16[3,256,256]{2,1,0:T(8,128)(2,1)S(1)} %collective-permute-done.1.refs_0_), channel_id=1, source_target_pairs={{0,192},{8,200},{16,208},{24,216},{32,224},{40,232},{48,240},{56,2... | collective-permute-start | bytes 1179656 | tf_op jit(solution)/shard_map/ppermute | solution.py:49
  23.1 0.2 halves.2
  23.3 0.1 collective-permute-start.5
  23.6 2.7 %collective-permute-start.6 = (bf16[3,128,256]{2,1,0:T(8,128)(2,1)S(1)}, bf16[3,128,256]{2,1,0:T(8,128)(2,1)S(1)}, u32[]{:S(2)}, u32[]{:S(2)}) collective-permute-start(bf16[3,128,256]{2,1,0:T(8,128)(2,1)S(1)} %get-tuple-element.67), channel_id=1, source_target_pairs={{0,192},{8,200},{16,208},{24,216},{32,224},{40,232},{48,240},{56,2... | collective-permute-start | bytes 589832 | tf_op jit(solution)/shard_map/ppermute | solution.py:49
  26.3 3.9 %first.1 = (f32[3,2,1024,128]{3,2,1,0:T(8,128)S(1)}, f32[3,2,16,128]{3,2,1,0:T(8,128)S(1)}) custom-call(s32[3]{0:T(128)S(1)} %pad_add_fusion.where, bf16[3,256,256]{2,1,0:T(8,128)(2,1)} %copy-done.5, bf16[3,256,256]{2,1,0:T(8,128)(2,1)} %copy-done.1, bf16[3,256,256]{2,1,0:T(8,128)(2,1)} %copy-done.2, bf16[512,4096]{1,0:T(8,128)(2,1)} %refs_6_.1, ...), custom_call_target="tpu_custom_call" | custom-call | tf_op jit(solution)/shard_map/first/pallas_call | solution.py:295
  30.3 9.9 %collective-permute-done.8.refs_0_ = bf16[3,256,256]{2,1,0:T(8,128)(2,1)S(1)} collective-permute-done((bf16[3,256,256]{2,1,0:T(8,128)(2,1)S(1)}, bf16[3,256,256]{2,1,0:T(8,128)(2,1)S(1)}, u32[]{:S(2)}, u32[]{:S(2)}) %collective-permute-start.8) | collective-permute-done | bytes 393248 | tf_op jit(solution)/shard_map/ppermute | solution.py:49
  40.2 0.0 collective-permute-done.5.refs_3_
  40.2 0.0 collective-permute-done.6.refs_4_
  40.2 1.3 %collective-permute-start.13 = (bf16[3,256,256]{2,1,0:T(8,128)(2,1)S(1)}, bf16[3,256,256]{2,1,0:T(8,128)(2,1)S(1)}, u32[]{:S(2)}, u32[]{:S(2)}) collective-permute-start(bf16[3,256,256]{2,1,0:T(8,128)(2,1)S(1)} %collective-permute-done.8.refs_0_), channel_id=1, source_target_pairs={{0,64},{8,72},{16,80},{24,88},{32,96},{40,104},{48,112},{56,120},{... | collective-permute-start | bytes 1179656 | tf_op jit(solution)/shard_map/ppermute | solution.py:49
  41.5 1.5 %collective-permute-start.14 = (bf16[3,256,256]{2,1,0:T(8,128)(2,1)S(1)}, bf16[3,256,256]{2,1,0:T(8,128)(2,1)S(1)}, u32[]{:S(2)}, u32[]{:S(2)}) collective-permute-start(bf16[3,256,256]{2,1,0:T(8,128)(2,1)S(1)} %collective-permute-done.8.refs_0_), channel_id=1, source_target_pairs={{0,192},{8,200},{16,208},{24,216},{32,224},{40,232},{48,240},{56,2... | collective-permute-start | bytes 1179656 | tf_op jit(solution)/shard_map/ppermute | solution.py:49
  43.0 0.1 multiply_exponential_fusion.power
  43.1 0.0 copy-start.17
  43.1 0.0 copy-start.18
  43.1 0.0 collective-permute-done.15.refs_1_
  43.2 1.7 %collective-permute-start.21 = (bf16[3,128,256]{2,1,0:T(8,128)(2,1)S(1)}, bf16[3,128,256]{2,1,0:T(8,128)(2,1)S(1)}, u32[]{:S(2)}, u32[]{:S(2)}) collective-permute-start(bf16[3,128,256]{2,1,0:T(8,128)(2,1)S(1)} %collective-permute-done.5.refs_3_), channel_id=1, source_target_pairs={{0,16},{8,24},{16,0},{24,8},{32,48},{40,56},{48,32},{56,40},{64,80... | collective-permute-start | bytes 589832 | tf_op jit(solution)/shard_map/ppermute | solution.py:49
  44.9 0.0 collective-permute-done.16.refs_2_
  44.9 0.7 copy-done.9
  45.7 4.7 %second.1 = (f32[3,2,1024,128]{3,2,1,0:T(8,128)S(1)}, f32[3,2,16,128]{3,2,1,0:T(8,128)S(1)}) custom-call(s32[3]{0:T(128)S(1)} %pad_add_fusion.where, bf16[3,256,256]{2,1,0:T(8,128)(2,1)} %copy-done.7, bf16[3,256,256]{2,1,0:T(8,128)(2,1)} %copy-done.8, bf16[3,256,256]{2,1,0:T(8,128)(2,1)} %copy-done.9, bf16[3,128,256]{2,1,0:T(8,128)(2,1)} %copy-done.13, ...), custom_call_target="tpu_custom_call" | custom-call | tf_op jit(solution)/shard_map/second/pallas_call | solution.py:295
  50.4 1.3 %collective-permute-done.13.right.refs_1_ = bf16[3,256,256]{2,1,0:T(8,128)(2,1)S(1)} collective-permute-done((bf16[3,256,256]{2,1,0:T(8,128)(2,1)S(1)}, bf16[3,256,256]{2,1,0:T(8,128)(2,1)S(1)}, u32[]{:S(2)}, u32[]{:S(2)}) %collective-permute-start.13) | collective-permute-done | bytes 393248 | tf_op jit(solution)/shard_map/ppermute | solution.py:49
  51.7 0.2 halves.3
  51.9 1.0 %collective-permute-start.17 = (bf16[3,128,256]{2,1,0:T(8,128)(2,1)S(1)}, bf16[3,128,256]{2,1,0:T(8,128)(2,1)S(1)}, u32[]{:S(2)}, u32[]{:S(2)}) collective-permute-start(bf16[3,128,256]{2,1,0:T(8,128)(2,1)S(1)} %get-tuple-element.85), channel_id=1, source_target_pairs={{0,64},{8,72},{16,80},{24,88},{32,96},{40,104},{48,112},{56,120},{... | collective-permute-start | bytes 589832 | tf_op jit(solution)/shard_map/ppermute | solution.py:49
  52.8 1.8 %collective-permute-start.19 = (bf16[3,128,256]{2,1,0:T(8,128)(2,1)S(1)}, bf16[3,128,256]{2,1,0:T(8,128)(2,1)S(1)}, u32[]{:S(2)}, u32[]{:S(2)}) collective-permute-start(bf16[3,128,256]{2,1,0:T(8,128)(2,1)S(1)} %get-tuple-element.86), channel_id=1, source_target_pairs={{0,192},{8,200},{16,208},{24,216},{32,224},{40,232},{48,240},{56,2... | collective-permute-start | bytes 589832 | tf_op jit(solution)/shard_map/ppermute | solution.py:49
  54.7 2.7 %collective-permute-start.12 = (bf16[3,256,256]{2,1,0:T(8,128)(2,1)S(1)}, bf16[3,256,256]{2,1,0:T(8,128)(2,1)S(1)}, u32[]{:S(2)}, u32[]{:S(2)}) collective-permute-start(bf16[3,256,256]{2,1,0:T(8,128)(2,1)S(1)} %collective-permute-done.10.refs_3_), channel_id=1, source_target_pairs={{0,192},{8,200},{16,208},{24,216},{32,224},{40,232},{48,240},{56,2... | collective-permute-start | bytes 1179656 | tf_op jit(solution)/shard_map/ppermute | solution.py:49
  57.4 0.1 dynamic_slice.15
  57.5 0.1 collective-permute-start.22
  57.5 0.7 collective-permute-done.17.refs_4_
  58.2 0.8 collective-permute-start.18
  59.0 0.7 collective-permute-start.20
  59.8 6.1 %third.1 = (f32[3,2,1024,128]{3,2,1,0:T(8,128)S(1)}, f32[3,2,16,128]{3,2,1,0:T(8,128)S(1)}, bf16[1040,1024]{1,0:T(8,128)(2,1)S(1)}) custom-call(s32[3]{0:T(128)S(1)} %pad_add_fusion.where, bf16[3,256,256]{2,1,0:T(8,128)(2,1)} %copy-done.10, bf16[3,256,256]{2,1,0:T(8,128)(2,1)} %copy-done.3, bf16[3,256,256]{2,1,0:T(8,128)(2,1)} %copy-done.4, ...), custom_call_target="tpu_custom_call" | custom-call | tf_op jit(solution)/shard_map/third/pallas_call | solution.py:295
  65.9 4.2 %collective-permute-done.20.refs_3_ = bf16[3,128,256]{2,1,0:T(8,128)(2,1)S(1)} collective-permute-done((bf16[3,128,256]{2,1,0:T(8,128)(2,1)S(1)}, bf16[3,128,256]{2,1,0:T(8,128)(2,1)S(1)}, u32[]{:S(2)}, u32[]{:S(2)}) %collective-permute-start.20) | collective-permute-done | bytes 196640 | tf_op jit(solution)/shard_map/ppermute | solution.py:49
  70.1 5.0 %signals.1 = (f32[128,8,256]{2,1,0:T(8,128)S(1)}, f32[16,8,256]{2,1,0:T(8,128)S(1)}, f32[16,256]{1,0:T(8,128)S(1)}) custom-call(bf16[1040,1024]{1,0:T(8,128)(2,1)S(1)} %get-tuple-element.96.rows, bf16[3,256,256]{2,1,0:T(8,128)(2,1)S(1)} %collective-permute-done.11.refs_0_, bf16[3,256,256]{2,1,0:T(8,128)(2,1)S(1)} %collective-permute-done.12.refs_1_, ...), custom_call_target="tpu_custom_call" | custom-call | tf_op jit(solution)/shard_map/signals/pallas_call | solution.py:386
  75.1 0.4 collective-permute-start.23
  75.5 1.4 %collective-permute-start.24 = (f32[16,256]{1,0:T(8,128)S(1)}, f32[16,256]{1,0:T(8,128)S(1)}, u32[]{:S(2)}, u32[]{:S(2)}) collective-permute-start(f32[16,256]{1,0:T(8,128)S(1)} %get-tuple-element.115), channel_id=1, source_target_pairs={{0,32},{8,40},{16,48},{24,56},{32,0},{40,8},{48,16},{56,24},{64,96... | collective-permute-start | bytes 49160 | tf_op jit(solution)/shard_map/ppermute | solution.py:49
  76.8 1.6 %collective-permute-start.25 = (f32[16,256]{1,0:T(8,128)S(1)}, f32[16,256]{1,0:T(8,128)S(1)}, u32[]{:S(2)}, u32[]{:S(2)}) collective-permute-start(f32[16,256]{1,0:T(8,128)S(1)} %get-tuple-element.115), channel_id=1, source_target_pairs={{0,48},{8,56},{16,0},{24,8},{32,16},{40,24},{48,32},{56,40},{64,11... | collective-permute-start | bytes 49160 | tf_op jit(solution)/shard_map/ppermute | solution.py:49
  78.5 1.1 %collective-permute-done.23 = f32[16,256]{1,0:T(8,128)S(1)} collective-permute-done((f32[16,256]{1,0:T(8,128)S(1)}, f32[16,256]{1,0:T(8,128)S(1)}, u32[]{:S(2)}, u32[]{:S(2)}) %collective-permute-start.23) | collective-permute-done | bytes 16416 | tf_op jit(solution)/shard_map/ppermute | solution.py:49
  79.6 0.3 collective-permute-done.25
  79.9 0.1 collective-permute-start.26
  80.0 1.5 %collective-permute-start.27 = (f32[16,256]{1,0:T(8,128)S(1)}, f32[16,256]{1,0:T(8,128)S(1)}, u32[]{:S(2)}, u32[]{:S(2)}) collective-permute-start(f32[16,256]{1,0:T(8,128)S(1)} %fusion.2), channel_id=1, source_target_pairs={{0,128},{8,136},{16,144},{24,152},{32,160},{40,168},{48,176},{56,1... | collective-permute-start | bytes 49160 | tf_op jit(solution)/shard_map/ppermute | solution.py:49
  81.5 1.8 %collective-permute-start.28 = (f32[16,256]{1,0:T(8,128)S(1)}, f32[16,256]{1,0:T(8,128)S(1)}, u32[]{:S(2)}, u32[]{:S(2)}) collective-permute-start(f32[16,256]{1,0:T(8,128)S(1)} %fusion.2), channel_id=1, source_target_pairs={{0,192},{8,200},{16,208},{24,216},{32,224},{40,232},{48,240},{56,2... | collective-permute-start | bytes 49160 | tf_op jit(solution)/shard_map/ppermute | solution.py:49
  83.3 1.5 %queries.1 = (f32[128,8,256]{2,1,0:T(8,128)S(1)}, f32[128,8,256]{2,1,0:T(8,128)S(1)}) custom-call(bf16[1040,1024]{1,0:T(8,128)(2,1)S(1)} %get-tuple-element.96.rows, bf16[3,256,256]{2,1,0:T(8,128)(2,1)S(1)} %collective-permute-done.11.refs_0_, bf16[3,256,256]{2,1,0:T(8,128)(2,1)S(1)} %collective-permute-done.12.refs_1_, ...), custom_call_target="tpu_custom_call" | custom-call | tf_op jit(solution)/shard_map/queries/pallas_call | solution.py:430
  84.8 1.9 %gated.1 = (bf16[512,256]{1,0:T(8,128)(2,1)S(1)}, bf16[512,256]{1,0:T(8,128)(2,1)S(1)}) custom-call(s32[3]{0:T(128)S(1)} %pad_add_fusion.where, f32[128,8,256]{2,1,0:T(8,128)S(1)} %get-tuple-element.111.query, f32[128,8,256]{2,1,0:T(8,128)S(1)} %get-tuple-element.112.gated, f32[16,8,256]{2,1,0:T(8,128)S(1)} %get-tuple-element.113.before, ...), custom_call_target="tpu_custom_call" | custom-call | tf_op jit(solution)/shard_map/gated/pallas_call | solution.py:496
  86.7 6.1 %collective-permute-start.29 = (bf16[512,256]{1,0:T(8,128)(2,1)S(1)}, bf16[512,256]{1,0:T(8,128)(2,1)S(1)}, u32[]{:S(2)}, u32[]{:S(2)}) collective-permute-start(bf16[512,256]{1,0:T(8,128)(2,1)S(1)} %get-tuple-element.118), channel_id=1, source_target_pairs={{0,8},{8,0},{16,24},{24,16},{32,40},{40,32},{48,56},{56,48},{64,72... | collective-permute-start | bytes 786440 | tf_op jit(solution)/shard_map/ppermute | solution.py:49
  92.8 1.2 %collective-permute-done.29 = bf16[512,256]{1,0:T(8,128)(2,1)S(1)} collective-permute-done((bf16[512,256]{1,0:T(8,128)(2,1)S(1)}, bf16[512,256]{1,0:T(8,128)(2,1)S(1)}, u32[]{:S(2)}, u32[]{:S(2)}) %collective-permute-start.29) | collective-permute-done | bytes 262176 | tf_op jit(solution)/shard_map/ppermute | solution.py:49
  94.0 0.8 pad_maximum_fusion
  (70 shorter events, 0.4 us)
Async XLA Ops:
  0.0 43.0 %copy-start = (f32[3,7,512]{2,1,0:T(8,128)S(1)}, f32[3,7,512]{2,1,0:T(8,128)}, u32[]{:S(2)}) copy-start(f32[3,7,512]{2,1,0:T(8,128)} %param.8) | copy-start | bytes 129028
  0.0 23.1 %copy-start.16 = (f32[512,16]{0,1:T(8,128)S(1)}, f32[512,16]{0,1:T(8,128)}, u32[]{:S(2)}) copy-start(f32[512,16]{0,1:T(8,128)} %param.10) | copy-start | bytes 98308
  1.1 4.4 %collective-permute-start = (bf16[3,128,256]{2,1,0:T(8,128)(2,1)S(1)}, bf16[3,128,256]{2,1,0:T(8,128)(2,1)S(1)}, u32[]{:S(2)}, u32[]{:S(2)}) collective-permute-start(bf16[3,128,256]{2,1,0:T(8,128)(2,1)S(1)} %broadcast_select_fusion.4), channel_id=1, source_target_pairs={{0,8},{8,0},{16,24},{24,16},{32,40},{40,32},{48,56},{56,48},{64,72... | collective-permute-start | bytes 589832 | tf_op jit(solution)/shard_map/ppermute | solution.py:49
  5.5 14.9 %collective-permute-start.4 = (bf16[512,4096]{1,0:T(8,128)(2,1)}, bf16[512,4096]{1,0:T(8,128)(2,1)}, u32[]{:S(2)}, u32[]{:S(2)}) collective-permute-start(bf16[512,4096]{1,0:T(8,128)(2,1)} %refs_6_.1), channel_id=1, source_target_pairs={{0,8},{8,0},{16,24},{24,16},{32,40},{40,32},{48,56},{56,48},{64,72... | collective-permute-start | bytes 12582920 | tf_op jit(solution)/shard_map/ppermute | solution.py:49
  6.9 19.4 %copy-start.5 = (bf16[3,256,256]{2,1,0:T(8,128)(2,1)}, bf16[3,256,256]{2,1,0:T(8,128)(2,1)S(1)}, u32[]{:S(2)}) copy-start(bf16[3,256,256]{2,1,0:T(8,128)(2,1)S(1)} %pad_maximum_fusion.1.refs_0_) | copy-start | bytes 1179652
  8.0 4.8 %collective-permute-start.7 = (bf16[16,4096]{1,0:T(8,128)(2,1)S(1)}, bf16[16,4096]{1,0:T(8,128)(2,1)S(1)}, u32[]{:S(2)}, u32[]{:S(2)}) collective-permute-start(bf16[16,4096]{1,0:T(8,128)(2,1)S(1)} %slice.54), channel_id=1, source_target_pairs={{0,8},{8,0},{16,24},{24,16},{32,40},{40,32},{48,56},{56,48},{64,72... | collective-permute-start | bytes 393224 | tf_op jit(solution)/shard_map/ppermute | solution.py:49
  8.3 10.4 %collective-permute-start.1 = (bf16[3,256,256]{2,1,0:T(8,128)(2,1)S(1)}, bf16[3,256,256]{2,1,0:T(8,128)(2,1)S(1)}, u32[]{:S(2)}, u32[]{:S(2)}) collective-permute-start(bf16[3,256,256]{2,1,0:T(8,128)(2,1)S(1)} %pad_maximum_fusion.1.refs_0_), channel_id=1, source_target_pairs={{0,16},{8,24},{16,0},{24,8},{32,48},{40,56},{48,32},{56,40},{64,80... | collective-permute-start | bytes 1179656 | tf_op jit(solution)/shard_map/ppermute | solution.py:49
  8.4 11.9 %collective-permute-start.2 = (bf16[3,256,256]{2,1,0:T(8,128)(2,1)S(1)}, bf16[3,256,256]{2,1,0:T(8,128)(2,1)S(1)}, u32[]{:S(2)}, u32[]{:S(2)}) collective-permute-start(bf16[3,256,256]{2,1,0:T(8,128)(2,1)S(1)} %pad_maximum_fusion.1.refs_0_), channel_id=1, source_target_pairs={{0,64},{8,72},{16,80},{24,88},{32,96},{40,104},{48,112},{56,120},{... | collective-permute-start | bytes 1179656 | tf_op jit(solution)/shard_map/ppermute | solution.py:49
  9.5 10.9 %collective-permute-start.3 = (bf16[3,256,256]{2,1,0:T(8,128)(2,1)S(1)}, bf16[3,256,256]{2,1,0:T(8,128)(2,1)S(1)}, u32[]{:S(2)}, u32[]{:S(2)}) collective-permute-start(bf16[3,256,256]{2,1,0:T(8,128)(2,1)S(1)} %pad_maximum_fusion.1.refs_0_), channel_id=1, source_target_pairs={{0,192},{8,200},{16,208},{24,216},{32,224},{40,232},{48,240},{56,2... | collective-permute-start | bytes 1179656 | tf_op jit(solution)/shard_map/ppermute | solution.py:49
  13.7 9.8 %collective-permute-start.9 = (bf16[16,4096]{1,0:T(8,128)(2,1)S(1)}, bf16[16,4096]{1,0:T(8,128)(2,1)S(1)}, u32[]{:S(2)}, u32[]{:S(2)}) collective-permute-start(bf16[16,4096]{1,0:T(8,128)(2,1)S(1)} %broadcast_select_fusion.5), channel_id=1, source_target_pairs={{0,16},{8,24},{16,32},{24,40},{32,48},{40,56},{48,64},{56,72},{64,... | collective-permute-start | bytes 393224 | tf_op jit(solution)/shard_map/ppermute | solution.py:49
  18.7 26.2 %copy-start.7 = (bf16[3,256,256]{2,1,0:T(8,128)(2,1)}, bf16[3,256,256]{2,1,0:T(8,128)(2,1)S(1)}, u32[]{:S(2)}) copy-start(bf16[3,256,256]{2,1,0:T(8,128)(2,1)S(1)} %collective-permute-done.1.refs_0_) | copy-start | bytes 1179652
  18.7 21.5 %collective-permute-start.8 = (bf16[3,256,256]{2,1,0:T(8,128)(2,1)S(1)}, bf16[3,256,256]{2,1,0:T(8,128)(2,1)S(1)}, u32[]{:S(2)}, u32[]{:S(2)}) collective-permute-start(bf16[3,256,256]{2,1,0:T(8,128)(2,1)S(1)} %pad_maximum_fusion.1.refs_0_), channel_id=1, source_target_pairs={{0,32},{8,40},{16,48},{24,56},{32,0},{40,8},{48,16},{56,24},{64,96... | collective-permute-start | bytes 1179656 | tf_op jit(solution)/shard_map/ppermute | solution.py:49
  20.3 6.0 %copy-start.1 = (bf16[3,256,256]{2,1,0:T(8,128)(2,1)}, bf16[3,256,256]{2,1,0:T(8,128)(2,1)S(1)}, u32[]{:S(2)}) copy-start(bf16[3,256,256]{2,1,0:T(8,128)(2,1)S(1)} %collective-permute-done.2.right.refs_1_) | copy-start | bytes 1179652
  20.3 6.0 %copy-start.2 = (bf16[3,256,256]{2,1,0:T(8,128)(2,1)}, bf16[3,256,256]{2,1,0:T(8,128)(2,1)S(1)}, u32[]{:S(2)}) copy-start(bf16[3,256,256]{2,1,0:T(8,128)(2,1)S(1)} %collective-permute-done.3.left.refs_2_) | copy-start | bytes 1179652
  20.3 22.8 %collective-permute-start.15 = (bf16[3,256,256]{2,1,0:T(8,128)(2,1)S(1)}, bf16[3,256,256]{2,1,0:T(8,128)(2,1)S(1)}, u32[]{:S(2)}, u32[]{:S(2)}) collective-permute-start(bf16[3,256,256]{2,1,0:T(8,128)(2,1)S(1)} %collective-permute-done.1.refs_0_), channel_id=1, source_target_pairs={{0,64},{8,72},{16,80},{24,88},{32,96},{40,104},{48,112},{56,120},{... | collective-permute-start | bytes 1179656 | tf_op jit(solution)/shard_map/ppermute | solution.py:49
  21.6 23.3 %collective-permute-start.16 = (bf16[3,256,256]{2,1,0:T(8,128)(2,1)S(1)}, bf16[3,256,256]{2,1,0:T(8,128)(2,1)S(1)}, u32[]{:S(2)}, u32[]{:S(2)}) collective-permute-start(bf16[3,256,256]{2,1,0:T(8,128)(2,1)S(1)} %collective-permute-done.1.refs_0_), channel_id=1, source_target_pairs={{0,192},{8,200},{16,208},{24,216},{32,224},{40,232},{48,240},{56,2... | collective-permute-start | bytes 1179656 | tf_op jit(solution)/shard_map/ppermute | solution.py:49
  23.3 16.8 %collective-permute-start.5 = (bf16[3,128,256]{2,1,0:T(8,128)(2,1)S(1)}, bf16[3,128,256]{2,1,0:T(8,128)(2,1)S(1)}, u32[]{:S(2)}, u32[]{:S(2)}) collective-permute-start(bf16[3,128,256]{2,1,0:T(8,128)(2,1)S(1)} %get-tuple-element.66), channel_id=1, source_target_pairs={{0,64},{8,72},{16,80},{24,88},{32,96},{40,104},{48,112},{56,120},{... | collective-permute-start | bytes 589832 | tf_op jit(solution)/shard_map/ppermute | solution.py:49
  23.5 2.8 %copy-start.6 = (bf16[16,4096]{1,0:T(8,128)(2,1)}, bf16[16,4096]{1,0:T(8,128)(2,1)S(1)}, u32[]{:S(2)}) copy-start(bf16[16,4096]{1,0:T(8,128)(2,1)S(1)} %collective-permute-done.9.refs_5_.refs_7_.refs_8_) | copy-start | bytes 393220
  23.6 16.6 %collective-permute-start.6 = (bf16[3,128,256]{2,1,0:T(8,128)(2,1)S(1)}, bf16[3,128,256]{2,1,0:T(8,128)(2,1)S(1)}, u32[]{:S(2)}, u32[]{:S(2)}) collective-permute-start(bf16[3,128,256]{2,1,0:T(8,128)(2,1)S(1)} %get-tuple-element.67), channel_id=1, source_target_pairs={{0,192},{8,200},{16,208},{24,216},{32,224},{40,232},{48,240},{56,2... | collective-permute-start | bytes 589832 | tf_op jit(solution)/shard_map/ppermute | solution.py:49
  40.2 19.5 %copy-start.10 = (bf16[3,256,256]{2,1,0:T(8,128)(2,1)}, bf16[3,256,256]{2,1,0:T(8,128)(2,1)S(1)}, u32[]{:S(2)}) copy-start(bf16[3,256,256]{2,1,0:T(8,128)(2,1)S(1)} %collective-permute-done.8.refs_0_) | copy-start | bytes 1179652
  40.2 4.7 %copy-start.13 = (bf16[3,128,256]{2,1,0:T(8,128)(2,1)}, bf16[3,128,256]{2,1,0:T(8,128)(2,1)S(1)}, u32[]{:S(2)}) copy-start(bf16[3,128,256]{2,1,0:T(8,128)(2,1)S(1)} %collective-permute-done.5.refs_3_) | copy-start | bytes 589828
  40.2 4.7 %copy-start.12 = (bf16[3,128,256]{2,1,0:T(8,128)(2,1)}, bf16[3,128,256]{2,1,0:T(8,128)(2,1)S(1)}, u32[]{:S(2)}) copy-start(bf16[3,128,256]{2,1,0:T(8,128)(2,1)S(1)} %collective-permute-done.6.refs_4_) | copy-start | bytes 589828
  40.2 11.5 %collective-permute-start.13 = (bf16[3,256,256]{2,1,0:T(8,128)(2,1)S(1)}, bf16[3,256,256]{2,1,0:T(8,128)(2,1)S(1)}, u32[]{:S(2)}, u32[]{:S(2)}) collective-permute-start(bf16[3,256,256]{2,1,0:T(8,128)(2,1)S(1)} %collective-permute-done.8.refs_0_), channel_id=1, source_target_pairs={{0,64},{8,72},{16,80},{24,88},{32,96},{40,104},{48,112},{56,120},{... | collective-permute-start | bytes 1179656 | tf_op jit(solution)/shard_map/ppermute | solution.py:49
  41.5 10.2 %collective-permute-start.14 = (bf16[3,256,256]{2,1,0:T(8,128)(2,1)S(1)}, bf16[3,256,256]{2,1,0:T(8,128)(2,1)S(1)}, u32[]{:S(2)}, u32[]{:S(2)}) collective-permute-start(bf16[3,256,256]{2,1,0:T(8,128)(2,1)S(1)} %collective-permute-done.8.refs_0_), channel_id=1, source_target_pairs={{0,192},{8,200},{16,208},{24,216},{32,224},{40,232},{48,240},{56,2... | collective-permute-start | bytes 1179656 | tf_op jit(solution)/shard_map/ppermute | solution.py:49
  43.0 11.7 %collective-permute-start.10 = (bf16[3,256,256]{2,1,0:T(8,128)(2,1)S(1)}, bf16[3,256,256]{2,1,0:T(8,128)(2,1)S(1)}, u32[]{:S(2)}, u32[]{:S(2)}) collective-permute-start(bf16[3,256,256]{2,1,0:T(8,128)(2,1)S(1)} %collective-permute-done.8.refs_0_), channel_id=1, source_target_pairs={{0,16},{8,24},{16,0},{24,8},{32,48},{40,56},{48,32},{56,40},{64,80... | collective-permute-start | bytes 1179656 | tf_op jit(solution)/shard_map/ppermute | solution.py:49
  43.1 14.2 %copy-start.17 = (f32[512,16]{0,1:T(8,128)S(1)}, f32[512,16]{0,1:T(8,128)}, u32[]{:S(2)}) copy-start(f32[512,16]{0,1:T(8,128)} %param.9) | copy-start | bytes 98308
  43.1 14.2 %copy-start.18 = (f32[512]{0:T(512)S(1)}, f32[512]{0:T(512)}, u32[]{:S(2)}) copy-start(f32[512]{0:T(512)} %param.11) | copy-start | bytes 6148
  43.1 1.8 %copy-start.8 = (bf16[3,256,256]{2,1,0:T(8,128)(2,1)}, bf16[3,256,256]{2,1,0:T(8,128)(2,1)S(1)}, u32[]{:S(2)}) copy-start(bf16[3,256,256]{2,1,0:T(8,128)(2,1)S(1)} %collective-permute-done.15.refs_1_) | copy-start | bytes 1179652
  43.2 14.3 %collective-permute-start.21 = (bf16[3,128,256]{2,1,0:T(8,128)(2,1)S(1)}, bf16[3,128,256]{2,1,0:T(8,128)(2,1)S(1)}, u32[]{:S(2)}, u32[]{:S(2)}) collective-permute-start(bf16[3,128,256]{2,1,0:T(8,128)(2,1)S(1)} %collective-permute-done.5.refs_3_), channel_id=1, source_target_pairs={{0,16},{8,24},{16,0},{24,8},{32,48},{40,56},{48,32},{56,40},{64,80... | collective-permute-start | bytes 589832 | tf_op jit(solution)/shard_map/ppermute | solution.py:49
  44.9 0.7 copy-start.9
  51.7 8.0 %copy-start.3 = (bf16[3,256,256]{2,1,0:T(8,128)(2,1)}, bf16[3,256,256]{2,1,0:T(8,128)(2,1)S(1)}, u32[]{:S(2)}) copy-start(bf16[3,256,256]{2,1,0:T(8,128)(2,1)S(1)} %collective-permute-done.13.right.refs_1_) | copy-start | bytes 1179652
  51.7 8.1 %copy-start.4 = (bf16[3,256,256]{2,1,0:T(8,128)(2,1)}, bf16[3,256,256]{2,1,0:T(8,128)(2,1)S(1)}, u32[]{:S(2)}) copy-start(bf16[3,256,256]{2,1,0:T(8,128)(2,1)S(1)} %collective-permute-done.14.left.refs_2_) | copy-start | bytes 1179652
  51.9 6.3 %collective-permute-start.17 = (bf16[3,128,256]{2,1,0:T(8,128)(2,1)S(1)}, bf16[3,128,256]{2,1,0:T(8,128)(2,1)S(1)}, u32[]{:S(2)}, u32[]{:S(2)}) collective-permute-start(bf16[3,128,256]{2,1,0:T(8,128)(2,1)S(1)} %get-tuple-element.85), channel_id=1, source_target_pairs={{0,64},{8,72},{16,80},{24,88},{32,96},{40,104},{48,112},{56,120},{... | collective-permute-start | bytes 589832 | tf_op jit(solution)/shard_map/ppermute | solution.py:49
  52.8 6.2 %collective-permute-start.19 = (bf16[3,128,256]{2,1,0:T(8,128)(2,1)S(1)}, bf16[3,128,256]{2,1,0:T(8,128)(2,1)S(1)}, u32[]{:S(2)}, u32[]{:S(2)}) collective-permute-start(bf16[3,128,256]{2,1,0:T(8,128)(2,1)S(1)} %get-tuple-element.86), channel_id=1, source_target_pairs={{0,192},{8,200},{16,208},{24,216},{32,224},{40,232},{48,240},{56,2... | collective-permute-start | bytes 589832 | tf_op jit(solution)/shard_map/ppermute | solution.py:49
  54.7 5.1 %copy-start.11 = (bf16[3,256,256]{2,1,0:T(8,128)(2,1)}, bf16[3,256,256]{2,1,0:T(8,128)(2,1)S(1)}, u32[]{:S(2)}) copy-start(bf16[3,256,256]{2,1,0:T(8,128)(2,1)S(1)} %collective-permute-done.10.refs_3_) | copy-start | bytes 1179652
  54.7 15.5 %collective-permute-start.11 = (bf16[3,256,256]{2,1,0:T(8,128)(2,1)S(1)}, bf16[3,256,256]{2,1,0:T(8,128)(2,1)S(1)}, u32[]{:S(2)}, u32[]{:S(2)}) collective-permute-start(bf16[3,256,256]{2,1,0:T(8,128)(2,1)S(1)} %collective-permute-done.10.refs_3_), channel_id=1, source_target_pairs={{0,64},{8,72},{16,80},{24,88},{32,96},{40,104},{48,112},{56,120},{... | collective-permute-start | bytes 1179656 | tf_op jit(solution)/shard_map/ppermute | solution.py:49
  54.7 15.5 %collective-permute-start.12 = (bf16[3,256,256]{2,1,0:T(8,128)(2,1)S(1)}, bf16[3,256,256]{2,1,0:T(8,128)(2,1)S(1)}, u32[]{:S(2)}, u32[]{:S(2)}) collective-permute-start(bf16[3,256,256]{2,1,0:T(8,128)(2,1)S(1)} %collective-permute-done.10.refs_3_), channel_id=1, source_target_pairs={{0,192},{8,200},{16,208},{24,216},{32,224},{40,232},{48,240},{56,2... | collective-permute-start | bytes 1179656 | tf_op jit(solution)/shard_map/ppermute | solution.py:49
  57.5 8.4 %collective-permute-start.22 = (bf16[3,128,256]{2,1,0:T(8,128)(2,1)}, bf16[3,128,256]{2,1,0:T(8,128)(2,1)S(1)}, u32[]{:S(2)}, u32[]{:S(2)}) collective-permute-start(bf16[3,128,256]{2,1,0:T(8,128)(2,1)} %copy-done.12), channel_id=1, source_target_pairs={{0,16},{8,24},{16,0},{24,8},{32,48},{40,56},{48,32},{56,40},{64,80... | collective-permute-start | bytes 589832 | tf_op jit(solution)/shard_map/ppermute | solution.py:49
  58.2 1.5 %copy-start.14 = (bf16[3,128,256]{2,1,0:T(8,128)(2,1)}, bf16[3,128,256]{2,1,0:T(8,128)(2,1)S(1)}, u32[]{:S(2)}) copy-start(bf16[3,128,256]{2,1,0:T(8,128)(2,1)S(1)} %collective-permute-done.17.refs_4_) | copy-start | bytes 589828
  58.2 7.7 %collective-permute-start.18 = (bf16[3,128,256]{2,1,0:T(8,128)(2,1)S(1)}, bf16[3,128,256]{2,1,0:T(8,128)(2,1)S(1)}, u32[]{:S(2)}, u32[]{:S(2)}) collective-permute-start(bf16[3,128,256]{2,1,0:T(8,128)(2,1)S(1)} %collective-permute-done.17.refs_4_), channel_id=1, source_target_pairs={{0,16},{8,24},{16,0},{24,8},{32,48},{40,56},{48,32},{56,40},{64,80... | collective-permute-start | bytes 589832 | tf_op jit(solution)/shard_map/ppermute | solution.py:49
  59.0 0.8 copy-start.15
  59.0 11.1 %collective-permute-start.20 = (bf16[3,128,256]{2,1,0:T(8,128)(2,1)S(1)}, bf16[3,128,256]{2,1,0:T(8,128)(2,1)S(1)}, u32[]{:S(2)}, u32[]{:S(2)}) collective-permute-start(bf16[3,128,256]{2,1,0:T(8,128)(2,1)S(1)} %collective-permute-done.19.refs_5_), channel_id=1, source_target_pairs={{0,16},{8,24},{16,0},{24,8},{32,48},{40,56},{48,32},{56,40},{64,80... | collective-permute-start | bytes 589832 | tf_op jit(solution)/shard_map/ppermute | solution.py:49
  75.1 4.5 %collective-permute-start.23 = (f32[16,256]{1,0:T(8,128)S(1)}, f32[16,256]{1,0:T(8,128)S(1)}, u32[]{:S(2)}, u32[]{:S(2)}) collective-permute-start(f32[16,256]{1,0:T(8,128)S(1)} %get-tuple-element.115), channel_id=1, source_target_pairs={{0,16},{8,24},{16,32},{24,40},{32,48},{40,56},{48,0},{56,8},{64,80... | collective-permute-start | bytes 49160 | tf_op jit(solution)/shard_map/ppermute | solution.py:49
  75.5 4.1 %collective-permute-start.24 = (f32[16,256]{1,0:T(8,128)S(1)}, f32[16,256]{1,0:T(8,128)S(1)}, u32[]{:S(2)}, u32[]{:S(2)}) collective-permute-start(f32[16,256]{1,0:T(8,128)S(1)} %get-tuple-element.115), channel_id=1, source_target_pairs={{0,32},{8,40},{16,48},{24,56},{32,0},{40,8},{48,16},{56,24},{64,96... | collective-permute-start | bytes 49160 | tf_op jit(solution)/shard_map/ppermute | solution.py:49
  76.8 3.0 %collective-permute-start.25 = (f32[16,256]{1,0:T(8,128)S(1)}, f32[16,256]{1,0:T(8,128)S(1)}, u32[]{:S(2)}, u32[]{:S(2)}) collective-permute-start(f32[16,256]{1,0:T(8,128)S(1)} %get-tuple-element.115), channel_id=1, source_target_pairs={{0,48},{8,56},{16,0},{24,8},{32,16},{40,24},{48,32},{56,40},{64,11... | collective-permute-start | bytes 49160 | tf_op jit(solution)/shard_map/ppermute | solution.py:49
  79.9 4.8 %collective-permute-start.26 = (f32[16,256]{1,0:T(8,128)S(1)}, f32[16,256]{1,0:T(8,128)S(1)}, u32[]{:S(2)}, u32[]{:S(2)}) collective-permute-start(f32[16,256]{1,0:T(8,128)S(1)} %fusion.2), channel_id=1, source_target_pairs={{0,64},{8,72},{16,80},{24,88},{32,96},{40,104},{48,112},{56,120},{... | collective-permute-start | bytes 49160 | tf_op jit(solution)/shard_map/ppermute | solution.py:49
  80.0 4.8 %collective-permute-start.27 = (f32[16,256]{1,0:T(8,128)S(1)}, f32[16,256]{1,0:T(8,128)S(1)}, u32[]{:S(2)}, u32[]{:S(2)}) collective-permute-start(f32[16,256]{1,0:T(8,128)S(1)} %fusion.2), channel_id=1, source_target_pairs={{0,128},{8,136},{16,144},{24,152},{32,160},{40,168},{48,176},{56,1... | collective-permute-start | bytes 49160 | tf_op jit(solution)/shard_map/ppermute | solution.py:49
  81.5 3.2 %collective-permute-start.28 = (f32[16,256]{1,0:T(8,128)S(1)}, f32[16,256]{1,0:T(8,128)S(1)}, u32[]{:S(2)}, u32[]{:S(2)}) collective-permute-start(f32[16,256]{1,0:T(8,128)S(1)} %fusion.2), channel_id=1, source_target_pairs={{0,192},{8,200},{16,208},{24,216},{32,224},{40,232},{48,240},{56,2... | collective-permute-start | bytes 49160 | tf_op jit(solution)/shard_map/ppermute | solution.py:49
  86.7 7.2 %collective-permute-start.29 = (bf16[512,256]{1,0:T(8,128)(2,1)S(1)}, bf16[512,256]{1,0:T(8,128)(2,1)S(1)}, u32[]{:S(2)}, u32[]{:S(2)}) collective-permute-start(bf16[512,256]{1,0:T(8,128)(2,1)S(1)} %get-tuple-element.118), channel_id=1, source_target_pairs={{0,8},{8,0},{16,24},{24,16},{32,40},{40,32},{48,56},{56,48},{64,72... | collective-permute-start | bytes 786440 | tf_op jit(solution)/shard_map/ppermute | solution.py:49
